TPU v7x, 32 devices: a whole 2x2x4 slice. The times are simulated.
32 devices in a mesh: tile: 4 (over z), img: 8 (over y, x, core).
Axes of the slice: x: 2, y: 2, z: 4, core: 2. Of those that a mesh axis runs over, the one named last changes fastest.
Arguments:
- qkv: bfloat16 [8, 4, 8, 32, 1536], P('img', 'tile'), may hold values from -6 to 6
- cotangent: bfloat16 [8, 4, 8, 32, 1024], P('img', 'tile'), may hold values from -48 to 48
- dw_weight: float32 [25, 1536], replicated, may hold values from -1.25 to 1.25
- pw_weight: float32 [32, 1536], replicated, may hold values from -1 to 1
- tile_image: int32 [8, 4], P('img', 'tile'), may hold values from 0 to 2, as said below
- tile_row: int32 [8, 4], P('img', 'tile'), may hold values from 0 to 1, as said below
- tile_col: int32 [8, 4], P('img', 'tile'), may hold values from 0 to 1, as said below
- image_height: int32 [8, 2], P('img'), may hold values from 0 to 2, as said below
- image_width: int32 [8, 2], P('img'), may hold values from 0 to 2, as said below
Outputs:
- grad_qkv: bfloat16 [8, 4, 8, 32, 1536], P('img', 'tile')
- grad_dw: float32 [25, 1536], replicated
- grad_pw: float32 [32, 1536], replicated
Inputs may be any that keep to these rules, and one draw needn't show every extreme that they name: Within a group tile_image never falls; each image occupies height * width consecutive tiles; padding tiles come last; the first group holds 2 images of 1 x 2 tiles; the second group holds one image of 2 x 2 tiles. `tile_row`: the tile's row in its image's grid, row-major order; 0 on padding tiles. `tile_col`: the tile's column in its image's grid; 0 on padding tiles. `image_height`: used slots come first; an unused slot has height 0. `image_width`: used slots come first; an unused slot has width 0.
All inputs are finite; a program needn't handle non-finite values.
Results may differ from a plain program's by a relative error of at most 0.005.
Values may be sent and summed in bfloat16 or wider, within the bound.
No kernel may reach another device: no remote copies, remote signals or barrier semaphores. Data moves between devices by JAX's collectives and lax.ppermute only.
A program may use at most 64 MiB of HBM per device.

v0:
```python
import math

import jax
import jax.numpy as jnp
from jax import lax
from jax.sharding import PartitionSpec as P

PRECISE = lax.Precision.HIGHEST
EPSILON = 1e-06


def from_behind(value, axis, steps):
    count = lax.axis_size(axis)
    initial, last = (max(0, -steps), min(count, count - steps))
    return lax.ppermute(value, axis, [(source, source + steps) for source in range(initial, last)])


def shortened(x):

    def short(part):
        return part.astype(jnp.bfloat16) if part.dtype == jnp.float32 else part

    return jax.tree.map(short, x)


def widen_source(field, neighbours, image_wide):
    has_left, has_right, has_above, has_below = neighbours
    nothing = jnp.zeros((), field.dtype)
    side_cols = []
    for offset, outgoing in ((1, field[:, -2:]), (-1, field[:, :2])):
        side_cols.append(from_behind(outgoing, "tile", offset))
    widened = jnp.concatenate(
        [
            jnp.where(has_left, side_cols[0], nothing),
            field,
            jnp.where(has_right, side_cols[1], nothing),
        ],
        axis=1,
    )
    edge_rows = []
    for offset, outgoing in (
        (1, widened[-2:]),
        (2, widened[-2:]),
        (-1, widened[:2]),
        (-2, widened[:2]),
    ):
        edge_rows.append(from_behind(outgoing, "tile", offset))
    above_rows = jnp.where(image_wide == 1, edge_rows[0], edge_rows[1])
    below_rows = jnp.where(image_wide == 1, edge_rows[2], edge_rows[3])
    return jnp.concatenate(
        [
            jnp.where(has_above, above_rows, nothing),
            widened,
            jnp.where(has_below, below_rows, nothing),
        ],
        axis=0,
    )


def widen_grad(field, neighbours, image_wide):
    has_left, has_right, has_above, has_below = neighbours
    nothing = jnp.zeros((), field.dtype)
    side_cols = []
    for offset, outgoing in ((1, field[:, -2:]), (-1, field[:, :2])):
        side_cols.append(from_behind(shortened(outgoing), "tile", offset).astype(outgoing.dtype))
    widened = jnp.concatenate(
        [
            jnp.where(has_left, side_cols[0], nothing),
            field,
            jnp.where(has_right, side_cols[1], nothing),
        ],
        axis=1,
    )
    edge_rows = []
    for offset, outgoing in (
        (1, widened[-2:]),
        (2, widened[-2:]),
        (-1, widened[:2]),
        (-2, widened[:2]),
    ):
        edge_rows.append(from_behind(shortened(outgoing), "tile", offset).astype(outgoing.dtype))
    above_rows = jnp.where(image_wide == 1, edge_rows[0], edge_rows[1])
    below_rows = jnp.where(image_wide == 1, edge_rows[2], edge_rows[3])
    return jnp.concatenate(
        [
            jnp.where(has_above, above_rows, nothing),
            widened,
            jnp.where(has_below, below_rows, nothing),
        ],
        axis=0,
    )


def depthwise(padded, kernel, flipped):
    channels = padded.shape[2]
    shaped = kernel.reshape(5, 5, 1, channels)
    if flipped:
        shaped = shaped[::-1, ::-1]
    result = lax.conv_general_dilated(
        padded[None],
        shaped,
        (1, 1),
        "VALID",
        dimension_numbers=("NHWC", "HWIO", "NHWC"),
        feature_group_count=channels,
        precision=PRECISE,
    )
    return result[0]


def kernel_grad(padded, kernel, grad_mixed):

    def local_conv(weights):
        return depthwise(padded, weights, False)

    pullback = jax.vjp(local_conv, kernel)[1]
    return pullback(grad_mixed)[0]


def block_weights(pw_weight):
    head_dim, channels = pw_weight.shape
    per_block = 128 // head_dim
    nblocks = channels // 128
    pieces = pw_weight.reshape(head_dim, nblocks, per_block, head_dim).transpose(1, 0, 2, 3)
    identity = jnp.eye(per_block, dtype=jnp.float32)
    blocked = pieces[:, None, :, :, :] * identity[None, :, None, :, None]
    return blocked.reshape(nblocks, 128, 128)


def pointwise(flat, blocks, backward):
    positions, channels = flat.shape
    shaped = flat.reshape(positions, channels // 128, 128)
    if backward:
        result = jnp.einsum("pbo,bio->pbi", shaped, blocks, precision=PRECISE)
    else:
        result = jnp.einsum("pbi,bio->pbo", shaped, blocks, precision=PRECISE)
    return result.reshape(positions, channels)


def block_grad(flat_mixed, grad_merged, head_dim):
    positions, channels = flat_mixed.shape
    nblocks = channels // 128
    per_block = 128 // head_dim
    blocked = jnp.einsum(
        "pbi,pbo->bio",
        flat_mixed.reshape(positions, nblocks, 128),
        grad_merged.reshape(positions, nblocks, 128),
        precision=PRECISE,
    )
    blocked = blocked.reshape(nblocks, per_block, head_dim, per_block, head_dim)
    diagonal = jnp.einsum(
        "bgiho,gh->ibho", blocked, jnp.eye(per_block, dtype=jnp.float32), precision=PRECISE
    )
    return diagonal.reshape(head_dim, channels)


def head_parts(flat, head_count):
    positions = flat.shape[0]
    third = flat.shape[1] // 3
    return [
        flat[:, member * third : (member + 1) * third].reshape(
            positions, head_count, third // head_count
        )
        for member in range(3)
    ]


def image_total(states, key_sums, image_slot, slot_count):
    picker = (jnp.arange(slot_count) == image_slot).astype(jnp.float32)
    spread_states = picker[:, None, None, None] * states[None]
    spread_sums = picker[:, None, None] * key_sums[None]
    summed_states, summed_sums = lax.psum((spread_states, spread_sums), "tile")
    return (
        jnp.sum(picker[:, None, None, None] * summed_states, axis=0),
        jnp.sum(picker[:, None, None] * summed_sums, axis=0),
    )


def local(
    qkv, cotangent, dw_weight, pw_weight, tile_image, tile_row, tile_col, image_height, image_width
):
    tile_tall, tile_broad, channels = (qkv.shape[2], qkv.shape[3], qkv.shape[4])
    positions = tile_tall * tile_broad
    slot_count = image_height.shape[1]
    head_dim = pw_weight.shape[0]
    head_count = channels // (3 * head_dim)
    inner_width = head_count * head_dim
    image_slot = tile_image[0, 0]
    picker = jnp.arange(slot_count) == image_slot
    image_tall = jnp.sum(jnp.where(picker, image_height[0], 0))
    image_wide = jnp.sum(jnp.where(picker, image_width[0], 0))
    is_live = image_slot < slot_count
    grid_row = tile_row[0, 0]
    grid_col = tile_col[0, 0]
    neighbours = (
        is_live & (grid_col > 0),
        is_live & (grid_col < image_wide - 1),
        is_live & (grid_row > 0),
        is_live & (grid_row < image_tall - 1),
    )
    source = jnp.where(is_live, qkv[0, 0], jnp.zeros((), jnp.bfloat16))
    padded = widen_source(source, neighbours, image_wide).astype(jnp.float32)
    mixed_dw = depthwise(padded, dw_weight, False)
    flat_mixed = mixed_dw.reshape(positions, channels)
    blocks = block_weights(pw_weight)
    merged = pointwise(flat_mixed, blocks, False)
    central = padded[2 : 2 + tile_tall, 2 : 2 + tile_broad].reshape(positions, channels)
    scale_parts = []
    local_states = []
    local_sums = []
    for scale_input in (central, merged):
        raw_queries, raw_keys, values = head_parts(scale_input, head_count)
        queries = jax.nn.relu(raw_queries)
        key_rows = jax.nn.relu(raw_keys)
        scale_parts.append((raw_queries, raw_keys, queries, key_rows, values))
        local_states.append(
            jnp.einsum("phi,phj->ihj", key_rows, values, precision=PRECISE).reshape(
                head_dim, inner_width
            )
        )
        local_sums.append(jnp.sum(key_rows, axis=0).reshape(inner_width))
    states, key_sums = image_total(
        jnp.stack(local_states), jnp.stack(local_sums), image_slot, slot_count
    )
    cot_flat = cotangent[0, 0].astype(jnp.float32).reshape(positions, 2 * inner_width)
    grad_num_all = []
    local_gstates = []
    local_gsums = []
    for member in range(2):
        raw_queries, raw_keys, queries, key_rows, values = scale_parts[member]
        scale_state = states[member].reshape(head_dim, head_count, head_dim)
        scale_sum = key_sums[member].reshape(head_count, head_dim)
        numerator = jnp.einsum("phi,ihj->phj", queries, scale_state, precision=PRECISE)
        denominator = jnp.einsum("phi,hi->ph", queries, scale_sum, precision=PRECISE) + EPSILON
        result = numerator / denominator[..., None]
        grad_out = cot_flat[:, member * inner_width : (member + 1) * inner_width].reshape(
            positions, head_count, head_dim
        )
        grad_num = grad_out / denominator[..., None]
        grad_den = -jnp.sum(grad_out * result, axis=-1) / denominator
        grad_query = (
            jnp.einsum("phj,ihj->phi", grad_num, scale_state, precision=PRECISE)
            + grad_den[..., None] * scale_sum[None]
        )
        grad_num_all.append(grad_query)
        local_gstates.append(
            jnp.einsum("phi,phj->ihj", queries, grad_num, precision=PRECISE).reshape(
                head_dim, inner_width
            )
        )
        local_gsums.append(
            jnp.einsum("phi,ph->hi", queries, grad_den, precision=PRECISE).reshape(inner_width)
        )
    grad_states, grad_sums = image_total(
        jnp.stack(local_gstates), jnp.stack(local_gsums), image_slot, slot_count
    )
    scale_grads = []
    for member in range(2):
        raw_queries, raw_keys, queries, key_rows, values = scale_parts[member]
        gstate = grad_states[member].reshape(head_dim, head_count, head_dim)
        gsum = grad_sums[member].reshape(head_count, head_dim)
        grad_keys = jnp.einsum("phj,ihj->phi", values, gstate, precision=PRECISE) + gsum[None]
        grad_values = jnp.einsum("phi,ihj->phj", key_rows, gstate, precision=PRECISE)
        grad_queries = jnp.where(raw_queries > 0, grad_num_all[member], 0.0)
        grad_keys = jnp.where(raw_keys > 0, grad_keys, 0.0)
        scale_grads.append(
            jnp.concatenate(
                [
                    grad_queries.reshape(positions, inner_width),
                    grad_keys.reshape(positions, inner_width),
                    grad_values.reshape(positions, inner_width),
                ],
                axis=1,
            )
        )
    grad_merged = scale_grads[1]
    grad_mixed = pointwise(grad_merged, blocks, True)
    grad_pwk = block_grad(flat_mixed, grad_merged, head_dim)
    grad_field = grad_mixed.reshape(tile_tall, tile_broad, channels)
    grad_dwk = kernel_grad(padded, dw_weight, grad_field)
    grad_padded = widen_grad(grad_field, neighbours, image_wide)
    grad_through = depthwise(grad_padded, dw_weight, True)
    grad_source = scale_grads[0].reshape(tile_tall, tile_broad, channels) + grad_through
    grad_source = jnp.where(is_live, grad_source, 0.0).astype(jnp.bfloat16)
    summed_dw, summed_pw = lax.psum((grad_dwk, grad_pwk), ("tile", "img"))
    weight_norm = 1.0 / math.sqrt(positions * lax.axis_size("tile") * lax.axis_size("img"))
    return (grad_source[None, None], summed_dw * weight_norm, summed_pw * weight_norm)


def solution(mesh):
    placed = (
        P("img", "tile", None, None, None),
        P("img", "tile", None, None, None),
        P(),
        P(),
        P("img", "tile"),
        P("img", "tile"),
        P("img", "tile"),
        P("img", None),
        P("img", None),
    )
    return jax.shard_map(
        local,
        mesh=mesh,
        in_specs=placed,
        out_specs=(P("img", "tile", None, None, None), P(), P()),
        check_vma=False,
    )
```

profile of v0, /device:TPU:0, one launch (start us, length us, event | category | flops | bytes accessed | tf_op | source)
XLA Modules:
  0.0 420.8 jit_solution(15324009506606499923)
XLA Ops:
  10.0 4.9 %collective-permute-start = (bf16[8,2,1536]{2,1,0:T(2,128)(2,1)S(1)}, bf16[8,2,1536]{2,1,0:T(2,128)(2,1)S(1)}, u32[]{:S(2)}, u32[]{:S(2)}) collective-permute-start(bf16[8,2,1536]{2,1,0:T(2,128)(2,1)S(1)} %get-tuple-element.34), channel_id=1, source_target_pairs={{0,8},{8,16},{16,24},{1,9},{9,17},{17,25},{2,10},{10,18},{18,26},{... | collective-permute-start | bytes 147464 | tf_op jit(solution)/shard_map/ppermute | solution.py:15
  25.4 6.3 %collective-permute-start.3 = (bf16[2,36,1536]{2,1,0:T(8,128)(2,1)}, bf16[2,36,1536]{2,1,0:T(8,128)(2,1)}, u32[]{:S(2)}, u32[]{:S(2)}) collective-permute-start(bf16[2,36,1536]{2,1,0:T(8,128)(2,1)} %get-tuple-element.30), channel_id=1, source_target_pairs={{0,16},{8,24},{1,17},{9,25},{2,18},{10,26},{3,19},{11,27},{4,20},{... | collective-permute-start | bytes 663560 | tf_op jit(solution)/shard_map/ppermute | solution.py:15
  31.7 4.2 collective-permute-start.2
  41.5 2.2 mul.67
  47.6 5.8 %collective-permute-done.4 = bf16[2,36,1536]{2,1,0:T(8,128)(2,1)S(1)} collective-permute-done((bf16[2,36,1536]{2,1,0:T(8,128)(2,1)}, bf16[2,36,1536]{2,1,0:T(8,128)(2,1)S(1)}, u32[]{:S(2)}, u32[]{:S(2)}) %collective-permute-start.4) | collective-permute-done | bytes 221216 | tf_op jit(solution)/shard_map/ppermute | solution.py:15
  53.4 8.7 %collective-permute-done.5 = bf16[2,36,1536]{2,1,0:T(8,128)(2,1)S(1)} collective-permute-done((bf16[2,36,1536]{2,1,0:T(8,128)(2,1)}, bf16[2,36,1536]{2,1,0:T(8,128)(2,1)S(1)}, u32[]{:S(2)}, u32[]{:S(2)}) %collective-permute-start.5) | collective-permute-done | bytes 221216 | tf_op jit(solution)/shard_map/ppermute | solution.py:15
  62.2 2.3 fusion.70
  66.8 3.6 convolution_select_fusion
  76.0 2.8 fusion.43
  80.5 8.9 %psum.43 = f32[2,2,512]{2,1,0:T(2,128)S(1)} all-reduce(f32[2,2,512]{2,1,0:T(2,128)S(1)} %broadcast_multiply_fusion.5), channel_id=1, replica_groups=mesh['tile'=4,'img'=8] {'tile'}, use_global_device_ids=true, to_apply=%region_6.7 | all-reduce | flops 2048 | bytes 16384 | tf_op jit(solution)/shard_map/psum | solution.py:172
  93.7 2.6 fusion.48
  97.3 2.6 fusion.49
  101.5 2.1 fusion.78
  112.2 2.0 slice_compare_fusion.3
  116.4 32.2 %all-reduce.7.cloned.1.call-done = (f32[2,2,32,512]{3,2,1,0:T(8,128)}, f32[2,2,32,512]{3,2,1,0:T(8,128)}) async-done(((f32[2,2,32,512]{3,2,1,0:T(8,128)}, f32[2,2,32,512]{3,2,1,0:T(8,128)}), (f32[2,2,32,512]{3,2,1,0:T(8,128)}, f32[2,2,32,512]{3,2,1,0:T(8,128)})) %all-reduce.7.cloned.1.call-update) | async-done | bytes 524304 | tf_op jit(solution)/shard_map/psum | solution.py:172
  162.0 2.6 fusion.33
  167.2 10.9 %psum.45 = f32[2,2,512]{2,1,0:T(2,128)S(1)} all-reduce(f32[2,2,512]{2,1,0:T(2,128)S(1)} %broadcast_multiply_fusion.4), channel_id=1, replica_groups=mesh['tile'=4,'img'=8] {'tile'}, use_global_device_ids=true, to_apply=%region_12.13 | all-reduce | flops 2048 | bytes 16384 | tf_op jit(solution)/shard_map/psum | solution.py:172
  178.4 2.5 fusion.35
  182.1 2.6 fusion.41
  189.8 3.9 broadcast_in_dim_reshape_reshape.4
  195.9 33.5 %fusion.38 = f32[5,5,1536]{2,1,0:T(8,128)S(1)} fusion(f32[1,8,32,1536]{3,0,2,1:T(1,128)} %broadcast_in_dim_reshape_reshape.4, bf16[1,12,36,1536]{3,2,1,0:T(8,128)(2,1)} %get-tuple-element.26), kind=kOutput, calls=%fused_computation.50 | convolution fusion | flops 117964800 | bytes 3053568 | tf_op jit(solution)/shard_map/transpose(jvp())/conv_general_dilated | solution.py:99
  234.5 2.9 reshape.202
  237.5 2.2 fusion.27
  239.7 6.7 %fusion.6 = f32[4,1,12,32,32]{4,1,3,2,0:T(1,128)S(1)} fusion(pred[4,4,1,1,1]{0,2,4,3,1:T(4,128)(4,1)S(1)} %copy-done.38, f32[12,4,32,4,32]{4,3,2,1,0:T(4,128)} %reshape.202), kind=kOutput, calls=%fused_computation.7 | convolution fusion | flops 2359296 | bytes 983056 | tf_op jit(solution)/shard_map/bgiho,gh->ibho/dot_general | solution.py:151
  248.7 3.0 copy.171
  253.5 3.0 copy.172
  258.4 3.0 copy.170
  265.1 4.0 collective-permute-start.9
  269.1 3.3 collective-permute-start.8
  275.2 119.1 %all-reduce.5.cloned.1.call-done = (f32[25,1536]{1,0:T(8,128)}, f32[32,1536]{1,0:T(8,128)}) async-done(((f32[25,1536]{1,0:T(8,128)}, f32[32,1536]{1,0:T(8,128)}), (f32[25,1536]{1,0:T(8,128)}, f32[32,1536]{1,0:T(8,128)})) %all-reduce.5.cloned.1.call-update) | async-done | bytes 350224 | tf_op jit(solution)/shard_map/psum | solution.py:285
  398.4 4.7 %reshape.213 = f32[12,1,8,5,1536]{4,1,3,2,0:T(1,128)} reshape(f32[12,1,40,1536]{3,2,0,1:T(8,128)S(1)} %pad.2) | data formatting | bytes 5898240 | tf_op jit(solution)/shard_map/conv_general_dilated | solution.py:99
  406.0 3.4 fusion.8
  (223 shorter events, 99.4 us)
Async XLA Ops:
  7.2 9.1 %copy-start.8 = (bf16[1,1,8,32,1536]{4,3,2,1,0:T(8,128)(2,1)S(1)}, bf16[1,1,8,32,1536]{4,3,2,1,0:T(8,128)(2,1)}, u32[]{:S(2)}) copy-start(bf16[1,1,8,32,1536]{4,3,2,1,0:T(8,128)(2,1)} %param.9) | copy-start | bytes 2359300
  7.2 9.2 %copy-start.17 = (bf16[1,1,8,32,1024]{4,3,2,1,0:T(8,128)(2,1)S(1)}, bf16[1,1,8,32,1024]{4,3,2,1,0:T(8,128)(2,1)}, u32[]{:S(2)}) copy-start(bf16[1,1,8,32,1024]{4,3,2,1,0:T(8,128)(2,1)} %param.10) | copy-start | bytes 1572868
  7.2 141.4 %all-reduce.7.cloned.1.call-start = ((), (), s32[]{:S(2)}) async-start(), calls=%async_computation.1 | async-start | bytes 1048576 | tf_op jit(solution)/shard_map/psum | solution.py:172
  9.2 15.3 %copy-start.1 = (bf16[8,32,1536]{2,1,0:T(8,128)(2,1)}, bf16[8,32,1536]{2,1,0:T(8,128)(2,1)S(1)}, u32[]{:S(2)}) copy-start(bf16[8,32,1536]{2,1,0:T(8,128)(2,1)S(1)} %fusion.115) | copy-start | bytes 2359300
  10.0 14.3 %collective-permute-start = (bf16[8,2,1536]{2,1,0:T(2,128)(2,1)S(1)}, bf16[8,2,1536]{2,1,0:T(2,128)(2,1)S(1)}, u32[]{:S(2)}, u32[]{:S(2)}) collective-permute-start(bf16[8,2,1536]{2,1,0:T(2,128)(2,1)S(1)} %get-tuple-element.34), channel_id=1, source_target_pairs={{0,8},{8,16},{16,24},{1,9},{9,17},{17,25},{2,10},{10,18},{18,26},{... | collective-permute-start | bytes 147464 | tf_op jit(solution)/shard_map/ppermute | solution.py:15
  15.0 9.4 %collective-permute-start.1 = (bf16[8,2,1536]{2,1,0:T(2,128)(2,1)}, bf16[8,2,1536]{2,1,0:T(2,128)(2,1)S(1)}, u32[]{:S(2)}, u32[]{:S(2)}) collective-permute-start(bf16[8,2,1536]{2,1,0:T(2,128)(2,1)} %get-tuple-element.35), channel_id=1, source_target_pairs={{8,0},{16,8},{24,16},{9,1},{17,9},{25,17},{10,2},{18,10},{26,18},{... | collective-permute-start | bytes 147464 | tf_op jit(solution)/shard_map/ppermute | solution.py:15
  19.1 82.5 %copy-start.10 = (bf16[256,512]{0,1:T(8,128)(2,1)}, bf16[256,512]{0,1:T(8,128)(2,1)S(1)}, u32[]{:S(2)}) copy-start(bf16[256,512]{0,1:T(8,128)(2,1)S(1)} %slice.113) | copy-start | bytes 786436
  19.1 17.0 %copy-start.24 = (f32[32,1536]{1,0:T(8,128)S(1)}, f32[32,1536]{1,0:T(8,128)}, u32[]{:S(2)}) copy-start(f32[32,1536]{1,0:T(8,128)} %param.12) | copy-start | bytes 589828
  24.5 11.4 %copy-start.21 = (bf16[8,2,1536]{2,1,0:T(2,128)(2,1)}, bf16[8,2,1536]{2,1,0:T(2,128)(2,1)S(1)}, u32[]{:S(2)}) copy-start(bf16[8,2,1536]{2,1,0:T(2,128)(2,1)S(1)} %broadcast_select_fusion.1) | copy-start | bytes 147460
  24.5 13.1 %copy-start.16 = (f32[256,512]{1,0:T(8,128)S(1)}, f32[256,512]{1,0:T(8,128)}, u32[]{:S(2)}) copy-start(f32[256,512]{1,0:T(8,128)} %get-tuple-element.28) | copy-start | bytes 1572868
  25.4 21.2 %collective-permute-start.3 = (bf16[2,36,1536]{2,1,0:T(8,128)(2,1)}, bf16[2,36,1536]{2,1,0:T(8,128)(2,1)}, u32[]{:S(2)}, u32[]{:S(2)}) collective-permute-start(bf16[2,36,1536]{2,1,0:T(8,128)(2,1)} %get-tuple-element.30), channel_id=1, source_target_pairs={{0,16},{8,24},{1,17},{9,25},{2,18},{10,26},{3,19},{11,27},{4,20},{... | collective-permute-start | bytes 663560 | tf_op jit(solution)/shard_map/ppermute | solution.py:15
  31.7 15.0 %collective-permute-start.2 = (bf16[2,36,1536]{2,1,0:T(8,128)(2,1)}, bf16[2,36,1536]{2,1,0:T(8,128)(2,1)}, u32[]{:S(2)}, u32[]{:S(2)}) collective-permute-start(bf16[2,36,1536]{2,1,0:T(8,128)(2,1)} %get-tuple-element.30), channel_id=1, source_target_pairs={{0,8},{8,16},{16,24},{1,9},{9,17},{17,25},{2,10},{10,18},{18,26},{... | collective-permute-start | bytes 663560 | tf_op jit(solution)/shard_map/ppermute | solution.py:15
  43.7 18.4 %copy-start.2 = (bf16[8,32,1536]{2,1,0:T(8,128)(2,1)S(1)}, bf16[8,32,1536]{2,1,0:T(8,128)(2,1)}, u32[]{:S(2)}) copy-start(bf16[8,32,1536]{2,1,0:T(8,128)(2,1)} %copy-done.1) | copy-start | bytes 2359300
  43.7 45.7 %copy-start.34 = (f32[2]{0:T(128)}, f32[2]{0:T(128)S(1)}, u32[]{:S(2)}) copy-start(f32[2]{0:T(128)S(1)} %fusion.60) | copy-start | bytes 28
  43.7 9.7 %collective-permute-start.4 = (bf16[2,36,1536]{2,1,0:T(8,128)(2,1)}, bf16[2,36,1536]{2,1,0:T(8,128)(2,1)S(1)}, u32[]{:S(2)}, u32[]{:S(2)}) collective-permute-start(bf16[2,36,1536]{2,1,0:T(8,128)(2,1)} %get-tuple-element.31), channel_id=1, source_target_pairs={{8,0},{16,8},{24,16},{9,1},{17,9},{25,17},{10,2},{18,10},{26,18},{... | collective-permute-start | bytes 663560 | tf_op jit(solution)/shard_map/ppermute | solution.py:15
  45.1 17.0 %collective-permute-start.5 = (bf16[2,36,1536]{2,1,0:T(8,128)(2,1)}, bf16[2,36,1536]{2,1,0:T(8,128)(2,1)S(1)}, u32[]{:S(2)}, u32[]{:S(2)}) collective-permute-start(bf16[2,36,1536]{2,1,0:T(8,128)(2,1)} %get-tuple-element.31), channel_id=1, source_target_pairs={{16,0},{24,8},{17,1},{25,9},{18,2},{26,10},{19,3},{27,11},{20,4},{... | collective-permute-start | bytes 663560 | tf_op jit(solution)/shard_map/ppermute | solution.py:15
  108.8 5.4 %copy-start.40 = (f32[1,512]{1,0:T(1,128)S(1)}, f32[1,512]{1,0:T(1,128)}, u32[]{:S(2)}) copy-start(f32[1,512]{1,0:T(1,128)} %get-tuple-element.40) | copy-start | bytes 6148
  108.8 6.1 %copy-start.39 = (f32[1,512]{1,0:T(1,128)S(1)}, f32[1,512]{1,0:T(1,128)}, u32[]{:S(2)}) copy-start(f32[1,512]{1,0:T(1,128)} %get-tuple-element.41) | copy-start | bytes 6148
  109.7 38.9 %copy-start.35 = (f32[2]{0:T(128)S(1)}, f32[2]{0:T(128)}, u32[]{:S(2)}) copy-start(f32[2]{0:T(128)} %copy-done.34) | copy-start | bytes 28
  111.4 283.0 %all-reduce.5.cloned.1.call-start = ((), (), s32[]{:S(2)}) async-start(), calls=%async_computation | async-start | bytes 786432 | tf_op jit(solution)/shard_map/psum | solution.py:285
  116.4 34.2 %copy-start.7 = (f32[256,512]{0,1:T(8,128)S(1)}, f32[256,512]{0,1:T(8,128)}, u32[]{:S(2)}) copy-start(f32[256,512]{0,1:T(8,128)} %get-tuple-element.45) | copy-start | bytes 1572868
  149.8 5.2 %copy-start.6 = (f32[256,512]{0,1:T(8,128)S(1)}, f32[256,512]{0,1:T(8,128)}, u32[]{:S(2)}) copy-start(f32[256,512]{0,1:T(8,128)} %get-tuple-element.19) | copy-start | bytes 1572868
  152.0 8.3 %copy-start.5 = (f32[256,512]{0,1:T(8,128)S(1)}, f32[256,512]{0,1:T(8,128)}, u32[]{:S(2)}) copy-start(f32[256,512]{0,1:T(8,128)} %get-tuple-element.46) | copy-start | bytes 1572868
  230.9 32.4 %collective-permute-start.6 = (bf16[8,2,1536]{2,1,0:T(2,128)(2,1)}, bf16[8,2,1536]{2,1,0:T(2,128)(2,1)}, u32[]{:S(2)}, u32[]{:S(2)}) collective-permute-start(bf16[8,2,1536]{2,1,0:T(2,128)(2,1)} %get-tuple-element.32), channel_id=1, source_target_pairs={{0,8},{8,16},{16,24},{1,9},{9,17},{17,25},{2,10},{10,18},{18,26},{... | collective-permute-start | bytes 147464 | tf_op jit(solution)/shard_map/ppermute | solution.py:15
  232.9 31.2 %collective-permute-start.7 = (bf16[8,2,1536]{2,1,0:T(2,128)(2,1)}, bf16[8,2,1536]{2,1,0:T(2,128)(2,1)}, u32[]{:S(2)}, u32[]{:S(2)}) collective-permute-start(bf16[8,2,1536]{2,1,0:T(2,128)(2,1)} %get-tuple-element.33), channel_id=1, source_target_pairs={{8,0},{16,8},{24,16},{9,1},{17,9},{25,17},{10,2},{18,10},{26,18},{... | collective-permute-start | bytes 147464 | tf_op jit(solution)/shard_map/ppermute | solution.py:15
  239.7 6.7 %copy-start.11 = (bf16[256,512]{0,1:T(8,128)(2,1)S(1)}, bf16[256,512]{0,1:T(8,128)(2,1)}, u32[]{:S(2)}) copy-start(bf16[256,512]{0,1:T(8,128)(2,1)} %copy-done.10) | copy-start | bytes 786436
  239.7 6.7 %copy-start.19 = (pred[256,512]{0,1:T(32,128)(4,1)S(1)}, pred[256,512]{0,1:T(32,128)(4,1)}, u32[]{:S(2)}) copy-start(pred[256,512]{0,1:T(32,128)(4,1)} %get-tuple-element.18) | copy-start | bytes 393220
  239.7 6.8 %copy-start.33 = (f32[16,32]{1,0:T(8,128)S(1)}, f32[16,32]{1,0:T(8,128)}, u32[]{:S(2)}) copy-start(f32[16,32]{1,0:T(8,128)} %add.73) | copy-start | bytes 6148
  265.1 132.5 %collective-permute-start.9 = (bf16[2,36,1536]{2,1,0:T(8,128)(2,1)S(1)}, bf16[2,36,1536]{2,1,0:T(8,128)(2,1)S(1)}, u32[]{:S(2)}, u32[]{:S(2)}) collective-permute-start(bf16[2,36,1536]{2,1,0:T(8,128)(2,1)S(1)} %get-tuple-element.13), channel_id=1, source_target_pairs={{0,16},{8,24},{1,17},{9,25},{2,18},{10,26},{3,19},{11,27},{4,20},{... | collective-permute-start | bytes 663560 | tf_op jit(solution)/shard_map/ppermute | solution.py:15
  269.1 128.5 %collective-permute-start.8 = (bf16[2,36,1536]{2,1,0:T(8,128)(2,1)S(1)}, bf16[2,36,1536]{2,1,0:T(8,128)(2,1)S(1)}, u32[]{:S(2)}, u32[]{:S(2)}) collective-permute-start(bf16[2,36,1536]{2,1,0:T(8,128)(2,1)S(1)} %get-tuple-element.13), channel_id=1, source_target_pairs={{0,8},{8,16},{16,24},{1,9},{9,17},{17,25},{2,10},{10,18},{18,26},{... | collective-permute-start | bytes 663560 | tf_op jit(solution)/shard_map/ppermute | solution.py:15
  272.4 125.3 %collective-permute-start.10 = (bf16[2,36,1536]{2,1,0:T(8,128)(2,1)S(1)}, bf16[2,36,1536]{2,1,0:T(8,128)(2,1)S(1)}, u32[]{:S(2)}, u32[]{:S(2)}) collective-permute-start(bf16[2,36,1536]{2,1,0:T(8,128)(2,1)S(1)} %get-tuple-element.14), channel_id=1, source_target_pairs={{8,0},{16,8},{24,16},{9,1},{17,9},{25,17},{10,2},{18,10},{26,18},{... | collective-permute-start | bytes 663560 | tf_op jit(solution)/shard_map/ppermute | solution.py:15
  273.9 123.8 %collective-permute-start.11 = (bf16[2,36,1536]{2,1,0:T(8,128)(2,1)S(1)}, bf16[2,36,1536]{2,1,0:T(8,128)(2,1)S(1)}, u32[]{:S(2)}, u32[]{:S(2)}) collective-permute-start(bf16[2,36,1536]{2,1,0:T(8,128)(2,1)S(1)} %get-tuple-element.14), channel_id=1, source_target_pairs={{16,0},{24,8},{17,1},{25,9},{18,2},{26,10},{19,3},{27,11},{20,4},{... | collective-permute-start | bytes 663560 | tf_op jit(solution)/shard_map/ppermute | solution.py:15
  (28 other events, 76.8 us)
Sparse Core Ops, SparseCore 0:
  111.5 37.0 all-reduce.6
  263.4 130.9 all-reduce.4
where the time goes:
time: 427 us; the launch traced here: 421 us
  waiting for transfers between devices  166 us (39%)
  matrix products  82.2 us (19%)
  local copies, waits for them, and re-layouts  74.8 us (18%)
  starting transfers between devices  33.3 us (8%)
  other arithmetic  25.8 us (6%)
  blocking collectives  19.8 us (5%)
  between operations  19.1 us (4%)
    psum x1, waiting for transfers between devices, local(): summed_dw, summed_pw = lax.psum((grad_dwk, grad_pwk), ('tile', 'img'))  119 us
    conv_general_dilated x3, matrix products, depthwise(): lax.conv_general_dilated(padded[None], shaped, (1, 1), 'VALID', dimension...  40.4 us
    ppermute x12, starting transfers between devices, from_behind(): lax.ppermute(value, axis, [(source, source + steps) for source in range(i...  33.2 us
    psum x1, waiting for transfers between devices, image_total(): summed_states, summed_sums = lax.psum((spread_states, spread_sums), 'tile')  32.2 us
    psum x2, blocking collectives, image_total(): summed_states, summed_sums = lax.psum((spread_states, spread_sums), 'tile')  19.8 us
    concatenate x9, local copies, waits for them, and re-layouts, local(): jnp.concatenate([grad_queries.reshape(positions, inner_width), grad_keys....  18.2 us
    ppermute x12, waiting for transfers between devices, from_behind(): lax.ppermute(value, axis, [(source, source + steps) for source in range(i...  14.5 us
    conv_general_dilated x10, local copies, waits for them, and re-layouts, depthwise(): lax.conv_general_dilated(padded[None], shaped, (1, 1), 'VALID', dimension...  11.4 us
  transfers between devices with their start and end apart: 14, of which 4 were waited for; matrix products, arithmetic and copies ran while one was open for 12% of the time, Pallas kernels for 0%

commit v1 on v0

v1 whole, which is shorter than its diff:
```python
import functools
import math

import jax
import jax.numpy as jnp
from jax import lax
from jax.experimental import pallas as pl
from jax.experimental.pallas import tpu as pltpu
from jax.sharding import PartitionSpec as P

EPSILON = 1e-06
LANES = 256
REACH = 2
EDGE = 8
BF16 = jnp.bfloat16
F32 = jnp.float32
PARAMS = pltpu.CompilerParams(vmem_limit_bytes=40 * 1024 * 1024)
SMEM = pl.BlockSpec(memory_space=pltpu.SMEM)


class Place:
    def __init__(self, layout_refs):
        image_ref, row_ref, col_ref, tall_ref, wide_ref = layout_refs
        slot = image_ref[0, 0]
        slots = tall_ref.shape[1]
        tall = wide = start = jnp.int32(0)
        for s in range(slots):
            tall = jnp.where(slot == s, tall_ref[0, s], tall)
            wide = jnp.where(slot == s, wide_ref[0, s], wide)
            start = start + jnp.where(s < slot, tall_ref[0, s] * wide_ref[0, s], 0)
        self.live = slot < slots
        self.tall, self.wide = tall, wide
        self.row, self.col = row_ref[0, 0], col_ref[0, 0]
        self.within = self.row * wide + self.col
        self.index = start + self.within
        self.above = self.live & (self.row > 0)
        self.below = self.live & (self.row < tall - 1)

    def same_image(self, delta):
        other = self.within + delta
        return self.live & (other >= 0) & (other < self.tall * self.wide)


def halo_routes(count):
    if count == 4:
        return [
            ([(s, s ^ m) for s in range(count)], lambda t, m=m: (t ^ m) - t, lambda t, m=m: (t ^ m) - t)
            for m in range(1, count)
        ]
    routes = []
    for k in (1, -1, 2, -2, 3, -3):
        if abs(k) < count:
            pairs = [(s, s + k) for s in range(max(0, -k), min(count, count - k))]
            routes.append((pairs, lambda t, k=k: jnp.int32(k), lambda t, k=k: jnp.int32(-k)))
    return routes


def exchange(value, axis):
    count = lax.axis_size(axis)
    return [lax.ppermute(value, axis, [(s, s ^ m) for s in range(count)]) for m in range(1, count)]


def split(x):
    high = x.astype(BF16)
    return high, (x - high.astype(F32)).astype(BF16)


def contract(a, b, dims):
    return lax.dot_general(a, b, (dims, ((), ())), preferred_element_type=F32)


NN = ((1,), (0,))
NT = ((1,), (1,))
TN = ((0,), (0,))


def dot(a, b, dims):
    total = contract(a[0], b[0], dims)
    if b[1] is not None:
        total = total + contract(a[0], b[1], dims)
    if a[1] is not None:
        total = total + contract(a[1], b[0], dims)
    return total


def exact(x):
    return x.astype(BF16), None


def same_head(head_dim):
    rows = lax.broadcasted_iota(jnp.int32, (LANES, LANES), 0) // head_dim
    cols = lax.broadcasted_iota(jnp.int32, (LANES, LANES), 1) // head_dim
    return rows == cols


def spread(compact, mask):
    tall = jnp.concatenate([compact] * (LANES // compact.shape[0]), axis=0)
    return jnp.where(mask, tall, 0.0)


def gather_blocks(full, mask, head_dim):
    kept = jnp.where(mask, full, 0.0)
    return jnp.sum(kept.reshape(LANES // head_dim, head_dim, LANES), axis=0)


def payload(field, place, delta):
    tall, broad, lanes = field.shape
    size = REACH * broad
    top = field[:REACH].reshape(size, lanes)
    bottom = field[tall - REACH :].reshape(size, lanes)
    left = field[:, :EDGE].reshape(size, lanes)
    right = field[:, broad - EDGE :].reshape(size, lanes)
    rows = jnp.where(delta > 0, bottom, top)
    cols = jnp.where(place.col == 0, right, left)
    beside = (place.wide == 2) & (delta == jnp.where(place.col == 0, 1, -1))
    return jnp.where(beside, cols, rows)


def fill_padded(pad_ref, field, arrived_refs, deltas, place):
    tall, broad, lanes = field.shape
    full = tall + 2 * REACH
    pad_ref[:REACH] = jnp.zeros((REACH, broad + 2 * EDGE, lanes), F32)
    pad_ref[full - REACH :] = jnp.zeros((REACH, broad + 2 * EDGE, lanes), F32)
    pad_ref[REACH : REACH + tall, :EDGE] = jnp.zeros((tall, EDGE, lanes), F32)
    pad_ref[REACH : REACH + tall, EDGE + broad :] = jnp.zeros((tall, EDGE, lanes), F32)
    pad_ref[REACH : REACH + tall, EDGE : EDGE + broad] = field
    two = place.live & (place.wide == 2)
    one = place.live & (place.wide == 1)
    first, second = two & (place.col == 0), two & (place.col == 1)
    upper, lower = slice(0, REACH), slice(full - REACH, full)
    before, after = slice(0, EDGE), slice(EDGE + broad, 2 * EDGE + broad)
    for arrived_ref, delta in zip(arrived_refs, deltas):

        def rows(arrived_ref=arrived_ref):
            return arrived_ref[0].astype(F32).reshape(REACH, broad, lanes)

        def cols(arrived_ref=arrived_ref):
            return arrived_ref[0].astype(F32).reshape(tall, EDGE, lanes)

        def put(condition, where_rows, where_cols, value):
            @pl.when(condition)
            def _():
                pad_ref[where_rows, where_cols] = value()

        middle, height = slice(EDGE, EDGE + broad), slice(REACH, REACH + tall)
        put(place.above & ((one & (delta == -1)) | (two & (delta == -2))), upper, middle, rows)
        put(place.below & ((one & (delta == 1)) | (two & (delta == 2))), lower, middle, rows)
        put(second & (delta == -1), height, before, cols)
        put(first & (delta == 1), height, after, cols)
        put(place.above & first & (delta == -1), upper, after, lambda r=rows: r()[:, :EDGE])
        put(place.above & second & (delta == -3), upper, before, lambda r=rows: r()[:, broad - EDGE :])
        put(place.below & second & (delta == 1), lower, before, lambda r=rows: r()[:, broad - EDGE :])
        put(place.below & first & (delta == 3), lower, after, lambda r=rows: r()[:, :EDGE])


def fill_shifted(shift_ref, pad_ref):
    full, broad = shift_ref.shape[1:3]
    first = EDGE - REACH
    for y in range(full):
        for b in range(2 * REACH + 1):
            shift_ref[b, y] = pad_ref[y, first + b : first + b + broad]


def convolve(shift_ref, kernel_ref, y, flipped):
    taps = 2 * REACH + 1
    total = None
    for a in range(taps):
        for b in range(taps):
            tap = taps * a + b
            if flipped:
                tap = taps * taps - 1 - tap
            term = shift_ref[b, y + a] * kernel_ref[tap : tap + 1]
            total = term if total is None else total + term
    return total


def outgoing_kernel(routes, *refs):
    layout, field_ref, outs = refs[:5], refs[5], refs[6:]
    place = Place(layout)
    field = field_ref[0, 0].astype(F32)
    for (_, target, _), out_ref in zip(routes, outs):
        out_ref[0] = payload(field, place, target(place.index)).astype(BF16)


def forward_kernel(routes, per, head_dim, *refs):
    count = len(routes)
    layout, field_ref = refs[:5], refs[5]
    arrived = refs[6 : 6 + count]
    dw_ref, pw_ref, mixed_ref, merged_ref, state_ref, pad_ref, shift_ref, mix_ref, key0, key1 = refs[
        6 + count :
    ]
    step = pl.program_id(0)
    place = Place(layout)
    tall, broad = field_ref.shape[2:4]
    field = jnp.where(place.live, field_ref[0, 0].astype(F32), 0.0)
    fill_padded(pad_ref, field, arrived, [source(place.index) for _, _, source in routes], place)
    fill_shifted(shift_ref, pad_ref)

    def one_row(y, carry):
        mix_ref[y] = convolve(shift_ref, dw_ref, y, False)
        return carry

    lax.fori_loop(0, tall, one_row, 0)
    mixed = mix_ref[...].reshape(tall * broad, LANES)
    mixed_ref[...] = mixed
    mask = same_head(head_dim)
    blocks = split(spread(pw_ref[...], mask))
    merged = dot(split(mixed), blocks, NN)
    merged_ref[...] = merged
    flat = field.reshape(tall * broad, LANES)
    for part in range(per):

        @pl.when(step == per + part)
        def _():
            keys0, keys1 = jnp.maximum(flat, 0.0), jnp.maximum(merged, 0.0)
            key0[part] = keys0.astype(BF16)
            key1[part] = keys1
            lanes = slice(part * LANES, (part + 1) * LANES)
            state_ref[2 * head_dim :, lanes] = jnp.concatenate(
                [
                    jnp.sum(keys0, axis=0, keepdims=True),
                    jnp.sum(keys1, axis=0, keepdims=True),
                    jnp.zeros((6, LANES), F32),
                ],
                axis=0,
            )

        @pl.when(step == 2 * per + part)
        def _():
            lanes = slice(part * LANES, (part + 1) * LANES)
            state0 = contract(key0[part], flat.astype(BF16), TN)
            state1 = dot(split(key1[part]), split(merged), TN)
            state_ref[:head_dim, lanes] = gather_blocks(state0, mask, head_dim)
            state_ref[head_dim : 2 * head_dim, lanes] = gather_blocks(state1, mask, head_dim)


def total_of(own_ref, others, place):
    total = own_ref[...]
    for m, other in enumerate(others, 1):
        delta = (place.index ^ m) - place.index
        total = total + jnp.where(place.same_image(delta), other[...], 0.0)
    return total


def query_kernel(others, head_dim, *refs):
    layout, own_ref, received = refs[:5], refs[5], refs[6 : 6 + others]
    (source_ref, merged_ref, mixed_ref, cot0_ref, cot1_ref, pw_ref) = refs[6 + others : 12 + others]
    gstate_ref, grad0_ref, gmix_ref, gpw_ref = refs[12 + others :]
    place = Place(layout)
    total = total_of(own_ref, received, place)
    mask = same_head(head_dim)
    ones = (mask.astype(BF16), None)
    positions = merged_ref.shape[0]
    raw0 = jnp.where(place.live, source_ref[0, 0].astype(F32), 0.0).reshape(positions, LANES)
    sums = []
    for scale in range(2):
        raw = raw0 if scale == 0 else merged_ref[...]
        cot_ref = cot0_ref if scale == 0 else cot1_ref
        query = jnp.maximum(raw, 0.0)
        pair = exact(query) if scale == 0 else split(query)
        state = split(spread(total[scale * head_dim : (scale + 1) * head_dim], mask))
        key_sum = total[2 * head_dim + scale : 2 * head_dim + scale + 1]
        cot = cot_ref[0, 0].astype(F32).reshape(positions, LANES)
        over = 1.0 / (dot(split(query * key_sum), ones, NN) + EPSILON)
        result = dot(pair, state, NN) * over
        grad_num = cot * over
        grad_den = -dot(split(cot * result), ones, NN) * over
        num_pair = split(grad_num)
        grad = dot(num_pair, state, NT) + grad_den * key_sum
        grad = jnp.where(raw > 0, grad, 0.0)
        gstate = dot(pair, num_pair, TN)
        gstate_ref[scale * head_dim : (scale + 1) * head_dim] = gather_blocks(gstate, mask, head_dim)
        sums.append(jnp.sum(query * grad_den, axis=0, keepdims=True))
        if scale == 0:
            grad0_ref[...] = grad
        else:
            grad_pair = split(grad)
            gmix_ref[...] = dot(grad_pair, split(spread(pw_ref[...], mask)), NT)
            gpw_ref[...] = gather_blocks(dot(split(mixed_ref[...]), grad_pair, TN), mask, head_dim)
    gstate_ref[2 * head_dim :] = jnp.concatenate(sums + [jnp.zeros((6, LANES), F32)], axis=0)


def value_kernel(others, routes, head_dim, *refs):
    layout, own_ref, received = refs[:5], refs[5], refs[6 : 6 + others]
    refs = refs[6 + others :]
    (ksource_ref, vsource_ref, kmerged_ref, vmerged_ref, kmixed_ref, vmixed_ref) = refs[:6]
    (kpw_ref, vpw_ref, qgrad0_ref, qgmix_ref, qgpw_ref) = refs[6:11]
    grad0_ref, gmix_ref, gpw_ref = refs[11:14]
    outs = refs[14:]
    place = Place(layout)
    total = total_of(own_ref, received, place)
    mask = same_head(head_dim)
    positions = kmerged_ref.shape[0]
    tall, broad = ksource_ref.shape[2:4]
    grad0_ref[0] = qgrad0_ref[...]
    gmix_ref[0] = qgmix_ref[...]
    gpw_ref[0] = qgpw_ref[...]
    for scale in range(2):
        gstate = split(spread(total[scale * head_dim : (scale + 1) * head_dim], mask))
        gsum = total[2 * head_dim + scale : 2 * head_dim + scale + 1]
        if scale == 0:
            raw = jnp.where(place.live, ksource_ref[0, 0].astype(F32), 0.0).reshape(positions, LANES)
            values = jnp.where(place.live, vsource_ref[0, 0].astype(F32), 0.0).reshape(positions, LANES)
            key_pair, value_pair = exact(jnp.maximum(raw, 0.0)), exact(values)
        else:
            raw = kmerged_ref[...]
            key_pair, value_pair = split(jnp.maximum(raw, 0.0)), split(vmerged_ref[...])
        grad_keys = jnp.where(raw > 0, dot(value_pair, gstate, NT) + gsum, 0.0)
        grad_values = dot(key_pair, gstate, NN)
        if scale == 0:
            grad0_ref[1] = grad_keys
            grad0_ref[2] = grad_values
        else:
            for member, grad, mixed_ref, pw_ref in (
                (1, grad_keys, kmixed_ref, kpw_ref),
                (2, grad_values, vmixed_ref, vpw_ref),
            ):
                pair = split(grad)
                gmix_ref[member] = dot(pair, split(spread(pw_ref[...], mask)), NT)
                gpw_ref[member] = gather_blocks(dot(split(mixed_ref[...]), pair, TN), mask, head_dim)
    for (_, target, _), out_ref in zip(routes, outs):
        delta = target(place.index)
        for member in range(3):
            field = gmix_ref[member].reshape(tall, broad, LANES)
            out_ref[member] = payload(field, place, delta).astype(BF16)


def weight_kernel(routes, *refs):
    count = len(routes)
    layout, field_ref = refs[:5], refs[5]
    arrived = refs[6 : 6 + count]
    gmix_ref, gpw_ref, out_ref, pad_ref, shift_ref = refs[6 + count :]
    place = Place(layout)
    tall, broad = field_ref.shape[2:4]
    field = jnp.where(place.live, field_ref[0, 0].astype(F32), 0.0)
    fill_padded(pad_ref, field, arrived, [source(place.index) for _, _, source in routes], place)
    fill_shifted(shift_ref, pad_ref)
    taps = 2 * REACH + 1
    sub = 128
    for part in range(LANES // sub):
        lanes = slice(part * sub, (part + 1) * sub)

        def one_row(y, totals):
            grad = gmix_ref[0, pl.ds(pl.multiple_of(y * broad, broad), broad), lanes]
            new = []
            for a in range(taps):
                for b in range(taps):
                    term = shift_ref[b, y + a, :, lanes] * grad
                    new.append(totals[taps * a + b] + jnp.sum(term.reshape(broad // 8, 8, sub), axis=0))
            return tuple(new)

        zero = jnp.zeros((8, sub), F32)
        totals = lax.fori_loop(0, tall, one_row, (zero,) * (taps * taps))
        for tap in range(taps * taps):
            out_ref[tap : tap + 1, lanes] = jnp.sum(totals[tap], axis=0, keepdims=True)
    head_dim = gpw_ref.shape[1]
    start = out_ref.shape[0] - head_dim
    out_ref[taps * taps : start] = jnp.zeros((start - taps * taps, LANES), F32)
    out_ref[start:] = gpw_ref[0]


def backward_kernel(routes, *refs):
    count = len(routes)
    layout, gmix_ref = refs[:5], refs[5]
    arrived = refs[6 : 6 + count]
    dw_ref, grad0_ref, out_ref, pad_ref, shift_ref = refs[6 + count :]
    place = Place(layout)
    tall, broad = out_ref.shape[2:4]
    field = gmix_ref[0].reshape(tall, broad, LANES)
    fill_padded(pad_ref, field, arrived, [source(place.index) for _, _, source in routes], place)
    fill_shifted(shift_ref, pad_ref)

    def one_row(y, carry):
        grad = convolve(shift_ref, dw_ref, y, True)
        grad = grad + grad0_ref[0, pl.ds(pl.multiple_of(y * broad, broad), broad)]
        out_ref[0, 0, y] = jnp.where(place.live, grad, 0.0).astype(BF16)
        return carry

    lax.fori_loop(0, tall, one_row, 0)


def tile_spec(tall, broad, at):
    return pl.BlockSpec((1, 1, tall, broad, LANES), lambda j: (0, 0, 0, 0, at(j)))


def call(kernel, grid, in_specs, out_specs, out_shape, scratch, flops, moved):
    return pl.pallas_call(
        kernel,
        grid=(grid,),
        in_specs=in_specs,
        out_specs=out_specs,
        out_shape=out_shape,
        scratch_shapes=scratch,
        compiler_params=PARAMS,
        cost_estimate=pl.CostEstimate(flops=flops, bytes_accessed=moved, transcendentals=0),
    )


def local(
    qkv, cotangent, dw_weight, pw_weight, tile_image, tile_row, tile_col, image_height, image_width
):
    tall, broad, channels = qkv.shape[2:]
    positions = tall * broad
    head_dim = pw_weight.shape[0]
    taps = dw_weight.shape[0]
    third = channels // 3
    per = third // LANES
    steps = 3 * per
    tiles, groups = lax.axis_size("tile"), lax.axis_size("img")
    routes = halo_routes(tiles)
    layout = (tile_image, tile_row, tile_col, image_height, image_width)
    layout_specs = [SMEM] * 5
    shape = jax.ShapeDtypeStruct
    edge = REACH * broad
    state_rows = 2 * head_dim + 8

    same = lambda j: j
    flat_spec = lambda rows, at=same: pl.BlockSpec((rows, LANES), lambda j: (0, at(j)))
    member_spec = lambda rows: pl.BlockSpec((1, rows, LANES), lambda j: (j // per, 0, j % per))
    trio_spec = lambda rows: pl.BlockSpec((3, rows, LANES), lambda j: (0, 0, j))
    pad_scratch = [
        pltpu.VMEM((tall + 2 * REACH, broad + 2 * EDGE, LANES), F32),
        pltpu.VMEM((2 * REACH + 1, tall + 2 * REACH, broad, LANES), F32),
    ]
    conv_flops = 2 * taps * positions * channels

    sent = call(
        functools.partial(outgoing_kernel, routes),
        steps,
        layout_specs + [tile_spec(tall, broad, same)],
        [member_spec(edge)] * len(routes),
        [shape((3, edge, third), BF16)] * len(routes),
        [],
        positions * channels,
        2 * positions * channels,
    )(*layout, qkv)
    halo = [lax.ppermute(part, "tile", pairs) for part, (pairs, _, _) in zip(sent, routes)]

    mixed, merged, state = call(
        functools.partial(forward_kernel, routes, per, head_dim),
        steps,
        layout_specs
        + [tile_spec(tall, broad, same)]
        + [member_spec(edge)] * len(routes)
        + [flat_spec(taps), flat_spec(head_dim)],
        [flat_spec(positions), flat_spec(positions), pl.BlockSpec((state_rows, third), lambda j: (0, 0))],
        [
            shape((positions, channels), F32),
            shape((positions, channels), F32),
            shape((state_rows, third), F32),
        ],
        pad_scratch
        + [
            pltpu.VMEM((tall, broad, LANES), F32),
            pltpu.VMEM((per, positions, LANES), BF16),
            pltpu.VMEM((per, positions, LANES), F32),
        ],
        conv_flops * 4,
        12 * positions * channels,
    )(*layout, qkv, *halo, dw_weight, pw_weight)

    received = exchange(state, "tile")
    others = len(received)
    gstate, qgrad0, qgmix, qgpw = call(
        functools.partial(query_kernel, others, head_dim),
        per,
        layout_specs
        + [flat_spec(state_rows)] * (1 + others)
        + [tile_spec(tall, broad, same), flat_spec(positions), flat_spec(positions)]
        + [tile_spec(tall, broad, same), tile_spec(tall, broad, lambda j: j + per), flat_spec(head_dim)],
        [flat_spec(state_rows), flat_spec(positions), flat_spec(positions), flat_spec(head_dim)],
        [
            shape((state_rows, third), F32),
            shape((positions, third), F32),
            shape((positions, third), F32),
            shape((head_dim, third), F32),
        ],
        [],
        conv_flops,
        8 * positions * channels,
    )(*layout, state, *received, qkv, merged, mixed, cotangent, cotangent, pw_weight)

    received = exchange(gstate, "tile")
    k_at, v_at = (lambda j: j + per), (lambda j: j + 2 * per)
    results = call(
        functools.partial(value_kernel, others, routes, head_dim),
        per,
        layout_specs
        + [flat_spec(state_rows)] * (1 + others)
        + [tile_spec(tall, broad, k_at), tile_spec(tall, broad, v_at)]
        + [flat_spec(positions, k_at), flat_spec(positions, v_at)] * 2
        + [flat_spec(head_dim, k_at), flat_spec(head_dim, v_at)]
        + [flat_spec(positions), flat_spec(positions), flat_spec(head_dim)],
        [trio_spec(positions), trio_spec(positions), trio_spec(head_dim)] + [trio_spec(edge)] * len(routes),
        [
            shape((3, positions, third), F32),
            shape((3, positions, third), F32),
            shape((3, head_dim, third), F32),
        ]
        + [shape((3, edge, third), BF16)] * len(routes),
        [],
        conv_flops,
        16 * positions * channels,
    )(
        *layout, gstate, *received, qkv, qkv, merged, merged, mixed, mixed, pw_weight, pw_weight,
        qgrad0, qgmix, qgpw,
    )
    grad0, gmix, gpw = results[:3]
    grad_halo = [lax.ppermute(part, "tile", pairs) for part, (pairs, _, _) in zip(results[3:], routes)]

    gap = -(-taps // 8) * 8
    rows = gap + head_dim
    weights = call(
        functools.partial(weight_kernel, routes),
        steps,
        layout_specs
        + [tile_spec(tall, broad, same)]
        + [member_spec(edge)] * len(routes)
        + [member_spec(positions), member_spec(head_dim)],
        flat_spec(rows),
        shape((rows, channels), F32),
        pad_scratch,
        conv_flops * 4,
        8 * positions * channels,
    )(*layout, qkv, *halo, gmix, gpw)

    padded_rows = -(-rows // groups) * groups
    weights = jnp.pad(weights, ((0, padded_rows - rows), (0, 0)))
    parts = lax.all_to_all(weights.reshape(groups, padded_rows // groups, channels), "img", 0, 0)
    sums = [jnp.sum(parts, axis=0)]
    sums = sums + exchange(sums[0], "tile")
    while len(sums) > 1:
        sums = [sums[i] + sums[i + 1] for i in range(0, len(sums), 2)]
    norm = 1.0 / math.sqrt(positions * tiles * groups)
    share = (sums[0] * norm).astype(BF16)
    shares = lax.all_to_all(jnp.broadcast_to(share[None], (groups,) + share.shape), "img", 0, 0)
    whole = shares.reshape(padded_rows, channels).astype(F32)

    grad_source = call(
        functools.partial(backward_kernel, routes),
        steps,
        layout_specs
        + [member_spec(positions)]
        + [member_spec(edge)] * len(routes)
        + [flat_spec(taps), member_spec(positions)],
        tile_spec(tall, broad, same),
        shape((1, 1, tall, broad, channels), BF16),
        pad_scratch,
        conv_flops * 4,
        10 * positions * channels,
    )(*layout, gmix, *grad_halo, dw_weight, grad0)
    return grad_source, whole[:taps], whole[gap : gap + head_dim]


def solution(mesh):
    placed = (
        P("img", "tile", None, None, None),
        P("img", "tile", None, None, None),
        P(),
        P(),
        P("img", "tile"),
        P("img", "tile"),
        P("img", "tile"),
        P("img", None),
        P("img", None),
    )
    return jax.shard_map(
        local,
        mesh=mesh,
        in_specs=placed,
        out_specs=(P("img", "tile", None, None, None), P(), P()),
        check_vma=False,
    )
```

time: 427 us -> 128 us (0.30); the launches traced: 421 us -> 127 us
  waiting for transfers between devices: 166 us -> 41.7 us
  matrix products: 82.2 us -> 0 us
  local copies, waits for them, and re-layouts: 74.8 us -> 6.41 us
  Pallas kernels: 0 us -> 33.2 us
  other arithmetic: 25.8 us -> 3.44 us
  between operations: 19.1 us -> 2.75 us
  blocking collectives: 19.8 us -> 12.1 us
  starting transfers between devices: 33.3 us -> 27.9 us
    psum x2 -> x0, waiting for transfers between devices: 151 us -> none  [the longest x1 119 us: local(): summed_dw, summed_pw = lax.psum((grad_dwk, grad_pwk), ('tile', 'img'))]
    dot_general x20 -> x0, matrix products: 41.7 us -> none  [the longest x1 6.72 us: block_grad(): jnp.einsum('bgiho,gh->ibho', blocked, jnp.eye(per_block, dtype=jnp.float3...]
    conv_general_dilated x3 -> x0, matrix products: 40.4 us -> none  [depthwise(): lax.conv_general_dilated(padded[None], shaped, (1, 1), 'VALID', dimension...]
    pallas_call x0 -> x6, Pallas kernels: none -> 33.2 us  [the longest x1 9.96 us: local(): call(functools.partial(forward_kernel, routes, per, head_dim), steps, lay...]
    ppermute x12 -> x15, waiting for transfers between devices: 14.5 us -> 41.7 us  [the longest x9 21.7 us: exchange(): lax.ppermute(value, axis, [(s, s ^ m) for s in range(count)])]
    psum x2 -> x0, blocking collectives: 19.8 us -> none  [image_total(): summed_states, summed_sums = lax.psum((spread_states, spread_sums), 'tile')]
    another operation x17 -> x0, local copies, waits for them, and re-layouts: 19.1 us -> none  [the longest x1 3.92 us: depthwise(): return result[0]]
    concatenate x9 -> x0, local copies, waits for them, and re-layouts: 18.2 us -> none  [local(): jnp.concatenate([grad_queries.reshape(positions, inner_width), grad_keys....]
  transfers between devices with their start and end apart: 14 -> 16, of which waited for: 4 -> 8; matrix products, arithmetic and copies ran while one was open for 12% -> 1% of each run, Pallas kernels for 0% -> 6%
where the time goes in v1:
time: 128 us; the launch traced here: 127 us
  waiting for transfers between devices  41.7 us (33%)
  Pallas kernels  33.2 us (26%)
  starting transfers between devices  27.9 us (22%)
  blocking collectives  12.1 us (9%)
  local copies, waits for them, and re-layouts  6.41 us (5%)
  other arithmetic  3.44 us (3%)
  between operations  2.75 us (2%)
    ppermute x9, waiting for transfers between devices, exchange(): lax.ppermute(value, axis, [(s, s ^ m) for s in range(count)])  21.7 us
    ppermute x6, waiting for transfers between devices, local(): lax.ppermute(part, 'tile', pairs)  20.1 us
    ppermute x9, starting transfers between devices, exchange(): lax.ppermute(value, axis, [(s, s ^ m) for s in range(count)])  13.8 us
    all_to_all x1, blocking collectives, local(): lax.all_to_all(weights.reshape(groups, padded_rows // groups, channels),...  12.1 us
    ppermute x6, starting transfers between devices, local(): lax.ppermute(part, 'tile', pairs)  10 us
    pallas_call x1, Pallas kernels, local(): call(functools.partial(forward_kernel, routes, per, head_dim), steps, lay...  9.96 us
    pallas_call x1, Pallas kernels, local(): call(functools.partial(backward_kernel, routes), steps, layout_specs + [m...  7.74 us
    pallas_call x1, Pallas kernels, local(): call(functools.partial(weight_kernel, routes), steps, layout_specs + [til...  6.93 us
  transfers between devices with their start and end apart: 16, of which 8 were waited for; matrix products, arithmetic and copies ran while one was open for 1% of the time, Pallas kernels for 6%

profile of v1, /device:TPU:0, one launch (start us, length us, event | category | flops | bytes accessed | tf_op | source)
XLA Modules:
  0.0 127.5 jit_solution(1605138128260462867)
XLA Ops:
  2.6 1.1 copy-done
  5.0 1.2 shard_map.112
  6.2 3.1 %collective-permute-start = (bf16[3,64,512]{2,1,0:T(8,128)(2,1)S(1)}, bf16[3,64,512]{2,1,0:T(8,128)(2,1)S(1)}, u32[]{:S(2)}, u32[]{:S(2)}) collective-permute-start(bf16[3,64,512]{2,1,0:T(8,128)(2,1)S(1)} %get-tuple-element.19), channel_id=1, source_target_pairs={{0,8},{8,0},{16,24},{24,16},{1,9},{9,1},{17,25},{25,17},{2,10},{10... | collective-permute-start | bytes 589832 | tf_op jit(solution)/shard_map/ppermute | solution.py:437
  9.3 2.6 %collective-permute-start.1 = (bf16[3,64,512]{2,1,0:T(8,128)(2,1)S(1)}, bf16[3,64,512]{2,1,0:T(8,128)(2,1)S(1)}, u32[]{:S(2)}, u32[]{:S(2)}) collective-permute-start(bf16[3,64,512]{2,1,0:T(8,128)(2,1)S(1)} %get-tuple-element.20), channel_id=1, source_target_pairs={{0,16},{8,24},{16,0},{24,8},{1,17},{9,25},{17,1},{25,9},{2,18},{10... | collective-permute-start | bytes 589832 | tf_op jit(solution)/shard_map/ppermute | solution.py:437
  11.9 5.7 %collective-permute-done.refs_6_ = bf16[3,64,512]{2,1,0:T(8,128)(2,1)S(1)} collective-permute-done((bf16[3,64,512]{2,1,0:T(8,128)(2,1)S(1)}, bf16[3,64,512]{2,1,0:T(8,128)(2,1)S(1)}, u32[]{:S(2)}, u32[]{:S(2)}) %collective-permute-start) | collective-permute-done | bytes 196640 | tf_op jit(solution)/shard_map/ppermute | solution.py:437
  17.7 8.8 %collective-permute-done.1.refs_7_ = bf16[3,64,512]{2,1,0:T(8,128)(2,1)S(1)} collective-permute-done((bf16[3,64,512]{2,1,0:T(8,128)(2,1)S(1)}, bf16[3,64,512]{2,1,0:T(8,128)(2,1)S(1)}, u32[]{:S(2)}, u32[]{:S(2)}) %collective-permute-start.1) | collective-permute-done | bytes 196640 | tf_op jit(solution)/shard_map/ppermute | solution.py:437
  26.5 0.9 copy-done.1
  27.4 0.9 copy-done.3
  28.3 10.0 %shard_map.113 = (f32[256,1536]{1,0:T(8,128)S(1)}, f32[256,1536]{1,0:T(8,128)S(1)}, f32[72,512]{1,0:T(8,128)S(1)}) custom-call(s32[1,1]{1,0:T(1,128)S(6)} %copy.12.refs_0_, s32[1,1]{1,0:T(1,128)S(6)} %copy.13.refs_1_, s32[1,1]{1,0:T(1,128)S(6)} %copy.14.refs_2_, s32[1,2]{1,0:T(1,128)S(1)} %copy-done.5, s32[1,2]{1,0:T(1,128)S(1)} %copy-done.7, ...), custom_call_target="tpu_custom_call" | custom-call | flops 78643200 | bytes 4718592 | tf_op jit(solution)/shard_map/pallas_call | solution.py:439
  38.3 2.5 %collective-permute-start.5 = (f32[72,512]{1,0:T(8,128)S(1)}, f32[72,512]{1,0:T(8,128)S(1)}, u32[]{:S(2)}, u32[]{:S(2)}) collective-permute-start(f32[72,512]{1,0:T(8,128)S(1)} %get-tuple-element.22.refs_5_), channel_id=1, source_target_pairs={{0,24},{8,16},{16,8},{24,0},{1,25},{9,17},{17,9},{25,1},{2,26},{10... | collective-permute-start | bytes 442376 | tf_op jit(solution)/shard_map/ppermute | solution.py:60
  40.9 2.3 %collective-permute-start.4 = (f32[72,512]{1,0:T(8,128)S(1)}, f32[72,512]{1,0:T(8,128)S(1)}, u32[]{:S(2)}, u32[]{:S(2)}) collective-permute-start(f32[72,512]{1,0:T(8,128)S(1)} %get-tuple-element.22.refs_5_), channel_id=1, source_target_pairs={{0,16},{8,24},{16,0},{24,8},{1,17},{9,25},{17,1},{25,9},{2,18},{10... | collective-permute-start | bytes 442376 | tf_op jit(solution)/shard_map/ppermute | solution.py:60
  43.3 2.8 %collective-permute-done.5.refs_8_ = f32[72,512]{1,0:T(8,128)S(1)} collective-permute-done((f32[72,512]{1,0:T(8,128)S(1)}, f32[72,512]{1,0:T(8,128)S(1)}, u32[]{:S(2)}, u32[]{:S(2)}) %collective-permute-start.5) | collective-permute-done | bytes 147488 | tf_op jit(solution)/shard_map/ppermute | solution.py:60
  46.1 7.4 %collective-permute-done.4.refs_7_ = f32[72,512]{1,0:T(8,128)S(1)} collective-permute-done((f32[72,512]{1,0:T(8,128)S(1)}, f32[72,512]{1,0:T(8,128)S(1)}, u32[]{:S(2)}, u32[]{:S(2)}) %collective-permute-start.4) | collective-permute-done | bytes 147488 | tf_op jit(solution)/shard_map/ppermute | solution.py:60
  53.5 4.0 %shard_map.114 = (f32[72,512]{1,0:T(8,128)S(1)}, f32[256,512]{1,0:T(8,128)S(1)}, f32[256,512]{1,0:T(8,128)S(1)}, f32[32,512]{1,0:T(8,128)S(1)}) custom-call(s32[1,1]{1,0:T(1,128)S(6)} %copy.12.refs_0_, s32[1,1]{1,0:T(1,128)S(6)} %copy.13.refs_1_, s32[1,1]{1,0:T(1,128)S(6)} %copy.14.refs_2_, s32[1,2]{1,0:T(1,128)S(1)} %copy-done.5, s32[1,2]{1,0:T(1,128)S(1)} %copy-done.7, ...), custom_call_target="tpu_custom_call" | custom-call | flops 19660800 | bytes 3145728 | tf_op jit(solution)/shard_map/pallas_call | solution.py:464
  57.5 2.5 %collective-permute-start.8 = (f32[72,512]{1,0:T(8,128)S(1)}, f32[72,512]{1,0:T(8,128)S(1)}, u32[]{:S(2)}, u32[]{:S(2)}) collective-permute-start(f32[72,512]{1,0:T(8,128)S(1)} %get-tuple-element.25.refs_5_), channel_id=1, source_target_pairs={{0,24},{8,16},{16,8},{24,0},{1,25},{9,17},{17,9},{25,1},{2,26},{10... | collective-permute-start | bytes 442376 | tf_op jit(solution)/shard_map/ppermute | solution.py:60
  60.0 1.9 %collective-permute-start.6 = (f32[72,512]{1,0:T(8,128)S(1)}, f32[72,512]{1,0:T(8,128)S(1)}, u32[]{:S(2)}, u32[]{:S(2)}) collective-permute-start(f32[72,512]{1,0:T(8,128)S(1)} %get-tuple-element.25.refs_5_), channel_id=1, source_target_pairs={{0,8},{8,0},{16,24},{24,16},{1,9},{9,1},{17,25},{25,17},{2,10},{10... | collective-permute-start | bytes 442376 | tf_op jit(solution)/shard_map/ppermute | solution.py:60
  62.0 4.2 %collective-permute-done.8.refs_8_ = f32[72,512]{1,0:T(8,128)S(1)} collective-permute-done((f32[72,512]{1,0:T(8,128)S(1)}, f32[72,512]{1,0:T(8,128)S(1)}, u32[]{:S(2)}, u32[]{:S(2)}) %collective-permute-start.8) | collective-permute-done | bytes 147488 | tf_op jit(solution)/shard_map/ppermute | solution.py:60
  66.2 5.1 %collective-permute-done.7.refs_7_ = f32[72,512]{1,0:T(8,128)S(1)} collective-permute-done((f32[72,512]{1,0:T(8,128)S(1)}, f32[72,512]{1,0:T(8,128)S(1)}, u32[]{:S(2)}, u32[]{:S(2)}) %collective-permute-start.7) | collective-permute-done | bytes 147488 | tf_op jit(solution)/shard_map/ppermute | solution.py:60
  71.3 3.4 %shard_map.115 = (f32[3,256,512]{2,1,0:T(8,128)S(1)}, f32[3,256,512]{2,1,0:T(8,128)S(1)}, f32[3,32,512]{2,1,0:T(8,128)S(1)}, bf16[3,64,512]{2,1,0:T(8,128)(2,1)S...) custom-call(s32[1,1]{1,0:T(1,128)S(6)} %copy.12.refs_0_, s32[1,1]{1,0:T(1,128)S(6)} %copy.13.refs_1_, ...), custom_call_target="tpu_custom_call" | custom-call | flops 19660800 | bytes 6291456 | tf_op jit(solution)/shard_map/pallas_call | solution.py:485
  74.7 6.9 %shard_map.117 = f32[64,1536]{1,0:T(8,128)S(1)} custom-call(s32[1,1]{1,0:T(1,128)S(6)} %copy.12.refs_0_, s32[1,1]{1,0:T(1,128)S(6)} %copy.13.refs_1_, s32[1,1]{1,0:T(1,128)S(6)} %copy.14.refs_2_, s32[1,2]{1,0:T(1,128)S(1)} %copy-done.5, s32[1,2]{1,0:T(1,128)S(1)} %copy-done.7, bf16[1,1,8,32,1536]{4,3,2,1,0:T(8,128)(2,1)S(1)} %copy-done, ...), custom_call_target="tpu_custom_call" | custom-call | flops 78643200 | bytes 3145728 | tf_op jit(solution)/shard_map/pallas_call | solution.py:513
  81.7 12.1 %all_to_all.10 = f32[8,8,1536]{2,1,0:T(8,128)} all-to-all(f32[8,8,1536]{2,1,0:T(8,128)S(1)} %bitcast.5), channel_id=1, replica_groups=mesh['tile'=4,'img'=8] {'img'}, dimensions={0} | all-to-all | bytes 786432 | tf_op jit(solution)/shard_map/all_to_all | solution.py:529
  93.8 1.6 %reduce_sum.9 = f32[8,1536]{1,0:T(8,128)} reduce(f32[8,8,1536]{2,1,0:T(8,128)} %all_to_all.10, f32[]{:T(128)} %constant.2.clone.1), dimensions={0}, to_apply=%region_0.1 | reduce | flops 86016 | bytes 442372 | tf_op jit(solution)/shard_map/reduce_sum | solution.py:530
  95.4 1.5 %collective-permute-start.14 = (f32[8,1536]{1,0:T(8,128)}, f32[8,1536]{1,0:T(8,128)S(1)}, u32[]{:S(2)}, u32[]{:S(2)}) collective-permute-start(f32[8,1536]{1,0:T(8,128)} %reduce_sum.9), channel_id=1, source_target_pairs={{0,24},{8,16},{16,8},{24,0},{1,25},{9,17},{17,9},{25,1},{2,26},{10... | collective-permute-start | bytes 147464 | tf_op jit(solution)/shard_map/ppermute | solution.py:60
  96.9 2.9 %collective-permute-start.12 = (f32[8,1536]{1,0:T(8,128)}, f32[8,1536]{1,0:T(8,128)S(1)}, u32[]{:S(2)}, u32[]{:S(2)}) collective-permute-start(f32[8,1536]{1,0:T(8,128)} %reduce_sum.9), channel_id=1, source_target_pairs={{0,8},{8,0},{16,24},{24,16},{1,9},{9,1},{17,25},{25,17},{2,10},{10... | collective-permute-start | bytes 147464 | tf_op jit(solution)/shard_map/ppermute | solution.py:60
  99.8 2.0 %collective-permute-start.10 = (bf16[3,64,512]{2,1,0:T(8,128)(2,1)}, bf16[3,64,512]{2,1,0:T(8,128)(2,1)}, u32[]{:S(2)}, u32[]{:S(2)}) collective-permute-start(bf16[3,64,512]{2,1,0:T(8,128)(2,1)} %copy-done.10), channel_id=1, source_target_pairs={{0,16},{8,24},{16,0},{24,8},{1,17},{9,25},{17,1},{25,9},{2,18},{10... | collective-permute-start | bytes 589832 | tf_op jit(solution)/shard_map/ppermute | solution.py:509
  101.9 2.3 %collective-permute-start.11 = (bf16[3,64,512]{2,1,0:T(8,128)(2,1)}, bf16[3,64,512]{2,1,0:T(8,128)(2,1)}, u32[]{:S(2)}, u32[]{:S(2)}) collective-permute-start(bf16[3,64,512]{2,1,0:T(8,128)(2,1)} %copy-done.9), channel_id=1, source_target_pairs={{0,24},{8,16},{16,8},{24,0},{1,25},{9,17},{17,9},{25,1},{2,26},{10... | collective-permute-start | bytes 589832 | tf_op jit(solution)/shard_map/ppermute | solution.py:509
  104.2 2.1 %collective-permute-done.12 = f32[8,1536]{1,0:T(8,128)S(1)} collective-permute-done((f32[8,1536]{1,0:T(8,128)}, f32[8,1536]{1,0:T(8,128)S(1)}, u32[]{:S(2)}, u32[]{:S(2)}) %collective-permute-start.12) | collective-permute-done | bytes 49184 | tf_op jit(solution)/shard_map/ppermute | solution.py:60
  106.3 0.8 multiply_convert_fusion
  107.8 4.0 %all-to-all-start.1 = ((bf16[8,8,1536]{2,1,0:T(8,128)(2,1)}), bf16[8,8,1536]{2,1,0:T(8,128)(2,1)}, u32[]{:S(2)}, u32[]{:S(2)}) async-start(bf16[8,8,1536]{2,1,0:T(8,128)(2,1)} %broadcast_in_dim.2), calls=%async_computation.1 | async-start | bytes 393216 | tf_op jit(solution)/shard_map/all_to_all | solution.py:536
  111.8 5.5 %collective-permute-done.10.refs_7_ = bf16[3,64,512]{2,1,0:T(8,128)(2,1)} collective-permute-done((bf16[3,64,512]{2,1,0:T(8,128)(2,1)}, bf16[3,64,512]{2,1,0:T(8,128)(2,1)}, u32[]{:S(2)}, u32[]{:S(2)}) %collective-permute-start.10) | collective-permute-done | bytes 196640 | tf_op jit(solution)/shard_map/ppermute | solution.py:509
  117.4 7.7 %shard_map.116 = bf16[1,1,8,32,1536]{4,3,2,1,0:T(8,128)(2,1)} custom-call(s32[1,1]{1,0:T(1,128)S(6)} %copy.12.refs_0_, s32[1,1]{1,0:T(1,128)S(6)} %copy.13.refs_1_, s32[1,1]{1,0:T(1,128)S(6)} %copy.14.refs_2_, s32[1,2]{1,0:T(1,128)S(1)} %copy-done.6, s32[1,2]{1,0:T(1,128)S(1)} %copy-done.8, f32[3,256,512]{2,1,0:T(8,128)S(1)} %get-tuple-element.29.refs_5_.refs_9_, ...), custom_call_target="tpu_custom_call" | custom-call | flops 78643200 | bytes 3932160 | tf_op jit(solution)/shard_map/pallas_call | solution.py:539
  125.1 1.0 fusion
  (37 shorter events, 3.6 us)
Async XLA Ops:
  2.6 1.1 copy-start
  3.7 0.7 copy-start.5
  4.4 0.7 copy-start.7
  5.0 48.5 %copy-start.2 = (bf16[1,1,8,32,1024]{4,3,2,1,0:T(8,128)(2,1)S(1)}, bf16[1,1,8,32,1024]{4,3,2,1,0:T(8,128)(2,1)}, u32[]{:S(2)}) copy-start(bf16[1,1,8,32,1024]{4,3,2,1,0:T(8,128)(2,1)} %refs_13_.1) | copy-start | bytes 1572868
  6.2 11.4 %collective-permute-start = (bf16[3,64,512]{2,1,0:T(8,128)(2,1)S(1)}, bf16[3,64,512]{2,1,0:T(8,128)(2,1)S(1)}, u32[]{:S(2)}, u32[]{:S(2)}) collective-permute-start(bf16[3,64,512]{2,1,0:T(8,128)(2,1)S(1)} %get-tuple-element.19), channel_id=1, source_target_pairs={{0,8},{8,0},{16,24},{24,16},{1,9},{9,1},{17,25},{25,17},{2,10},{10... | collective-permute-start | bytes 589832 | tf_op jit(solution)/shard_map/ppermute | solution.py:437
  9.3 17.2 %collective-permute-start.1 = (bf16[3,64,512]{2,1,0:T(8,128)(2,1)S(1)}, bf16[3,64,512]{2,1,0:T(8,128)(2,1)S(1)}, u32[]{:S(2)}, u32[]{:S(2)}) collective-permute-start(bf16[3,64,512]{2,1,0:T(8,128)(2,1)S(1)} %get-tuple-element.20), channel_id=1, source_target_pairs={{0,16},{8,24},{16,0},{24,8},{1,17},{9,25},{17,1},{25,9},{2,18},{10... | collective-permute-start | bytes 589832 | tf_op jit(solution)/shard_map/ppermute | solution.py:437
  11.9 14.6 %collective-permute-start.2 = (bf16[3,64,512]{2,1,0:T(8,128)(2,1)S(1)}, bf16[3,64,512]{2,1,0:T(8,128)(2,1)S(1)}, u32[]{:S(2)}, u32[]{:S(2)}) collective-permute-start(bf16[3,64,512]{2,1,0:T(8,128)(2,1)S(1)} %get-tuple-element.21), channel_id=1, source_target_pairs={{0,24},{8,16},{16,8},{24,0},{1,25},{9,17},{17,9},{25,1},{2,26},{10... | collective-permute-start | bytes 589832 | tf_op jit(solution)/shard_map/ppermute | solution.py:437
  26.5 0.9 copy-start.1
  27.4 0.9 copy-start.3
  38.3 7.8 %collective-permute-start.5 = (f32[72,512]{1,0:T(8,128)S(1)}, f32[72,512]{1,0:T(8,128)S(1)}, u32[]{:S(2)}, u32[]{:S(2)}) collective-permute-start(f32[72,512]{1,0:T(8,128)S(1)} %get-tuple-element.22.refs_5_), channel_id=1, source_target_pairs={{0,24},{8,16},{16,8},{24,0},{1,25},{9,17},{17,9},{25,1},{2,26},{10... | collective-permute-start | bytes 442376 | tf_op jit(solution)/shard_map/ppermute | solution.py:60
  40.9 12.7 %collective-permute-start.4 = (f32[72,512]{1,0:T(8,128)S(1)}, f32[72,512]{1,0:T(8,128)S(1)}, u32[]{:S(2)}, u32[]{:S(2)}) collective-permute-start(f32[72,512]{1,0:T(8,128)S(1)} %get-tuple-element.22.refs_5_), channel_id=1, source_target_pairs={{0,16},{8,24},{16,0},{24,8},{1,17},{9,25},{17,1},{25,9},{2,18},{10... | collective-permute-start | bytes 442376 | tf_op jit(solution)/shard_map/ppermute | solution.py:60
  43.2 10.3 %collective-permute-start.3 = (f32[72,512]{1,0:T(8,128)S(1)}, f32[72,512]{1,0:T(8,128)S(1)}, u32[]{:S(2)}, u32[]{:S(2)}) collective-permute-start(f32[72,512]{1,0:T(8,128)S(1)} %get-tuple-element.22.refs_5_), channel_id=1, source_target_pairs={{0,8},{8,0},{16,24},{24,16},{1,9},{9,1},{17,25},{25,17},{2,10},{10... | collective-permute-start | bytes 442376 | tf_op jit(solution)/shard_map/ppermute | solution.py:60
  57.5 8.6 %collective-permute-start.8 = (f32[72,512]{1,0:T(8,128)S(1)}, f32[72,512]{1,0:T(8,128)S(1)}, u32[]{:S(2)}, u32[]{:S(2)}) collective-permute-start(f32[72,512]{1,0:T(8,128)S(1)} %get-tuple-element.25.refs_5_), channel_id=1, source_target_pairs={{0,24},{8,16},{16,8},{24,0},{1,25},{9,17},{17,9},{25,1},{2,26},{10... | collective-permute-start | bytes 442376 | tf_op jit(solution)/shard_map/ppermute | solution.py:60
  60.0 11.2 %collective-permute-start.7 = (f32[72,512]{1,0:T(8,128)S(1)}, f32[72,512]{1,0:T(8,128)S(1)}, u32[]{:S(2)}, u32[]{:S(2)}) collective-permute-start(f32[72,512]{1,0:T(8,128)S(1)} %get-tuple-element.25.refs_5_), channel_id=1, source_target_pairs={{0,16},{8,24},{16,0},{24,8},{1,17},{9,25},{17,1},{25,9},{2,18},{10... | collective-permute-start | bytes 442376 | tf_op jit(solution)/shard_map/ppermute | solution.py:60
  60.0 11.2 %collective-permute-start.6 = (f32[72,512]{1,0:T(8,128)S(1)}, f32[72,512]{1,0:T(8,128)S(1)}, u32[]{:S(2)}, u32[]{:S(2)}) collective-permute-start(f32[72,512]{1,0:T(8,128)S(1)} %get-tuple-element.25.refs_5_), channel_id=1, source_target_pairs={{0,8},{8,0},{16,24},{24,16},{1,9},{9,1},{17,25},{25,17},{2,10},{10... | collective-permute-start | bytes 442376 | tf_op jit(solution)/shard_map/ppermute | solution.py:60
  74.7 7.0 %copy-start.9 = (bf16[3,64,512]{2,1,0:T(8,128)(2,1)}, bf16[3,64,512]{2,1,0:T(8,128)(2,1)S(1)}, u32[]{:S(2)}) copy-start(bf16[3,64,512]{2,1,0:T(8,128)(2,1)S(1)} %get-tuple-element.32) | copy-start | bytes 589828
  74.7 7.0 %copy-start.10 = (bf16[3,64,512]{2,1,0:T(8,128)(2,1)}, bf16[3,64,512]{2,1,0:T(8,128)(2,1)S(1)}, u32[]{:S(2)}) copy-start(bf16[3,64,512]{2,1,0:T(8,128)(2,1)S(1)} %get-tuple-element.31) | copy-start | bytes 589828
  74.7 7.0 %copy-start.11 = (bf16[3,64,512]{2,1,0:T(8,128)(2,1)}, bf16[3,64,512]{2,1,0:T(8,128)(2,1)S(1)}, u32[]{:S(2)}) copy-start(bf16[3,64,512]{2,1,0:T(8,128)(2,1)S(1)} %get-tuple-element.30) | copy-start | bytes 589828
  81.7 35.7 %copy-start.4 = (f32[25,1536]{1,0:T(8,128)S(1)}, f32[25,1536]{1,0:T(8,128)}, u32[]{:S(2)}) copy-start(f32[25,1536]{1,0:T(8,128)} %refs_9_.7) | copy-start | bytes 460804
  81.7 35.7 %copy-start.6 = (s32[1,2]{1,0:T(1,128)S(1)}, s32[1,2]{1,0:T(1,128)}, u32[]{:S(2)}) copy-start(s32[1,2]{1,0:T(1,128)} %refs_3_.11) | copy-start | bytes 28
  81.7 35.7 %copy-start.8 = (s32[1,2]{1,0:T(1,128)S(1)}, s32[1,2]{1,0:T(1,128)}, u32[]{:S(2)}) copy-start(s32[1,2]{1,0:T(1,128)} %refs_4_.11) | copy-start | bytes 28
  95.4 6.5 %collective-permute-start.14 = (f32[8,1536]{1,0:T(8,128)}, f32[8,1536]{1,0:T(8,128)S(1)}, u32[]{:S(2)}, u32[]{:S(2)}) collective-permute-start(f32[8,1536]{1,0:T(8,128)} %reduce_sum.9), channel_id=1, source_target_pairs={{0,24},{8,16},{16,8},{24,0},{1,25},{9,17},{17,9},{25,1},{2,26},{10... | collective-permute-start | bytes 147464 | tf_op jit(solution)/shard_map/ppermute | solution.py:60
  96.9 7.3 %collective-permute-start.13 = (f32[8,1536]{1,0:T(8,128)}, f32[8,1536]{1,0:T(8,128)S(1)}, u32[]{:S(2)}, u32[]{:S(2)}) collective-permute-start(f32[8,1536]{1,0:T(8,128)} %reduce_sum.9), channel_id=1, source_target_pairs={{0,16},{8,24},{16,0},{24,8},{1,17},{9,25},{17,1},{25,9},{2,18},{10... | collective-permute-start | bytes 147464 | tf_op jit(solution)/shard_map/ppermute | solution.py:60
  96.9 9.4 %collective-permute-start.12 = (f32[8,1536]{1,0:T(8,128)}, f32[8,1536]{1,0:T(8,128)S(1)}, u32[]{:S(2)}, u32[]{:S(2)}) collective-permute-start(f32[8,1536]{1,0:T(8,128)} %reduce_sum.9), channel_id=1, source_target_pairs={{0,8},{8,0},{16,24},{24,16},{1,9},{9,1},{17,25},{25,17},{2,10},{10... | collective-permute-start | bytes 147464 | tf_op jit(solution)/shard_map/ppermute | solution.py:60
  99.8 12.0 %collective-permute-start.9 = (bf16[3,64,512]{2,1,0:T(8,128)(2,1)}, bf16[3,64,512]{2,1,0:T(8,128)(2,1)S(1)}, u32[]{:S(2)}, u32[]{:S(2)}) collective-permute-start(bf16[3,64,512]{2,1,0:T(8,128)(2,1)} %copy-done.11), channel_id=1, source_target_pairs={{0,8},{8,0},{16,24},{24,16},{1,9},{9,1},{17,25},{25,17},{2,10},{10... | collective-permute-start | bytes 589832 | tf_op jit(solution)/shard_map/ppermute | solution.py:509
  99.8 17.5 %collective-permute-start.10 = (bf16[3,64,512]{2,1,0:T(8,128)(2,1)}, bf16[3,64,512]{2,1,0:T(8,128)(2,1)}, u32[]{:S(2)}, u32[]{:S(2)}) collective-permute-start(bf16[3,64,512]{2,1,0:T(8,128)(2,1)} %copy-done.10), channel_id=1, source_target_pairs={{0,16},{8,24},{16,0},{24,8},{1,17},{9,25},{17,1},{25,9},{2,18},{10... | collective-permute-start | bytes 589832 | tf_op jit(solution)/shard_map/ppermute | solution.py:509
  101.9 15.4 %collective-permute-start.11 = (bf16[3,64,512]{2,1,0:T(8,128)(2,1)}, bf16[3,64,512]{2,1,0:T(8,128)(2,1)}, u32[]{:S(2)}, u32[]{:S(2)}) collective-permute-start(bf16[3,64,512]{2,1,0:T(8,128)(2,1)} %copy-done.9), channel_id=1, source_target_pairs={{0,24},{8,16},{16,8},{24,0},{1,25},{9,17},{17,9},{25,1},{2,26},{10... | collective-permute-start | bytes 589832 | tf_op jit(solution)/shard_map/ppermute | solution.py:509
  107.8 17.3 %all-to-all-start.1 = ((bf16[8,8,1536]{2,1,0:T(8,128)(2,1)}), bf16[8,8,1536]{2,1,0:T(8,128)(2,1)}, u32[]{:S(2)}, u32[]{:S(2)}) async-start(bf16[8,8,1536]{2,1,0:T(8,128)(2,1)} %broadcast_in_dim.2), calls=%async_computation.1 | async-start | bytes 393216 | tf_op jit(solution)/shard_map/all_to_all | solution.py:536

commit v2 on v1

v2 whole, which is shorter than its diff:
```python
import functools
import math

import jax
import jax.numpy as jnp
from jax import lax
from jax.experimental import pallas as pl
from jax.experimental.pallas import tpu as pltpu
from jax.sharding import PartitionSpec as P

EPSILON = 1e-06
LANES = 256
REACH = 2
EDGE = 8
COST = 1000
BF16 = jnp.bfloat16
F32 = jnp.float32
PARAMS = pltpu.CompilerParams(vmem_limit_bytes=16 * 1024 * 1024)
SMEM = pl.BlockSpec(memory_space=pltpu.SMEM)


class Place:
    def __init__(self, layout_refs):
        image_ref, row_ref, col_ref, tall_ref, wide_ref = layout_refs
        slot = image_ref[0, 0]
        slots = tall_ref.shape[1]
        tall = wide = start = jnp.int32(0)
        for s in range(slots):
            tall = jnp.where(slot == s, tall_ref[0, s], tall)
            wide = jnp.where(slot == s, wide_ref[0, s], wide)
            start = start + jnp.where(s < slot, tall_ref[0, s] * wide_ref[0, s], 0)
        self.live = slot < slots
        self.tall, self.wide = tall, wide
        self.row, self.col = row_ref[0, 0], col_ref[0, 0]
        self.within = self.row * wide + self.col
        self.index = start + self.within
        self.above = self.live & (self.row > 0)
        self.below = self.live & (self.row < tall - 1)

    def same_image(self, delta):
        other = self.within + delta
        return self.live & (other >= 0) & (other < self.tall * self.wide)


class Routes:
    def __init__(self, count):
        self.count = count
        self.relayed = count == 4
        self.shifts = [k for k in (1, -1, 2, -2, 3, -3) if abs(k) < count]
        self.sent = 2 if self.relayed else len(self.shifts)
        self.arriving = 3 if self.relayed else len(self.shifts)

    def targets(self, place):
        if not self.relayed:
            return [jnp.int32(k) for k in self.shifts]
        near, far, last = ((place.index ^ m) - place.index for m in (1, 2, 3))
        return [near, jnp.where(place.same_image(far), far, last)]

    def sources(self, place):
        if not self.relayed:
            return [jnp.int32(-k) for k in self.shifts]
        return [(place.index ^ m) - place.index for m in (1, 2, 3)]

    def move(self, sent):
        count = self.count
        if not self.relayed:
            return [
                lax.ppermute(part, "tile", [(s, s + k) for s in range(max(0, -k), min(count, count - k))])
                for part, k in zip(sent, self.shifts)
            ]
        near, far = (
            lax.ppermute(part, "tile", [(s, s ^ m) for s in range(count)]) for part, m in zip(sent, (1, 2))
        )
        return [near, far, lax.ppermute(far, "tile", [(s, s ^ 1) for s in range(count)])]


def exchange(value, axis, masks=None):
    count = lax.axis_size(axis)
    masks = range(1, count) if masks is None else masks
    return [lax.ppermute(value, axis, [(s, s ^ m) for s in range(count)]) for m in masks]


def split(x):
    high = x.astype(BF16)
    return high, (x - high.astype(F32)).astype(BF16)


def contract(a, b, dims):
    return lax.dot_general(a, b, (dims, ((), ())), preferred_element_type=F32)


NN = ((1,), (0,))
NT = ((1,), (1,))
TN = ((0,), (0,))


def dot(a, b, dims):
    total = contract(a[0], b[0], dims)
    if b[1] is not None:
        total = total + contract(a[0], b[1], dims)
    if a[1] is not None:
        total = total + contract(a[1], b[0], dims)
    return total


def exact(x):
    return x.astype(BF16), None


def same_head(head_dim):
    rows = lax.broadcasted_iota(jnp.int32, (LANES, LANES), 0) // head_dim
    cols = lax.broadcasted_iota(jnp.int32, (LANES, LANES), 1) // head_dim
    return rows == cols


def spread(compact, mask):
    tall = jnp.concatenate([compact] * (LANES // compact.shape[0]), axis=0)
    return jnp.where(mask, tall, 0.0)


def gather_blocks(full, mask, head_dim):
    kept = jnp.where(mask, full, 0.0)
    return jnp.sum(kept.reshape(LANES // head_dim, head_dim, LANES), axis=0)


def payload(field, place, delta):
    tall, broad, lanes = field.shape
    size = REACH * broad
    top = field[:REACH].reshape(size, lanes)
    bottom = field[tall - REACH :].reshape(size, lanes)
    left = field[:, :EDGE].reshape(size, lanes)
    right = field[:, broad - EDGE :].reshape(size, lanes)
    rows = jnp.where(delta > 0, bottom, top)
    cols = jnp.where(place.col == 0, right, left)
    beside = (place.wide == 2) & (delta == jnp.where(place.col == 0, 1, -1))
    return jnp.where(beside, cols, rows)


def edge_of(ref, size):
    rows = ref[0] if len(ref.shape) == 3 else ref[:size]
    return rows.astype(F32)


def pack_state(state, total):
    rows = jnp.concatenate([state, total, jnp.zeros((7, LANES), F32)], axis=0)
    return jnp.concatenate(split(rows), axis=0)


def unpack_state(ref, offset):
    rows = ref[offset:].astype(F32)
    half = rows.shape[0] // 2
    return rows[:half] + rows[half:]


def total_state(own_ref, others, place, offset, others_offset):
    total = unpack_state(own_ref, offset)
    for m, other in enumerate(others, 1):
        delta = (place.index ^ m) - place.index
        total = total + jnp.where(place.same_image(delta), unpack_state(other, others_offset), 0.0)
    return total


def fill_padded(pad_ref, field, arrived_refs, deltas, place):
    tall, broad, lanes = field.shape
    full = tall + 2 * REACH
    pad_ref[:REACH] = jnp.zeros((REACH, broad + 2 * EDGE, lanes), F32)
    pad_ref[full - REACH :] = jnp.zeros((REACH, broad + 2 * EDGE, lanes), F32)
    pad_ref[REACH : REACH + tall, :EDGE] = jnp.zeros((tall, EDGE, lanes), F32)
    pad_ref[REACH : REACH + tall, EDGE + broad :] = jnp.zeros((tall, EDGE, lanes), F32)
    pad_ref[REACH : REACH + tall, EDGE : EDGE + broad] = field
    two = place.live & (place.wide == 2)
    one = place.live & (place.wide == 1)
    first, second = two & (place.col == 0), two & (place.col == 1)
    upper, lower = slice(0, REACH), slice(full - REACH, full)
    before, after = slice(0, EDGE), slice(EDGE + broad, 2 * EDGE + broad)
    for arrived_ref, delta in zip(arrived_refs, deltas):

        def rows(arrived_ref=arrived_ref):
            return edge_of(arrived_ref, REACH * broad).reshape(REACH, broad, lanes)

        def cols(arrived_ref=arrived_ref):
            return edge_of(arrived_ref, REACH * broad).reshape(tall, EDGE, lanes)

        def put(condition, where_rows, where_cols, value):
            @pl.when(condition)
            def _():
                pad_ref[where_rows, where_cols] = value()

        middle, height = slice(EDGE, EDGE + broad), slice(REACH, REACH + tall)
        put(place.above & ((one & (delta == -1)) | (two & (delta == -2))), upper, middle, rows)
        put(place.below & ((one & (delta == 1)) | (two & (delta == 2))), lower, middle, rows)
        put(second & (delta == -1), height, before, cols)
        put(first & (delta == 1), height, after, cols)
        put(place.above & first & (delta == -1), upper, after, lambda r=rows: r()[:, :EDGE])
        put(place.above & second & (delta == -3), upper, before, lambda r=rows: r()[:, broad - EDGE :])
        put(place.below & second & (delta == 1), lower, before, lambda r=rows: r()[:, broad - EDGE :])
        put(place.below & first & (delta == 3), lower, after, lambda r=rows: r()[:, :EDGE])


def fill_shifted(shift_ref, pad_ref):
    full, broad = shift_ref.shape[1:3]
    first = EDGE - REACH
    for y in range(full):
        for b in range(2 * REACH + 1):
            shift_ref[b, y] = pad_ref[y, first + b : first + b + broad]


def convolve(shift_ref, kernel_ref, y, flipped):
    taps = 2 * REACH + 1
    total = None
    for a in range(taps):
        for b in range(taps):
            tap = taps * a + b
            if flipped:
                tap = taps * taps - 1 - tap
            term = shift_ref[b, y + a] * kernel_ref[tap : tap + 1]
            total = term if total is None else total + term
    return total


def read_field(ref, place):
    return jnp.where(place.live, ref[0, 0].astype(F32), 0.0)


def outgoing_kernel(routes, *refs):
    layout, field_ref, outs = refs[:5], refs[5], refs[6:]
    place = Place(layout)
    field = field_ref[0, 0].astype(F32)
    for delta, out_ref in zip(routes.targets(place), outs):
        out_ref[0] = payload(field, place, delta).astype(BF16)


def source_state_kernel(routes, head_dim, *refs):
    layout, (query_ref, key_ref, value_ref), outs = refs[:5], refs[5:8], refs[8:]
    place = Place(layout)
    field = query_ref[0, 0].astype(F32)
    size = REACH * field.shape[1]
    positions = field.shape[0] * field.shape[1]
    keys = jnp.maximum(read_field(key_ref, place), 0.0).reshape(positions, LANES)
    values = read_field(value_ref, place).reshape(positions, LANES)
    state = contract(keys.astype(BF16), values.astype(BF16), TN)
    state = gather_blocks(state, same_head(head_dim), head_dim)
    packed = pack_state(state, jnp.sum(keys, axis=0, keepdims=True))
    for delta, out_ref in zip(routes.targets(place), outs):
        out_ref[:size] = payload(field, place, delta).astype(BF16)
        out_ref[size:] = packed


def convolve_all(routes, place, field, arrived, pad_ref, shift_ref, mix_ref, kernel_ref, flipped):
    fill_padded(pad_ref, field, arrived, routes.sources(place), place)
    fill_shifted(shift_ref, pad_ref)

    def one_row(y, carry):
        mix_ref[y] = convolve(shift_ref, kernel_ref, y, flipped)
        return carry

    lax.fori_loop(0, field.shape[0], one_row, 0)


def forward_kernel(routes, per, head_dim, with_state, *refs):
    count = routes.arriving
    layout, field_ref = refs[:5], refs[5]
    arrived = refs[6 : 6 + count]
    refs = refs[6 + count :]
    dw_ref, pw_ref, mixed_ref, merged_ref = refs[:4]
    if with_state:
        state_ref, pad_ref, shift_ref, mix_ref, key_ref = refs[4:]
    else:
        pad_ref, shift_ref, mix_ref = refs[4:]
    step = pl.program_id(0)
    place = Place(layout)
    field = read_field(field_ref, place)
    convolve_all(routes, place, field, arrived, pad_ref, shift_ref, mix_ref, dw_ref, False)
    mixed = mix_ref[...].reshape(-1, LANES)
    mixed_ref[0] = mixed
    mask = same_head(head_dim)
    merged = dot(split(mixed), split(spread(pw_ref[...], mask)), NN)
    merged_ref[0] = merged
    if not with_state:
        return
    for part in range(per):

        @pl.when(step == part)
        def _():
            key_ref[part] = jnp.maximum(merged, 0.0)

        @pl.when(step == per + part)
        def _():
            keys = key_ref[part]
            state = gather_blocks(dot(split(keys), split(merged), TN), mask, head_dim)
            lanes = slice(part * LANES, (part + 1) * LANES)
            state_ref[:, lanes] = pack_state(state, jnp.sum(keys, axis=0, keepdims=True))


def query_gradients(raw, exactly, total, cot_ref, head_dim, mask):
    ones = (mask.astype(BF16), None)
    query = jnp.maximum(raw, 0.0)
    pair = exact(query) if exactly else split(query)
    state = split(spread(total[:head_dim], mask))
    key_sum = total[head_dim : head_dim + 1]
    cot = cot_ref[0, 0].astype(F32).reshape(raw.shape)
    over = 1.0 / (dot(split(query * key_sum), ones, NN) + EPSILON)
    result = dot(pair, state, NN) * over
    grad_num = cot * over
    grad_den = -dot(split(cot * result), ones, NN) * over
    num_pair = split(grad_num)
    grad = jnp.where(raw > 0, dot(num_pair, state, NT) + grad_den * key_sum, 0.0)
    gstate = gather_blocks(dot(pair, num_pair, TN), mask, head_dim)
    return grad, pack_state(gstate, jnp.sum(query * grad_den, axis=0, keepdims=True))


def source_query_kernel(others, offset, others_offset, head_dim, *refs):
    layout, own_ref, received = refs[:5], refs[5], refs[6 : 6 + others]
    source_ref, cot_ref, grad_ref, gstate_ref = refs[6 + others :]
    place = Place(layout)
    total = total_state(own_ref, received, place, offset, others_offset)
    raw = read_field(source_ref, place).reshape(-1, LANES)
    grad_ref[0], gstate_ref[...] = query_gradients(raw, True, total, cot_ref, head_dim, same_head(head_dim))


def merged_query_kernel(others, routes, head_dim, *refs):
    layout, own_ref, received = refs[:5], refs[5], refs[6 : 6 + others]
    refs = refs[6 + others :]
    merged_ref, mixed_ref, cot_ref, pw_ref, packed_ref, gstate_ref, gmix_ref, gpw_ref = refs[:8]
    outs = refs[8:]
    tall, broad = cot_ref.shape[2:4]
    place = Place(layout)
    mask = same_head(head_dim)
    total = total_state(own_ref, received, place, 0, 0)
    grad, gstate_ref[...] = query_gradients(merged_ref[0], False, total, cot_ref, head_dim, mask)
    pair = split(grad)
    gmix = dot(pair, split(spread(pw_ref[...], mask)), NT)
    gmix_ref[0] = gmix
    gpw_ref[0] = gather_blocks(dot(split(mixed_ref[0]), pair, TN), mask, head_dim)
    field = gmix.reshape(tall, broad, LANES)
    for delta, out_ref in zip(routes.targets(place), outs):
        out_ref[: REACH * broad] = payload(field, place, delta).astype(BF16)
        out_ref[REACH * broad :] = packed_ref[...]


def key_gradients(raw, key_pair, value_pair, total, head_dim, mask):
    gstate = split(spread(total[:head_dim], mask))
    gsum = total[head_dim : head_dim + 1]
    grad_keys = jnp.where(raw > 0, dot(value_pair, gstate, NT) + gsum, 0.0)
    return grad_keys, dot(key_pair, gstate, NN)


def source_value_kernel(others, offset, others_offset, head_dim, *refs):
    layout, own_ref, received = refs[:5], refs[5], refs[6 : 6 + others]
    key_ref, value_ref, grad_ref = refs[6 + others :]
    place = Place(layout)
    total = total_state(own_ref, received, place, offset, others_offset)
    raw = read_field(key_ref, place).reshape(-1, LANES)
    values = read_field(value_ref, place).reshape(-1, LANES)
    grad_ref[0], grad_ref[1] = key_gradients(
        raw, exact(jnp.maximum(raw, 0.0)), exact(values), total, head_dim, same_head(head_dim)
    )


def merged_value_kernel(others, routes, tall, head_dim, *refs):
    layout, own_ref, received = refs[:5], refs[5], refs[6 : 6 + others]
    merged_ref, mixed_ref, kpw_ref, vpw_ref, gmix_ref, gpw_ref = refs[6 + others : 12 + others]
    outs = refs[12 + others :]
    place = Place(layout)
    mask = same_head(head_dim)
    total = total_state(own_ref, received, place, 0, 0)
    raw = merged_ref[0]
    grads = key_gradients(raw, split(jnp.maximum(raw, 0.0)), split(merged_ref[1]), total, head_dim, mask)
    for member, (grad, pw_ref) in enumerate(zip(grads, (kpw_ref, vpw_ref))):
        pair = split(grad)
        gmix = dot(pair, split(spread(pw_ref[...], mask)), NT)
        gmix_ref[member] = gmix
        gpw_ref[member] = gather_blocks(dot(split(mixed_ref[member]), pair, TN), mask, head_dim)
        field = gmix.reshape(tall, -1, LANES)
        for delta, out_ref in zip(routes.targets(place), outs):
            out_ref[member] = payload(field, place, delta).astype(BF16)


def weight_kernel(routes, halves, *refs):
    count = routes.arriving
    layout, field_ref = refs[:5], refs[5]
    arrived = refs[6 : 6 + count]
    refs = refs[6 + count :]
    gmix_ref, gpw_ref, spot_ref = refs[:3]
    outs, (pad_ref, shift_ref, sum_ref) = refs[3:-3], refs[-3:]
    place = Place(layout)
    field = read_field(field_ref, place)
    tall, broad = field.shape[:2]
    fill_padded(pad_ref, field, arrived, routes.sources(place), place)
    fill_shifted(shift_ref, pad_ref)
    taps = 2 * REACH + 1
    sub = 128
    for part in range(LANES // sub):
        lanes = slice(part * sub, (part + 1) * sub)

        def one_row(y, totals):
            grad = gmix_ref[0, pl.ds(pl.multiple_of(y * broad, broad), broad), lanes]
            new = []
            for a in range(taps):
                for b in range(taps):
                    term = shift_ref[b, y + a, :, lanes] * grad
                    new.append(totals[taps * a + b] + jnp.sum(term.reshape(broad // 8, 8, sub), axis=0))
            return tuple(new)

        zero = jnp.zeros((8, sub), F32)
        totals = lax.fori_loop(0, tall, one_row, (zero,) * (taps * taps))
        for tap in range(taps * taps):
            sum_ref[tap : tap + 1, lanes] = jnp.sum(totals[tap], axis=0, keepdims=True)
    start = sum_ref.shape[0] - gpw_ref.shape[1]
    sum_ref[taps * taps : start] = jnp.zeros((start - taps * taps, LANES), F32)
    sum_ref[start:] = gpw_ref[0]
    if not halves:
        outs[0][...] = sum_ref[...]
        return
    rows = outs[0].shape[1]
    odd = spot_ref[0] % 2 == 1
    for part in range(outs[0].shape[0]):
        even_rows = sum_ref[2 * part * rows : (2 * part + 1) * rows]
        odd_rows = sum_ref[(2 * part + 1) * rows : (2 * part + 2) * rows]
        outs[0][part] = jnp.where(odd, even_rows, odd_rows)
        outs[1][part] = jnp.where(odd, odd_rows, even_rows)


def scatter_kernel(spot_ref, keep_q, come_q, keep_kv, come_kv, own_ref, *outs):
    quarter = spot_ref[0] // 2
    third = keep_q.shape[2]
    for m, out_ref in enumerate((own_ref,) + outs):
        at = quarter ^ m
        out_ref[:, :third] = keep_q[at] + come_q[at]
        out_ref[:, third:] = keep_kv[at] + come_kv[at]


def sum_kernel(norm, *refs):
    parts, out_ref = [ref[...] for ref in refs[:-1]], refs[-1]
    while len(parts) > 1:
        parts = [parts[i] + parts[i + 1] for i in range(0, len(parts), 2)]
    out_ref[...] = parts[0] * norm


def collect_kernel(spot_ref, *refs):
    parts, out_ref = refs[:-1], refs[-1]
    quarter = spot_ref[0] // 2
    for m, part in enumerate(parts):
        out_ref[quarter ^ m] = part[...]


def finish_kernel(taps, spot_ref, own_ref, come_ref, dw_ref, pw_ref, whole_ref):
    odd = spot_ref[0] % 2 == 1
    quarters, rows = own_ref.shape[:2]
    for part in range(quarters):
        own, come = own_ref[part], come_ref[part]
        whole_ref[2 * part * rows : (2 * part + 1) * rows] = jnp.where(odd, come, own)
        whole_ref[(2 * part + 1) * rows : (2 * part + 2) * rows] = jnp.where(odd, own, come)
    dw_ref[...] = whole_ref[:taps]
    pw_ref[...] = whole_ref[whole_ref.shape[0] - pw_ref.shape[0] :]


def backward_kernel(routes, *refs):
    count = routes.arriving
    layout, gmix_ref = refs[:5], refs[5]
    arrived = refs[6 : 6 + count]
    dw_ref, grad0_ref = refs[6 + count : 8 + count]
    out_ref, pad_ref, shift_ref, mix_ref = refs[8 + count :]
    place = Place(layout)
    tall, broad = out_ref.shape[2:4]
    field = gmix_ref[0].reshape(tall, broad, LANES)
    convolve_all(routes, place, field, arrived, pad_ref, shift_ref, mix_ref, dw_ref, True)
    grad = mix_ref[...] + grad0_ref[0].reshape(tall, broad, LANES)
    out_ref[0, 0] = jnp.where(place.live, grad, 0.0).astype(BF16)


def call(kernel, grid, in_specs, out_specs, out_shape, scratch=(), after=(), onto=()):
    inputs, extra = len(in_specs), len(onto) + len(after)

    def body(*refs):
        kernel(*refs[:inputs], *refs[inputs + extra :])

    run = pl.pallas_call(
        body,
        grid=(grid,),
        in_specs=list(in_specs) + [pl.BlockSpec(memory_space=pl.ANY)] * extra,
        out_specs=out_specs,
        out_shape=out_shape,
        scratch_shapes=list(scratch),
        input_output_aliases={inputs: 0} if onto else {},
        compiler_params=PARAMS,
        cost_estimate=pl.CostEstimate(flops=COST, bytes_accessed=COST, transcendentals=0),
    )
    return lambda *args: run(*args, *onto, *after)


def local(
    qkv, cotangent, dw_weight, pw_weight, tile_image, tile_row, tile_col, image_height, image_width
):
    tall, broad, channels = qkv.shape[2:]
    positions = tall * broad
    head_dim = pw_weight.shape[0]
    taps = dw_weight.shape[0]
    third = channels // 3
    per = third // LANES
    tiles, groups = lax.axis_size("tile"), lax.axis_size("img")
    routes = Routes(tiles)
    layout = (tile_image, tile_row, tile_col, image_height, image_width)
    head_specs = [SMEM] * 5
    edge = REACH * broad
    packed = 2 * (head_dim + 8)
    shape = jax.ShapeDtypeStruct
    spot = lax.axis_index("img").astype(jnp.int32).reshape(1)

    def tile_spec(first):
        return pl.BlockSpec((1, 1, tall, broad, LANES), lambda j: (0, 0, 0, 0, first * per + j))

    def flat_spec(rows, first=0):
        return pl.BlockSpec((rows, LANES), lambda j: (0, first * per + j))

    def member_spec(rows):
        return pl.BlockSpec((1, rows, LANES), lambda j: (j // per, 0, j % per))

    def pair_spec(rows):
        return pl.BlockSpec((2, rows, LANES), lambda j: (0, 0, j))

    def whole_spec(*dims):
        return pl.BlockSpec(dims, lambda j: (0,) * len(dims))

    pad_scratch = [
        pltpu.VMEM((tall + 2 * REACH, broad + 2 * EDGE, LANES), F32),
        pltpu.VMEM((2 * REACH + 1, tall + 2 * REACH, broad, LANES), F32),
    ]
    mix_scratch = [pltpu.VMEM((tall, broad, LANES), F32)]
    low, high = edge, edge + packed

    sent_kv = call(
        functools.partial(outgoing_kernel, routes),
        2 * per,
        head_specs + [tile_spec(1)],
        [member_spec(edge)] * routes.sent,
        [shape((2, edge, third), BF16)] * routes.sent,
    )(*layout, qkv)
    halo_kv = routes.move(sent_kv)
    sent_q = call(
        functools.partial(source_state_kernel, routes, head_dim),
        per,
        head_specs + [tile_spec(0), tile_spec(1), tile_spec(2)],
        [flat_spec(high)] * routes.sent,
        [shape((high, third), BF16)] * routes.sent,
    )(*layout, qkv, qkv, qkv)
    halo_q = routes.move(sent_q)

    def forward(first, count, halo, halo_spec):
        with_state = first > 0
        outs = [member_spec(positions)] * 2
        shapes = [shape((count, positions, third), F32)] * 2
        scratch = pad_scratch + mix_scratch
        if with_state:
            outs.append(whole_spec(packed, third))
            shapes.append(shape((packed, third), BF16))
            scratch = scratch + [pltpu.VMEM((per, positions, LANES), F32)]
        return call(
            functools.partial(forward_kernel, routes, per, head_dim, with_state),
            count * per,
            head_specs
            + [tile_spec(first)]
            + [halo_spec] * routes.arriving
            + [flat_spec(taps, first), flat_spec(head_dim, first)],
            outs,
            shapes,
            scratch,
        )(*layout, qkv, *halo, dw_weight, pw_weight)

    mixed_kv, merged_kv, state = forward(1, 2, halo_kv, member_spec(edge))
    state_from = exchange(state, "tile")
    others = len(state_from)
    mixed_q, merged_q = forward(0, 1, halo_q, flat_spec(high))

    source_from = halo_q if routes.relayed else exchange(sent_q[0][low:], "tile")
    from_rows, from_offset = (high, low) if routes.relayed else (packed, 0)
    grad0_q, gstate0 = call(
        functools.partial(source_query_kernel, others, low, from_offset, head_dim),
        per,
        head_specs
        + [flat_spec(high)]
        + [flat_spec(from_rows)] * others
        + [tile_spec(0), tile_spec(0)],
        [member_spec(positions), flat_spec(packed)],
        [shape((1, positions, third), F32), shape((packed, third), BF16)],
    )(*layout, sent_q[0], *source_from, qkv, cotangent)

    gstate, gmix_q, gpw_q, *sent_q2 = call(
        functools.partial(merged_query_kernel, others, routes, head_dim),
        per,
        head_specs
        + [flat_spec(packed)] * (1 + others)
        + [member_spec(positions), member_spec(positions), tile_spec(1), flat_spec(head_dim), flat_spec(packed)],
        [flat_spec(packed), member_spec(positions), member_spec(head_dim)] + [flat_spec(high)] * routes.sent,
        [
            shape((packed, third), BF16),
            shape((1, positions, third), F32),
            shape((1, head_dim, third), F32),
        ]
        + [shape((high, third), BF16)] * routes.sent,
    )(*layout, state, *state_from, merged_q, mixed_q, cotangent, pw_weight, gstate0)
    gstate_from = exchange(gstate, "tile")
    halo_q2 = routes.move(sent_q2)

    gap = -(-taps // 8) * 8
    rows = gap + head_dim
    halves = groups == 8 and rows % groups == 0
    eighth = rows // groups

    def weights(first, count, halo, halo_spec, gmix, gpw, after=()):
        if halves:
            outs = [pl.BlockSpec((4, eighth, LANES), lambda j: (0, 0, j))] * 2
            shapes = [shape((4, eighth, count * third), F32)] * 2
        else:
            outs, shapes = [flat_spec(rows)], [shape((rows, count * third), F32)]
        return call(
            functools.partial(weight_kernel, routes, halves),
            count * per,
            head_specs
            + [tile_spec(first)]
            + [halo_spec] * routes.arriving
            + [member_spec(positions), member_spec(head_dim), SMEM],
            outs,
            shapes,
            pad_scratch + [pltpu.VMEM((rows, LANES), F32)],
            after,
        )(*layout, qkv, *halo, gmix, gpw, spot)

    weights_q = weights(0, 1, halo_q, flat_spec(high), gmix_q, gpw_q)

    gmix_kv, gpw_kv, *sent_kv2 = call(
        functools.partial(merged_value_kernel, others, routes, tall, head_dim),
        per,
        head_specs
        + [flat_spec(packed)] * (1 + others)
        + [pair_spec(positions)] * 2
        + [flat_spec(head_dim, 1), flat_spec(head_dim, 2)],
        [pair_spec(positions), pair_spec(head_dim)] + [pair_spec(edge)] * routes.sent,
        [shape((2, positions, third), F32), shape((2, head_dim, third), F32)]
        + [shape((2, edge, third), BF16)] * routes.sent,
        after=(weights_q[0],),
    )(*layout, gstate, *gstate_from, merged_kv, mixed_kv, pw_weight, pw_weight)
    halo_kv2 = routes.move(sent_kv2)
    weights_kv = weights(1, 2, halo_kv, member_spec(edge), gmix_kv, gpw_kv, (halo_q2[1],))

    back_from = halo_q2 if routes.relayed else exchange(sent_q2[0][low:], "tile")
    grad0_kv = call(
        functools.partial(source_value_kernel, others, low, from_offset, head_dim),
        per,
        head_specs
        + [flat_spec(high)]
        + [flat_spec(from_rows)] * others
        + [tile_spec(1), tile_spec(2)],
        pair_spec(positions),
        shape((2, positions, third), F32),
    )(*layout, sent_q2[0], *back_from, qkv, qkv)

    def backward(first, count, gmix, halo, halo_spec, grad0, onto=()):
        return call(
            functools.partial(backward_kernel, routes),
            count * per,
            head_specs
            + [member_spec(positions)]
            + [halo_spec] * routes.arriving
            + [flat_spec(taps, first), member_spec(positions)],
            tile_spec(first),
            shape((1, 1, tall, broad, channels), BF16),
            pad_scratch + mix_scratch,
            onto=onto,
        )(*layout, gmix, *halo, dw_weight, grad0)

    grad_query = backward(0, 1, gmix_q, halo_q2, flat_spec(high), grad0_q)
    grad_source = backward(1, 2, gmix_kv, halo_kv2, member_spec(edge), grad0_kv, (grad_query,))
    norm = 1.0 / math.sqrt(positions * tiles * groups)
    if halves:
        come_q = exchange(weights_q[0], "img", (1,))[0]
        come_kv = exchange(weights_kv[0], "img", (1,))[0]
        part = shape((eighth, channels), F32)
        parts = call(
            scatter_kernel,
            1,
            [SMEM]
            + [whole_spec(4, eighth, third)] * 2
            + [whole_spec(4, eighth, 2 * third)] * 2,
            [whole_spec(eighth, channels)] * 4,
            [part] * 4,
        )(spot, weights_q[1], come_q, weights_kv[1], come_kv)
        count = lax.axis_size("img")
        moved = [
            lax.ppermute(part_m, "img", [(s, s ^ (2 * m)) for s in range(count)])
            for m, part_m in enumerate(parts[1:], 1)
        ]

        def add(values, factor, after):
            return call(
                functools.partial(sum_kernel, factor),
                1,
                [whole_spec(eighth, channels)] * len(values),
                whole_spec(eighth, channels),
                part,
                after=after,
            )(*values)

        share = add([parts[0]] + moved, 1.0, (grad_query, halo_kv2[1]))
        share = add([share] + exchange(share, "tile"), norm, (grad0_kv,))
        quarters = call(
            collect_kernel,
            1,
            [SMEM] + [whole_spec(eighth, channels)] * 4,
            whole_spec(4, eighth, channels),
            shape((4, eighth, channels), F32),
            after=(grad_source,),
        )(spot, share, *exchange(share, "img", (2, 4, 6)))
        grad_dw, grad_pw = call(
            functools.partial(finish_kernel, taps),
            1,
            [SMEM] + [whole_spec(4, eighth, channels)] * 2,
            [whole_spec(taps, channels), whole_spec(head_dim, channels)],
            [shape((taps, channels), F32), shape((head_dim, channels), F32)],
            [pltpu.VMEM((rows, channels), F32)],
        )(spot, quarters, exchange(quarters, "img", (1,))[0])
    else:
        whole = jnp.concatenate([weights_q[0], weights_kv[0]], axis=1)
        whole = lax.psum(whole, ("tile", "img")) * norm
        grad_dw, grad_pw = whole[:taps], whole[gap:]

    return grad_source, grad_dw, grad_pw


def solution(mesh):
    placed = (
        P("img", "tile", None, None, None),
        P("img", "tile", None, None, None),
        P(),
        P(),
        P("img", "tile"),
        P("img", "tile"),
        P("img", "tile"),
        P("img", None),
        P("img", None),
    )
    return jax.shard_map(
        local,
        mesh=mesh,
        in_specs=placed,
        out_specs=(P("img", "tile", None, None, None), P(), P()),
        check_vma=False,
    )
```

time: 128 us -> 109 us (0.85)
  waiting for transfers between devices: 41.7 us -> 20.5 us
  blocking collectives: 12.1 us -> 0 us
  starting transfers between devices: 27.9 us -> 38 us
  Pallas kernels: 33.2 us -> 40.4 us
  other arithmetic: 3.44 us -> 0 us
    ppermute x9 -> x15, waiting for transfers between devices: 21.7 us -> 9.54 us  [exchange(): lax.ppermute(value, axis, [(s, s ^ m) for s in range(count)])]
    all_to_all x1 -> x0, blocking collectives: 12.1 us -> none  [local(): lax.all_to_all(weights.reshape(groups, padded_rows // groups, channels),...]
    ppermute x6 -> x15, starting transfers between devices: 10 us -> 21.1 us  [the longest x8 16.3 us: move(): lax.ppermute(part, 'tile', [(s, s ^ m) for s in range(count)])]
    ppermute x6 -> x15, waiting for transfers between devices: 20.1 us -> 11 us  [the longest x8 7.57 us: move(): lax.ppermute(part, 'tile', [(s, s ^ m) for s in range(count)])]
    pallas_call x6 -> x17, Pallas kernels: 33.2 us -> 40.4 us  [call(): return lambda *args: run(*args, *onto, *after)]
    all_to_all x1 -> x0, starting transfers between devices: 4.01 us -> none  [local(): lax.all_to_all(jnp.broadcast_to(share[None], (groups,) + share.shape), 'i...]
    ppermute x9 -> x15, starting transfers between devices: 13.8 us -> 16.9 us  [exchange(): lax.ppermute(value, axis, [(s, s ^ m) for s in range(count)])]
    unnamed x24 -> x42, local copies, waits for them, and re-layouts: 4.33 us -> 6.81 us
  transfers between devices with their start and end apart: 16 -> 30, of which waited for: 8 -> 7; matrix products, arithmetic and copies ran while one was open for 1% -> 0% of each run, Pallas kernels for 6% -> 32%
where the time goes in v2:
time: 109 us
  Pallas kernels  40.4 us (37%)
  starting transfers between devices  38 us (35%)
  waiting for transfers between devices  20.5 us (19%)
  local copies, waits for them, and re-layouts  6.81 us (6%)
  between operations  2.94 us (3%)
    pallas_call x17, Pallas kernels, call(): return lambda *args: run(*args, *onto, *after)  40.4 us
    ppermute x15, starting transfers between devices, exchange(): lax.ppermute(value, axis, [(s, s ^ m) for s in range(count)])  16.9 us
    ppermute x8, starting transfers between devices, move(): lax.ppermute(part, 'tile', [(s, s ^ m) for s in range(count)])  16.3 us
    ppermute x15, waiting for transfers between devices, exchange(): lax.ppermute(value, axis, [(s, s ^ m) for s in range(count)])  9.54 us
    ppermute x8, waiting for transfers between devices, move(): lax.ppermute(part, 'tile', [(s, s ^ m) for s in range(count)])  7.57 us
    unnamed x42, local copies, waits for them, and re-layouts  6.81 us
    ppermute x3, starting transfers between devices, local(): lax.ppermute(part_m, 'img', [(s, s ^ 2 * m) for s in range(count)])  3.55 us
    ppermute x4, waiting for transfers between devices, move(): lax.ppermute(far, 'tile', [(s, s ^ 1) for s in range(count)])  3.39 us
  transfers between devices with their start and end apart: 30, of which 7 were waited for; matrix products, arithmetic and copies ran while one was open for 0% of the time, Pallas kernels for 32%

profile of v2, /device:TPU:0, one launch (start us, length us, event | category | flops | bytes accessed | tf_op | source)
XLA Modules:
  0.0 108.6 jit_solution(13411994831665377153)
XLA Ops:
  2.6 1.1 %copy-done = bf16[1,1,8,32,1536]{4,3,2,1,0:T(8,128)(2,1)S(1)} copy-done((bf16[1,1,8,32,1536]{4,3,2,1,0:T(8,128)(2,1)S(1)}, bf16[1,1,8,32,1536]{4,3,2,1,0:T(8,128)(2,1)}, u32[]{:S(2)}) %copy-start) | copy-done | bytes 786456
  4.7 4.1 %collective-permute-start.1 = (bf16[2,64,512]{2,1,0:T(8,128)(2,1)S(1)}, bf16[2,64,512]{2,1,0:T(8,128)(2,1)S(1)}, u32[]{:S(2)}, u32[]{:S(2)}) collective-permute-start(bf16[2,64,512]{2,1,0:T(8,128)(2,1)S(1)} %get-tuple-element.34), channel_id=1, source_target_pairs={{0,16},{8,24},{16,0},{24,8},{1,17},{9,25},{17,1},{25,9},{2,18},{10... | collective-permute-start | bytes 393224 | tf_op jit(solution)/shard_map/ppermute | solution.py:72
  8.8 1.2 %shard_map.114 = (bf16[144,512]{1,0:T(8,128)(2,1)S(1)}, bf16[144,512]{1,0:T(8,128)(2,1)S(1)}) custom-call(s32[1,1]{1,0:T(1,128)S(6)} %copy.14.refs_0_, s32[1,1]{1,0:T(1,128)S(6)} %copy.15.refs_1_, s32[1,1]{1,0:T(1,128)S(6)} %copy.16.refs_2_, s32[1,2]{1,0:T(1,128)S(1)} %copy-done.17, s32[1,2]{1,0:T(1,128)S(1)} %copy-done.18, ...), custom_call_target="tpu_custom_call" | custom-call | flops 1000 | bytes 1000 | tf_op jit(solution)/shard_map/pallas_call | solution.py:489
  10.1 1.9 %collective-permute-start = (bf16[2,64,512]{2,1,0:T(8,128)(2,1)S(1)}, bf16[2,64,512]{2,1,0:T(8,128)(2,1)S(1)}, u32[]{:S(2)}, u32[]{:S(2)}) collective-permute-start(bf16[2,64,512]{2,1,0:T(8,128)(2,1)S(1)} %get-tuple-element.33), channel_id=1, source_target_pairs={{0,8},{8,0},{16,24},{24,16},{1,9},{9,1},{17,25},{25,17},{2,10},{10... | collective-permute-start | bytes 393224 | tf_op jit(solution)/shard_map/ppermute | solution.py:72
  12.0 7.2 %collective-permute-done.1.refs_7_ = bf16[2,64,512]{2,1,0:T(8,128)(2,1)S(1)} collective-permute-done((bf16[2,64,512]{2,1,0:T(8,128)(2,1)S(1)}, bf16[2,64,512]{2,1,0:T(8,128)(2,1)S(1)}, u32[]{:S(2)}, u32[]{:S(2)}) %collective-permute-start.1) | collective-permute-done | bytes 131104 | tf_op jit(solution)/shard_map/ppermute | solution.py:72
  19.1 2.0 %collective-permute-start.6 = (bf16[144,512]{1,0:T(8,128)(2,1)S(1)}, bf16[144,512]{1,0:T(8,128)(2,1)S(1)}, u32[]{:S(2)}, u32[]{:S(2)}) collective-permute-start(bf16[144,512]{1,0:T(8,128)(2,1)S(1)} %get-tuple-element.36.refs_5_), channel_id=1, source_target_pairs={{0,8},{8,0},{16,24},{24,16},{1,9},{9,1},{17,25},{25,17},{2,10},{10... | collective-permute-start | bytes 442376 | tf_op jit(solution)/shard_map/ppermute | solution.py:72
  22.2 3.4 %collective-permute-done.2.refs_8_ = bf16[2,64,512]{2,1,0:T(8,128)(2,1)S(1)} collective-permute-done((bf16[2,64,512]{2,1,0:T(8,128)(2,1)S(1)}, bf16[2,64,512]{2,1,0:T(8,128)(2,1)S(1)}, u32[]{:S(2)}, u32[]{:S(2)}) %collective-permute-start.2) | collective-permute-done | bytes 131104 | tf_op jit(solution)/shard_map/ppermute | solution.py:74
  25.6 6.8 %shard_map.113 = (f32[2,256,512]{2,1,0:T(8,128)S(1)}, f32[2,256,512]{2,1,0:T(8,128)S(1)}, bf16[80,512]{1,0:T(8,128)(2,1)S(1)}) custom-call(s32[1,1]{1,0:T(1,128)S(6)} %copy.14.refs_0_, s32[1,1]{1,0:T(1,128)S(6)} %copy.15.refs_1_, s32[1,1]{1,0:T(1,128)S(6)} %copy.16.refs_2_, s32[1,2]{1,0:T(1,128)S(1)} %copy-done.17, s32[1,2]{1,0:T(1,128)S(1)} %copy-done.18, ...), custom_call_target="tpu_custom_call" | custom-call | flops 1000 | bytes 1000 | tf_op jit(solution)/shard_map/pallas_call | solution.py:489
  33.4 2.7 %collective-permute-start.5 = (bf16[80,512]{1,0:T(8,128)(2,1)S(1)}, bf16[80,512]{1,0:T(8,128)(2,1)S(1)}, u32[]{:S(2)}, u32[]{:S(2)}) collective-permute-start(bf16[80,512]{1,0:T(8,128)(2,1)S(1)} %get-tuple-element.35.refs_5_), channel_id=1, source_target_pairs={{0,24},{8,16},{16,8},{24,0},{1,25},{9,17},{17,9},{25,1},{2,26},{10... | collective-permute-start | bytes 245768 | tf_op jit(solution)/shard_map/ppermute | solution.py:80
  36.2 1.6 %collective-permute-start.3 = (bf16[80,512]{1,0:T(8,128)(2,1)S(1)}, bf16[80,512]{1,0:T(8,128)(2,1)S(1)}, u32[]{:S(2)}, u32[]{:S(2)}) collective-permute-start(bf16[80,512]{1,0:T(8,128)(2,1)S(1)} %get-tuple-element.35.refs_5_), channel_id=1, source_target_pairs={{0,8},{8,0},{16,24},{24,16},{1,9},{9,1},{17,25},{25,17},{2,10},{10... | collective-permute-start | bytes 245768 | tf_op jit(solution)/shard_map/ppermute | solution.py:80
  37.8 3.3 %shard_map.115 = (f32[1,256,512]{2,1,0:T(8,128)S(1)}, f32[1,256,512]{2,1,0:T(8,128)S(1)}) custom-call(s32[1,1]{1,0:T(1,128)S(6)} %copy.14.refs_0_, s32[1,1]{1,0:T(1,128)S(6)} %copy.15.refs_1_, s32[1,1]{1,0:T(1,128)S(6)} %copy.16.refs_2_, s32[1,2]{1,0:T(1,128)S(1)} %copy-done.17, s32[1,2]{1,0:T(1,128)S(1)} %copy-done.18, ...), custom_call_target="tpu_custom_call" | custom-call | flops 1000 | bytes 1000 | tf_op jit(solution)/shard_map/pallas_call | solution.py:489
  41.1 2.3 %shard_map.116 = (f32[1,256,512]{2,1,0:T(8,128)S(1)}, bf16[80,512]{1,0:T(8,128)(2,1)S(1)}) custom-call(s32[1,1]{1,0:T(1,128)S(6)} %copy.14.refs_0_, s32[1,1]{1,0:T(1,128)S(6)} %copy.15.refs_1_, s32[1,1]{1,0:T(1,128)S(6)} %copy.16.refs_2_, s32[1,2]{1,0:T(1,128)S(1)} %copy-done.17, s32[1,2]{1,0:T(1,128)S(1)} %copy-done.18, ...), custom_call_target="tpu_custom_call" | custom-call | flops 1000 | bytes 1000 | tf_op jit(solution)/shard_map/pallas_call | solution.py:489
  44.3 3.7 %shard_map.117 = (bf16[80,512]{1,0:T(8,128)(2,1)}, f32[1,256,512]{2,1,0:T(8,128)S(1)}, f32[1,32,512]{2,1,0:T(8,128)S(1)}, bf16[144,512]{1,0:T(8,128)(2,1)}, bf16[144,512]{1,0:T(8,128)(2,1)}) custom-call(s32[1,1]{1,0:T(1,128)S(6)} %copy.14.refs_0_, s32[1,1]{1,0:T(1,128)S(6)} %copy.15.refs_1_, s32[1,1]{1,0:T(1,128)S(6)} %copy.16.refs_2_, ...), custom_call_target="tpu_custom_call" | custom-call | flops 1000 | bytes 1000 | tf_op jit(solution)/shard_map/pallas_call | solution.py:489
  48.6 1.3 %collective-permute-start.16 = (bf16[144,512]{1,0:T(8,128)(2,1)}, bf16[144,512]{1,0:T(8,128)(2,1)S(1)}, u32[]{:S(2)}, u32[]{:S(2)}) collective-permute-start(bf16[144,512]{1,0:T(8,128)(2,1)} %get-tuple-element.51), channel_id=1, source_target_pairs={{0,16},{8,24},{16,0},{24,8},{1,17},{9,25},{17,1},{25,9},{2,18},{10... | collective-permute-start | bytes 442376 | tf_op jit(solution)/shard_map/ppermute | solution.py:72
  49.9 1.4 %collective-permute-start.11 = (bf16[80,512]{1,0:T(8,128)(2,1)}, bf16[80,512]{1,0:T(8,128)(2,1)}, u32[]{:S(2)}, u32[]{:S(2)}) collective-permute-start(bf16[80,512]{1,0:T(8,128)(2,1)} %get-tuple-element.41.refs_5_), channel_id=1, source_target_pairs={{0,24},{8,16},{16,8},{24,0},{1,25},{9,17},{17,9},{25,1},{2,26},{10... | collective-permute-start | bytes 245768 | tf_op jit(solution)/shard_map/ppermute | solution.py:80
  51.4 2.0 %collective-permute-start.10 = (bf16[80,512]{1,0:T(8,128)(2,1)}, bf16[80,512]{1,0:T(8,128)(2,1)}, u32[]{:S(2)}, u32[]{:S(2)}) collective-permute-start(bf16[80,512]{1,0:T(8,128)(2,1)} %get-tuple-element.41.refs_5_), channel_id=1, source_target_pairs={{0,16},{8,24},{16,0},{24,8},{1,17},{9,25},{17,1},{25,9},{2,18},{10... | collective-permute-start | bytes 245768 | tf_op jit(solution)/shard_map/ppermute | solution.py:80
  56.4 2.7 %shard_map.118 = (f32[4,8,512]{2,1,0:T(8,128)S(1)}, f32[4,8,512]{2,1,0:T(8,128)S(1)}) custom-call(s32[1,1]{1,0:T(1,128)S(6)} %copy.14.refs_0_, s32[1,1]{1,0:T(1,128)S(6)} %copy.15.refs_1_, s32[1,1]{1,0:T(1,128)S(6)} %copy.16.refs_2_, s32[1,2]{1,0:T(1,128)S(1)} %copy-done.17, s32[1,2]{1,0:T(1,128)S(1)} %copy-done.18, ...), custom_call_target="tpu_custom_call" | custom-call | flops 1000 | bytes 1000 | tf_op jit(solution)/shard_map/pallas_call | solution.py:489
  59.1 4.2 %collective-permute-done.10.refs_7_ = bf16[80,512]{1,0:T(8,128)(2,1)} collective-permute-done((bf16[80,512]{1,0:T(8,128)(2,1)}, bf16[80,512]{1,0:T(8,128)(2,1)}, u32[]{:S(2)}, u32[]{:S(2)}) %collective-permute-start.10) | collective-permute-done | bytes 81952 | tf_op jit(solution)/shard_map/ppermute | solution.py:80
  63.3 3.1 %shard_map.119 = (f32[2,256,512]{2,1,0:T(8,128)S(1)}, f32[2,32,512]{2,1,0:T(8,128)S(1)}, bf16[2,64,512]{2,1,0:T(8,128)(2,1)S(1)}, bf16[2,64,512]{2,1,0:T(8,128)(2,1)S(1)}) custom-call(s32[1,1]{1,0:T(1,128)S(6)} %copy.14.refs_0_, s32[1,1]{1,0:T(1,128)S(6)} %copy.15.refs_1_, s32[1,1]{1,0:T(1,128)S(6)} %copy.16.refs_2_, s32[1,2]{1,0:T(1,128)S(1)} %copy-done.17, ...), custom_call_target="tpu_custom_call" | custom-call | flops 1000 | bytes 1000 | tf_op jit(solution)/shard_map/pallas_call | solution.py:489
  66.5 4.9 %shard_map.123 = (f32[4,8,1024]{2,1,0:T(8,128)S(1)}, f32[4,8,1024]{2,1,0:T(8,128)S(1)}) custom-call(s32[1,1]{1,0:T(1,128)S(6)} %copy.14.refs_0_, s32[1,1]{1,0:T(1,128)S(6)} %copy.15.refs_1_, s32[1,1]{1,0:T(1,128)S(6)} %copy.16.refs_2_, s32[1,2]{1,0:T(1,128)S(1)} %copy-done.17, s32[1,2]{1,0:T(1,128)S(1)} %copy-done.18, ...), custom_call_target="tpu_custom_call" | custom-call | flops 1000 | bytes 1000 | tf_op jit(solution)/shard_map/pallas_call | solution.py:489
  72.0 3.4 %collective-permute-start.13 = (bf16[2,64,512]{2,1,0:T(8,128)(2,1)S(1)}, bf16[2,64,512]{2,1,0:T(8,128)(2,1)S(1)}, u32[]{:S(2)}, u32[]{:S(2)}) collective-permute-start(bf16[2,64,512]{2,1,0:T(8,128)(2,1)S(1)} %get-tuple-element.49), channel_id=1, source_target_pairs={{0,16},{8,24},{16,0},{24,8},{1,17},{9,25},{17,1},{25,9},{2,18},{10... | collective-permute-start | bytes 393224 | tf_op jit(solution)/shard_map/ppermute | solution.py:72
  75.4 1.3 %collective-permute-done.18.refs_2_ = f32[4,8,512]{2,1,0:T(8,128)S(1)} collective-permute-done((f32[4,8,512]{2,1,0:T(8,128)S(1)}, f32[4,8,512]{2,1,0:T(8,128)S(1)}, u32[]{:S(2)}, u32[]{:S(2)}) %collective-permute-start.18) | collective-permute-done | bytes 65568 | tf_op jit(solution)/shard_map/ppermute | solution.py:80
  76.7 1.5 %collective-permute-start.20 = (f32[8,1536]{1,0:T(8,128)S(1)}, f32[8,1536]{1,0:T(8,128)S(1)}, u32[]{:S(2)}, u32[]{:S(2)}) collective-permute-start(f32[8,1536]{1,0:T(8,128)S(1)} %get-tuple-element.58), channel_id=1, source_target_pairs={{0,2},{1,3},{2,0},{3,1},{4,6},{5,7},{6,4},{7,5},{8,10},{9,11},{10,... | collective-permute-start | bytes 147464 | tf_op jit(solution)/shard_map/ppermute | solution.py:690
  78.2 1.5 %collective-permute-start.21 = (f32[8,1536]{1,0:T(8,128)S(1)}, f32[8,1536]{1,0:T(8,128)S(1)}, u32[]{:S(2)}, u32[]{:S(2)}) collective-permute-start(f32[8,1536]{1,0:T(8,128)S(1)} %get-tuple-element.59), channel_id=1, source_target_pairs={{0,4},{1,5},{2,6},{3,7},{4,0},{5,1},{6,2},{7,3},{8,12},{9,13},{10,... | collective-permute-start | bytes 147464 | tf_op jit(solution)/shard_map/ppermute | solution.py:690
  80.3 2.4 %collective-permute-start.12 = (bf16[2,64,512]{2,1,0:T(8,128)(2,1)S(1)}, bf16[2,64,512]{2,1,0:T(8,128)(2,1)S(1)}, u32[]{:S(2)}, u32[]{:S(2)}) collective-permute-start(bf16[2,64,512]{2,1,0:T(8,128)(2,1)S(1)} %get-tuple-element.48), channel_id=1, source_target_pairs={{0,8},{8,0},{16,24},{24,16},{1,9},{9,1},{17,25},{25,17},{2,10},{10... | collective-permute-start | bytes 393224 | tf_op jit(solution)/shard_map/ppermute | solution.py:72
  82.7 3.3 %shard_map.121.refs_11_.refs_4_ = bf16[1,1,8,32,1536]{4,3,2,1,0:T(8,128)(2,1)} custom-call(s32[1,1]{1,0:T(1,128)S(6)} %copy.14.refs_0_, s32[1,1]{1,0:T(1,128)S(6)} %copy.15.refs_1_, s32[1,1]{1,0:T(1,128)S(6)} %copy.16.refs_2_, s32[1,2]{1,0:T(1,128)S(1)} %copy-done.17, s32[1,2]{1,0:T(1,128)S(1)} %copy-done.18, ...), custom_call_target="tpu_custom_call" | custom-call | flops 1000 | bytes 1000 | tf_op jit(solution)/shard_map/pallas_call | solution.py:489
  87.2 3.8 %collective-permute-start.25 = (f32[8,1536]{1,0:T(8,128)S(1)}, f32[8,1536]{1,0:T(8,128)S(1)}, u32[]{:S(2)}, u32[]{:S(2)}) collective-permute-start(f32[8,1536]{1,0:T(8,128)S(1)} %shard_map.125.refs_0_), channel_id=1, source_target_pairs={{0,24},{8,16},{16,8},{24,0},{1,25},{9,17},{17,9},{25,1},{2,26},{10... | collective-permute-start | bytes 147464 | tf_op jit(solution)/shard_map/ppermute | solution.py:80
  91.7 1.7 %shard_map.120.refs_10_.refs_4_ = f32[2,256,512]{2,1,0:T(8,128)S(1)} custom-call(s32[1,1]{1,0:T(1,128)S(6)} %copy.14.refs_0_, s32[1,1]{1,0:T(1,128)S(6)} %copy.15.refs_1_, s32[1,1]{1,0:T(1,128)S(6)} %copy.16.refs_2_, s32[1,2]{1,0:T(1,128)S(1)} %copy-done.17, s32[1,2]{1,0:T(1,128)S(1)} %copy-done.18, bf16[144,512]{1,0:T(8,128)(2,1)} %get-tuple-element.50.refs_5_, ...), custom_call_target="tpu_custom_call" | custom-call | flops 1000 | bytes 1000 | tf_op jit(solution)/shard_map/pallas_call | solution.py:489
  93.4 2.6 %collective-permute-done.24.refs_2_ = f32[8,1536]{1,0:T(8,128)S(1)} collective-permute-done((f32[8,1536]{1,0:T(8,128)S(1)}, f32[8,1536]{1,0:T(8,128)S(1)}, u32[]{:S(2)}, u32[]{:S(2)}) %collective-permute-start.24) | collective-permute-done | bytes 49184 | tf_op jit(solution)/shard_map/ppermute | solution.py:80
  96.0 2.5 %collective-permute-start.28 = (f32[8,1536]{1,0:T(8,128)S(1)}, f32[8,1536]{1,0:T(8,128)S(1)}, u32[]{:S(2)}, u32[]{:S(2)}) collective-permute-start(f32[8,1536]{1,0:T(8,128)S(1)} %shard_map.126.refs_1_), channel_id=1, source_target_pairs={{0,6},{1,7},{2,4},{3,5},{4,2},{5,3},{6,0},{7,1},{8,14},{9,15},{10,... | collective-permute-start | bytes 147464 | tf_op jit(solution)/shard_map/ppermute | solution.py:80
  99.6 5.5 %shard_map.122.refs_5_ = bf16[1,1,8,32,1536]{4,3,2,1,0:T(8,128)(2,1)} custom-call(s32[1,1]{1,0:T(1,128)S(6)} %copy.14.refs_0_, s32[1,1]{1,0:T(1,128)S(6)} %copy.15.refs_1_, s32[1,1]{1,0:T(1,128)S(6)} %copy.16.refs_2_, s32[1,2]{1,0:T(1,128)S(1)} %copy-done.17, s32[1,2]{1,0:T(1,128)S(1)} %copy-done.18, ...), custom_call_target="tpu_custom_call", output_to_operand_aliasing={{}: (11, {})} | custom-call | flops 1000 | bytes 1000 | tf_op jit(solution)/shard_map/pallas_call | solution.py:489
  106.4 1.4 %collective-permute-done.29.refs_2_ = f32[4,8,1536]{2,1,0:T(8,128)S(1)} collective-permute-done((f32[4,8,1536]{2,1,0:T(8,128)S(1)}, f32[4,8,1536]{2,1,0:T(8,128)S(1)}, u32[]{:S(2)}, u32[]{:S(2)}) %collective-permute-start.29) | collective-permute-done | bytes 196640 | tf_op jit(solution)/shard_map/ppermute | solution.py:80
  (87 shorter events, 13.6 us)
Async XLA Ops:
  4.7 20.9 %copy-start.4 = (f32[32,1536]{1,0:T(8,128)S(1)}, f32[32,1536]{1,0:T(8,128)}, u32[]{:S(2)}) copy-start(f32[32,1536]{1,0:T(8,128)} %refs_12_.3) | copy-start | bytes 589828
  4.7 20.9 %copy-start.5 = (f32[25,1536]{1,0:T(8,128)S(1)}, f32[25,1536]{1,0:T(8,128)}, u32[]{:S(2)}) copy-start(f32[25,1536]{1,0:T(8,128)} %refs_9_.11) | copy-start | bytes 460804
  4.7 14.4 %collective-permute-start.1 = (bf16[2,64,512]{2,1,0:T(8,128)(2,1)S(1)}, bf16[2,64,512]{2,1,0:T(8,128)(2,1)S(1)}, u32[]{:S(2)}, u32[]{:S(2)}) collective-permute-start(bf16[2,64,512]{2,1,0:T(8,128)(2,1)S(1)} %get-tuple-element.34), channel_id=1, source_target_pairs={{0,16},{8,24},{16,0},{24,8},{1,17},{9,25},{17,1},{25,9},{2,18},{10... | collective-permute-start | bytes 393224 | tf_op jit(solution)/shard_map/ppermute | solution.py:72
  10.0 11.6 %collective-permute-start.7 = (bf16[144,512]{1,0:T(8,128)(2,1)S(1)}, bf16[144,512]{1,0:T(8,128)(2,1)S(1)}, u32[]{:S(2)}, u32[]{:S(2)}) collective-permute-start(bf16[144,512]{1,0:T(8,128)(2,1)S(1)} %get-tuple-element.37), channel_id=1, source_target_pairs={{0,16},{8,24},{16,0},{24,8},{1,17},{9,25},{17,1},{25,9},{2,18},{10... | collective-permute-start | bytes 442376 | tf_op jit(solution)/shard_map/ppermute | solution.py:72
  10.1 12.1 %collective-permute-start = (bf16[2,64,512]{2,1,0:T(8,128)(2,1)S(1)}, bf16[2,64,512]{2,1,0:T(8,128)(2,1)S(1)}, u32[]{:S(2)}, u32[]{:S(2)}) collective-permute-start(bf16[2,64,512]{2,1,0:T(8,128)(2,1)S(1)} %get-tuple-element.33), channel_id=1, source_target_pairs={{0,8},{8,0},{16,24},{24,16},{1,9},{9,1},{17,25},{25,17},{2,10},{10... | collective-permute-start | bytes 393224 | tf_op jit(solution)/shard_map/ppermute | solution.py:72
  19.1 6.4 %collective-permute-start.2 = (bf16[2,64,512]{2,1,0:T(8,128)(2,1)S(1)}, bf16[2,64,512]{2,1,0:T(8,128)(2,1)S(1)}, u32[]{:S(2)}, u32[]{:S(2)}) collective-permute-start(bf16[2,64,512]{2,1,0:T(8,128)(2,1)S(1)} %collective-permute-done.1.refs_7_), channel_id=1, source_target_pairs={{0,8},{8,0},{16,24},{24,16},{1,9},{9,1},{17,25},{25,17},{2,10},{10... | collective-permute-start | bytes 393224 | tf_op jit(solution)/shard_map/ppermute | solution.py:74
  19.1 18.7 %collective-permute-start.6 = (bf16[144,512]{1,0:T(8,128)(2,1)S(1)}, bf16[144,512]{1,0:T(8,128)(2,1)S(1)}, u32[]{:S(2)}, u32[]{:S(2)}) collective-permute-start(bf16[144,512]{1,0:T(8,128)(2,1)S(1)} %get-tuple-element.36.refs_5_), channel_id=1, source_target_pairs={{0,8},{8,0},{16,24},{24,16},{1,9},{9,1},{17,25},{25,17},{2,10},{10... | collective-permute-start | bytes 442376 | tf_op jit(solution)/shard_map/ppermute | solution.py:72
  21.6 16.2 %collective-permute-start.8 = (bf16[144,512]{1,0:T(8,128)(2,1)S(1)}, bf16[144,512]{1,0:T(8,128)(2,1)S(1)}, u32[]{:S(2)}, u32[]{:S(2)}) collective-permute-start(bf16[144,512]{1,0:T(8,128)(2,1)S(1)} %collective-permute-done.7.refs_7_), channel_id=1, source_target_pairs={{0,8},{8,0},{16,24},{24,16},{1,9},{9,1},{17,25},{25,17},{2,10},{10... | collective-permute-start | bytes 442376 | tf_op jit(solution)/shard_map/ppermute | solution.py:74
  33.4 10.8 %collective-permute-start.5 = (bf16[80,512]{1,0:T(8,128)(2,1)S(1)}, bf16[80,512]{1,0:T(8,128)(2,1)S(1)}, u32[]{:S(2)}, u32[]{:S(2)}) collective-permute-start(bf16[80,512]{1,0:T(8,128)(2,1)S(1)} %get-tuple-element.35.refs_5_), channel_id=1, source_target_pairs={{0,24},{8,16},{16,8},{24,0},{1,25},{9,17},{17,9},{25,1},{2,26},{10... | collective-permute-start | bytes 245768 | tf_op jit(solution)/shard_map/ppermute | solution.py:80
  36.2 8.1 %collective-permute-start.4 = (bf16[80,512]{1,0:T(8,128)(2,1)S(1)}, bf16[80,512]{1,0:T(8,128)(2,1)S(1)}, u32[]{:S(2)}, u32[]{:S(2)}) collective-permute-start(bf16[80,512]{1,0:T(8,128)(2,1)S(1)} %get-tuple-element.35.refs_5_), channel_id=1, source_target_pairs={{0,16},{8,24},{16,0},{24,8},{1,17},{9,25},{17,1},{25,9},{2,18},{10... | collective-permute-start | bytes 245768 | tf_op jit(solution)/shard_map/ppermute | solution.py:80
  36.2 8.1 %collective-permute-start.3 = (bf16[80,512]{1,0:T(8,128)(2,1)S(1)}, bf16[80,512]{1,0:T(8,128)(2,1)S(1)}, u32[]{:S(2)}, u32[]{:S(2)}) collective-permute-start(bf16[80,512]{1,0:T(8,128)(2,1)S(1)} %get-tuple-element.35.refs_5_), channel_id=1, source_target_pairs={{0,8},{8,0},{16,24},{24,16},{1,9},{9,1},{17,25},{25,17},{2,10},{10... | collective-permute-start | bytes 245768 | tf_op jit(solution)/shard_map/ppermute | solution.py:80
  48.6 17.9 %collective-permute-start.16 = (bf16[144,512]{1,0:T(8,128)(2,1)}, bf16[144,512]{1,0:T(8,128)(2,1)S(1)}, u32[]{:S(2)}, u32[]{:S(2)}) collective-permute-start(bf16[144,512]{1,0:T(8,128)(2,1)} %get-tuple-element.51), channel_id=1, source_target_pairs={{0,16},{8,24},{16,0},{24,8},{1,17},{9,25},{17,1},{25,9},{2,18},{10... | collective-permute-start | bytes 442376 | tf_op jit(solution)/shard_map/ppermute | solution.py:72
  49.9 9.1 %collective-permute-start.11 = (bf16[80,512]{1,0:T(8,128)(2,1)}, bf16[80,512]{1,0:T(8,128)(2,1)}, u32[]{:S(2)}, u32[]{:S(2)}) collective-permute-start(bf16[80,512]{1,0:T(8,128)(2,1)} %get-tuple-element.41.refs_5_), channel_id=1, source_target_pairs={{0,24},{8,16},{16,8},{24,0},{1,25},{9,17},{17,9},{25,1},{2,26},{10... | collective-permute-start | bytes 245768 | tf_op jit(solution)/shard_map/ppermute | solution.py:80
  51.4 11.9 %collective-permute-start.10 = (bf16[80,512]{1,0:T(8,128)(2,1)}, bf16[80,512]{1,0:T(8,128)(2,1)}, u32[]{:S(2)}, u32[]{:S(2)}) collective-permute-start(bf16[80,512]{1,0:T(8,128)(2,1)} %get-tuple-element.41.refs_5_), channel_id=1, source_target_pairs={{0,16},{8,24},{16,0},{24,8},{1,17},{9,25},{17,1},{25,9},{2,18},{10... | collective-permute-start | bytes 245768 | tf_op jit(solution)/shard_map/ppermute | solution.py:80
  53.4 9.9 %collective-permute-start.9 = (bf16[80,512]{1,0:T(8,128)(2,1)}, bf16[80,512]{1,0:T(8,128)(2,1)}, u32[]{:S(2)}, u32[]{:S(2)}) collective-permute-start(bf16[80,512]{1,0:T(8,128)(2,1)} %get-tuple-element.41.refs_5_), channel_id=1, source_target_pairs={{0,8},{8,0},{16,24},{24,16},{1,9},{9,1},{17,25},{25,17},{2,10},{10... | collective-permute-start | bytes 245768 | tf_op jit(solution)/shard_map/ppermute | solution.py:80
  54.3 25.4 %collective-permute-start.15 = (bf16[144,512]{1,0:T(8,128)(2,1)}, bf16[144,512]{1,0:T(8,128)(2,1)S(1)}, u32[]{:S(2)}, u32[]{:S(2)}) collective-permute-start(bf16[144,512]{1,0:T(8,128)(2,1)} %get-tuple-element.50.refs_5_), channel_id=1, source_target_pairs={{0,8},{8,0},{16,24},{24,16},{1,9},{9,1},{17,25},{25,17},{2,10},{10... | collective-permute-start | bytes 442376 | tf_op jit(solution)/shard_map/ppermute | solution.py:72
  71.4 5.2 %collective-permute-start.19 = (f32[4,8,1024]{2,1,0:T(8,128)S(1)}, f32[4,8,1024]{2,1,0:T(8,128)S(1)}, u32[]{:S(2)}, u32[]{:S(2)}) collective-permute-start(f32[4,8,1024]{2,1,0:T(8,128)S(1)} %get-tuple-element.56), channel_id=1, source_target_pairs={{0,1},{1,0},{2,3},{3,2},{4,5},{5,4},{6,7},{7,6},{8,9},{9,8},{10,11... | collective-permute-start | bytes 393224 | tf_op jit(solution)/shard_map/ppermute | solution.py:80
  71.5 11.2 %collective-permute-start.17 = (bf16[144,512]{1,0:T(8,128)(2,1)S(1)}, bf16[144,512]{1,0:T(8,128)(2,1)S(1)}, u32[]{:S(2)}, u32[]{:S(2)}) collective-permute-start(bf16[144,512]{1,0:T(8,128)(2,1)S(1)} %collective-permute-done.16.refs_7_.refs_12_), channel_id=1, source_target_pairs={{0,8},{8,0},{16,24},{24,16},{1,9},{9,1},{17,25},{25,17},{2,10},{10... | collective-permute-start | bytes 442376 | tf_op jit(solution)/shard_map/ppermute | solution.py:74
  72.0 8.2 %collective-permute-start.13 = (bf16[2,64,512]{2,1,0:T(8,128)(2,1)S(1)}, bf16[2,64,512]{2,1,0:T(8,128)(2,1)S(1)}, u32[]{:S(2)}, u32[]{:S(2)}) collective-permute-start(bf16[2,64,512]{2,1,0:T(8,128)(2,1)S(1)} %get-tuple-element.49), channel_id=1, source_target_pairs={{0,16},{8,24},{16,0},{24,8},{1,17},{9,25},{17,1},{25,9},{2,18},{10... | collective-permute-start | bytes 393224 | tf_op jit(solution)/shard_map/ppermute | solution.py:72
  75.4 1.3 %collective-permute-start.18 = (f32[4,8,512]{2,1,0:T(8,128)S(1)}, f32[4,8,512]{2,1,0:T(8,128)S(1)}, u32[]{:S(2)}, u32[]{:S(2)}) collective-permute-start(f32[4,8,512]{2,1,0:T(8,128)S(1)} %get-tuple-element.46.refs_13_), channel_id=1, source_target_pairs={{0,1},{1,0},{2,3},{3,2},{4,5},{5,4},{6,7},{7,6},{8,9},{9,8},{10,11... | collective-permute-start | bytes 196616 | tf_op jit(solution)/shard_map/ppermute | solution.py:80
  76.7 9.3 %collective-permute-start.20 = (f32[8,1536]{1,0:T(8,128)S(1)}, f32[8,1536]{1,0:T(8,128)S(1)}, u32[]{:S(2)}, u32[]{:S(2)}) collective-permute-start(f32[8,1536]{1,0:T(8,128)S(1)} %get-tuple-element.58), channel_id=1, source_target_pairs={{0,2},{1,3},{2,0},{3,1},{4,6},{5,7},{6,4},{7,5},{8,10},{9,11},{10,... | collective-permute-start | bytes 147464 | tf_op jit(solution)/shard_map/ppermute | solution.py:690
  78.2 7.8 %collective-permute-start.21 = (f32[8,1536]{1,0:T(8,128)S(1)}, f32[8,1536]{1,0:T(8,128)S(1)}, u32[]{:S(2)}, u32[]{:S(2)}) collective-permute-start(f32[8,1536]{1,0:T(8,128)S(1)} %get-tuple-element.59), channel_id=1, source_target_pairs={{0,4},{1,5},{2,6},{3,7},{4,0},{5,1},{6,2},{7,3},{8,12},{9,13},{10,... | collective-permute-start | bytes 147464 | tf_op jit(solution)/shard_map/ppermute | solution.py:690
  79.8 6.3 %collective-permute-start.22 = (f32[8,1536]{1,0:T(8,128)S(1)}, f32[8,1536]{1,0:T(8,128)S(1)}, u32[]{:S(2)}, u32[]{:S(2)}) collective-permute-start(f32[8,1536]{1,0:T(8,128)S(1)} %get-tuple-element.60), channel_id=1, source_target_pairs={{0,6},{1,7},{2,4},{3,5},{4,2},{5,3},{6,0},{7,1},{8,14},{9,15},{10,... | collective-permute-start | bytes 147464 | tf_op jit(solution)/shard_map/ppermute | solution.py:690
  80.3 19.3 %collective-permute-start.12 = (bf16[2,64,512]{2,1,0:T(8,128)(2,1)S(1)}, bf16[2,64,512]{2,1,0:T(8,128)(2,1)S(1)}, u32[]{:S(2)}, u32[]{:S(2)}) collective-permute-start(bf16[2,64,512]{2,1,0:T(8,128)(2,1)S(1)} %get-tuple-element.48), channel_id=1, source_target_pairs={{0,8},{8,0},{16,24},{24,16},{1,9},{9,1},{17,25},{25,17},{2,10},{10... | collective-permute-start | bytes 393224 | tf_op jit(solution)/shard_map/ppermute | solution.py:72
  82.7 16.9 %collective-permute-start.14 = (bf16[2,64,512]{2,1,0:T(8,128)(2,1)S(1)}, bf16[2,64,512]{2,1,0:T(8,128)(2,1)S(1)}, u32[]{:S(2)}, u32[]{:S(2)}) collective-permute-start(bf16[2,64,512]{2,1,0:T(8,128)(2,1)S(1)} %collective-permute-done.13.refs_7_.refs_5_), channel_id=1, source_target_pairs={{0,8},{8,0},{16,24},{24,16},{1,9},{9,1},{17,25},{25,17},{2,10},{10... | collective-permute-start | bytes 393224 | tf_op jit(solution)/shard_map/ppermute | solution.py:74
  87.2 6.2 %collective-permute-start.25 = (f32[8,1536]{1,0:T(8,128)S(1)}, f32[8,1536]{1,0:T(8,128)S(1)}, u32[]{:S(2)}, u32[]{:S(2)}) collective-permute-start(f32[8,1536]{1,0:T(8,128)S(1)} %shard_map.125.refs_0_), channel_id=1, source_target_pairs={{0,24},{8,16},{16,8},{24,0},{1,25},{9,17},{17,9},{25,1},{2,26},{10... | collective-permute-start | bytes 147464 | tf_op jit(solution)/shard_map/ppermute | solution.py:80
  91.0 5.0 %collective-permute-start.24 = (f32[8,1536]{1,0:T(8,128)S(1)}, f32[8,1536]{1,0:T(8,128)S(1)}, u32[]{:S(2)}, u32[]{:S(2)}) collective-permute-start(f32[8,1536]{1,0:T(8,128)S(1)} %shard_map.125.refs_0_), channel_id=1, source_target_pairs={{0,16},{8,24},{16,0},{24,8},{1,17},{9,25},{17,1},{25,9},{2,18},{10... | collective-permute-start | bytes 147464 | tf_op jit(solution)/shard_map/ppermute | solution.py:80
  91.0 5.0 %collective-permute-start.23 = (f32[8,1536]{1,0:T(8,128)S(1)}, f32[8,1536]{1,0:T(8,128)S(1)}, u32[]{:S(2)}, u32[]{:S(2)}) collective-permute-start(f32[8,1536]{1,0:T(8,128)S(1)} %shard_map.125.refs_0_), channel_id=1, source_target_pairs={{0,8},{8,0},{16,24},{24,16},{1,9},{9,1},{17,25},{25,17},{2,10},{10... | collective-permute-start | bytes 147464 | tf_op jit(solution)/shard_map/ppermute | solution.py:80
  96.0 9.1 %collective-permute-start.28 = (f32[8,1536]{1,0:T(8,128)S(1)}, f32[8,1536]{1,0:T(8,128)S(1)}, u32[]{:S(2)}, u32[]{:S(2)}) collective-permute-start(f32[8,1536]{1,0:T(8,128)S(1)} %shard_map.126.refs_1_), channel_id=1, source_target_pairs={{0,6},{1,7},{2,4},{3,5},{4,2},{5,3},{6,0},{7,1},{8,14},{9,15},{10,... | collective-permute-start | bytes 147464 | tf_op jit(solution)/shard_map/ppermute | solution.py:80
  98.5 6.6 %collective-permute-start.27 = (f32[8,1536]{1,0:T(8,128)S(1)}, f32[8,1536]{1,0:T(8,128)S(1)}, u32[]{:S(2)}, u32[]{:S(2)}) collective-permute-start(f32[8,1536]{1,0:T(8,128)S(1)} %shard_map.126.refs_1_), channel_id=1, source_target_pairs={{0,4},{1,5},{2,6},{3,7},{4,0},{5,1},{6,2},{7,3},{8,12},{9,13},{10,... | collective-permute-start | bytes 147464 | tf_op jit(solution)/shard_map/ppermute | solution.py:80
  99.0 6.1 %collective-permute-start.26 = (f32[8,1536]{1,0:T(8,128)S(1)}, f32[8,1536]{1,0:T(8,128)S(1)}, u32[]{:S(2)}, u32[]{:S(2)}) collective-permute-start(f32[8,1536]{1,0:T(8,128)S(1)} %shard_map.126.refs_1_), channel_id=1, source_target_pairs={{0,2},{1,3},{2,0},{3,1},{4,6},{5,7},{6,4},{7,5},{8,10},{9,11},{10,... | collective-permute-start | bytes 147464 | tf_op jit(solution)/shard_map/ppermute | solution.py:80
  106.3 1.5 %collective-permute-start.29 = (f32[4,8,1536]{2,1,0:T(8,128)S(1)}, f32[4,8,1536]{2,1,0:T(8,128)S(1)}, u32[]{:S(2)}, u32[]{:S(2)}) collective-permute-start(f32[4,8,1536]{2,1,0:T(8,128)S(1)} %shard_map.127.refs_1_), channel_id=1, source_target_pairs={{0,1},{1,0},{2,3},{3,2},{4,5},{5,4},{6,7},{7,6},{8,9},{9,8},{10,11... | collective-permute-start | bytes 589832 | tf_op jit(solution)/shard_map/ppermute | solution.py:80
  (19 other events, 90.9 us)

commit v3 on v2

v3 whole, which is shorter than its diff:
```python
import functools
import math

import jax
import jax.numpy as jnp
from jax import lax
from jax.experimental import pallas as pl
from jax.experimental.pallas import tpu as pltpu
from jax.sharding import PartitionSpec as P

EPSILON = 1e-06
LANES = 256
REACH = 2
EDGE = 8
BYTES_PER_US = 3_690_000
BF16 = jnp.bfloat16
F32 = jnp.float32
PARAMS = pltpu.CompilerParams(vmem_limit_bytes=16 * 1024 * 1024)
SMEM = pl.BlockSpec(memory_space=pltpu.SMEM)


class Place:
    def __init__(self, info_ref):
        slots = (info_ref.shape[0] - 4) // 2
        slot = info_ref[0]
        tall = wide = start = jnp.int32(0)
        for s in range(slots):
            tall_s, wide_s = info_ref[4 + s], info_ref[4 + slots + s]
            tall = jnp.where(slot == s, tall_s, tall)
            wide = jnp.where(slot == s, wide_s, wide)
            start = start + jnp.where(s < slot, tall_s * wide_s, 0)
        self.live = slot < slots
        self.tall, self.wide = tall, wide
        self.row, self.col = info_ref[1], info_ref[2]
        self.group = info_ref[3]
        self.within = self.row * wide + self.col
        self.index = start + self.within
        self.above = self.live & (self.row > 0)
        self.below = self.live & (self.row < tall - 1)

    def same_image(self, delta):
        other = self.within + delta
        return self.live & (other >= 0) & (other < self.tall * self.wide)


class Routes:
    def __init__(self, count):
        self.count = count
        self.relayed = count == 4
        self.shifts = [k for k in (1, -1, 2, -2, 3, -3) if abs(k) < count]
        self.sent = 2 if self.relayed else len(self.shifts)
        self.arriving = 3 if self.relayed else len(self.shifts)

    def targets(self, place):
        if not self.relayed:
            return [jnp.int32(k) for k in self.shifts]
        near, far, last = ((place.index ^ m) - place.index for m in (1, 2, 3))
        return [near, jnp.where(place.same_image(far), far, last)]

    def sources(self, place):
        if not self.relayed:
            return [jnp.int32(-k) for k in self.shifts]
        return [(place.index ^ m) - place.index for m in (1, 2, 3)]

    def move(self, sent, direct=False, hand_on=lambda far: far):
        count = self.count
        if not self.relayed:
            return [
                lax.ppermute(part, "tile", [(s, s + k) for s in range(max(0, -k), min(count, count - k))])
                for part, k in zip(sent, self.shifts)
            ]
        near, far = (
            lax.ppermute(part, "tile", [(s, s ^ m) for s in range(count)]) for part, m in zip(sent, (1, 2))
        )
        if direct:
            return [near, far, lax.ppermute(sent[1], "tile", [(s, s ^ 3) for s in range(count)])]
        return [near, far, lax.ppermute(hand_on(far), "tile", [(s, s ^ 1) for s in range(count)])]


def exchange(value, axis, masks=None):
    count = lax.axis_size(axis)
    masks = range(1, count) if masks is None else masks
    return [lax.ppermute(value, axis, [(s, s ^ m) for s in range(count)]) for m in masks]


def split(x):
    high = x.astype(BF16)
    return high, (x - high.astype(F32)).astype(BF16)


def contract(a, b, dims):
    return lax.dot_general(a, b, (dims, ((), ())), preferred_element_type=F32)


NN = ((1,), (0,))
NT = ((1,), (1,))
TN = ((0,), (0,))


def dot(a, b, dims):
    total = contract(a[0], b[0], dims)
    if b[1] is not None:
        total = total + contract(a[0], b[1], dims)
    if a[1] is not None:
        total = total + contract(a[1], b[0], dims)
    return total


def exact(x):
    return x.astype(BF16), None


def same_head(head_dim):
    rows = lax.broadcasted_iota(jnp.int32, (LANES, LANES), 0) // head_dim
    cols = lax.broadcasted_iota(jnp.int32, (LANES, LANES), 1) // head_dim
    return rows == cols


def spread(compact, mask):
    tall = jnp.concatenate([compact] * (LANES // compact.shape[0]), axis=0)
    return jnp.where(mask, tall, 0.0)


def gather_blocks(full, mask, head_dim):
    kept = jnp.where(mask, full, 0.0)
    return jnp.sum(kept.reshape(LANES // head_dim, head_dim, LANES), axis=0)


def payload(field, place, delta):
    tall, broad, lanes = field.shape
    size = REACH * broad
    top = field[:REACH].reshape(size, lanes)
    bottom = field[tall - REACH :].reshape(size, lanes)
    left = field[:, :EDGE].reshape(size, lanes)
    right = field[:, broad - EDGE :].reshape(size, lanes)
    rows = jnp.where(delta > 0, bottom, top)
    cols = jnp.where(place.col == 0, right, left)
    beside = (place.wide == 2) & (delta == jnp.where(place.col == 0, 1, -1))
    return jnp.where(beside, cols, rows)


def edge_of(ref, size):
    rows = ref[0] if len(ref.shape) == 3 else ref[:size]
    return rows.astype(F32)


def pack_state(state, total):
    rows = jnp.concatenate([state, total, jnp.zeros((7, state.shape[1]), F32)], axis=0)
    return jnp.concatenate(split(rows), axis=0)


def unpack_state(ref, offset):
    rows = ref[offset:].astype(F32)
    half = rows.shape[0] // 2
    return rows[:half] + rows[half:]


def total_state(own_ref, others, place, offset, others_offset):
    total = unpack_state(own_ref, offset)
    for m, other in enumerate(others, 1):
        delta = (place.index ^ m) - place.index
        total = total + jnp.where(place.same_image(delta), unpack_state(other, others_offset), 0.0)
    return total


def fill_padded(pad_ref, field, arrived_refs, deltas, place):
    tall, broad, lanes = field.shape
    size = REACH * broad
    two = place.live & (place.wide == 2)
    one = place.live & (place.wide == 1)
    first, second = two & (place.col == 0), two & (place.col == 1)

    def choose(condition, value, other):
        return jnp.where(condition, value, other)

    above = below = jnp.zeros((REACH, broad, lanes), F32)
    above_side = below_side = jnp.zeros((REACH, EDGE, lanes), F32)
    side = jnp.zeros((tall, EDGE, lanes), F32)
    for arrived_ref, delta in zip(arrived_refs, deltas):
        edges = edge_of(arrived_ref, size)
        rows, cols = edges.reshape(REACH, broad, lanes), edges.reshape(tall, EDGE, lanes)
        begin, end = rows[:, :EDGE], rows[:, broad - EDGE :]
        above = choose((one & (delta == -1)) | (two & (delta == -2)), rows, above)
        below = choose((one & (delta == 1)) | (two & (delta == 2)), rows, below)
        side = choose((first & (delta == 1)) | (second & (delta == -1)), cols, side)
        above_side = choose(first & (delta == -1), begin, choose(second & (delta == -3), end, above_side))
        below_side = choose(second & (delta == 1), end, choose(first & (delta == 3), begin, below_side))
    column = lax.broadcasted_iota(jnp.int32, (1, EDGE, lanes), 1)
    reached = (first & (column < REACH)) | (second & (column >= EDGE - REACH))
    upper, lower = slice(0, REACH), slice(REACH + tall, 2 * REACH + tall)
    pad_ref[upper, :broad] = choose(place.above, above, 0.0)
    pad_ref[lower, :broad] = choose(place.below, below, 0.0)
    pad_ref[upper, broad:] = choose(reached & place.above, above_side, 0.0)
    pad_ref[lower, broad:] = choose(reached & place.below, below_side, 0.0)
    pad_ref[REACH : REACH + tall, broad:] = choose(reached, side, 0.0)
    pad_ref[REACH : REACH + tall, :broad] = field


def convolve(pad_ref, kernel_ref, mix_ref, flipped):
    taps = 2 * REACH + 1
    tall, broad, lanes = mix_ref.shape
    ring = broad + EDGE
    sub = 128
    for start in range(0, lanes, sub):
        at = slice(start, start + sub)
        for y in range(tall):
            rows = [pad_ref[y + a, :, at] for a in range(taps)]
            total = None
            for b in range(taps):
                part = None
                for a in range(taps):
                    tap = taps * a + b
                    if flipped:
                        tap = taps * taps - 1 - tap
                    term = rows[a] * kernel_ref[tap : tap + 1, at]
                    part = term if part is None else part + term
                if b != REACH:
                    part = pltpu.roll(part, (REACH - b) % ring, 0)
                total = part[:broad] if total is None else total + part[:broad]
            mix_ref[y, :, at] = total


def read_field(ref, place, at=slice(None)):
    return jnp.where(place.live, ref[0, 0, :, :, at].astype(F32), 0.0)


def outgoing_kernel(routes, layout, key_ref, value_ref, *outs):
    place = Place(layout)
    for member, field_ref in enumerate((key_ref, value_ref)):
        field = field_ref[0, 0].astype(F32)
        for delta, out_ref in zip(routes.targets(place), outs):
            out_ref[member] = payload(field, place, delta).astype(BF16)


def source_state_kernel(routes, head_dim, *refs):
    layout, (query_ref, key_ref, value_ref), outs = refs[0], refs[1:4], refs[4:]
    place = Place(layout)
    mask = same_head(head_dim)
    for at in parts_of(query_ref.shape[4]):
        field = query_ref[0, 0, :, :, at].astype(F32)
        size = REACH * field.shape[1]
        keys = read_field(key_ref, place, at).reshape(-1, LANES)
        keys = jnp.maximum(keys, 0.0)
        values = read_field(value_ref, place, at).reshape(-1, LANES)
        state = gather_blocks(contract(keys.astype(BF16), values.astype(BF16), TN), mask, head_dim)
        packed = pack_state(state, jnp.sum(keys, axis=0, keepdims=True))
        for delta, out_ref in zip(routes.targets(place), outs):
            out_ref[:size, at] = payload(field, place, delta).astype(BF16)
            out_ref[size:, at] = packed


def forward_kernel(routes, per, head_dim, with_state, *refs):
    count = routes.arriving
    layout, field_ref = refs[:2]
    arrived = refs[2 : 2 + count]
    refs = refs[2 + count :]
    dw_ref, pw_ref, mixed_ref, merged_ref, padded_ref = refs[:5]
    if with_state:
        state_ref, mix_ref, key_ref = refs[5:]
    else:
        (mix_ref,) = refs[5:]
    step = pl.program_id(0)
    place = Place(layout)
    field = read_field(field_ref, place)
    padded = padded_ref.at[0]
    fill_padded(padded, field, arrived, routes.sources(place), place)
    convolve(padded, dw_ref, mix_ref, False)
    mixed = mix_ref[...].reshape(-1, LANES)
    mixed_ref[0] = mixed
    mask = same_head(head_dim)
    merged = dot(split(mixed), split(spread(pw_ref[...], mask)), NN)
    merged_ref[0] = merged
    if not with_state:
        return
    for part in range(per):

        @pl.when(step == part)
        def _():
            key_ref[part] = jnp.maximum(merged, 0.0)

        @pl.when(step == per + part)
        def _():
            keys = key_ref[part]
            state = gather_blocks(dot(split(keys), split(merged), TN), mask, head_dim)
            lanes = slice(part * LANES, (part + 1) * LANES)
            state_ref[:, lanes] = pack_state(state, jnp.sum(keys, axis=0, keepdims=True))


def parts_of(lanes):
    return [slice(start, start + LANES) for start in range(0, lanes, LANES)]


def query_gradients(raw, exactly, total, cot, head_dim, mask):
    ones = (mask.astype(BF16), None)
    query = jnp.maximum(raw, 0.0)
    pair = exact(query) if exactly else split(query)
    state = split(spread(total[:head_dim], mask))
    key_sum = total[head_dim : head_dim + 1]
    over = 1.0 / (dot(split(query * key_sum), ones, NN) + EPSILON)
    result = dot(pair, state, NN) * over
    grad_num = cot * over
    grad_den = -dot(split(cot * result), ones, NN) * over
    num_pair = split(grad_num)
    grad = jnp.where(raw > 0, dot(num_pair, state, NT) + grad_den * key_sum, 0.0)
    gstate = gather_blocks(dot(pair, num_pair, TN), mask, head_dim)
    return grad, pack_state(gstate, jnp.sum(query * grad_den, axis=0, keepdims=True))


def source_query_kernel(others, offset, others_offset, head_dim, *refs):
    layout, own_ref, received = refs[0], refs[1], refs[2 : 2 + others]
    source_ref, cot_ref, grad_ref, gstate_ref = refs[2 + others :]
    place = Place(layout)
    mask = same_head(head_dim)
    total = total_state(own_ref, received, place, offset, others_offset)
    for at in parts_of(gstate_ref.shape[1]):
        raw = read_field(source_ref, place, at).reshape(-1, LANES)
        cot = cot_ref[0, 0, :, :, at].astype(F32).reshape(raw.shape)
        grad_ref[0, :, at], gstate_ref[:, at] = query_gradients(raw, True, total[:, at], cot, head_dim, mask)


def merged_query_kernel(others, head_dim, *refs):
    layout, own_ref, received = refs[0], refs[1], refs[2 : 2 + others]
    merged_ref, mixed_ref, cot_ref, pw_ref, gstate_ref, gmix_ref, gpw_ref = refs[2 + others :]
    place = Place(layout)
    mask = same_head(head_dim)
    total = total_state(own_ref, received, place, 0, 0)
    for at in parts_of(gstate_ref.shape[1]):
        raw = merged_ref[0, :, at]
        cot = cot_ref[0, 0, :, :, at].astype(F32).reshape(raw.shape)
        grad, gstate_ref[:, at] = query_gradients(raw, False, total[:, at], cot, head_dim, mask)
        pair = split(grad)
        gmix_ref[0, :, at] = dot(pair, split(spread(pw_ref[:, at], mask)), NT)
        gpw_ref[0, :, at] = gather_blocks(dot(split(mixed_ref[0, :, at]), pair, TN), mask, head_dim)


def key_gradients(raw, key_pair, value_pair, total, head_dim, mask):
    gstate = split(spread(total[:head_dim], mask))
    gsum = total[head_dim : head_dim + 1]
    grad_keys = jnp.where(raw > 0, dot(value_pair, gstate, NT) + gsum, 0.0)
    return grad_keys, dot(key_pair, gstate, NN)


def source_value_kernel(others, offset, others_offset, head_dim, *refs):
    layout, own_ref, received = refs[0], refs[1], refs[2 : 2 + others]
    key_ref, value_ref, grad_ref = refs[2 + others :]
    place = Place(layout)
    mask = same_head(head_dim)
    total = total_state(own_ref, received, place, offset, others_offset)
    for at in parts_of(grad_ref.shape[2]):
        raw = read_field(key_ref, place, at).reshape(-1, LANES)
        values = read_field(value_ref, place, at).reshape(-1, LANES)
        grad_ref[0, :, at], grad_ref[1, :, at] = key_gradients(
            raw, exact(jnp.maximum(raw, 0.0)), exact(values), total[:, at], head_dim, mask
        )


def merged_value_kernel(others, routes, tall, head_dim, *refs):
    layout, own_ref, received = refs[0], refs[1], refs[2 : 2 + others]
    merged_ref, mixed_ref, kpw_ref, vpw_ref, qgmix_ref, packed_ref, gmix_ref, gpw_ref = refs[2 + others : 10 + others]
    outs = refs[10 + others :]
    place = Place(layout)
    mask = same_head(head_dim)
    total = total_state(own_ref, received, place, 0, 0)
    size = (outs[0].shape[0] - packed_ref.shape[0]) // 3

    def send(member, at, gmix):
        field = gmix.reshape(tall, -1, LANES)
        for delta, out_ref in zip(routes.targets(place), outs):
            out_ref[member * size : (member + 1) * size, at] = payload(field, place, delta).astype(BF16)

    for at in parts_of(gmix_ref.shape[2]):
        for out_ref in outs:
            out_ref[3 * size :, at] = packed_ref[:, at]
        send(0, at, qgmix_ref[0, :, at])
        raw = merged_ref[0, :, at]
        pairs = split(jnp.maximum(raw, 0.0)), split(merged_ref[1, :, at])
        grads = key_gradients(raw, *pairs, total[:, at], head_dim, mask)
        for member, (grad, pw_ref) in enumerate(zip(grads, (kpw_ref, vpw_ref))):
            pair = split(grad)
            gmix = dot(pair, split(spread(pw_ref[:, at], mask)), NT)
            gmix_ref[member, :, at] = gmix
            gpw_ref[member, :, at] = gather_blocks(dot(split(mixed_ref[member, :, at]), pair, TN), mask, head_dim)
            send(1 + member, at, gmix)


def weight_kernel(routes, halves, *refs):
    layout, padded_ref, gmix_ref, gpw_ref = refs[:4]
    refs = refs[4:]
    place = Place(layout)
    ring, sub = padded_ref.shape[2], 128
    tall, broad = padded_ref.shape[1] - 2 * REACH, ring - EDGE
    outs, sum_ref = refs[:-1], refs[-1]
    taps = 2 * REACH + 1
    for part in range(LANES // sub):
        lanes = slice(part * sub, (part + 1) * sub)

        def one_row(y, totals):
            grad = gmix_ref[0, pl.ds(pl.multiple_of(y * broad, broad), broad), lanes]
            grad = jnp.concatenate([grad, jnp.zeros((EDGE, sub), F32)], axis=0)
            moved = [grad if b == REACH else pltpu.roll(grad, (b - REACH) % ring, 0) for b in range(taps)]
            new = list(totals)
            for a in range(taps):
                row = padded_ref[0, y + a, :, lanes]
                for b in range(taps):
                    term = (row * moved[b]).reshape(ring // 8, 8, sub)
                    new[taps * a + b] = new[taps * a + b] + jnp.sum(term, axis=0)
            return tuple(new)

        zero = jnp.zeros((8, sub), F32)
        totals = lax.fori_loop(0, tall, one_row, (zero,) * (taps * taps), unroll=2)
        for tap in range(taps * taps):
            sum_ref[tap : tap + 1, lanes] = jnp.sum(totals[tap], axis=0, keepdims=True)
    start = sum_ref.shape[0] - gpw_ref.shape[1]
    sum_ref[taps * taps : start] = jnp.zeros((start - taps * taps, LANES), F32)
    sum_ref[start:] = gpw_ref[0]
    if not halves:
        outs[0][...] = sum_ref[...]
        return
    rows = outs[0].shape[1]
    odd = place.group % 2 == 1
    for part in range(outs[0].shape[0]):
        even_rows = sum_ref[2 * part * rows : (2 * part + 1) * rows]
        odd_rows = sum_ref[(2 * part + 1) * rows : (2 * part + 2) * rows]
        outs[0][part] = jnp.where(odd, even_rows, odd_rows)
        outs[1][part] = jnp.where(odd, odd_rows, even_rows)


def scatter_kernel(layout, keep_q, come_q, keep_kv, come_kv, own_ref, *outs):
    quarter = Place(layout).group // 2
    third = keep_q.shape[2]
    for m, out_ref in enumerate((own_ref,) + outs):
        at = quarter ^ m
        out_ref[:, :third] = keep_q[at] + come_q[at]
        out_ref[:, third:] = keep_kv[at] + come_kv[at]


def sum_kernel(norm, *refs):
    parts, out_ref = [ref[...] for ref in refs[:-1]], refs[-1]
    while len(parts) > 1:
        parts = [parts[i] + parts[i + 1] for i in range(0, len(parts), 2)]
    out_ref[...] = parts[0] * norm


def collect_kernel(layout, *refs):
    parts, out_ref = refs[:-1], refs[-1]
    quarter = Place(layout).group // 2
    for m, part in enumerate(parts):
        out_ref[quarter ^ m] = part[...]


def finish_kernel(taps, layout, own_ref, come_ref, dw_ref, pw_ref, whole_ref):
    odd = Place(layout).group % 2 == 1
    quarters, rows = own_ref.shape[:2]
    for part in range(quarters):
        own, come = own_ref[part], come_ref[part]
        whole_ref[2 * part * rows : (2 * part + 1) * rows] = jnp.where(odd, come, own)
        whole_ref[(2 * part + 1) * rows : (2 * part + 2) * rows] = jnp.where(odd, own, come)
    dw_ref[...] = whole_ref[:taps]
    pw_ref[...] = whole_ref[whole_ref.shape[0] - pw_ref.shape[0] :]


def copy_kernel(in_ref, out_ref):
    out_ref[...] = in_ref[...]


def backward_kernel(routes, *refs):
    count = routes.arriving
    layout, gmix_ref = refs[:2]
    arrived = refs[2 : 2 + count]
    dw_ref, grad0_ref, out_ref, pad_ref, mix_ref = refs[2 + count :]
    place = Place(layout)
    tall, broad = out_ref.shape[2:4]
    field = gmix_ref[0].reshape(tall, broad, LANES)
    fill_padded(pad_ref, field, arrived, routes.sources(place), place)
    convolve(pad_ref, dw_ref, mix_ref, True)
    grad = mix_ref[...] + grad0_ref[0].reshape(tall, broad, LANES)
    out_ref[0, 0] = jnp.where(place.live, grad, 0.0).astype(BF16)


def call(cost, kernel, grid, in_specs, out_specs, out_shape, scratch=(), after=(), onto=()):
    inputs, extra = len(in_specs), len(onto) + len(after)

    def body(*refs):
        kernel(*refs[:inputs], *refs[inputs + extra :])

    run = pl.pallas_call(
        body,
        grid=(grid,),
        in_specs=list(in_specs) + [pl.BlockSpec(memory_space=pl.ANY)] * extra,
        out_specs=out_specs,
        out_shape=out_shape,
        scratch_shapes=list(scratch),
        input_output_aliases={inputs: 0} if onto else {},
        compiler_params=PARAMS,
        cost_estimate=pl.CostEstimate(
            flops=0, bytes_accessed=int(cost * BYTES_PER_US), transcendentals=0
        ),
    )
    return lambda *args: run(*args, *onto, *after)


def in_hbm(x):
    return pltpu.with_memory_space_constraint(x, pltpu.HBM)


def local(
    qkv, cotangent, dw_weight, pw_weight, tile_image, tile_row, tile_col, image_height, image_width
):
    tall, broad, channels = qkv.shape[2:]
    positions = tall * broad
    head_dim = pw_weight.shape[0]
    taps = dw_weight.shape[0]
    third = channels // 3
    per = third // LANES
    tiles, groups = lax.axis_size("tile"), lax.axis_size("img")
    routes = Routes(tiles)
    head_specs = [SMEM]
    edge = REACH * broad
    packed = 2 * (head_dim + 8)
    padded_shape = (tall + 2 * REACH, broad + EDGE)
    shape = jax.ShapeDtypeStruct
    spot = lax.axis_index("img").astype(jnp.int32)
    scalars = (tile_image, tile_row, tile_col, spot, image_height, image_width)
    layout = jnp.concatenate([x.reshape(-1) for x in scalars])
    qkv, cotangent = in_hbm(qkv), in_hbm(cotangent)

    def tile_spec(first):
        return pl.BlockSpec((1, 1, tall, broad, LANES), lambda j: (0, 0, 0, 0, first * per + j))

    def third_spec(first):
        return pl.BlockSpec((1, 1, tall, broad, third), lambda j: (0, 0, 0, 0, first))

    def flat_spec(rows, first=0):
        return pl.BlockSpec((rows, LANES), lambda j: (0, first * per + j))

    def wide_spec(rows, first=0):
        return pl.BlockSpec((rows, third), lambda j: (0, first))

    def member_spec(*dims):
        return pl.BlockSpec((1, *dims, LANES), lambda j: (j // per,) + (0,) * len(dims) + (j % per,))

    def edge_spec(first):
        return pl.BlockSpec((edge, LANES), lambda j: (first + j // per, j % per))

    def whole_spec(*dims):
        return pl.BlockSpec(dims, lambda j: (0,) * len(dims))

    mix_scratch = [pltpu.VMEM((tall, broad, LANES), F32)]
    low, high = edge, edge + packed

    sent_kv = call(
        1.2,
        functools.partial(outgoing_kernel, routes),
        1,
        head_specs + [third_spec(1), third_spec(2)],
        [whole_spec(2, edge, third)] * routes.sent,
        [shape((2, edge, third), BF16)] * routes.sent,
    )(layout, qkv, qkv)
    halo_kv = routes.move(sent_kv)
    sent_q = call(
        1.5,
        functools.partial(source_state_kernel, routes, head_dim),
        1,
        head_specs + [third_spec(0), third_spec(1), third_spec(2)],
        [whole_spec(high, third)] * routes.sent,
        [shape((high, third), BF16)] * routes.sent,
        after=(halo_kv[0],),
    )(layout, qkv, qkv, qkv)
    halo_q = routes.move(sent_q, direct=True)

    def forward(first, count, halo, halo_spec):
        with_state = first > 0
        outs = [member_spec(positions)] * 2 + [member_spec(*padded_shape)]
        shapes = [pltpu.HBM((count, positions, third), F32)] * 2
        shapes.append(pltpu.HBM((count, *padded_shape, third), F32))
        scratch = mix_scratch
        if with_state:
            outs.append(whole_spec(packed, third))
            shapes.append(shape((packed, third), BF16))
            scratch = scratch + [pltpu.VMEM((per, positions, LANES), F32)]
        return call(
            1.7 * count * per,
            functools.partial(forward_kernel, routes, per, head_dim, with_state),
            count * per,
            head_specs
            + [tile_spec(first)]
            + [halo_spec] * routes.arriving
            + [flat_spec(taps, first), flat_spec(head_dim, first)],
            outs,
            shapes,
            scratch,
        )(layout, qkv, *halo, dw_weight, pw_weight)

    mixed_kv, merged_kv, padded_kv, state = forward(1, 2, halo_kv, member_spec(edge))
    state_from = exchange(state, "tile")
    others = len(state_from)
    mixed_q, merged_q, padded_q = forward(0, 1, halo_q, flat_spec(high))

    source_from = halo_q if routes.relayed else exchange(sent_q[0][low:], "tile")
    from_rows, from_offset = (high, low) if routes.relayed else (packed, 0)
    grad0_q, gstate0 = call(
        2.9,
        functools.partial(source_query_kernel, others, low, from_offset, head_dim),
        1,
        head_specs
        + [whole_spec(high, third)]
        + [whole_spec(from_rows, third)] * others
        + [third_spec(0), third_spec(0)],
        [whole_spec(1, positions, third), whole_spec(packed, third)],
        [pltpu.HBM((1, positions, third), F32), shape((packed, third), BF16)],
    )(layout, sent_q[0], *source_from, qkv, cotangent)

    gstate, gmix_q, gpw_q = call(
        3.2,
        functools.partial(merged_query_kernel, others, head_dim),
        1,
        head_specs
        + [whole_spec(packed, third)] * (1 + others)
        + [whole_spec(1, positions, third)] * 2
        + [third_spec(1), wide_spec(head_dim)],
        [whole_spec(packed, third), whole_spec(1, positions, third), whole_spec(1, head_dim, third)],
        [
            shape((packed, third), BF16),
            shape((1, positions, third), F32),
            shape((1, head_dim, third), F32),
        ],
        after=(gstate0,),
    )(layout, state, *state_from, in_hbm(merged_q), in_hbm(mixed_q), cotangent, pw_weight)
    gstate_from = exchange(gstate, "tile")

    gap = -(-taps // 8) * 8
    rows = gap + head_dim
    halves = groups == 8 and rows % groups == 0
    eighth = rows // groups

    def weights(count, padded, gmix, gpw, after=()):
        if halves:
            outs = [pl.BlockSpec((4, eighth, LANES), lambda j: (0, 0, j))] * 2
            shapes = [shape((4, eighth, count * third), F32)] * 2
        else:
            outs, shapes = [flat_spec(rows)], [shape((rows, count * third), F32)]
        return call(
            1.2 * count * per,
            functools.partial(weight_kernel, routes, halves),
            count * per,
            head_specs + [member_spec(*padded_shape), member_spec(positions), member_spec(head_dim)],
            outs,
            shapes,
            [pltpu.VMEM((rows, LANES), F32)],
            after,
        )(layout, in_hbm(padded), gmix, gpw)

    weights_q = weights(1, padded_q, gmix_q, gpw_q)
    total_rows = 3 * edge + packed
    gmix_kv, gpw_kv, *sent_back = call(
        3.2,
        functools.partial(merged_value_kernel, others, routes, tall, head_dim),
        1,
        head_specs
        + [whole_spec(packed, third)] * (1 + others)
        + [whole_spec(2, positions, third)] * 2
        + [wide_spec(head_dim, 1), wide_spec(head_dim, 2)]
        + [whole_spec(1, positions, third), whole_spec(packed, third)],
        [whole_spec(2, positions, third), whole_spec(2, head_dim, third)]
        + [whole_spec(total_rows, third)] * routes.sent,
        [shape((2, positions, third), F32), shape((2, head_dim, third), F32)]
        + [shape((total_rows, third), BF16)] * routes.sent,
        after=(weights_q[0],),
    )(
        layout, gstate, *gstate_from, in_hbm(merged_kv), in_hbm(mixed_kv), pw_weight, pw_weight,
        gmix_q, gstate0,
    )
    weights_kv = weights(2, padded_kv, gmix_kv, gpw_kv)

    def after_weights(far):
        return call(
            0.5,
            copy_kernel,
            1,
            [whole_spec(total_rows, third)],
            whole_spec(total_rows, third),
            shape((total_rows, third), BF16),
            after=(weights_kv[0],),
        )(far)

    halo_back = routes.move(sent_back, hand_on=after_weights)

    back_from = halo_back if routes.relayed else exchange(sent_back[0][3 * edge :], "tile")
    back_rows, back_offset = (total_rows, 3 * edge) if routes.relayed else (packed, 0)
    grad0_kv = call(
        1.5,
        functools.partial(source_value_kernel, others, 3 * edge, back_offset, head_dim),
        1,
        head_specs
        + [whole_spec(total_rows, third)]
        + [whole_spec(back_rows, third)] * others
        + [third_spec(1), third_spec(2)],
        whole_spec(2, positions, third),
        shape((2, positions, third), F32),
    )(layout, sent_back[0], *back_from, qkv, qkv)

    def backward(first, count, gmix, grad0, onto=()):
        return call(
            1.2 * count * per,
            functools.partial(backward_kernel, routes),
            count * per,
            head_specs
            + [member_spec(positions)]
            + [edge_spec(first)] * routes.arriving
            + [flat_spec(taps, first), member_spec(positions)],
            tile_spec(first),
            pltpu.HBM((1, 1, tall, broad, channels), BF16),
            [pltpu.VMEM((*padded_shape, LANES), F32)] + mix_scratch,
            onto=onto,
        )(layout, gmix, *halo_back, dw_weight, grad0)

    grad_query = in_hbm(backward(0, 1, gmix_q, in_hbm(grad0_q)))
    grad_source = backward(1, 2, gmix_kv, grad0_kv, (grad_query,))

    norm = 1.0 / math.sqrt(positions * tiles * groups)
    if halves:
        come_q = exchange(weights_q[0], "img", (1,))[0]
        come_kv = exchange(weights_kv[0], "img", (1,))[0]
        part = shape((eighth, channels), F32)
        parts = call(
            0.5,
            scatter_kernel,
            1,
            [SMEM]
            + [whole_spec(4, eighth, third)] * 2
            + [whole_spec(4, eighth, 2 * third)] * 2,
            [whole_spec(eighth, channels)] * 4,
            [part] * 4,
        )(layout, weights_q[1], come_q, weights_kv[1], come_kv)
        count = lax.axis_size("img")
        moved = [
            lax.ppermute(part_m, "img", [(s, s ^ (2 * m)) for s in range(count)])
            for m, part_m in enumerate(parts[1:], 1)
        ]

        def add(values, factor, after):
            return call(
                0.3,
                functools.partial(sum_kernel, factor),
                1,
                [whole_spec(eighth, channels)] * len(values),
                whole_spec(eighth, channels),
                part,
                after=after,
            )(*values)

        share = add([parts[0]] + moved, 1.0, (grad_query,))
        share = add([share] + exchange(share, "tile"), norm, (grad0_kv,))
        quarters = call(
            0.5,
            collect_kernel,
            1,
            [SMEM] + [whole_spec(eighth, channels)] * 4,
            whole_spec(4, eighth, channels),
            shape((4, eighth, channels), F32),
            after=(in_hbm(grad_source),),
        )(layout, share, *exchange(share, "img", (2, 4, 6)))
        grad_dw, grad_pw = call(
            0.8,
            functools.partial(finish_kernel, taps),
            1,
            [SMEM] + [whole_spec(4, eighth, channels)] * 2,
            [whole_spec(taps, channels), whole_spec(head_dim, channels)],
            [shape((taps, channels), F32), shape((head_dim, channels), F32)],
            [pltpu.VMEM((rows, channels), F32)],
        )(layout, quarters, exchange(quarters, "img", (1,))[0])
    else:
        whole = jnp.concatenate([weights_q[0], weights_kv[0]], axis=1)
        whole = lax.psum(whole, ("tile", "img")) * norm
        grad_dw, grad_pw = whole[:taps], whole[gap:]

    return grad_source, grad_dw, grad_pw


def solution(mesh):
    placed = (
        P("img", "tile", None, None, None),
        P("img", "tile", None, None, None),
        P(),
        P(),
        P("img", "tile"),
        P("img", "tile"),
        P("img", "tile"),
        P("img", None),
        P("img", None),
    )
    return jax.shard_map(
        local,
        mesh=mesh,
        in_specs=placed,
        out_specs=(P("img", "tile", None, None, None), P(), P()),
        check_vma=False,
    )
```

time: 109 us -> 101 us (0.927)
  local copies, waits for them, and re-layouts: 6.81 us -> 0.76 us
  waiting for transfers between devices: 20.5 us -> 17.9 us
    ppermute x8 -> x6, starting transfers between devices: 16.3 us -> 8.58 us  [move(): lax.ppermute(part, 'tile', [(s, s ^ m) for s in range(count)])]
    unnamed x42 -> x4, local copies, waits for them, and re-layouts: 6.81 us -> 0.01 us
    ppermute x15, starting transfers between devices: 16.9 us -> 21.7 us  [exchange(): lax.ppermute(value, axis, [(s, s ^ m) for s in range(count)])]
    ppermute x4 -> x3, starting transfers between devices: 1.17 us -> 3.75 us  [the longest x1 3.23 us: move(): lax.ppermute(sent[1], 'tile', [(s, s ^ 3) for s in range(count)])]
    ppermute x15, waiting for transfers between devices: 9.54 us -> 7.01 us  [exchange(): lax.ppermute(value, axis, [(s, s ^ m) for s in range(count)])]
    pallas_call x17 -> x18, Pallas kernels: 40.4 us -> 41.1 us  [call(): return lambda *args: run(*args, *onto, *after)]
    ppermute x4 -> x3, waiting for transfers between devices: 3.39 us -> 2.73 us  [the longest x2 2.73 us: move(): lax.ppermute(hand_on(far), 'tile', [(s, s ^ 1) for s in range(count)])]
    ppermute x8 -> x6, waiting for transfers between devices: 7.57 us -> 7.89 us  [move(): lax.ppermute(part, 'tile', [(s, s ^ m) for s in range(count)])]
  transfers between devices with their start and end apart: 30 -> 27, of which waited for: 7 -> 11; matrix products, arithmetic and copies ran while one was open for 0% -> 0% of each run, Pallas kernels for 32% -> 32%
where the time goes in v3:
time: 101 us; the launch traced here: 100 us
  Pallas kernels  41.1 us (41%)
  starting transfers between devices  37.6 us (37%)
  waiting for transfers between devices  17.9 us (18%)
  between operations  2.72 us (3%)
    pallas_call x18, Pallas kernels, call(): return lambda *args: run(*args, *onto, *after)  41.1 us
    ppermute x15, starting transfers between devices, exchange(): lax.ppermute(value, axis, [(s, s ^ m) for s in range(count)])  21.7 us
    ppermute x6, starting transfers between devices, move(): lax.ppermute(part, 'tile', [(s, s ^ m) for s in range(count)])  8.58 us
    ppermute x6, waiting for transfers between devices, move(): lax.ppermute(part, 'tile', [(s, s ^ m) for s in range(count)])  7.89 us
    ppermute x15, waiting for transfers between devices, exchange(): lax.ppermute(value, axis, [(s, s ^ m) for s in range(count)])  7.01 us
    ppermute x3, starting transfers between devices, local(): lax.ppermute(part_m, 'img', [(s, s ^ 2 * m) for s in range(count)])  3.55 us
    ppermute x1, starting transfers between devices, move(): lax.ppermute(sent[1], 'tile', [(s, s ^ 3) for s in range(count)])  3.23 us
    ppermute x2, waiting for transfers between devices, move(): lax.ppermute(hand_on(far), 'tile', [(s, s ^ 1) for s in range(count)])  2.73 us
  transfers between devices with their start and end apart: 27, of which 11 were waited for; matrix products, arithmetic and copies ran while one was open for 0% of the time, Pallas kernels for 32%

profile of v3, /device:TPU:0, one launch (start us, length us, event | category | flops | bytes accessed | tf_op | source)
XLA Modules:
  0.0 100.1 jit_solution(16670652719735781772)
XLA Ops:
  3.3 1.2 %shard_map.112 = (bf16[2,64,512]{2,1,0:T(8,128)(2,1)S(1)}, bf16[2,64,512]{2,1,0:T(8,128)(2,1)S(1)}) custom-call(s32[8]{0:T(128)S(1)} %concatenate.3.refs_0_, bf16[1,1,8,32,1536]{4,3,2,1,0:T(8,128)(2,1)} %refs_6_.7, bf16[1,1,8,32,1536]{4,3,2,1,0:T(8,128)(2,1)} %refs_6_.7), custom_call_target="tpu_custom_call" | custom-call | bytes 4428000 | tf_op jit(solution)/shard_map/pallas_call | solution.py:499
  4.5 3.1 %collective-permute-start = (bf16[2,64,512]{2,1,0:T(8,128)(2,1)S(1)}, bf16[2,64,512]{2,1,0:T(8,128)(2,1)S(1)}, u32[]{:S(2)}, u32[]{:S(2)}) collective-permute-start(bf16[2,64,512]{2,1,0:T(8,128)(2,1)S(1)} %get-tuple-element.33), channel_id=1, source_target_pairs={{0,8},{8,0},{16,24},{24,16},{1,9},{9,1},{17,25},{25,17},{2,10},{10... | collective-permute-start | bytes 393224 | tf_op jit(solution)/shard_map/ppermute | solution.py:73
  7.6 2.6 %collective-permute-start.1 = (bf16[2,64,512]{2,1,0:T(8,128)(2,1)S(1)}, bf16[2,64,512]{2,1,0:T(8,128)(2,1)S(1)}, u32[]{:S(2)}, u32[]{:S(2)}) collective-permute-start(bf16[2,64,512]{2,1,0:T(8,128)(2,1)S(1)} %get-tuple-element.34), channel_id=1, source_target_pairs={{0,16},{8,24},{16,0},{24,8},{1,17},{9,25},{17,1},{25,9},{2,18},{10... | collective-permute-start | bytes 393224 | tf_op jit(solution)/shard_map/ppermute | solution.py:73
  10.2 2.8 %collective-permute-done.refs_2_.refs_4_ = bf16[2,64,512]{2,1,0:T(8,128)(2,1)S(1)} collective-permute-done((bf16[2,64,512]{2,1,0:T(8,128)(2,1)S(1)}, bf16[2,64,512]{2,1,0:T(8,128)(2,1)S(1)}, u32[]{:S(2)}, u32[]{:S(2)}) %collective-permute-start) | collective-permute-done | bytes 131104 | tf_op jit(solution)/shard_map/ppermute | solution.py:73
  13.0 1.5 %shard_map.114 = (bf16[144,512]{1,0:T(8,128)(2,1)S(1)}, bf16[144,512]{1,0:T(8,128)(2,1)S(1)}) custom-call(s32[8]{0:T(128)S(1)} %concatenate.3.refs_0_, bf16[1,1,8,32,1536]{4,3,2,1,0:T(8,128)(2,1)} %refs_6_.7, bf16[1,1,8,32,1536]{4,3,2,1,0:T(8,128)(2,1)} %refs_6_.7, bf16[1,1,8,32,1536]{4,3,2,1,0:T(8,128)(2,1)} %refs_6_.7, ...), custom_call_target="tpu_custom_call" | custom-call | bytes 5535000 | tf_op jit(solution)/shard_map/pallas_call | solution.py:499
  14.9 1.5 %collective-permute-done.1.refs_3_ = bf16[2,64,512]{2,1,0:T(8,128)(2,1)S(1)} collective-permute-done((bf16[2,64,512]{2,1,0:T(8,128)(2,1)S(1)}, bf16[2,64,512]{2,1,0:T(8,128)(2,1)S(1)}, u32[]{:S(2)}, u32[]{:S(2)}) %collective-permute-start.1) | collective-permute-done | bytes 131104 | tf_op jit(solution)/shard_map/ppermute | solution.py:73
  16.8 3.2 %collective-permute-start.8 = (bf16[144,512]{1,0:T(8,128)(2,1)S(1)}, bf16[144,512]{1,0:T(8,128)(2,1)S(1)}, u32[]{:S(2)}, u32[]{:S(2)}) collective-permute-start(bf16[144,512]{1,0:T(8,128)(2,1)S(1)} %get-tuple-element.37), channel_id=1, source_target_pairs={{0,24},{8,16},{16,8},{24,0},{1,25},{9,17},{17,9},{25,1},{2,26},{10... | collective-permute-start | bytes 442376 | tf_op jit(solution)/shard_map/ppermute | solution.py:76
  20.0 1.7 %collective-permute-done.2.refs_4_ = bf16[2,64,512]{2,1,0:T(8,128)(2,1)S(1)} collective-permute-done((bf16[2,64,512]{2,1,0:T(8,128)(2,1)S(1)}, bf16[2,64,512]{2,1,0:T(8,128)(2,1)S(1)}, u32[]{:S(2)}, u32[]{:S(2)}) %collective-permute-start.2) | collective-permute-done | bytes 131104 | tf_op jit(solution)/shard_map/ppermute | solution.py:77
  21.7 6.7 %shard_map.113 = (f32[2,256,512]{2,1,0:T(8,128)}, f32[2,256,512]{2,1,0:T(8,128)}, f32[2,12,40,512]{3,2,1,0:T(8,128)}, bf16[80,512]{1,0:T(8,128)(2,1)S(1)}) custom-call(s32[8]{0:T(128)S(1)} %concatenate.3.refs_0_, bf16[1,1,8,32,1536]{4,3,2,1,0:T(8,128)(2,1)} %refs_6_.7, bf16[2,64,512]{2,1,0:T(8,128)(2,1)S(1)} %collective-permute-done.refs_2_.refs_4_, ...), custom_call_target="tpu_custom_call" | custom-call | bytes 25092000 | tf_op jit(solution)/shard_map/pallas_call | solution.py:499
  28.3 7.9 %collective-permute-start.5 = (bf16[80,512]{1,0:T(8,128)(2,1)S(1)}, bf16[80,512]{1,0:T(8,128)(2,1)S(1)}, u32[]{:S(2)}, u32[]{:S(2)}) collective-permute-start(bf16[80,512]{1,0:T(8,128)(2,1)S(1)} %get-tuple-element.35.refs_1_), channel_id=1, source_target_pairs={{0,24},{8,16},{16,8},{24,0},{1,25},{9,17},{17,9},{25,1},{2,26},{10... | collective-permute-start | bytes 245768 | tf_op jit(solution)/shard_map/ppermute | solution.py:83
  36.8 3.7 %shard_map.115 = (f32[1,256,512]{2,1,0:T(8,128)}, f32[1,256,512]{2,1,0:T(8,128)}, f32[1,12,40,512]{3,2,1,0:T(8,128)}) custom-call(s32[8]{0:T(128)S(1)} %concatenate.3.refs_0_, bf16[1,1,8,32,1536]{4,3,2,1,0:T(8,128)(2,1)} %refs_6_.7, bf16[144,512]{1,0:T(8,128)(2,1)S(1)} %collective-permute-done.6.refs_2_, ...), custom_call_target="tpu_custom_call" | custom-call | bytes 12546000 | tf_op jit(solution)/shard_map/pallas_call | solution.py:499
  40.6 3.0 %shard_map.116 = (f32[1,256,512]{2,1,0:T(8,128)}, bf16[80,512]{1,0:T(8,128)(2,1)S(1)}) custom-call(s32[8]{0:T(128)S(1)} %concatenate.3.refs_0_, bf16[144,512]{1,0:T(8,128)(2,1)S(1)} %get-tuple-element.36.refs_1_, bf16[144,512]{1,0:T(8,128)(2,1)S(1)} %collective-permute-done.6.refs_2_, bf16[144,512]{1,0:T(8,128)(2,1)S(1)} %collective-permute-done.7.refs_3_, ...), custom_call_target="tpu_custom_call" | custom-call | bytes 10701000 | tf_op jit(solution)/shard_map/pallas_call | solution.py:499
  43.5 3.2 %shard_map.117 = (bf16[80,512]{1,0:T(8,128)(2,1)S(1)}, f32[1,256,512]{2,1,0:T(8,128)S(1)}, f32[1,32,512]{2,1,0:T(8,128)S(1)}) custom-call(s32[8]{0:T(128)S(1)} %concatenate.3.refs_0_, bf16[80,512]{1,0:T(8,128)(2,1)S(1)} %get-tuple-element.35.refs_1_, bf16[80,512]{1,0:T(8,128)(2,1)S(1)} %collective-permute-done.3.refs_2_, ...), custom_call_target="tpu_custom_call" | custom-call | bytes 11808000 | tf_op jit(solution)/shard_map/pallas_call | solution.py:499
  46.7 3.9 %collective-permute-start.11 = (bf16[80,512]{1,0:T(8,128)(2,1)S(1)}, bf16[80,512]{1,0:T(8,128)(2,1)S(1)}, u32[]{:S(2)}, u32[]{:S(2)}) collective-permute-start(bf16[80,512]{1,0:T(8,128)(2,1)S(1)} %get-tuple-element.41.refs_1_), channel_id=1, source_target_pairs={{0,24},{8,16},{16,8},{24,0},{1,25},{9,17},{17,9},{25,1},{2,26},{10... | collective-permute-start | bytes 245768 | tf_op jit(solution)/shard_map/ppermute | solution.py:83
  51.3 2.6 %shard_map.118 = (f32[4,8,512]{2,1,0:T(8,128)S(1)}, f32[4,8,512]{2,1,0:T(8,128)S(1)}) custom-call(s32[8]{0:T(128)S(1)} %concatenate.3.refs_0_, f32[1,12,40,512]{3,2,1,0:T(8,128)} %get-tuple-element.45.refs_1_, f32[1,256,512]{2,1,0:T(8,128)S(1)} %get-tuple-element.44.refs_2_.refs_9_.refs_1_, f32[1,32,512]{2,1,0:T(8,128)S(1)} %get-tuple-element.46.refs_3_), custom_call_target="tpu_custom_call" | custom-call | bytes 8856000 | tf_op jit(solution)/shard_map/pallas_call | solution.py:499
  53.9 2.1 %collective-permute-done.10.refs_3_ = bf16[80,512]{1,0:T(8,128)(2,1)S(1)} collective-permute-done((bf16[80,512]{1,0:T(8,128)(2,1)S(1)}, bf16[80,512]{1,0:T(8,128)(2,1)S(1)}, u32[]{:S(2)}, u32[]{:S(2)}) %collective-permute-start.10) | collective-permute-done | bytes 81952 | tf_op jit(solution)/shard_map/ppermute | solution.py:83
  56.0 3.2 %shard_map.119 = (f32[2,256,512]{2,1,0:T(8,128)S(1)}, f32[2,32,512]{2,1,0:T(8,128)S(1)}, bf16[272,512]{1,0:T(8,128)(2,1)S(1)}, bf16[272,512]{1,0:T(8,128)(2,1)S(1)}) custom-call(s32[8]{0:T(128)S(1)} %concatenate.3.refs_0_, bf16[80,512]{1,0:T(8,128)(2,1)S(1)} %get-tuple-element.41.refs_1_, bf16[80,512]{1,0:T(8,128)(2,1)S(1)} %collective-permute-done.9.refs_2_, ...), custom_call_target="tpu_custom_call" | custom-call | bytes 11808000 | tf_op jit(solution)/shard_map/pallas_call | solution.py:499
  59.2 2.4 %collective-permute-start.13 = (bf16[272,512]{1,0:T(8,128)(2,1)S(1)}, bf16[272,512]{1,0:T(8,128)(2,1)S(1)}, u32[]{:S(2)}, u32[]{:S(2)}) collective-permute-start(bf16[272,512]{1,0:T(8,128)(2,1)S(1)} %get-tuple-element.50), channel_id=1, source_target_pairs={{0,16},{8,24},{16,0},{24,8},{1,17},{9,25},{17,1},{25,9},{2,18},{10... | collective-permute-start | bytes 835592 | tf_op jit(solution)/shard_map/ppermute | solution.py:73
  61.6 4.5 %shard_map.120 = (f32[4,8,1024]{2,1,0:T(8,128)S(1)}, f32[4,8,1024]{2,1,0:T(8,128)S(1)}) custom-call(s32[8]{0:T(128)S(1)} %concatenate.3.refs_0_, f32[2,12,40,512]{3,2,1,0:T(8,128)} %get-tuple-element.51.refs_1_, f32[2,256,512]{2,1,0:T(8,128)S(1)} %get-tuple-element.48.refs_2_.refs_1_, f32[2,32,512]{2,1,0:T(8,128)S(1)} %get-tuple-element.52.refs_3_), custom_call_target="tpu_custom_call" | custom-call | bytes 17712000 | tf_op jit(solution)/shard_map/pallas_call | solution.py:499
  66.1 3.7 %collective-permute-done.13.refs_0_.refs_3_ = bf16[272,512]{1,0:T(8,128)(2,1)S(1)} collective-permute-done((bf16[272,512]{1,0:T(8,128)(2,1)S(1)}, bf16[272,512]{1,0:T(8,128)(2,1)S(1)}, u32[]{:S(2)}, u32[]{:S(2)}) %collective-permute-start.13) | collective-permute-done | bytes 278560 | tf_op jit(solution)/shard_map/ppermute | solution.py:73
  72.0 1.6 %collective-permute-start.17 = (f32[8,1536]{1,0:T(8,128)S(1)}, f32[8,1536]{1,0:T(8,128)S(1)}, u32[]{:S(2)}, u32[]{:S(2)}) collective-permute-start(f32[8,1536]{1,0:T(8,128)S(1)} %get-tuple-element.58), channel_id=1, source_target_pairs={{0,2},{1,3},{2,0},{3,1},{4,6},{5,7},{6,4},{7,5},{8,10},{9,11},{10,... | collective-permute-start | bytes 147464 | tf_op jit(solution)/shard_map/ppermute | solution.py:737
  73.5 1.5 %collective-permute-start.18 = (f32[8,1536]{1,0:T(8,128)S(1)}, f32[8,1536]{1,0:T(8,128)S(1)}, u32[]{:S(2)}, u32[]{:S(2)}) collective-permute-start(f32[8,1536]{1,0:T(8,128)S(1)} %get-tuple-element.59), channel_id=1, source_target_pairs={{0,4},{1,5},{2,6},{3,7},{4,0},{5,1},{6,2},{7,3},{8,12},{9,13},{10,... | collective-permute-start | bytes 147464 | tf_op jit(solution)/shard_map/ppermute | solution.py:737
  75.5 1.1 %collective-permute-done.14.refs_4_ = bf16[272,512]{1,0:T(8,128)(2,1)S(1)} collective-permute-done((bf16[272,512]{1,0:T(8,128)(2,1)S(1)}, bf16[272,512]{1,0:T(8,128)(2,1)S(1)}, u32[]{:S(2)}, u32[]{:S(2)}) %collective-permute-start.14) | collective-permute-done | bytes 278560 | tf_op jit(solution)/shard_map/ppermute | solution.py:77
  76.6 3.1 %shard_map.123.refs_7_.refs_4_ = bf16[1,1,8,32,1536]{4,3,2,1,0:T(8,128)(2,1)} custom-call(s32[8]{0:T(128)S(1)} %concatenate.3.refs_0_, f32[1,256,512]{2,1,0:T(8,128)S(1)} %get-tuple-element.44.refs_2_.refs_9_.refs_1_, bf16[272,512]{1,0:T(8,128)(2,1)S(1)} %collective-permute-done.12.refs_2_, bf16[272,512]{1,0:T(8,128)(2,1)S(1)} %collective-permute-done.13.refs_0_.refs_3_, ...), custom_call_target="tpu_custom_call" | custom-call | bytes 8856000 | tf_op jit(solution)/shard_map/pallas_call | solution.py:499
  80.1 3.5 %collective-permute-start.22 = (f32[8,1536]{1,0:T(8,128)S(1)}, f32[8,1536]{1,0:T(8,128)S(1)}, u32[]{:S(2)}, u32[]{:S(2)}) collective-permute-start(f32[8,1536]{1,0:T(8,128)S(1)} %shard_map.126.refs_0_), channel_id=1, source_target_pairs={{0,24},{8,16},{16,8},{24,0},{1,25},{9,17},{17,9},{25,1},{2,26},{10... | collective-permute-start | bytes 147464 | tf_op jit(solution)/shard_map/ppermute | solution.py:83
  84.5 1.5 %shard_map.122.refs_6_.refs_4_ = f32[2,256,512]{2,1,0:T(8,128)S(1)} custom-call(s32[8]{0:T(128)S(1)} %concatenate.3.refs_0_, bf16[272,512]{1,0:T(8,128)(2,1)S(1)} %get-tuple-element.49.refs_1_, bf16[272,512]{1,0:T(8,128)(2,1)S(1)} %collective-permute-done.12.refs_2_, bf16[272,512]{1,0:T(8,128)(2,1)S(1)} %collective-permute-done.13.refs_0_.refs_3_, ...), custom_call_target="tpu_custom_call" | custom-call | bytes 5535000 | tf_op jit(solution)/shard_map/pallas_call | solution.py:499
  86.1 2.5 %collective-permute-done.21.refs_2_ = f32[8,1536]{1,0:T(8,128)S(1)} collective-permute-done((f32[8,1536]{1,0:T(8,128)S(1)}, f32[8,1536]{1,0:T(8,128)S(1)}, u32[]{:S(2)}, u32[]{:S(2)}) %collective-permute-start.21) | collective-permute-done | bytes 49184 | tf_op jit(solution)/shard_map/ppermute | solution.py:83
  88.6 1.4 %collective-permute-start.25 = (f32[8,1536]{1,0:T(8,128)S(1)}, f32[8,1536]{1,0:T(8,128)S(1)}, u32[]{:S(2)}, u32[]{:S(2)}) collective-permute-start(f32[8,1536]{1,0:T(8,128)S(1)} %shard_map.127.refs_1_), channel_id=1, source_target_pairs={{0,6},{1,7},{2,4},{3,5},{4,2},{5,3},{6,0},{7,1},{8,14},{9,15},{10,... | collective-permute-start | bytes 147464 | tf_op jit(solution)/shard_map/ppermute | solution.py:83
  90.7 1.5 %collective-permute-start.23 = (f32[8,1536]{1,0:T(8,128)S(1)}, f32[8,1536]{1,0:T(8,128)S(1)}, u32[]{:S(2)}, u32[]{:S(2)}) collective-permute-start(f32[8,1536]{1,0:T(8,128)S(1)} %shard_map.127.refs_1_), channel_id=1, source_target_pairs={{0,2},{1,3},{2,0},{3,1},{4,6},{5,7},{6,4},{7,5},{8,10},{9,11},{10,... | collective-permute-start | bytes 147464 | tf_op jit(solution)/shard_map/ppermute | solution.py:83
  92.2 4.5 %shard_map.124.refs_5_ = bf16[1,1,8,32,1536]{4,3,2,1,0:T(8,128)(2,1)} custom-call(s32[8]{0:T(128)S(1)} %concatenate.3.refs_0_, f32[2,256,512]{2,1,0:T(8,128)S(1)} %get-tuple-element.48.refs_2_.refs_1_, bf16[272,512]{1,0:T(8,128)(2,1)S(1)} %collective-permute-done.12.refs_2_, ...), custom_call_target="tpu_custom_call", output_to_operand_aliasing={{}: (7, {})} | custom-call | bytes 17712000 | tf_op jit(solution)/shard_map/pallas_call | solution.py:499
  97.3 1.4 %collective-permute-done.26.refs_2_ = f32[4,8,1536]{2,1,0:T(8,128)S(1)} collective-permute-done((f32[4,8,1536]{2,1,0:T(8,128)S(1)}, f32[4,8,1536]{2,1,0:T(8,128)S(1)}, u32[]{:S(2)}, u32[]{:S(2)}) %collective-permute-start.26) | collective-permute-done | bytes 196640 | tf_op jit(solution)/shard_map/ppermute | solution.py:83
  98.7 1.3 %shard_map.129 = (f32[25,1536]{1,0:T(8,128)}, f32[32,1536]{1,0:T(8,128)}) custom-call(s32[8]{0:T(128)S(1)} %concatenate.3.refs_0_, f32[4,8,1536]{2,1,0:T(8,128)S(1)} %shard_map.128.refs_1_, f32[4,8,1536]{2,1,0:T(8,128)S(1)} %collective-permute-done.26.refs_2_), custom_call_target="tpu_custom_call" | custom-call | bytes 2952000 | tf_op jit(solution)/shard_map/pallas_call | solution.py:499
  (45 shorter events, 8.1 us)
Async XLA Ops:
  3.3 18.3 %copy-start = (f32[32,1536]{1,0:T(8,128)S(1)}, f32[32,1536]{1,0:T(8,128)}, u32[]{:S(2)}) copy-start(f32[32,1536]{1,0:T(8,128)} %refs_8_.3) | copy-start | bytes 589828
  3.3 18.3 %copy-start.1 = (f32[25,1536]{1,0:T(8,128)S(1)}, f32[25,1536]{1,0:T(8,128)}, u32[]{:S(2)}) copy-start(f32[25,1536]{1,0:T(8,128)} %refs_5_.11) | copy-start | bytes 460804
  4.5 8.4 %collective-permute-start = (bf16[2,64,512]{2,1,0:T(8,128)(2,1)S(1)}, bf16[2,64,512]{2,1,0:T(8,128)(2,1)S(1)}, u32[]{:S(2)}, u32[]{:S(2)}) collective-permute-start(bf16[2,64,512]{2,1,0:T(8,128)(2,1)S(1)} %get-tuple-element.33), channel_id=1, source_target_pairs={{0,8},{8,0},{16,24},{24,16},{1,9},{9,1},{17,25},{25,17},{2,10},{10... | collective-permute-start | bytes 393224 | tf_op jit(solution)/shard_map/ppermute | solution.py:73
  7.6 8.7 %collective-permute-start.1 = (bf16[2,64,512]{2,1,0:T(8,128)(2,1)S(1)}, bf16[2,64,512]{2,1,0:T(8,128)(2,1)S(1)}, u32[]{:S(2)}, u32[]{:S(2)}) collective-permute-start(bf16[2,64,512]{2,1,0:T(8,128)(2,1)S(1)} %get-tuple-element.34), channel_id=1, source_target_pairs={{0,16},{8,24},{16,0},{24,8},{1,17},{9,25},{17,1},{25,9},{2,18},{10... | collective-permute-start | bytes 393224 | tf_op jit(solution)/shard_map/ppermute | solution.py:73
  14.4 21.8 %collective-permute-start.6 = (bf16[144,512]{1,0:T(8,128)(2,1)S(1)}, bf16[144,512]{1,0:T(8,128)(2,1)S(1)}, u32[]{:S(2)}, u32[]{:S(2)}) collective-permute-start(bf16[144,512]{1,0:T(8,128)(2,1)S(1)} %get-tuple-element.36.refs_1_), channel_id=1, source_target_pairs={{0,8},{8,0},{16,24},{24,16},{1,9},{9,1},{17,25},{25,17},{2,10},{10... | collective-permute-start | bytes 442376 | tf_op jit(solution)/shard_map/ppermute | solution.py:73
  16.3 5.3 %collective-permute-start.2 = (bf16[2,64,512]{2,1,0:T(8,128)(2,1)S(1)}, bf16[2,64,512]{2,1,0:T(8,128)(2,1)S(1)}, u32[]{:S(2)}, u32[]{:S(2)}) collective-permute-start(bf16[2,64,512]{2,1,0:T(8,128)(2,1)S(1)} %collective-permute-done.1.refs_3_), channel_id=1, source_target_pairs={{0,8},{8,0},{16,24},{24,16},{1,9},{9,1},{17,25},{25,17},{2,10},{10... | collective-permute-start | bytes 393224 | tf_op jit(solution)/shard_map/ppermute | solution.py:77
  16.8 20.1 %collective-permute-start.8 = (bf16[144,512]{1,0:T(8,128)(2,1)S(1)}, bf16[144,512]{1,0:T(8,128)(2,1)S(1)}, u32[]{:S(2)}, u32[]{:S(2)}) collective-permute-start(bf16[144,512]{1,0:T(8,128)(2,1)S(1)} %get-tuple-element.37), channel_id=1, source_target_pairs={{0,24},{8,16},{16,8},{24,0},{1,25},{9,17},{17,9},{25,1},{2,26},{10... | collective-permute-start | bytes 442376 | tf_op jit(solution)/shard_map/ppermute | solution.py:76
  20.0 16.8 %collective-permute-start.7 = (bf16[144,512]{1,0:T(8,128)(2,1)S(1)}, bf16[144,512]{1,0:T(8,128)(2,1)S(1)}, u32[]{:S(2)}, u32[]{:S(2)}) collective-permute-start(bf16[144,512]{1,0:T(8,128)(2,1)S(1)} %get-tuple-element.37), channel_id=1, source_target_pairs={{0,16},{8,24},{16,0},{24,8},{1,17},{9,25},{17,1},{25,9},{2,18},{10... | collective-permute-start | bytes 442376 | tf_op jit(solution)/shard_map/ppermute | solution.py:73
  28.3 15.2 %collective-permute-start.5 = (bf16[80,512]{1,0:T(8,128)(2,1)S(1)}, bf16[80,512]{1,0:T(8,128)(2,1)S(1)}, u32[]{:S(2)}, u32[]{:S(2)}) collective-permute-start(bf16[80,512]{1,0:T(8,128)(2,1)S(1)} %get-tuple-element.35.refs_1_), channel_id=1, source_target_pairs={{0,24},{8,16},{16,8},{24,0},{1,25},{9,17},{17,9},{25,1},{2,26},{10... | collective-permute-start | bytes 245768 | tf_op jit(solution)/shard_map/ppermute | solution.py:83
  36.3 7.3 %collective-permute-start.4 = (bf16[80,512]{1,0:T(8,128)(2,1)S(1)}, bf16[80,512]{1,0:T(8,128)(2,1)S(1)}, u32[]{:S(2)}, u32[]{:S(2)}) collective-permute-start(bf16[80,512]{1,0:T(8,128)(2,1)S(1)} %get-tuple-element.35.refs_1_), channel_id=1, source_target_pairs={{0,16},{8,24},{16,0},{24,8},{1,17},{9,25},{17,1},{25,9},{2,18},{10... | collective-permute-start | bytes 245768 | tf_op jit(solution)/shard_map/ppermute | solution.py:83
  36.3 7.3 %collective-permute-start.3 = (bf16[80,512]{1,0:T(8,128)(2,1)S(1)}, bf16[80,512]{1,0:T(8,128)(2,1)S(1)}, u32[]{:S(2)}, u32[]{:S(2)}) collective-permute-start(bf16[80,512]{1,0:T(8,128)(2,1)S(1)} %get-tuple-element.35.refs_1_), channel_id=1, source_target_pairs={{0,8},{8,0},{16,24},{24,16},{1,9},{9,1},{17,25},{25,17},{2,10},{10... | collective-permute-start | bytes 245768 | tf_op jit(solution)/shard_map/ppermute | solution.py:83
  46.7 7.1 %collective-permute-start.11 = (bf16[80,512]{1,0:T(8,128)(2,1)S(1)}, bf16[80,512]{1,0:T(8,128)(2,1)S(1)}, u32[]{:S(2)}, u32[]{:S(2)}) collective-permute-start(bf16[80,512]{1,0:T(8,128)(2,1)S(1)} %get-tuple-element.41.refs_1_), channel_id=1, source_target_pairs={{0,24},{8,16},{16,8},{24,0},{1,25},{9,17},{17,9},{25,1},{2,26},{10... | collective-permute-start | bytes 245768 | tf_op jit(solution)/shard_map/ppermute | solution.py:83
  50.6 5.3 %collective-permute-start.10 = (bf16[80,512]{1,0:T(8,128)(2,1)S(1)}, bf16[80,512]{1,0:T(8,128)(2,1)S(1)}, u32[]{:S(2)}, u32[]{:S(2)}) collective-permute-start(bf16[80,512]{1,0:T(8,128)(2,1)S(1)} %get-tuple-element.41.refs_1_), channel_id=1, source_target_pairs={{0,16},{8,24},{16,0},{24,8},{1,17},{9,25},{17,1},{25,9},{2,18},{10... | collective-permute-start | bytes 245768 | tf_op jit(solution)/shard_map/ppermute | solution.py:83
  50.6 5.3 %collective-permute-start.9 = (bf16[80,512]{1,0:T(8,128)(2,1)S(1)}, bf16[80,512]{1,0:T(8,128)(2,1)S(1)}, u32[]{:S(2)}, u32[]{:S(2)}) collective-permute-start(bf16[80,512]{1,0:T(8,128)(2,1)S(1)} %get-tuple-element.41.refs_1_), channel_id=1, source_target_pairs={{0,8},{8,0},{16,24},{24,16},{1,9},{9,1},{17,25},{25,17},{2,10},{10... | collective-permute-start | bytes 245768 | tf_op jit(solution)/shard_map/ppermute | solution.py:83
  59.2 10.6 %collective-permute-start.13 = (bf16[272,512]{1,0:T(8,128)(2,1)S(1)}, bf16[272,512]{1,0:T(8,128)(2,1)S(1)}, u32[]{:S(2)}, u32[]{:S(2)}) collective-permute-start(bf16[272,512]{1,0:T(8,128)(2,1)S(1)} %get-tuple-element.50), channel_id=1, source_target_pairs={{0,16},{8,24},{16,0},{24,8},{1,17},{9,25},{17,1},{25,9},{2,18},{10... | collective-permute-start | bytes 835592 | tf_op jit(solution)/shard_map/ppermute | solution.py:73
  61.6 14.0 %collective-permute-start.12 = (bf16[272,512]{1,0:T(8,128)(2,1)S(1)}, bf16[272,512]{1,0:T(8,128)(2,1)S(1)}, u32[]{:S(2)}, u32[]{:S(2)}) collective-permute-start(bf16[272,512]{1,0:T(8,128)(2,1)S(1)} %get-tuple-element.49.refs_1_), channel_id=1, source_target_pairs={{0,8},{8,0},{16,24},{24,16},{1,9},{9,1},{17,25},{25,17},{2,10},{10... | collective-permute-start | bytes 835592 | tf_op jit(solution)/shard_map/ppermute | solution.py:73
  69.8 6.8 %collective-permute-start.14 = (bf16[272,512]{1,0:T(8,128)(2,1)S(1)}, bf16[272,512]{1,0:T(8,128)(2,1)S(1)}, u32[]{:S(2)}, u32[]{:S(2)}) collective-permute-start(bf16[272,512]{1,0:T(8,128)(2,1)S(1)} %shard_map.121), channel_id=1, source_target_pairs={{0,8},{8,0},{16,24},{24,16},{1,9},{9,1},{17,25},{25,17},{2,10},{10... | collective-permute-start | bytes 835592 | tf_op jit(solution)/shard_map/ppermute | solution.py:77
  69.9 1.5 %collective-permute-start.16 = (f32[4,8,1024]{2,1,0:T(8,128)S(1)}, f32[4,8,1024]{2,1,0:T(8,128)S(1)}, u32[]{:S(2)}, u32[]{:S(2)}) collective-permute-start(f32[4,8,1024]{2,1,0:T(8,128)S(1)} %get-tuple-element.53.refs_1_), channel_id=1, source_target_pairs={{0,1},{1,0},{2,3},{3,2},{4,5},{5,4},{6,7},{7,6},{8,9},{9,8},{10,11... | collective-permute-start | bytes 393224 | tf_op jit(solution)/shard_map/ppermute | solution.py:83
  70.0 1.4 %collective-permute-start.15 = (f32[4,8,512]{2,1,0:T(8,128)S(1)}, f32[4,8,512]{2,1,0:T(8,128)S(1)}, u32[]{:S(2)}, u32[]{:S(2)}) collective-permute-start(f32[4,8,512]{2,1,0:T(8,128)S(1)} %get-tuple-element.47.refs_11_), channel_id=1, source_target_pairs={{0,1},{1,0},{2,3},{3,2},{4,5},{5,4},{6,7},{7,6},{8,9},{9,8},{10,11... | collective-permute-start | bytes 196616 | tf_op jit(solution)/shard_map/ppermute | solution.py:83
  72.0 7.8 %collective-permute-start.17 = (f32[8,1536]{1,0:T(8,128)S(1)}, f32[8,1536]{1,0:T(8,128)S(1)}, u32[]{:S(2)}, u32[]{:S(2)}) collective-permute-start(f32[8,1536]{1,0:T(8,128)S(1)} %get-tuple-element.58), channel_id=1, source_target_pairs={{0,2},{1,3},{2,0},{3,1},{4,6},{5,7},{6,4},{7,5},{8,10},{9,11},{10,... | collective-permute-start | bytes 147464 | tf_op jit(solution)/shard_map/ppermute | solution.py:737
  73.5 6.2 %collective-permute-start.18 = (f32[8,1536]{1,0:T(8,128)S(1)}, f32[8,1536]{1,0:T(8,128)S(1)}, u32[]{:S(2)}, u32[]{:S(2)}) collective-permute-start(f32[8,1536]{1,0:T(8,128)S(1)} %get-tuple-element.59), channel_id=1, source_target_pairs={{0,4},{1,5},{2,6},{3,7},{4,0},{5,1},{6,2},{7,3},{8,12},{9,13},{10,... | collective-permute-start | bytes 147464 | tf_op jit(solution)/shard_map/ppermute | solution.py:737
  75.1 5.0 %collective-permute-start.19 = (f32[8,1536]{1,0:T(8,128)S(1)}, f32[8,1536]{1,0:T(8,128)S(1)}, u32[]{:S(2)}, u32[]{:S(2)}) collective-permute-start(f32[8,1536]{1,0:T(8,128)S(1)} %get-tuple-element.60), channel_id=1, source_target_pairs={{0,6},{1,7},{2,4},{3,5},{4,2},{5,3},{6,0},{7,1},{8,14},{9,15},{10,... | collective-permute-start | bytes 147464 | tf_op jit(solution)/shard_map/ppermute | solution.py:737
  80.1 6.1 %collective-permute-start.22 = (f32[8,1536]{1,0:T(8,128)S(1)}, f32[8,1536]{1,0:T(8,128)S(1)}, u32[]{:S(2)}, u32[]{:S(2)}) collective-permute-start(f32[8,1536]{1,0:T(8,128)S(1)} %shard_map.126.refs_0_), channel_id=1, source_target_pairs={{0,24},{8,16},{16,8},{24,0},{1,25},{9,17},{17,9},{25,1},{2,26},{10... | collective-permute-start | bytes 147464 | tf_op jit(solution)/shard_map/ppermute | solution.py:83
  83.6 5.0 %collective-permute-start.21 = (f32[8,1536]{1,0:T(8,128)S(1)}, f32[8,1536]{1,0:T(8,128)S(1)}, u32[]{:S(2)}, u32[]{:S(2)}) collective-permute-start(f32[8,1536]{1,0:T(8,128)S(1)} %shard_map.126.refs_0_), channel_id=1, source_target_pairs={{0,16},{8,24},{16,0},{24,8},{1,17},{9,25},{17,1},{25,9},{2,18},{10... | collective-permute-start | bytes 147464 | tf_op jit(solution)/shard_map/ppermute | solution.py:83
  83.6 5.0 %collective-permute-start.20 = (f32[8,1536]{1,0:T(8,128)S(1)}, f32[8,1536]{1,0:T(8,128)S(1)}, u32[]{:S(2)}, u32[]{:S(2)}) collective-permute-start(f32[8,1536]{1,0:T(8,128)S(1)} %shard_map.126.refs_0_), channel_id=1, source_target_pairs={{0,8},{8,0},{16,24},{24,16},{1,9},{9,1},{17,25},{25,17},{2,10},{10... | collective-permute-start | bytes 147464 | tf_op jit(solution)/shard_map/ppermute | solution.py:83
  88.6 8.0 %collective-permute-start.25 = (f32[8,1536]{1,0:T(8,128)S(1)}, f32[8,1536]{1,0:T(8,128)S(1)}, u32[]{:S(2)}, u32[]{:S(2)}) collective-permute-start(f32[8,1536]{1,0:T(8,128)S(1)} %shard_map.127.refs_1_), channel_id=1, source_target_pairs={{0,6},{1,7},{2,4},{3,5},{4,2},{5,3},{6,0},{7,1},{8,14},{9,15},{10,... | collective-permute-start | bytes 147464 | tf_op jit(solution)/shard_map/ppermute | solution.py:83
  90.1 6.6 %collective-permute-start.24 = (f32[8,1536]{1,0:T(8,128)S(1)}, f32[8,1536]{1,0:T(8,128)S(1)}, u32[]{:S(2)}, u32[]{:S(2)}) collective-permute-start(f32[8,1536]{1,0:T(8,128)S(1)} %shard_map.127.refs_1_), channel_id=1, source_target_pairs={{0,4},{1,5},{2,6},{3,7},{4,0},{5,1},{6,2},{7,3},{8,12},{9,13},{10,... | collective-permute-start | bytes 147464 | tf_op jit(solution)/shard_map/ppermute | solution.py:83
  90.7 6.0 %collective-permute-start.23 = (f32[8,1536]{1,0:T(8,128)S(1)}, f32[8,1536]{1,0:T(8,128)S(1)}, u32[]{:S(2)}, u32[]{:S(2)}) collective-permute-start(f32[8,1536]{1,0:T(8,128)S(1)} %shard_map.127.refs_1_), channel_id=1, source_target_pairs={{0,2},{1,3},{2,0},{3,1},{4,6},{5,7},{6,4},{7,5},{8,10},{9,11},{10,... | collective-permute-start | bytes 147464 | tf_op jit(solution)/shard_map/ppermute | solution.py:83
  97.2 1.5 %collective-permute-start.26 = (f32[4,8,1536]{2,1,0:T(8,128)S(1)}, f32[4,8,1536]{2,1,0:T(8,128)S(1)}, u32[]{:S(2)}, u32[]{:S(2)}) collective-permute-start(f32[4,8,1536]{2,1,0:T(8,128)S(1)} %shard_map.128.refs_1_), channel_id=1, source_target_pairs={{0,1},{1,0},{2,3},{3,2},{4,5},{5,4},{6,7},{7,6},{8,9},{9,8},{10,11... | collective-permute-start | bytes 589832 | tf_op jit(solution)/shard_map/ppermute | solution.py:83

commit v4 on v3

v4 whole, which is shorter than its diff:
```python
import functools
import math

import jax
import jax.numpy as jnp
from jax import lax
from jax.experimental import pallas as pl
from jax.experimental.pallas import tpu as pltpu
from jax.sharding import PartitionSpec as P

EPSILON = 1e-06
LANES = 256
REACH = 2
EDGE = 8
BYTES_PER_US = 3_690_000
BF16 = jnp.bfloat16
F32 = jnp.float32
PARAMS = pltpu.CompilerParams(vmem_limit_bytes=16 * 1024 * 1024)


class Place:
    def __init__(self, info_ref):
        slots = (info_ref.shape[0] - 4) // 2
        slot = info_ref[0]
        tall = wide = start = jnp.int32(0)
        for s in range(slots):
            tall_s, wide_s = info_ref[4 + s], info_ref[4 + slots + s]
            tall = jnp.where(slot == s, tall_s, tall)
            wide = jnp.where(slot == s, wide_s, wide)
            start = start + jnp.where(s < slot, tall_s * wide_s, 0)
        self.live = slot < slots
        self.tall, self.wide = tall, wide
        self.row, self.col = info_ref[1], info_ref[2]
        self.group = info_ref[3]
        self.within = self.row * wide + self.col
        self.index = start + self.within
        self.above = self.live & (self.row > 0)
        self.below = self.live & (self.row < tall - 1)

    def same_image(self, delta):
        other = self.within + delta
        return self.live & (other >= 0) & (other < self.tall * self.wide)


class Routes:
    def __init__(self, count):
        self.count = count
        self.relayed = count == 4
        self.shifts = [k for k in (1, -1, 2, -2, 3, -3) if abs(k) < count]
        self.sent = 2 if self.relayed else len(self.shifts)
        self.arriving = 3 if self.relayed else len(self.shifts)

    def targets(self, place, direct=False):
        if not self.relayed:
            return [jnp.int32(k) for k in self.shifts]
        near, far, last = ((place.index ^ m) - place.index for m in (1, 2, 3))
        if direct:
            return [near, far, last, last]
        return [near, jnp.where(place.same_image(far), far, last)]

    def sources(self, place, direct=False):
        if not self.relayed:
            return [jnp.int32(-k) for k in self.shifts]
        near, far, last = ((place.index ^ m) - place.index for m in (1, 2, 3))
        if direct:
            outer = jnp.abs(last) == 3
            return [near, far, jnp.where(outer, 0, last), jnp.where(outer, last, 0)]
        return [near, far, last]

    def direct_rows(self, edge):
        return [edge, edge, edge, REACH * EDGE] if self.relayed else [edge] * self.sent

    def move(self, sent, hand_on=lambda near, far: far):
        count = self.count
        if not self.relayed:
            return [
                lax.ppermute(part, "tile", [(s, s + k) for s in range(max(0, -k), min(count, count - k))])
                for part, k in zip(sent, self.shifts)
            ]
        near, far = (
            lax.ppermute(part, "tile", [(s, s ^ m) for s in range(count)]) for part, m in zip(sent, (1, 2))
        )
        return [near, far, lax.ppermute(hand_on(near, far), "tile", [(s, s ^ 1) for s in range(count)])]

    def move_direct(self, sent):
        if not self.relayed:
            return self.move(sent)
        targets = ((1, 0, 3, 2), (2, 3, 0, 1), (0, 2, 1, 3), (3, 1, 2, 0))
        return [lax.ppermute(part, "tile", list(enumerate(to))) for part, to in zip(sent, targets)]


def exchange(value, axis, masks=None):
    count = lax.axis_size(axis)
    masks = range(1, count) if masks is None else masks
    return [lax.ppermute(value, axis, [(s, s ^ m) for s in range(count)]) for m in masks]


def split(x):
    high = x.astype(BF16)
    return high, (x - high.astype(F32)).astype(BF16)


def contract(a, b, dims):
    return lax.dot_general(a, b, (dims, ((), ())), preferred_element_type=F32)


NN = ((1,), (0,))
NT = ((1,), (1,))
TN = ((0,), (0,))


def dot(a, b, dims):
    total = contract(a[0], b[0], dims)
    if b[1] is not None:
        total = total + contract(a[0], b[1], dims)
    if a[1] is not None:
        total = total + contract(a[1], b[0], dims)
    return total


def exact(x):
    return x.astype(BF16), None


def same_head(head_dim):
    rows = lax.broadcasted_iota(jnp.int32, (LANES, LANES), 0) // head_dim
    cols = lax.broadcasted_iota(jnp.int32, (LANES, LANES), 1) // head_dim
    return rows == cols


def spread(compact, mask):
    tall = jnp.concatenate([compact] * (LANES // compact.shape[0]), axis=0)
    return jnp.where(mask, tall, 0.0)


def gather_blocks(full, mask, head_dim):
    kept = jnp.where(mask, full, 0.0)
    return jnp.sum(kept.reshape(LANES // head_dim, head_dim, LANES), axis=0)


def payload(field, place, delta):
    tall, broad, lanes = field.shape
    size = REACH * broad
    top = field[:REACH].reshape(size, lanes)
    bottom = field[tall - REACH :].reshape(size, lanes)
    left = field[:, :EDGE].reshape(size, lanes)
    right = field[:, broad - EDGE :].reshape(size, lanes)
    rows = jnp.where(delta > 0, bottom, top)
    cols = jnp.where(place.col == 0, right, left)
    beside = (place.wide == 2) & (delta == jnp.where(place.col == 0, 1, -1))
    return jnp.where(beside, cols, rows)


def lanes_at(block):
    start = block * LANES
    return pl.ds(start if isinstance(start, int) else pl.multiple_of(start, LANES), LANES)


def pack_state(state, total):
    rows = jnp.concatenate([state, total, jnp.zeros((7, state.shape[1]), F32)], axis=0)
    return jnp.concatenate(split(rows), axis=0)


def unpack_state(ref, offset):
    rows = ref[offset:].astype(F32)
    half = rows.shape[0] // 2
    return rows[:half] + rows[half:]


def total_state(own_ref, others, place, offset, others_offset):
    total = unpack_state(own_ref, offset)
    for m, other in enumerate(others, 1):
        delta = (place.index ^ m) - place.index
        total = total + jnp.where(place.same_image(delta), unpack_state(other, others_offset), 0.0)
    return total


def corner_payload(field, delta):
    tall, broad, lanes = field.shape
    corner = jnp.where(delta > 0, field[tall - REACH :, broad - EDGE :], field[:REACH, :EDGE])
    return corner.reshape(REACH * EDGE, lanes)


def fill_padded(pad_ref, field, arrived, deltas, place):
    tall, broad, lanes = field.shape
    two = place.live & (place.wide == 2)
    one = place.live & (place.wide == 1)
    first, second = two & (place.col == 0), two & (place.col == 1)

    def choose(condition, value, other):
        return jnp.where(condition, value, other)

    above = below = jnp.zeros((REACH, broad, lanes), F32)
    above_side = below_side = jnp.zeros((REACH, EDGE, lanes), F32)
    side = jnp.zeros((tall, EDGE, lanes), F32)
    for edges, delta in zip(arrived, deltas):
        edges = edges.astype(F32)
        if edges.shape[0] == REACH * EDGE:
            corner = edges.reshape(REACH, EDGE, lanes)
            above_side = choose(second & (delta == -3), corner, above_side)
            below_side = choose(first & (delta == 3), corner, below_side)
            continue
        rows, cols = edges.reshape(REACH, broad, lanes), edges.reshape(tall, EDGE, lanes)
        begin, end = rows[:, :EDGE], rows[:, broad - EDGE :]
        above = choose((one & (delta == -1)) | (two & (delta == -2)), rows, above)
        below = choose((one & (delta == 1)) | (two & (delta == 2)), rows, below)
        side = choose((first & (delta == 1)) | (second & (delta == -1)), cols, side)
        above_side = choose(first & (delta == -1), begin, choose(second & (delta == -3), end, above_side))
        below_side = choose(second & (delta == 1), end, choose(first & (delta == 3), begin, below_side))
    column = lax.broadcasted_iota(jnp.int32, (1, EDGE, lanes), 1)
    reached = (first & (column < REACH)) | (second & (column >= EDGE - REACH))
    upper, lower = slice(0, REACH), slice(REACH + tall, 2 * REACH + tall)
    pad_ref[upper, :broad] = choose(place.above, above, 0.0)
    pad_ref[lower, :broad] = choose(place.below, below, 0.0)
    pad_ref[upper, broad:] = choose(reached & place.above, above_side, 0.0)
    pad_ref[lower, broad:] = choose(reached & place.below, below_side, 0.0)
    pad_ref[REACH : REACH + tall, broad:] = choose(reached, side, 0.0)
    pad_ref[REACH : REACH + tall, :broad] = field


def convolve(pad_ref, kernel_ref, mix_ref, flipped):
    taps = 2 * REACH + 1
    tall, broad, lanes = mix_ref.shape
    ring = broad + EDGE
    sub = 128
    for start in range(0, lanes, sub):
        at = slice(start, start + sub)
        for y in range(tall):
            rows = [pad_ref[y + a, :, at] for a in range(taps)]
            total = None
            for b in range(taps):
                part = None
                for a in range(taps):
                    tap = taps * a + b
                    if flipped:
                        tap = taps * taps - 1 - tap
                    term = rows[a] * kernel_ref[tap : tap + 1, at]
                    part = term if part is None else part + term
                if b != REACH:
                    part = pltpu.roll(part, (REACH - b) % ring, 0)
                total = part[:broad] if total is None else total + part[:broad]
            mix_ref[y, :, at] = total


def read_field(ref, place, at=slice(None)):
    return jnp.where(place.live, ref[0, 0, :, :, at].astype(F32), 0.0)


def outgoing_kernel(routes, layout, key_ref, value_ref, *outs):
    place = Place(layout)
    for member, field_ref in enumerate((key_ref, value_ref)):
        field = field_ref[0, 0].astype(F32)
        for delta, out_ref in zip(routes.targets(place, True), outs):
            full = out_ref.shape[1] == REACH * field.shape[1]
            sent = payload(field, place, delta) if full else corner_payload(field, delta)
            out_ref[member] = sent.astype(BF16)


def thirds(ref, at):
    third = ref.shape[4] // 3
    return [slice(member * third + at.start, member * third + at.stop) for member in range(3)]


def source_state_kernel(routes, head_dim, layout, field_ref, *refs):
    weight_refs, outs, held, sems = refs[:2], refs[2:-3], refs[-3:-1], refs[-1]
    loads = [pltpu.make_async_copy(a, b, sems.at[i]) for i, (a, b) in enumerate(zip(weight_refs, held))]
    for load in loads:
        load.start()
    place = Place(layout)
    mask = same_head(head_dim)
    size = REACH * field_ref.shape[3]
    for at in parts_of(outs[0].shape[1]):
        query_at, key_at, value_at = thirds(field_ref, at)
        field = field_ref[0, 0, :, :, query_at].astype(F32)
        keys = jnp.maximum(read_field(field_ref, place, key_at).reshape(-1, LANES), 0.0)
        values = read_field(field_ref, place, value_at).reshape(-1, LANES)
        state = gather_blocks(contract(keys.astype(BF16), values.astype(BF16), TN), mask, head_dim)
        packed = pack_state(state, jnp.sum(keys, axis=0, keepdims=True))
        for delta, out_ref in zip(routes.targets(place), outs):
            out_ref[:size, at] = payload(field, place, delta).astype(BF16)
            out_ref[size:, at] = packed
    for load in loads:
        load.wait()


def forward_kernel(routes, first, count, head_dim, direct, *refs):
    layout, field_ref = refs[:2]
    place = Place(layout)
    deltas = routes.sources(place, direct)
    arrived, refs = refs[2 : 2 + len(deltas)], refs[2 + len(deltas) :]
    dw_ref, pw_ref, mixed_ref, merged_ref, padded_ref = refs[:5]
    mix_ref = refs[-1]
    mask = same_head(head_dim)
    per = mixed_ref.shape[2] // LANES
    size = REACH * field_ref.shape[3]

    def one_block(block, carry):
        at, member, within = lanes_at(first * per + block), block // per, lanes_at(block % per)
        field = read_field(field_ref, place, at)
        if len(arrived[0].shape) == 3:
            edges = [ref[member, :, within] for ref in arrived]
        else:
            edges = [ref[:size, within] for ref in arrived]
        padded = padded_ref.at[member, :, :, within]
        fill_padded(padded, field, edges, deltas, place)
        convolve(padded, dw_ref.at[:, at], mix_ref, False)
        mixed = mix_ref[...].reshape(-1, LANES)
        mixed_ref[member, :, within] = mixed
        merged_ref[member, :, within] = dot(split(mixed), split(spread(pw_ref[:, at], mask)), NN)
        return carry

    lax.fori_loop(0, count * per, one_block, 0)
    if first == 0:
        return
    state_ref = refs[-2]
    for at in parts_of(state_ref.shape[1]):
        keys = jnp.maximum(merged_ref[0, :, at], 0.0)
        state = gather_blocks(dot(split(keys), split(merged_ref[1, :, at]), TN), mask, head_dim)
        state_ref[:, at] = pack_state(state, jnp.sum(keys, axis=0, keepdims=True))


def parts_of(lanes):
    return [slice(start, start + LANES) for start in range(0, lanes, LANES)]


def query_gradients(raw, exactly, total, cot, head_dim, mask):
    ones = (mask.astype(BF16), None)
    query = jnp.maximum(raw, 0.0)
    pair = exact(query) if exactly else split(query)
    state = split(spread(total[:head_dim], mask))
    key_sum = total[head_dim : head_dim + 1]
    over = 1.0 / (dot(split(query * key_sum), ones, NN) + EPSILON)
    result = dot(pair, state, NN) * over
    grad_num = cot * over
    grad_den = -dot(split(cot * result), ones, NN) * over
    num_pair = split(grad_num)
    grad = jnp.where(raw > 0, dot(num_pair, state, NT) + grad_den * key_sum, 0.0)
    gstate = gather_blocks(dot(pair, num_pair, TN), mask, head_dim)
    return grad, pack_state(gstate, jnp.sum(query * grad_den, axis=0, keepdims=True))


def source_query_kernel(others, offset, others_offset, head_dim, *refs):
    layout, own_ref, received = refs[0], refs[1], refs[2 : 2 + others]
    source_ref, cot_ref, grad_ref, gstate_ref = refs[2 + others :]
    place = Place(layout)
    mask = same_head(head_dim)
    total = total_state(own_ref, received, place, offset, others_offset)
    for at in parts_of(gstate_ref.shape[1]):
        raw = read_field(source_ref, place, at).reshape(-1, LANES)
        cot = cot_ref[0, 0, :, :, at].astype(F32).reshape(raw.shape)
        grad_ref[0, :, at], gstate_ref[:, at] = query_gradients(raw, True, total[:, at], cot, head_dim, mask)


def merged_query_kernel(others, head_dim, *refs):
    layout, own_ref, received = refs[0], refs[1], refs[2 : 2 + others]
    merged_ref, mixed_ref, cot_ref, pw_ref, gstate_ref, gmix_ref, gpw_ref = refs[2 + others :]
    place = Place(layout)
    mask = same_head(head_dim)
    total = total_state(own_ref, received, place, 0, 0)
    third = gstate_ref.shape[1]
    for at in parts_of(third):
        raw = merged_ref[0, :, at]
        cot = cot_ref[0, 0, :, :, third + at.start : third + at.stop].astype(F32).reshape(raw.shape)
        grad, gstate_ref[:, at] = query_gradients(raw, False, total[:, at], cot, head_dim, mask)
        pair = split(grad)
        gmix_ref[0, :, at] = dot(pair, split(spread(pw_ref[:, at], mask)), NT)
        gpw_ref[0, :, at] = gather_blocks(dot(split(mixed_ref[0, :, at]), pair, TN), mask, head_dim)


def key_gradients(raw, key_pair, value_pair, total, head_dim, mask):
    gstate = split(spread(total[:head_dim], mask))
    gsum = total[head_dim : head_dim + 1]
    grad_keys = jnp.where(raw > 0, dot(value_pair, gstate, NT) + gsum, 0.0)
    return grad_keys, dot(key_pair, gstate, NN)


def source_value_kernel(others, offset, others_offset, head_dim, *refs):
    layout, own_ref, received = refs[0], refs[1], refs[2 : 2 + others]
    field_ref, grad_ref = refs[2 + others :]
    place = Place(layout)
    mask = same_head(head_dim)
    total = total_state(own_ref, received, place, offset, others_offset)
    for at in parts_of(grad_ref.shape[2]):
        _, key_at, value_at = thirds(field_ref, at)
        raw = read_field(field_ref, place, key_at).reshape(-1, LANES)
        values = read_field(field_ref, place, value_at).reshape(-1, LANES)
        grad_ref[0, :, at], grad_ref[1, :, at] = key_gradients(
            raw, exact(jnp.maximum(raw, 0.0)), exact(values), total[:, at], head_dim, mask
        )


def merged_value_kernel(others, routes, tall, head_dim, *refs):
    layout, own_ref, received = refs[0], refs[1], refs[2 : 2 + others]
    merged_ref, mixed_ref, pw_ref, qgmix_ref, packed_ref, gmix_ref, gpw_ref = refs[2 + others : 9 + others]
    outs = refs[9 + others :]
    place = Place(layout)
    mask = same_head(head_dim)
    total = total_state(own_ref, received, place, 0, 0)
    size = (outs[0].shape[0] - packed_ref.shape[0]) // 3

    def send(member, at, gmix):
        field = gmix.reshape(tall, -1, LANES)
        for delta, out_ref in zip(routes.targets(place), outs):
            out_ref[member * size : (member + 1) * size, at] = payload(field, place, delta).astype(BF16)

    for at in parts_of(gmix_ref.shape[2]):
        for out_ref in outs:
            out_ref[3 * size :, at] = packed_ref[:, at]
        send(0, at, qgmix_ref[0, :, at])
        raw = merged_ref[0, :, at]
        pairs = split(jnp.maximum(raw, 0.0)), split(merged_ref[1, :, at])
        grads = key_gradients(raw, *pairs, total[:, at], head_dim, mask)
        third = gmix_ref.shape[2]
        for member, grad in enumerate(grads):
            pair = split(grad)
            begin = (1 + member) * third + at.start
            gmix = dot(pair, split(spread(pw_ref[:, begin : begin + LANES], mask)), NT)
            gmix_ref[member, :, at] = gmix
            gpw_ref[member, :, at] = gather_blocks(dot(split(mixed_ref[member, :, at]), pair, TN), mask, head_dim)
            send(1 + member, at, gmix)


def weight_kernel(halves, layout, padded_ref, gmix_ref, gpw_ref, *refs):
    outs, sum_ref = refs[:-1], refs[-1]
    ring, sub = padded_ref.shape[2], 128
    tall, broad = padded_ref.shape[1] - 2 * REACH, ring - EDGE
    taps = 2 * REACH + 1
    count, head_dim, third = gpw_ref.shape
    start = sum_ref.shape[0] - head_dim
    odd = Place(layout).group % 2 == 1
    each = third // sub

    def one_block(block, carry):
        member = block // each
        at = pl.ds(pl.multiple_of(block % each * sub, sub), sub)
        out_at = pl.ds(pl.multiple_of(block * sub, sub), sub)

        def one_row(y, totals):
            grad = gmix_ref[member, pl.ds(pl.multiple_of(y * broad, broad), broad), at]
            grad = jnp.concatenate([grad, jnp.zeros((EDGE, sub), F32)], axis=0)
            moved = [grad if b == REACH else pltpu.roll(grad, (b - REACH) % ring, 0) for b in range(taps)]
            new = list(totals)
            for a in range(taps):
                row = padded_ref[member, y + a, :, at]
                for b in range(taps):
                    term = (row * moved[b]).reshape(ring // 8, 8, sub)
                    new[taps * a + b] = new[taps * a + b] + jnp.sum(term, axis=0)
            return tuple(new)

        zero = jnp.zeros((8, sub), F32)
        totals = lax.fori_loop(0, tall, one_row, (zero,) * (taps * taps), unroll=2)
        for tap in range(taps * taps):
            sum_ref[tap : tap + 1] = jnp.sum(totals[tap], axis=0, keepdims=True)
        sum_ref[taps * taps : start] = jnp.zeros((start - taps * taps, sub), F32)
        sum_ref[start:] = gpw_ref[member, :, at]
        if not halves:
            outs[0][:, out_at] = sum_ref[...]
            return carry
        rows = outs[0].shape[1]
        for part in range(outs[0].shape[0]):
            even_rows = sum_ref[2 * part * rows : (2 * part + 1) * rows]
            odd_rows = sum_ref[(2 * part + 1) * rows : (2 * part + 2) * rows]
            outs[0][part, :, out_at] = jnp.where(odd, even_rows, odd_rows)
            outs[1][part, :, out_at] = jnp.where(odd, odd_rows, even_rows)
        return carry

    lax.fori_loop(0, count * each, one_block, 0)


def scatter_kernel(layout, keep_q, come_q, keep_kv, come_kv, own_ref, *outs):
    quarter = Place(layout).group // 2
    third = keep_q.shape[2]
    for m, out_ref in enumerate((own_ref,) + outs):
        at = quarter ^ m
        out_ref[:, :third] = keep_q[at] + come_q[at]
        out_ref[:, third:] = keep_kv[at] + come_kv[at]


def sum_kernel(norm, *refs):
    parts, out_ref = [ref[...] for ref in refs[:-1]], refs[-1]
    while len(parts) > 1:
        parts = [parts[i] + parts[i + 1] for i in range(0, len(parts), 2)]
    out_ref[...] = parts[0] * norm


def collect_kernel(layout, *refs):
    parts, out_ref = refs[:-1], refs[-1]
    quarter = Place(layout).group // 2
    for m, part in enumerate(parts):
        out_ref[quarter ^ m] = part[...]


def finish_kernel(taps, layout, own_ref, come_ref, dw_ref, pw_ref, whole_ref):
    odd = Place(layout).group % 2 == 1
    quarters, rows = own_ref.shape[:2]
    for part in range(quarters):
        own, come = own_ref[part], come_ref[part]
        whole_ref[2 * part * rows : (2 * part + 1) * rows] = jnp.where(odd, come, own)
        whole_ref[(2 * part + 1) * rows : (2 * part + 2) * rows] = jnp.where(odd, own, come)
    dw_ref[...] = whole_ref[:taps]
    pw_ref[...] = whole_ref[whole_ref.shape[0] - pw_ref.shape[0] :]


def copy_kernel(*refs):
    half = len(refs) // 2
    for in_ref, out_ref in zip(refs[:half], refs[half:]):
        out_ref[...] = in_ref[...]


def backward_kernel(routes, first, *refs):
    layout, gmix_ref = refs[:2]
    arrived = refs[2 : 2 + routes.arriving]
    dw_ref, grad0_ref, out_ref, pad_ref, mix_ref, done_ref, sems = refs[2 + routes.arriving :]
    place = Place(layout)
    deltas = routes.sources(place)
    tall, broad = out_ref.shape[2:4]
    count, _, third = gmix_ref.shape
    per, size = third // LANES, REACH * broad

    def one_block(block, carry):
        at, member, within = lanes_at(first * per + block), block // per, lanes_at(block % per)
        begin = pl.multiple_of((first + member) * size, size)
        edges = [ref[pl.ds(begin, size), within] for ref in arrived]
        field = gmix_ref[member, :, within].reshape(tall, broad, LANES)
        fill_padded(pad_ref, field, edges, deltas, place)
        convolve(pad_ref, dw_ref.at[:, at], mix_ref, True)
        grad = mix_ref[...] + grad0_ref[member, :, within].reshape(tall, broad, LANES)
        done_ref[block] = jnp.where(place.live, grad, 0.0).astype(BF16)
        write(block).start()
        return carry

    def write(block):
        target = out_ref.at[0, 0, :, :, lanes_at(first * per + block)]
        return pltpu.make_async_copy(done_ref.at[block], target, sems.at[block])

    lax.fori_loop(0, count * per, one_block, 0)
    for block in range(count * per):
        write(block).wait()


def in_hbm(x):
    return pltpu.with_memory_space_constraint(x, pltpu.HBM)


def call(cost, kernel, out_shape, args, scratch=(), after=(), in_place=0, out_space=pltpu.VMEM, onto=()):
    inputs, extra = len(args), len(onto) + len(after)

    def body(*refs):
        kernel(*refs[:inputs], *refs[inputs + extra :])

    spaces = [pltpu.SMEM if x.dtype == jnp.int32 else pltpu.VMEM for x in args]
    spaces[inputs - in_place :] = [pl.ANY] * in_place
    spaces += [out_space] * len(onto) + [pl.ANY] * len(after)
    return pl.pallas_call(
        body,
        in_specs=[pl.BlockSpec(memory_space=space) for space in spaces],
        out_specs=jax.tree.map(lambda _: pl.BlockSpec(memory_space=out_space), out_shape),
        out_shape=out_shape,
        scratch_shapes=list(scratch),
        input_output_aliases={inputs: 0} if onto else {},
        compiler_params=PARAMS,
        cost_estimate=pl.CostEstimate(
            flops=0, bytes_accessed=int(cost * BYTES_PER_US), transcendentals=0
        ),
    )(*args, *onto, *after)


def local(
    qkv, cotangent, dw_weight, pw_weight, tile_image, tile_row, tile_col, image_height, image_width
):
    tall, broad, channels = qkv.shape[2:]
    positions = tall * broad
    head_dim = pw_weight.shape[0]
    taps = dw_weight.shape[0]
    third = channels // 3
    tiles, groups = lax.axis_size("tile"), lax.axis_size("img")
    routes = Routes(tiles)
    edge = REACH * broad
    packed = 2 * (head_dim + 8)
    padded_shape = (tall + 2 * REACH, broad + EDGE)
    spot = lax.axis_index("img").astype(jnp.int32)
    scalars = (tile_image, tile_row, tile_col, spot, image_height, image_width)
    layout = jnp.concatenate([x.reshape(-1) for x in scalars])
    part = functools.partial

    def wide(*dims):
        return jax.ShapeDtypeStruct(dims, F32)

    def narrow(*dims):
        return jax.ShapeDtypeStruct(dims, BF16)

    mix_scratch = [pltpu.VMEM((tall, broad, LANES), F32)]
    low, high = edge, edge + packed

    sent_kv = pl.pallas_call(
        part(outgoing_kernel, routes),
        grid=(1,),
        in_specs=[pl.BlockSpec(memory_space=pltpu.SMEM)]
        + [pl.BlockSpec((1, 1, tall, broad, third), lambda j, m=m: (0, 0, 0, 0, m)) for m in (1, 2)],
        out_specs=[pl.BlockSpec((2, size, third), lambda j: (0, 0, 0)) for size in routes.direct_rows(edge)],
        out_shape=[narrow(2, size, third) for size in routes.direct_rows(edge)],
        compiler_params=PARAMS,
    )(layout, in_hbm(qkv), in_hbm(qkv))
    halo_kv = routes.move_direct(sent_kv)
    *sent_q, dw_weight, pw_weight = call(
        1.0,
        part(source_state_kernel, routes, head_dim),
        [narrow(high, third)] * routes.sent + [wide(taps, channels), wide(head_dim, channels)],
        (layout, qkv, in_hbm(dw_weight), in_hbm(pw_weight)),
        [pltpu.SemaphoreType.DMA((2,))],
        in_place=2,
    )
    sent_q = call(0.3, copy_kernel, [narrow(high, third)] * routes.sent, sent_q, after=tuple(halo_kv))

    def forward(first, count, halo, direct):
        return call(
            1.5 * count * third / LANES,
            part(forward_kernel, routes, first, count, head_dim, direct),
            [wide(count, positions, third)] * 2
            + [wide(count, *padded_shape, third)]
            + [narrow(packed, third)] * (first > 0),
            (layout, qkv, *halo, dw_weight, pw_weight),
            mix_scratch,
        )

    mixed_kv, merged_kv, padded_kv, state = forward(1, 2, halo_kv, True)

    def copied(far, tokens):
        return call(0.3, copy_kernel, jax.ShapeDtypeStruct(far.shape, far.dtype), (far,), after=tokens)

    halo_q = routes.move(sent_q, hand_on=lambda near, far: copied(far, (state,)))
    state_from = exchange(state, "tile")
    others = len(state_from)
    mixed_q, merged_q, padded_q = forward(0, 1, halo_q, False)

    gstate, gmix_q, gpw_q = call(
        3.0,
        part(merged_query_kernel, others, head_dim),
        [narrow(packed, third), wide(1, positions, third), wide(1, head_dim, third)],
        (layout, state, *state_from, merged_q, mixed_q, cotangent, pw_weight),
    )
    gstate_from = exchange(gstate, "tile")

    source_from = halo_q if routes.relayed else exchange(sent_q[0][low:], "tile")
    from_offset = low if routes.relayed else 0
    grad0_q, gstate0 = call(
        2.5,
        part(source_query_kernel, others, low, from_offset, head_dim),
        [wide(1, positions, third), narrow(packed, third)],
        (layout, sent_q[0], *source_from, qkv, cotangent),
        after=(gstate,),
    )

    gap = -(-taps // 8) * 8
    rows = gap + head_dim
    halves = groups == 8 and rows % groups == 0
    eighth = rows // groups

    def weights(count, padded, gmix, gpw):
        return call(
            1.0 * count * third / LANES,
            part(weight_kernel, halves),
            [wide(4, eighth, count * third)] * 2 if halves else [wide(rows, count * third)],
            (layout, padded, gmix, gpw),
            [pltpu.VMEM((rows, 128), F32)],
        )

    weights_q = weights(1, padded_q, gmix_q, gpw_q)
    total_rows = 3 * edge + packed
    gmix_kv, gpw_kv, *sent_back = call(
        3.0,
        part(merged_value_kernel, others, routes, tall, head_dim),
        [wide(2, positions, third), wide(2, head_dim, third)] + [narrow(total_rows, third)] * routes.sent,
        (layout, gstate, *gstate_from, merged_kv, mixed_kv, pw_weight, gmix_q, gstate0),
        after=(weights_q[0],),
    )
    weights_kv = weights(2, padded_kv, gmix_kv, gpw_kv)

    norm = 1.0 / math.sqrt(positions * tiles * groups)
    ready = weights_kv
    if halves:
        come_q = exchange(weights_q[0], "img", (1,))[0]
        come_kv = exchange(weights_kv[0], "img", (1,))[0]
        share_shape = wide(eighth, channels)
        shares = call(
            0.5, scatter_kernel, [share_shape] * 4, (layout, weights_q[1], come_q, weights_kv[1], come_kv)
        )
        moved = [
            lax.ppermute(share, "img", [(s, s ^ (2 * m)) for s in range(groups)])
            for m, share in enumerate(shares[1:], 1)
        ]
        ready = shares[:1]

    halo_back = routes.move(sent_back, hand_on=lambda near, far: copied(far, (near, *ready)))

    back_from = halo_back if routes.relayed else exchange(sent_back[0][3 * edge :], "tile")
    back_offset = 3 * edge if routes.relayed else 0
    grad0_kv = call(
        1.5,
        part(source_value_kernel, others, 3 * edge, back_offset, head_dim),
        wide(2, positions, third),
        (layout, sent_back[0], *back_from, qkv),
    )

    def backward(first, gmix, grad0, onto=()):
        blocks = gmix.shape[0] * third // LANES
        return call(
            1.0 * blocks,
            part(backward_kernel, routes, first),
            pltpu.HBM((1, 1, tall, broad, channels), BF16),
            (layout, gmix, *halo_back, dw_weight, grad0),
            [pltpu.VMEM((*padded_shape, LANES), F32)]
            + mix_scratch
            + [pltpu.VMEM((blocks, tall, broad, LANES), BF16), pltpu.SemaphoreType.DMA((blocks,))],
            out_space=pltpu.HBM,
            onto=onto,
        )

    grad_query = in_hbm(backward(0, gmix_q, grad0_q))
    grad_source = backward(1, gmix_kv, grad0_kv, (grad_query,))

    if halves:
        total = call(0.3, part(sum_kernel, 1.0), share_shape, [shares[0]] + moved)
        total = call(
            0.3, part(sum_kernel, norm), share_shape, [total] + exchange(total, "tile"), after=(grad_query,)
        )
        quarters = call(
            0.5,
            collect_kernel,
            wide(4, eighth, channels),
            (layout, total, *exchange(total, "img", (2, 4, 6))),
            after=(in_hbm(grad_source),),
        )
        grad_dw, grad_pw = call(
            0.8,
            part(finish_kernel, taps),
            [wide(taps, channels), wide(head_dim, channels)],
            (layout, quarters, exchange(quarters, "img", (1,))[0]),
            [pltpu.VMEM((rows, channels), F32)],
        )
    else:
        whole = jnp.concatenate([weights_q[0], weights_kv[0]], axis=1)
        whole = lax.psum(whole, ("tile", "img")) * norm
        grad_dw, grad_pw = whole[:taps], whole[gap:]
    return grad_source, grad_dw, grad_pw


def solution(mesh):
    placed = (
        P("img", "tile", None, None, None),
        P("img", "tile", None, None, None),
        P(),
        P(),
        P("img", "tile"),
        P("img", "tile"),
        P("img", "tile"),
        P("img", None),
        P("img", None),
    )
    return jax.shard_map(
        local,
        mesh=mesh,
        in_specs=placed,
        out_specs=(P("img", "tile", None, None, None), P(), P()),
        check_vma=False,
    )
```

time: 101 us -> 91.4 us (0.905)
  Pallas kernels: 41.1 us -> 32.6 us
  starting transfers between devices: 37.6 us -> 35.6 us
  waiting for transfers between devices: 17.9 us -> 19.3 us
    ppermute x6 -> x9, waiting for transfers between devices: 3.04 us -> 12.5 us  [the longest x3 4.51 us: local(): lax.ppermute(share, 'img', [(s, s ^ 2 * m) for s in range(groups)])]
    pallas_call x18 -> x20, Pallas kernels: 41.1 us -> 32.6 us  [the longest x19 31.5 us: call(): pl.pallas_call(body, in_specs=[pl.BlockSpec(memory_space=space) for space...]
    ppermute x6 -> x9, starting transfers between devices: 7.31 us -> 12.6 us  [the longest x4 8.26 us: move_direct(): lax.ppermute(part, 'tile', list(enumerate(to)))]
    ppermute x15, waiting for transfers between devices: 7.01 us -> 2.67 us  [exchange(): lax.ppermute(value, axis, [(s, s ^ m) for s in range(count)])]
    ppermute x15, starting transfers between devices: 21.7 us -> 17.5 us  [exchange(): lax.ppermute(value, axis, [(s, s ^ m) for s in range(count)])]
    ppermute x6 -> x4, waiting for transfers between devices: 7.89 us -> 4.06 us  [move(): lax.ppermute(part, 'tile', [(s, s ^ m) for s in range(count)])]
    ppermute x6 -> x4, starting transfers between devices: 8.58 us -> 5.5 us  [move(): lax.ppermute(part, 'tile', [(s, s ^ m) for s in range(count)])]
  transfers between devices with their start and end apart: 27 -> 28, of which waited for: 11 -> 12; matrix products, arithmetic and copies ran while one was open for 0% -> 0% of each run, Pallas kernels for 32% -> 27%
where the time goes in v4:
time: 91.4 us; the launch traced here: 91.1 us
  starting transfers between devices  35.6 us (39%)
  Pallas kernels  32.6 us (36%)
  waiting for transfers between devices  19.3 us (21%)
  between operations  2.92 us (3%)
    pallas_call x19, Pallas kernels, call(): pl.pallas_call(body, in_specs=[pl.BlockSpec(memory_space=space) for space...  31.5 us
    ppermute x15, starting transfers between devices, exchange(): lax.ppermute(value, axis, [(s, s ^ m) for s in range(count)])  17.5 us
    ppermute x4, starting transfers between devices, move_direct(): lax.ppermute(part, 'tile', list(enumerate(to)))  8.26 us
    ppermute x4, starting transfers between devices, move(): lax.ppermute(part, 'tile', [(s, s ^ m) for s in range(count)])  5.5 us
    ppermute x3, waiting for transfers between devices, local(): lax.ppermute(share, 'img', [(s, s ^ 2 * m) for s in range(groups)])  4.51 us
    ppermute x4, waiting for transfers between devices, move_direct(): lax.ppermute(part, 'tile', list(enumerate(to)))  4.17 us
    ppermute x4, waiting for transfers between devices, move(): lax.ppermute(part, 'tile', [(s, s ^ m) for s in range(count)])  4.06 us
    ppermute x2, waiting for transfers between devices, move(): lax.ppermute(hand_on(near, far), 'tile', [(s, s ^ 1) for s in range(count)])  3.86 us
  transfers between devices with their start and end apart: 28, of which 12 were waited for; matrix products, arithmetic and copies ran while one was open for 0% of the time, Pallas kernels for 27%

profile of v4, /device:TPU:0, one launch (start us, length us, event | category | flops | bytes accessed | tf_op | source)
XLA Modules:
  0.0 91.1 jit_solution(8191075719412679698)
XLA Ops:
  4.6 3.1 %collective-permute-start = (bf16[2,64,512]{2,1,0:T(8,128)(2,1)S(1)}, bf16[2,64,512]{2,1,0:T(8,128)(2,1)S(1)}, u32[]{:S(2)}, u32[]{:S(2)}) collective-permute-start(bf16[2,64,512]{2,1,0:T(8,128)(2,1)S(1)} %get-tuple-element.39), channel_id=1, source_target_pairs={{0,8},{8,0},{16,24},{24,16},{1,9},{9,1},{17,25},{25,17},{2,10},{10... | collective-permute-start | bytes 393224 | tf_op jit(solution)/shard_map/ppermute | solution.py:89
  7.7 2.6 %collective-permute-start.1 = (bf16[2,64,512]{2,1,0:T(8,128)(2,1)S(1)}, bf16[2,64,512]{2,1,0:T(8,128)(2,1)S(1)}, u32[]{:S(2)}, u32[]{:S(2)}) collective-permute-start(bf16[2,64,512]{2,1,0:T(8,128)(2,1)S(1)} %get-tuple-element.40), channel_id=1, source_target_pairs={{0,16},{8,24},{16,0},{24,8},{1,17},{9,25},{17,1},{25,9},{2,18},{10... | collective-permute-start | bytes 393224 | tf_op jit(solution)/shard_map/ppermute | solution.py:89
  10.9 1.9 %collective-permute-start.3 = (bf16[2,16,512]{2,1,0:T(8,128)(2,1)S(1)}, bf16[2,16,512]{2,1,0:T(8,128)(2,1)S(1)}, u32[]{:S(2)}, u32[]{:S(2)}) collective-permute-start(bf16[2,16,512]{2,1,0:T(8,128)(2,1)S(1)} %get-tuple-element.42), channel_id=1, source_target_pairs={{0,24},{8,8},{16,16},{24,0},{1,25},{9,9},{17,17},{25,1},{2,26},{10... | collective-permute-start | bytes 98312 | tf_op jit(solution)/shard_map/ppermute | solution.py:89
  12.9 1.6 %shard_map.113 = (bf16[144,512]{1,0:T(8,128)(2,1)S(1)}, bf16[144,512]{1,0:T(8,128)(2,1)S(1)}, f32[25,1536]{1,0:T(8,128)S(1)}, f32[32,1536]{1,0:T(8,128)S(1)}) custom-call(s32[8]{0:T(128)S(1)} %concatenate.3.layout.refs_0_, bf16[1,1,8,32,1536]{4,3,2,1,0:T(8,128)(2,1)S(1)} %copy-done, f32[25,1536]{1,0:T(8,128)} %refs_2_.1, f32[32,1536]{1,0:T(8,128)} %refs_3_.1), custom_call_target="tpu_custom_call" | custom-call | bytes 3690000 | tf_op jit(solution)/shard_map/pallas_call | solution.py:554
  14.5 4.2 %collective-permute-done.3.refs_5_ = bf16[2,16,512]{2,1,0:T(8,128)(2,1)S(1)} collective-permute-done((bf16[2,16,512]{2,1,0:T(8,128)(2,1)S(1)}, bf16[2,16,512]{2,1,0:T(8,128)(2,1)S(1)}, u32[]{:S(2)}, u32[]{:S(2)}) %collective-permute-start.3) | collective-permute-done | bytes 32800 | tf_op jit(solution)/shard_map/ppermute | solution.py:89
  18.7 2.9 %collective-permute-start.8 = (bf16[144,512]{1,0:T(8,128)(2,1)S(1)}, bf16[144,512]{1,0:T(8,128)(2,1)S(1)}, u32[]{:S(2)}, u32[]{:S(2)}) collective-permute-start(bf16[144,512]{1,0:T(8,128)(2,1)S(1)} %get-tuple-element.49), channel_id=1, source_target_pairs={{0,16},{8,24},{16,0},{24,8},{1,17},{9,25},{17,1},{25,9},{2,18},{10... | collective-permute-start | bytes 442376 | tf_op jit(solution)/shard_map/ppermute | solution.py:81
  21.6 4.8 %shard_map.114 = (f32[2,256,512]{2,1,0:T(8,128)S(1)}, f32[2,256,512]{2,1,0:T(8,128)S(1)}, f32[2,12,40,512]{3,2,1,0:T(8,128)S(1)}, bf16[80,512]{1,0:T(8,128)(2,1)S(1)}) custom-call(s32[8]{0:T(128)S(1)} %concatenate.3.layout.refs_0_, bf16[1,1,8,32,1536]{4,3,2,1,0:T(8,128)(2,1)S(1)} %copy-done, bf16[2,64,512]{2,1,0:T(8,128)(2,1)S(1)} %collective-permute-done.refs_2_, ...), custom_call_target="tpu_custom_call" | custom-call | bytes 22140000 | tf_op jit(solution)/shard_map/pallas_call | solution.py:554
  26.4 1.6 %collective-permute-done.8.refs_0_.refs_3_ = bf16[144,512]{1,0:T(8,128)(2,1)S(1)} collective-permute-done((bf16[144,512]{1,0:T(8,128)(2,1)S(1)}, bf16[144,512]{1,0:T(8,128)(2,1)S(1)}, u32[]{:S(2)}, u32[]{:S(2)}) %collective-permute-start.8) | collective-permute-done | bytes 147488 | tf_op jit(solution)/shard_map/ppermute | solution.py:81
  28.5 1.9 %collective-permute-start.6 = (bf16[80,512]{1,0:T(8,128)(2,1)S(1)}, bf16[80,512]{1,0:T(8,128)(2,1)S(1)}, u32[]{:S(2)}, u32[]{:S(2)}) collective-permute-start(bf16[80,512]{1,0:T(8,128)(2,1)S(1)} %get-tuple-element.45.refs_1_), channel_id=1, source_target_pairs={{0,24},{8,16},{16,8},{24,0},{1,25},{9,17},{17,9},{25,1},{2,26},{10... | collective-permute-start | bytes 245768 | tf_op jit(solution)/shard_map/ppermute | solution.py:95
  31.5 1.3 %collective-permute-start.4 = (bf16[80,512]{1,0:T(8,128)(2,1)S(1)}, bf16[80,512]{1,0:T(8,128)(2,1)S(1)}, u32[]{:S(2)}, u32[]{:S(2)}) collective-permute-start(bf16[80,512]{1,0:T(8,128)(2,1)S(1)} %get-tuple-element.45.refs_1_), channel_id=1, source_target_pairs={{0,8},{8,0},{16,24},{24,16},{1,9},{9,1},{17,25},{25,17},{2,10},{10... | collective-permute-start | bytes 245768 | tf_op jit(solution)/shard_map/ppermute | solution.py:95
  32.9 3.9 %collective-permute-done.9.refs_4_ = bf16[144,512]{1,0:T(8,128)(2,1)S(1)} collective-permute-done((bf16[144,512]{1,0:T(8,128)(2,1)S(1)}, bf16[144,512]{1,0:T(8,128)(2,1)S(1)}, u32[]{:S(2)}, u32[]{:S(2)}) %collective-permute-start.9) | collective-permute-done | bytes 147488 | tf_op jit(solution)/shard_map/ppermute | solution.py:83
  36.7 2.4 %shard_map.117 = (f32[1,256,512]{2,1,0:T(8,128)S(1)}, f32[1,256,512]{2,1,0:T(8,128)S(1)}, f32[1,12,40,512]{3,2,1,0:T(8,128)S(1)}) custom-call(s32[8]{0:T(128)S(1)} %concatenate.3.layout.refs_0_, bf16[1,1,8,32,1536]{4,3,2,1,0:T(8,128)(2,1)S(1)} %copy-done, bf16[144,512]{1,0:T(8,128)(2,1)S(1)} %collective-permute-done.7.refs_2_, ...), custom_call_target="tpu_custom_call" | custom-call | bytes 11070000 | tf_op jit(solution)/shard_map/pallas_call | solution.py:554
  39.2 2.5 %shard_map.118 = (bf16[80,512]{1,0:T(8,128)(2,1)S(1)}, f32[1,256,512]{2,1,0:T(8,128)S(1)}, f32[1,32,512]{2,1,0:T(8,128)S(1)}) custom-call(s32[8]{0:T(128)S(1)} %concatenate.3.layout.refs_0_, bf16[80,512]{1,0:T(8,128)(2,1)S(1)} %get-tuple-element.45.refs_1_, bf16[80,512]{1,0:T(8,128)(2,1)S(1)} %collective-permute-done.4.refs_2_, ...), custom_call_target="tpu_custom_call" | custom-call | bytes 11070000 | tf_op jit(solution)/shard_map/pallas_call | solution.py:554
  41.7 2.1 %collective-permute-start.12 = (bf16[80,512]{1,0:T(8,128)(2,1)S(1)}, bf16[80,512]{1,0:T(8,128)(2,1)S(1)}, u32[]{:S(2)}, u32[]{:S(2)}) collective-permute-start(bf16[80,512]{1,0:T(8,128)(2,1)S(1)} %get-tuple-element.52.refs_7_.refs_1_), channel_id=1, source_target_pairs={{0,24},{8,16},{16,8},{24,0},{1,25},{9,17},{17,9},{25,1},{2,26},{10... | collective-permute-start | bytes 245768 | tf_op jit(solution)/shard_map/ppermute | solution.py:95
  43.8 2.4 %collective-permute-start.10 = (bf16[80,512]{1,0:T(8,128)(2,1)S(1)}, bf16[80,512]{1,0:T(8,128)(2,1)S(1)}, u32[]{:S(2)}, u32[]{:S(2)}) collective-permute-start(bf16[80,512]{1,0:T(8,128)(2,1)S(1)} %get-tuple-element.52.refs_7_.refs_1_), channel_id=1, source_target_pairs={{0,8},{8,0},{16,24},{24,16},{1,9},{9,1},{17,25},{25,17},{2,10},{10... | collective-permute-start | bytes 245768 | tf_op jit(solution)/shard_map/ppermute | solution.py:95
  46.2 2.1 %shard_map.120 = (f32[4,8,512]{2,1,0:T(8,128)S(1)}, f32[4,8,512]{2,1,0:T(8,128)S(1)}) custom-call(s32[8]{0:T(128)S(1)} %concatenate.3.layout.refs_0_, f32[1,12,40,512]{3,2,1,0:T(8,128)S(1)} %get-tuple-element.57.refs_1_, f32[1,256,512]{2,1,0:T(8,128)S(1)} %get-tuple-element.55.refs_2_.refs_8_.refs_1_, f32[1,32,512]{2,1,0:T(8,128)S(1)} %get-tuple-element.58.refs_3_), custom_call_target="tpu_custom_call" | custom-call | bytes 7380000 | tf_op jit(solution)/shard_map/pallas_call | solution.py:554
  48.2 1.8 %shard_map.119 = (f32[1,256,512]{2,1,0:T(8,128)S(1)}, bf16[80,512]{1,0:T(8,128)(2,1)S(1)}) custom-call(s32[8]{0:T(128)S(1)} %concatenate.3.layout.refs_0_, bf16[144,512]{1,0:T(8,128)(2,1)S(1)} %get-tuple-element.48.refs_1_, bf16[144,512]{1,0:T(8,128)(2,1)S(1)} %collective-permute-done.7.refs_2_, bf16[144,512]{1,0:T(8,128)(2,1)S(1)} %collective-permute-done.8.refs_0_.refs_3_, ...), custom_call_target="tpu_custom_call" | custom-call | bytes 9225000 | tf_op jit(solution)/shard_map/pallas_call | solution.py:554
  50.1 2.3 %shard_map.121 = (f32[2,256,512]{2,1,0:T(8,128)S(1)}, f32[2,32,512]{2,1,0:T(8,128)S(1)}, bf16[272,512]{1,0:T(8,128)(2,1)S(1)}, bf16[272,512]{1,0:T(8,128)(2,1)S(1)}) custom-call(s32[8]{0:T(128)S(1)} %concatenate.3.layout.refs_0_, bf16[80,512]{1,0:T(8,128)(2,1)S(1)} %get-tuple-element.52.refs_7_.refs_1_, bf16[80,512]{1,0:T(8,128)(2,1)S(1)} %collective-permute-done.10.refs_2_, ...), custom_call_target="tpu_custom_call" | custom-call | bytes 11070000 | tf_op jit(solution)/shard_map/pallas_call | solution.py:554
  52.4 1.5 %collective-permute-start.14 = (bf16[272,512]{1,0:T(8,128)(2,1)S(1)}, bf16[272,512]{1,0:T(8,128)(2,1)S(1)}, u32[]{:S(2)}, u32[]{:S(2)}) collective-permute-start(bf16[272,512]{1,0:T(8,128)(2,1)S(1)} %get-tuple-element.62), channel_id=1, source_target_pairs={{0,16},{8,24},{16,0},{24,8},{1,17},{9,25},{17,1},{25,9},{2,18},{10... | collective-permute-start | bytes 835592 | tf_op jit(solution)/shard_map/ppermute | solution.py:81
  55.0 3.6 %shard_map.122 = (f32[4,8,1024]{2,1,0:T(8,128)S(1)}, f32[4,8,1024]{2,1,0:T(8,128)S(1)}) custom-call(s32[8]{0:T(128)S(1)} %concatenate.3.layout.refs_0_, f32[2,12,40,512]{3,2,1,0:T(8,128)S(1)} %get-tuple-element.64.refs_1_, f32[2,256,512]{2,1,0:T(8,128)S(1)} %get-tuple-element.60.refs_2_.refs_1_, f32[2,32,512]{2,1,0:T(8,128)S(1)} %get-tuple-element.65.refs_3_), custom_call_target="tpu_custom_call" | custom-call | bytes 14760000 | tf_op jit(solution)/shard_map/pallas_call | solution.py:554
  60.7 2.3 %collective-permute-done.14.refs_0_.refs_3_ = bf16[272,512]{1,0:T(8,128)(2,1)S(1)} collective-permute-done((bf16[272,512]{1,0:T(8,128)(2,1)S(1)}, bf16[272,512]{1,0:T(8,128)(2,1)S(1)}, u32[]{:S(2)}, u32[]{:S(2)}) %collective-permute-start.14) | collective-permute-done | bytes 278560 | tf_op jit(solution)/shard_map/ppermute | solution.py:81
  63.5 1.5 %collective-permute-start.18 = (f32[8,1536]{1,0:T(8,128)S(1)}, f32[8,1536]{1,0:T(8,128)S(1)}, u32[]{:S(2)}, u32[]{:S(2)}) collective-permute-start(f32[8,1536]{1,0:T(8,128)S(1)} %get-tuple-element.70), channel_id=1, source_target_pairs={{0,2},{1,3},{2,0},{3,1},{4,6},{5,7},{6,4},{7,5},{8,10},{9,11},{10,... | collective-permute-start | bytes 147464 | tf_op jit(solution)/shard_map/ppermute | solution.py:689
  65.0 1.5 %collective-permute-start.19 = (f32[8,1536]{1,0:T(8,128)S(1)}, f32[8,1536]{1,0:T(8,128)S(1)}, u32[]{:S(2)}, u32[]{:S(2)}) collective-permute-start(f32[8,1536]{1,0:T(8,128)S(1)} %get-tuple-element.71), channel_id=1, source_target_pairs={{0,4},{1,5},{2,6},{3,7},{4,0},{5,1},{6,2},{7,3},{8,12},{9,13},{10,... | collective-permute-start | bytes 147464 | tf_op jit(solution)/shard_map/ppermute | solution.py:689
  69.1 2.4 %collective-permute-done.20.refs_3_ = f32[8,1536]{1,0:T(8,128)S(1)} collective-permute-done((f32[8,1536]{1,0:T(8,128)S(1)}, f32[8,1536]{1,0:T(8,128)S(1)}, u32[]{:S(2)}, u32[]{:S(2)}) %collective-permute-start.20) | collective-permute-done | bytes 49184 | tf_op jit(solution)/shard_map/ppermute | solution.py:689
  71.5 1.7 %collective-permute-start.23 = (f32[8,1536]{1,0:T(8,128)S(1)}, f32[8,1536]{1,0:T(8,128)S(1)}, u32[]{:S(2)}, u32[]{:S(2)}) collective-permute-start(f32[8,1536]{1,0:T(8,128)S(1)} %shard_map.128.refs_0_), channel_id=1, source_target_pairs={{0,24},{8,16},{16,8},{24,0},{1,25},{9,17},{17,9},{25,1},{2,26},{10... | collective-permute-start | bytes 147464 | tf_op jit(solution)/shard_map/ppermute | solution.py:95
  73.2 1.6 %collective-permute-start.22 = (f32[8,1536]{1,0:T(8,128)S(1)}, f32[8,1536]{1,0:T(8,128)S(1)}, u32[]{:S(2)}, u32[]{:S(2)}) collective-permute-start(f32[8,1536]{1,0:T(8,128)S(1)} %shard_map.128.refs_0_), channel_id=1, source_target_pairs={{0,16},{8,24},{16,0},{24,8},{1,17},{9,25},{17,1},{25,9},{2,18},{10... | collective-permute-start | bytes 147464 | tf_op jit(solution)/shard_map/ppermute | solution.py:95
  76.0 2.7 %shard_map.126.refs_7_.refs_4_ = bf16[1,1,8,32,1536]{4,3,2,1,0:T(8,128)(2,1)} custom-call(s32[8]{0:T(128)S(1)} %concatenate.3.layout.refs_0_, f32[1,256,512]{2,1,0:T(8,128)S(1)} %get-tuple-element.55.refs_2_.refs_8_.refs_1_, bf16[272,512]{1,0:T(8,128)(2,1)S(1)} %collective-permute-done.13.refs_1_.refs_2_, ...), custom_call_target="tpu_custom_call" | custom-call | bytes 7380000 | tf_op jit(solution)/shard_map/pallas_call | solution.py:554
  79.5 1.5 %collective-permute-start.25 = (f32[8,1536]{1,0:T(8,128)S(1)}, f32[8,1536]{1,0:T(8,128)S(1)}, u32[]{:S(2)}, u32[]{:S(2)}) collective-permute-start(f32[8,1536]{1,0:T(8,128)S(1)} %shard_map.129.refs_1_), channel_id=1, source_target_pairs={{0,4},{1,5},{2,6},{3,7},{4,0},{5,1},{6,2},{7,3},{8,12},{9,13},{10,... | collective-permute-start | bytes 147464 | tf_op jit(solution)/shard_map/ppermute | solution.py:95
  81.0 1.5 %collective-permute-start.24 = (f32[8,1536]{1,0:T(8,128)S(1)}, f32[8,1536]{1,0:T(8,128)S(1)}, u32[]{:S(2)}, u32[]{:S(2)}) collective-permute-start(f32[8,1536]{1,0:T(8,128)S(1)} %shard_map.129.refs_1_), channel_id=1, source_target_pairs={{0,2},{1,3},{2,0},{3,1},{4,6},{5,7},{6,4},{7,5},{8,10},{9,11},{10,... | collective-permute-start | bytes 147464 | tf_op jit(solution)/shard_map/ppermute | solution.py:95
  83.6 4.1 %shard_map.127.refs_5_ = bf16[1,1,8,32,1536]{4,3,2,1,0:T(8,128)(2,1)} custom-call(s32[8]{0:T(128)S(1)} %concatenate.3.layout.refs_0_, f32[2,256,512]{2,1,0:T(8,128)S(1)} %get-tuple-element.60.refs_2_.refs_1_, bf16[272,512]{1,0:T(8,128)(2,1)S(1)} %collective-permute-done.13.refs_1_.refs_2_, ...), custom_call_target="tpu_custom_call", output_to_operand_aliasing={{}: (7, {})} | custom-call | bytes 14760000 | tf_op jit(solution)/shard_map/pallas_call | solution.py:554
  88.4 1.4 %collective-permute-done.27.refs_2_ = f32[4,8,1536]{2,1,0:T(8,128)S(1)} collective-permute-done((f32[4,8,1536]{2,1,0:T(8,128)S(1)}, f32[4,8,1536]{2,1,0:T(8,128)S(1)}, u32[]{:S(2)}, u32[]{:S(2)}) %collective-permute-start.27) | collective-permute-done | bytes 196640 | tf_op jit(solution)/shard_map/ppermute | solution.py:95
  89.8 1.3 %shard_map.131 = (f32[25,1536]{1,0:T(8,128)}, f32[32,1536]{1,0:T(8,128)}) custom-call(s32[8]{0:T(128)S(1)} %concatenate.3.layout.refs_0_, f32[4,8,1536]{2,1,0:T(8,128)S(1)} %shard_map.130.refs_1_, f32[4,8,1536]{2,1,0:T(8,128)S(1)} %collective-permute-done.27.refs_2_), custom_call_target="tpu_custom_call" | custom-call | bytes 2952000 | tf_op jit(solution)/shard_map/pallas_call | solution.py:554
  (49 shorter events, 14.3 us)
Async XLA Ops:
  0.6 12.2 %copy-start = (bf16[1,1,8,32,1536]{4,3,2,1,0:T(8,128)(2,1)S(1)}, bf16[1,1,8,32,1536]{4,3,2,1,0:T(8,128)(2,1)}, u32[]{:S(2)}) copy-start(bf16[1,1,8,32,1536]{4,3,2,1,0:T(8,128)(2,1)} %refs_5_.3) | copy-start | bytes 2359300
  4.6 14.1 %collective-permute-start = (bf16[2,64,512]{2,1,0:T(8,128)(2,1)S(1)}, bf16[2,64,512]{2,1,0:T(8,128)(2,1)S(1)}, u32[]{:S(2)}, u32[]{:S(2)}) collective-permute-start(bf16[2,64,512]{2,1,0:T(8,128)(2,1)S(1)} %get-tuple-element.39), channel_id=1, source_target_pairs={{0,8},{8,0},{16,24},{24,16},{1,9},{9,1},{17,25},{25,17},{2,10},{10... | collective-permute-start | bytes 393224 | tf_op jit(solution)/shard_map/ppermute | solution.py:89
  7.7 11.0 %collective-permute-start.1 = (bf16[2,64,512]{2,1,0:T(8,128)(2,1)S(1)}, bf16[2,64,512]{2,1,0:T(8,128)(2,1)S(1)}, u32[]{:S(2)}, u32[]{:S(2)}) collective-permute-start(bf16[2,64,512]{2,1,0:T(8,128)(2,1)S(1)} %get-tuple-element.40), channel_id=1, source_target_pairs={{0,16},{8,24},{16,0},{24,8},{1,17},{9,25},{17,1},{25,9},{2,18},{10... | collective-permute-start | bytes 393224 | tf_op jit(solution)/shard_map/ppermute | solution.py:89
  10.2 8.4 %collective-permute-start.2 = (bf16[2,64,512]{2,1,0:T(8,128)(2,1)S(1)}, bf16[2,64,512]{2,1,0:T(8,128)(2,1)S(1)}, u32[]{:S(2)}, u32[]{:S(2)}) collective-permute-start(bf16[2,64,512]{2,1,0:T(8,128)(2,1)S(1)} %get-tuple-element.41), channel_id=1, source_target_pairs={{0,0},{8,16},{16,8},{24,24},{1,1},{9,17},{17,9},{25,25},{2,2},{10,... | collective-permute-start | bytes 393224 | tf_op jit(solution)/shard_map/ppermute | solution.py:89
  10.9 7.7 %collective-permute-start.3 = (bf16[2,16,512]{2,1,0:T(8,128)(2,1)S(1)}, bf16[2,16,512]{2,1,0:T(8,128)(2,1)S(1)}, u32[]{:S(2)}, u32[]{:S(2)}) collective-permute-start(bf16[2,16,512]{2,1,0:T(8,128)(2,1)S(1)} %get-tuple-element.42), channel_id=1, source_target_pairs={{0,24},{8,8},{16,16},{24,0},{1,25},{9,9},{17,17},{25,1},{2,26},{10... | collective-permute-start | bytes 98312 | tf_op jit(solution)/shard_map/ppermute | solution.py:89
  18.7 20.5 %copy-start.1 = (bf16[1,1,8,32,1024]{4,3,2,1,0:T(8,128)(2,1)S(1)}, bf16[1,1,8,32,1024]{4,3,2,1,0:T(8,128)(2,1)}, u32[]{:S(2)}) copy-start(bf16[1,1,8,32,1024]{4,3,2,1,0:T(8,128)(2,1)} %refs_6_.1) | copy-start | bytes 1572868
  18.7 9.3 %collective-permute-start.8 = (bf16[144,512]{1,0:T(8,128)(2,1)S(1)}, bf16[144,512]{1,0:T(8,128)(2,1)S(1)}, u32[]{:S(2)}, u32[]{:S(2)}) collective-permute-start(bf16[144,512]{1,0:T(8,128)(2,1)S(1)} %get-tuple-element.49), channel_id=1, source_target_pairs={{0,16},{8,24},{16,0},{24,8},{1,17},{9,25},{17,1},{25,9},{2,18},{10... | collective-permute-start | bytes 442376 | tf_op jit(solution)/shard_map/ppermute | solution.py:81
  21.6 11.3 %collective-permute-start.7 = (bf16[144,512]{1,0:T(8,128)(2,1)S(1)}, bf16[144,512]{1,0:T(8,128)(2,1)S(1)}, u32[]{:S(2)}, u32[]{:S(2)}) collective-permute-start(bf16[144,512]{1,0:T(8,128)(2,1)S(1)} %get-tuple-element.48.refs_1_), channel_id=1, source_target_pairs={{0,8},{8,0},{16,24},{24,16},{1,9},{9,1},{17,25},{25,17},{2,10},{10... | collective-permute-start | bytes 442376 | tf_op jit(solution)/shard_map/ppermute | solution.py:81
  28.0 8.7 %collective-permute-start.9 = (bf16[144,512]{1,0:T(8,128)(2,1)S(1)}, bf16[144,512]{1,0:T(8,128)(2,1)S(1)}, u32[]{:S(2)}, u32[]{:S(2)}) collective-permute-start(bf16[144,512]{1,0:T(8,128)(2,1)S(1)} %shard_map.116), channel_id=1, source_target_pairs={{0,8},{8,0},{16,24},{24,16},{1,9},{9,1},{17,25},{25,17},{2,10},{10... | collective-permute-start | bytes 442376 | tf_op jit(solution)/shard_map/ppermute | solution.py:83
  28.5 10.7 %collective-permute-start.6 = (bf16[80,512]{1,0:T(8,128)(2,1)S(1)}, bf16[80,512]{1,0:T(8,128)(2,1)S(1)}, u32[]{:S(2)}, u32[]{:S(2)}) collective-permute-start(bf16[80,512]{1,0:T(8,128)(2,1)S(1)} %get-tuple-element.45.refs_1_), channel_id=1, source_target_pairs={{0,24},{8,16},{16,8},{24,0},{1,25},{9,17},{17,9},{25,1},{2,26},{10... | collective-permute-start | bytes 245768 | tf_op jit(solution)/shard_map/ppermute | solution.py:95
  30.4 8.8 %collective-permute-start.5 = (bf16[80,512]{1,0:T(8,128)(2,1)S(1)}, bf16[80,512]{1,0:T(8,128)(2,1)S(1)}, u32[]{:S(2)}, u32[]{:S(2)}) collective-permute-start(bf16[80,512]{1,0:T(8,128)(2,1)S(1)} %get-tuple-element.45.refs_1_), channel_id=1, source_target_pairs={{0,16},{8,24},{16,0},{24,8},{1,17},{9,25},{17,1},{25,9},{2,18},{10... | collective-permute-start | bytes 245768 | tf_op jit(solution)/shard_map/ppermute | solution.py:95
  31.5 7.6 %collective-permute-start.4 = (bf16[80,512]{1,0:T(8,128)(2,1)S(1)}, bf16[80,512]{1,0:T(8,128)(2,1)S(1)}, u32[]{:S(2)}, u32[]{:S(2)}) collective-permute-start(bf16[80,512]{1,0:T(8,128)(2,1)S(1)} %get-tuple-element.45.refs_1_), channel_id=1, source_target_pairs={{0,8},{8,0},{16,24},{24,16},{1,9},{9,1},{17,25},{25,17},{2,10},{10... | collective-permute-start | bytes 245768 | tf_op jit(solution)/shard_map/ppermute | solution.py:95
  41.7 8.3 %collective-permute-start.12 = (bf16[80,512]{1,0:T(8,128)(2,1)S(1)}, bf16[80,512]{1,0:T(8,128)(2,1)S(1)}, u32[]{:S(2)}, u32[]{:S(2)}) collective-permute-start(bf16[80,512]{1,0:T(8,128)(2,1)S(1)} %get-tuple-element.52.refs_7_.refs_1_), channel_id=1, source_target_pairs={{0,24},{8,16},{16,8},{24,0},{1,25},{9,17},{17,9},{25,1},{2,26},{10... | collective-permute-start | bytes 245768 | tf_op jit(solution)/shard_map/ppermute | solution.py:95
  43.8 6.3 %collective-permute-start.11 = (bf16[80,512]{1,0:T(8,128)(2,1)S(1)}, bf16[80,512]{1,0:T(8,128)(2,1)S(1)}, u32[]{:S(2)}, u32[]{:S(2)}) collective-permute-start(bf16[80,512]{1,0:T(8,128)(2,1)S(1)} %get-tuple-element.52.refs_7_.refs_1_), channel_id=1, source_target_pairs={{0,16},{8,24},{16,0},{24,8},{1,17},{9,25},{17,1},{25,9},{2,18},{10... | collective-permute-start | bytes 245768 | tf_op jit(solution)/shard_map/ppermute | solution.py:95
  43.8 6.3 %collective-permute-start.10 = (bf16[80,512]{1,0:T(8,128)(2,1)S(1)}, bf16[80,512]{1,0:T(8,128)(2,1)S(1)}, u32[]{:S(2)}, u32[]{:S(2)}) collective-permute-start(bf16[80,512]{1,0:T(8,128)(2,1)S(1)} %get-tuple-element.52.refs_7_.refs_1_), channel_id=1, source_target_pairs={{0,8},{8,0},{16,24},{24,16},{1,9},{9,1},{17,25},{25,17},{2,10},{10... | collective-permute-start | bytes 245768 | tf_op jit(solution)/shard_map/ppermute | solution.py:95
  52.4 10.6 %collective-permute-start.14 = (bf16[272,512]{1,0:T(8,128)(2,1)S(1)}, bf16[272,512]{1,0:T(8,128)(2,1)S(1)}, u32[]{:S(2)}, u32[]{:S(2)}) collective-permute-start(bf16[272,512]{1,0:T(8,128)(2,1)S(1)} %get-tuple-element.62), channel_id=1, source_target_pairs={{0,16},{8,24},{16,0},{24,8},{1,17},{9,25},{17,1},{25,9},{2,18},{10... | collective-permute-start | bytes 835592 | tf_op jit(solution)/shard_map/ppermute | solution.py:81
  53.8 9.3 %collective-permute-start.13 = (bf16[272,512]{1,0:T(8,128)(2,1)S(1)}, bf16[272,512]{1,0:T(8,128)(2,1)S(1)}, u32[]{:S(2)}, u32[]{:S(2)}) collective-permute-start(bf16[272,512]{1,0:T(8,128)(2,1)S(1)} %get-tuple-element.61.refs_1_), channel_id=1, source_target_pairs={{0,8},{8,0},{16,24},{24,16},{1,9},{9,1},{17,25},{25,17},{2,10},{10... | collective-permute-start | bytes 835592 | tf_op jit(solution)/shard_map/ppermute | solution.py:81
  58.6 1.5 %collective-permute-start.16 = (f32[4,8,1024]{2,1,0:T(8,128)S(1)}, f32[4,8,1024]{2,1,0:T(8,128)S(1)}, u32[]{:S(2)}, u32[]{:S(2)}) collective-permute-start(f32[4,8,1024]{2,1,0:T(8,128)S(1)} %get-tuple-element.67), channel_id=1, source_target_pairs={{0,1},{1,0},{2,3},{3,2},{4,5},{5,4},{6,7},{7,6},{8,9},{9,8},{10,11... | collective-permute-start | bytes 393224 | tf_op jit(solution)/shard_map/ppermute | solution.py:95
  58.7 1.4 %collective-permute-start.15 = (f32[4,8,512]{2,1,0:T(8,128)S(1)}, f32[4,8,512]{2,1,0:T(8,128)S(1)}, u32[]{:S(2)}, u32[]{:S(2)}) collective-permute-start(f32[4,8,512]{2,1,0:T(8,128)S(1)} %get-tuple-element.59.refs_10_), channel_id=1, source_target_pairs={{0,1},{1,0},{2,3},{3,2},{4,5},{5,4},{6,7},{7,6},{8,9},{9,8},{10,11... | collective-permute-start | bytes 196616 | tf_op jit(solution)/shard_map/ppermute | solution.py:95
  63.2 12.8 %collective-permute-start.17 = (bf16[272,512]{1,0:T(8,128)(2,1)S(1)}, bf16[272,512]{1,0:T(8,128)(2,1)S(1)}, u32[]{:S(2)}, u32[]{:S(2)}) collective-permute-start(bf16[272,512]{1,0:T(8,128)(2,1)S(1)} %shard_map.124), channel_id=1, source_target_pairs={{0,8},{8,0},{16,24},{24,16},{1,9},{9,1},{17,25},{25,17},{2,10},{10... | collective-permute-start | bytes 835592 | tf_op jit(solution)/shard_map/ppermute | solution.py:83
  63.5 4.3 %collective-permute-start.18 = (f32[8,1536]{1,0:T(8,128)S(1)}, f32[8,1536]{1,0:T(8,128)S(1)}, u32[]{:S(2)}, u32[]{:S(2)}) collective-permute-start(f32[8,1536]{1,0:T(8,128)S(1)} %get-tuple-element.70), channel_id=1, source_target_pairs={{0,2},{1,3},{2,0},{3,1},{4,6},{5,7},{6,4},{7,5},{8,10},{9,11},{10,... | collective-permute-start | bytes 147464 | tf_op jit(solution)/shard_map/ppermute | solution.py:689
  65.0 4.1 %collective-permute-start.19 = (f32[8,1536]{1,0:T(8,128)S(1)}, f32[8,1536]{1,0:T(8,128)S(1)}, u32[]{:S(2)}, u32[]{:S(2)}) collective-permute-start(f32[8,1536]{1,0:T(8,128)S(1)} %get-tuple-element.71), channel_id=1, source_target_pairs={{0,4},{1,5},{2,6},{3,7},{4,0},{5,1},{6,2},{7,3},{8,12},{9,13},{10,... | collective-permute-start | bytes 147464 | tf_op jit(solution)/shard_map/ppermute | solution.py:689
  66.5 5.0 %collective-permute-start.20 = (f32[8,1536]{1,0:T(8,128)S(1)}, f32[8,1536]{1,0:T(8,128)S(1)}, u32[]{:S(2)}, u32[]{:S(2)}) collective-permute-start(f32[8,1536]{1,0:T(8,128)S(1)} %get-tuple-element.72), channel_id=1, source_target_pairs={{0,6},{1,7},{2,4},{3,5},{4,2},{5,3},{6,0},{7,1},{8,14},{9,15},{10,... | collective-permute-start | bytes 147464 | tf_op jit(solution)/shard_map/ppermute | solution.py:689
  71.5 7.1 %collective-permute-start.23 = (f32[8,1536]{1,0:T(8,128)S(1)}, f32[8,1536]{1,0:T(8,128)S(1)}, u32[]{:S(2)}, u32[]{:S(2)}) collective-permute-start(f32[8,1536]{1,0:T(8,128)S(1)} %shard_map.128.refs_0_), channel_id=1, source_target_pairs={{0,24},{8,16},{16,8},{24,0},{1,25},{9,17},{17,9},{25,1},{2,26},{10... | collective-permute-start | bytes 147464 | tf_op jit(solution)/shard_map/ppermute | solution.py:95
  73.2 5.6 %collective-permute-start.22 = (f32[8,1536]{1,0:T(8,128)S(1)}, f32[8,1536]{1,0:T(8,128)S(1)}, u32[]{:S(2)}, u32[]{:S(2)}) collective-permute-start(f32[8,1536]{1,0:T(8,128)S(1)} %shard_map.128.refs_0_), channel_id=1, source_target_pairs={{0,16},{8,24},{16,0},{24,8},{1,17},{9,25},{17,1},{25,9},{2,18},{10... | collective-permute-start | bytes 147464 | tf_op jit(solution)/shard_map/ppermute | solution.py:95
  74.8 4.2 %collective-permute-start.21 = (f32[8,1536]{1,0:T(8,128)S(1)}, f32[8,1536]{1,0:T(8,128)S(1)}, u32[]{:S(2)}, u32[]{:S(2)}) collective-permute-start(f32[8,1536]{1,0:T(8,128)S(1)} %shard_map.128.refs_0_), channel_id=1, source_target_pairs={{0,8},{8,0},{16,24},{24,16},{1,9},{9,1},{17,25},{25,17},{2,10},{10... | collective-permute-start | bytes 147464 | tf_op jit(solution)/shard_map/ppermute | solution.py:95
  79.0 8.7 %collective-permute-start.26 = (f32[8,1536]{1,0:T(8,128)S(1)}, f32[8,1536]{1,0:T(8,128)S(1)}, u32[]{:S(2)}, u32[]{:S(2)}) collective-permute-start(f32[8,1536]{1,0:T(8,128)S(1)} %shard_map.129.refs_1_), channel_id=1, source_target_pairs={{0,6},{1,7},{2,4},{3,5},{4,2},{5,3},{6,0},{7,1},{8,14},{9,15},{10,... | collective-permute-start | bytes 147464 | tf_op jit(solution)/shard_map/ppermute | solution.py:95
  79.5 8.2 %collective-permute-start.25 = (f32[8,1536]{1,0:T(8,128)S(1)}, f32[8,1536]{1,0:T(8,128)S(1)}, u32[]{:S(2)}, u32[]{:S(2)}) collective-permute-start(f32[8,1536]{1,0:T(8,128)S(1)} %shard_map.129.refs_1_), channel_id=1, source_target_pairs={{0,4},{1,5},{2,6},{3,7},{4,0},{5,1},{6,2},{7,3},{8,12},{9,13},{10,... | collective-permute-start | bytes 147464 | tf_op jit(solution)/shard_map/ppermute | solution.py:95
  81.0 6.7 %collective-permute-start.24 = (f32[8,1536]{1,0:T(8,128)S(1)}, f32[8,1536]{1,0:T(8,128)S(1)}, u32[]{:S(2)}, u32[]{:S(2)}) collective-permute-start(f32[8,1536]{1,0:T(8,128)S(1)} %shard_map.129.refs_1_), channel_id=1, source_target_pairs={{0,2},{1,3},{2,0},{3,1},{4,6},{5,7},{6,4},{7,5},{8,10},{9,11},{10,... | collective-permute-start | bytes 147464 | tf_op jit(solution)/shard_map/ppermute | solution.py:95
  88.3 1.5 %collective-permute-start.27 = (f32[4,8,1536]{2,1,0:T(8,128)S(1)}, f32[4,8,1536]{2,1,0:T(8,128)S(1)}, u32[]{:S(2)}, u32[]{:S(2)}) collective-permute-start(f32[4,8,1536]{2,1,0:T(8,128)S(1)} %shard_map.130.refs_1_), channel_id=1, source_target_pairs={{0,1},{1,0},{2,3},{3,2},{4,5},{5,4},{6,7},{7,6},{8,9},{9,8},{10,11... | collective-permute-start | bytes 589832 | tf_op jit(solution)/shard_map/ppermute | solution.py:95

commit v5 on v4

--- a/solution.py
+++ b/solution.py
@@ -218,9 +218,9 @@
     pad_ref[REACH : REACH + tall, :broad] = field
 
 
-def convolve(pad_ref, kernel_ref, mix_ref, flipped):
+def convolve(pad_ref, kernel_ref, emit, flipped):
     taps = 2 * REACH + 1
-    tall, broad, lanes = mix_ref.shape
+    tall, broad, lanes = pad_ref.shape[0] - 2 * REACH, pad_ref.shape[1] - EDGE, pad_ref.shape[2]
     ring = broad + EDGE
     sub = 128
     for start in range(0, lanes, sub):
@@ -234,12 +234,13 @@
                     tap = taps * a + b
                     if flipped:
                         tap = taps * taps - 1 - tap
-                    term = rows[a] * kernel_ref[tap : tap + 1, at]
+                    row = rows[a][:broad] if b == REACH else rows[a]
+                    term = row * kernel_ref[tap : tap + 1, at]
                     part = term if part is None else part + term
                 if b != REACH:
                     part = pltpu.roll(part, (REACH - b) % ring, 0)
                 total = part[:broad] if total is None else total + part[:broad]
-            mix_ref[y, :, at] = total
+            emit(y, at, total)
 
 
 def read_field(ref, place, at=slice(None)):
@@ -289,7 +290,6 @@
     deltas = routes.sources(place, direct)
     arrived, refs = refs[2 : 2 + len(deltas)], refs[2 + len(deltas) :]
     dw_ref, pw_ref, mixed_ref, merged_ref, padded_ref = refs[:5]
-    mix_ref = refs[-1]
     mask = same_head(head_dim)
     per = mixed_ref.shape[2] // LANES
     size = REACH * field_ref.shape[3]
@@ -303,16 +303,21 @@
             edges = [ref[:size, within] for ref in arrived]
         padded = padded_ref.at[member, :, :, within]
         fill_padded(padded, field, edges, deltas, place)
-        convolve(padded, dw_ref.at[:, at], mix_ref, False)
-        mixed = mix_ref[...].reshape(-1, LANES)
-        mixed_ref[member, :, within] = mixed
+        target = mixed_ref.at[member, :, within]
+        broad = field.shape[1]
+
+        def emit(y, sub, total):
+            target[y * broad : (y + 1) * broad, sub] = total
+
+        convolve(padded, dw_ref.at[:, at], emit, False)
+        mixed = target[...]
         merged_ref[member, :, within] = dot(split(mixed), split(spread(pw_ref[:, at], mask)), NN)
         return carry
 
-    lax.fori_loop(0, count * per, one_block, 0)
+    lax.fori_loop(0, count * per, one_block, 0, unroll=2)
     if first == 0:
         return
-    state_ref = refs[-2]
+    state_ref = refs[5]
     for at in parts_of(state_ref.shape[1]):
         keys = jnp.maximum(merged_ref[0, :, at], 0.0)
         state = gather_blocks(dot(split(keys), split(merged_ref[1, :, at]), TN), mask, head_dim)
@@ -437,13 +442,14 @@
 
         def one_row(y, totals):
             grad = gmix_ref[member, pl.ds(pl.multiple_of(y * broad, broad), broad), at]
-            grad = jnp.concatenate([grad, jnp.zeros((EDGE, sub), F32)], axis=0)
-            moved = [grad if b == REACH else pltpu.roll(grad, (b - REACH) % ring, 0) for b in range(taps)]
+            longer = jnp.concatenate([grad, jnp.zeros((EDGE, sub), F32)], axis=0)
+            moved = [grad if b == REACH else pltpu.roll(longer, (b - REACH) % ring, 0) for b in range(taps)]
             new = list(totals)
             for a in range(taps):
                 row = padded_ref[member, y + a, :, at]
                 for b in range(taps):
-                    term = (row * moved[b]).reshape(ring // 8, 8, sub)
+                    term = row[: moved[b].shape[0]] * moved[b]
+                    term = term.reshape(term.shape[0] // 8, 8, sub)
                     new[taps * a + b] = new[taps * a + b] + jnp.sum(term, axis=0)
             return tuple(new)
 
@@ -510,7 +516,7 @@
 def backward_kernel(routes, first, *refs):
     layout, gmix_ref = refs[:2]
     arrived = refs[2 : 2 + routes.arriving]
-    dw_ref, grad0_ref, out_ref, pad_ref, mix_ref, done_ref, sems = refs[2 + routes.arriving :]
+    dw_ref, grad0_ref, out_ref, pad_ref, done_ref, sems = refs[2 + routes.arriving :]
     place = Place(layout)
     deltas = routes.sources(place)
     tall, broad = out_ref.shape[2:4]
@@ -523,9 +529,13 @@
         edges = [ref[pl.ds(begin, size), within] for ref in arrived]
         field = gmix_ref[member, :, within].reshape(tall, broad, LANES)
         fill_padded(pad_ref, field, edges, deltas, place)
-        convolve(pad_ref, dw_ref.at[:, at], mix_ref, True)
-        grad = mix_ref[...] + grad0_ref[member, :, within].reshape(tall, broad, LANES)
-        done_ref[block] = jnp.where(place.live, grad, 0.0).astype(BF16)
+        grad0 = grad0_ref.at[member, :, within]
+
+        def emit(y, sub, total):
+            total = total + grad0[y * broad : (y + 1) * broad, sub]
+            done_ref[block, y, :, sub] = jnp.where(place.live, total, 0.0).astype(BF16)
+
+        convolve(pad_ref, dw_ref.at[:, at], emit, True)
         write(block).start()
         return carry
 
@@ -589,7 +599,6 @@
     def narrow(*dims):
         return jax.ShapeDtypeStruct(dims, BF16)
 
-    mix_scratch = [pltpu.VMEM((tall, broad, LANES), F32)]
     low, high = edge, edge + packed
 
     sent_kv = pl.pallas_call(
@@ -620,7 +629,6 @@
             + [wide(count, *padded_shape, third)]
             + [narrow(packed, third)] * (first > 0),
             (layout, qkv, *halo, dw_weight, pw_weight),
-            mix_scratch,
         )
 
     mixed_kv, merged_kv, padded_kv, state = forward(1, 2, halo_kv, True)
@@ -710,7 +718,6 @@
             pltpu.HBM((1, 1, tall, broad, channels), BF16),
             (layout, gmix, *halo_back, dw_weight, grad0),
             [pltpu.VMEM((*padded_shape, LANES), F32)]
-            + mix_scratch
             + [pltpu.VMEM((blocks, tall, broad, LANES), BF16), pltpu.SemaphoreType.DMA((blocks,))],
             out_space=pltpu.HBM,
             onto=onto,
@@ -722,7 +729,7 @@
     if halves:
         total = call(0.3, part(sum_kernel, 1.0), share_shape, [shares[0]] + moved)
         total = call(
-            0.3, part(sum_kernel, norm), share_shape, [total] + exchange(total, "tile"), after=(grad_query,)
+            0.3, part(sum_kernel, norm), share_shape, [total] + exchange(total, "tile"), after=(grad_query, grad0_kv)
         )
         quarters = call(
             0.5,

time: 91.4 us -> 90.5 us (level)
  transfers between devices with their start and end apart: 28 -> 28, of which waited for: 12 -> 9; matrix products, arithmetic and copies ran while one was open for 0% -> 0% of each run, Pallas kernels for 27% -> 27%
where the time goes in v5:
time: 90.5 us; the launch traced here: 90.3 us
  starting transfers between devices  35.3 us (39%)
  Pallas kernels  32.1 us (35%)
  waiting for transfers between devices  19.2 us (21%)
  between operations  2.94 us (3%)
    pallas_call x19, Pallas kernels, call(): pl.pallas_call(body, in_specs=[pl.BlockSpec(memory_space=space) for space...  31 us
    ppermute x15, starting transfers between devices, exchange(): lax.ppermute(value, axis, [(s, s ^ m) for s in range(count)])  17.5 us
    ppermute x4, starting transfers between devices, move_direct(): lax.ppermute(part, 'tile', list(enumerate(to)))  8.26 us
    ppermute x4, starting transfers between devices, move(): lax.ppermute(part, 'tile', [(s, s ^ m) for s in range(count)])  5.38 us
    ppermute x3, waiting for transfers between devices, local(): lax.ppermute(share, 'img', [(s, s ^ 2 * m) for s in range(groups)])  4.54 us
    ppermute x4, waiting for transfers between devices, move_direct(): lax.ppermute(part, 'tile', list(enumerate(to)))  4.17 us
    ppermute x4, waiting for transfers between devices, move(): lax.ppermute(part, 'tile', [(s, s ^ m) for s in range(count)])  4.12 us
    ppermute x2, waiting for transfers between devices, move(): lax.ppermute(hand_on(near, far), 'tile', [(s, s ^ 1) for s in range(count)])  3.97 us
  transfers between devices with their start and end apart: 28, of which 9 were waited for; matrix products, arithmetic and copies ran while one was open for 0% of the time, Pallas kernels for 27%

profile of v5, /device:TPU:0, one launch (start us, length us, event | category | flops | bytes accessed | tf_op | source)
XLA Modules:
  0.0 90.3 jit_solution(14746522111994306714)
XLA Ops:
  4.6 3.1 %collective-permute-start = (bf16[2,64,512]{2,1,0:T(8,128)(2,1)S(1)}, bf16[2,64,512]{2,1,0:T(8,128)(2,1)S(1)}, u32[]{:S(2)}, u32[]{:S(2)}) collective-permute-start(bf16[2,64,512]{2,1,0:T(8,128)(2,1)S(1)} %get-tuple-element.39), channel_id=1, source_target_pairs={{0,8},{8,0},{16,24},{24,16},{1,9},{9,1},{17,25},{25,17},{2,10},{10... | collective-permute-start | bytes 393224 | tf_op jit(solution)/shard_map/ppermute | solution.py:89
  7.7 2.6 %collective-permute-start.1 = (bf16[2,64,512]{2,1,0:T(8,128)(2,1)S(1)}, bf16[2,64,512]{2,1,0:T(8,128)(2,1)S(1)}, u32[]{:S(2)}, u32[]{:S(2)}) collective-permute-start(bf16[2,64,512]{2,1,0:T(8,128)(2,1)S(1)} %get-tuple-element.40), channel_id=1, source_target_pairs={{0,16},{8,24},{16,0},{24,8},{1,17},{9,25},{17,1},{25,9},{2,18},{10... | collective-permute-start | bytes 393224 | tf_op jit(solution)/shard_map/ppermute | solution.py:89
  10.9 1.9 %collective-permute-start.3 = (bf16[2,16,512]{2,1,0:T(8,128)(2,1)S(1)}, bf16[2,16,512]{2,1,0:T(8,128)(2,1)S(1)}, u32[]{:S(2)}, u32[]{:S(2)}) collective-permute-start(bf16[2,16,512]{2,1,0:T(8,128)(2,1)S(1)} %get-tuple-element.42), channel_id=1, source_target_pairs={{0,24},{8,8},{16,16},{24,0},{1,25},{9,9},{17,17},{25,1},{2,26},{10... | collective-permute-start | bytes 98312 | tf_op jit(solution)/shard_map/ppermute | solution.py:89
  12.9 1.6 %shard_map.113 = (bf16[144,512]{1,0:T(8,128)(2,1)S(1)}, bf16[144,512]{1,0:T(8,128)(2,1)S(1)}, f32[25,1536]{1,0:T(8,128)S(1)}, f32[32,1536]{1,0:T(8,128)S(1)}) custom-call(s32[8]{0:T(128)S(1)} %concatenate.3.layout.refs_0_, bf16[1,1,8,32,1536]{4,3,2,1,0:T(8,128)(2,1)S(1)} %copy-done, f32[25,1536]{1,0:T(8,128)} %refs_2_.1, f32[32,1536]{1,0:T(8,128)} %refs_3_.1), custom_call_target="tpu_custom_call" | custom-call | bytes 3690000 | tf_op jit(solution)/shard_map/pallas_call | solution.py:564
  14.5 4.2 %collective-permute-done.3.refs_5_ = bf16[2,16,512]{2,1,0:T(8,128)(2,1)S(1)} collective-permute-done((bf16[2,16,512]{2,1,0:T(8,128)(2,1)S(1)}, bf16[2,16,512]{2,1,0:T(8,128)(2,1)S(1)}, u32[]{:S(2)}, u32[]{:S(2)}) %collective-permute-start.3) | collective-permute-done | bytes 32800 | tf_op jit(solution)/shard_map/ppermute | solution.py:89
  18.7 2.9 %collective-permute-start.8 = (bf16[144,512]{1,0:T(8,128)(2,1)S(1)}, bf16[144,512]{1,0:T(8,128)(2,1)S(1)}, u32[]{:S(2)}, u32[]{:S(2)}) collective-permute-start(bf16[144,512]{1,0:T(8,128)(2,1)S(1)} %get-tuple-element.49), channel_id=1, source_target_pairs={{0,16},{8,24},{16,0},{24,8},{1,17},{9,25},{17,1},{25,9},{2,18},{10... | collective-permute-start | bytes 442376 | tf_op jit(solution)/shard_map/ppermute | solution.py:81
  21.6 4.6 %shard_map.114 = (f32[2,256,512]{2,1,0:T(8,128)S(1)}, f32[2,256,512]{2,1,0:T(8,128)S(1)}, f32[2,12,40,512]{3,2,1,0:T(8,128)S(1)}, bf16[80,512]{1,0:T(8,128)(2,1)S(1)}) custom-call(s32[8]{0:T(128)S(1)} %concatenate.3.layout.refs_0_, bf16[1,1,8,32,1536]{4,3,2,1,0:T(8,128)(2,1)S(1)} %copy-done, bf16[2,64,512]{2,1,0:T(8,128)(2,1)S(1)} %collective-permute-done.refs_2_, ...), custom_call_target="tpu_custom_call" | custom-call | bytes 22140000 | tf_op jit(solution)/shard_map/pallas_call | solution.py:564
  26.2 1.8 %collective-permute-done.8.refs_0_.refs_3_ = bf16[144,512]{1,0:T(8,128)(2,1)S(1)} collective-permute-done((bf16[144,512]{1,0:T(8,128)(2,1)S(1)}, bf16[144,512]{1,0:T(8,128)(2,1)S(1)}, u32[]{:S(2)}, u32[]{:S(2)}) %collective-permute-start.8) | collective-permute-done | bytes 147488 | tf_op jit(solution)/shard_map/ppermute | solution.py:81
  28.3 2.0 %collective-permute-start.6 = (bf16[80,512]{1,0:T(8,128)(2,1)S(1)}, bf16[80,512]{1,0:T(8,128)(2,1)S(1)}, u32[]{:S(2)}, u32[]{:S(2)}) collective-permute-start(bf16[80,512]{1,0:T(8,128)(2,1)S(1)} %get-tuple-element.45.refs_1_), channel_id=1, source_target_pairs={{0,24},{8,16},{16,8},{24,0},{1,25},{9,17},{17,9},{25,1},{2,26},{10... | collective-permute-start | bytes 245768 | tf_op jit(solution)/shard_map/ppermute | solution.py:95
  32.7 4.0 %collective-permute-done.9.refs_4_ = bf16[144,512]{1,0:T(8,128)(2,1)S(1)} collective-permute-done((bf16[144,512]{1,0:T(8,128)(2,1)S(1)}, bf16[144,512]{1,0:T(8,128)(2,1)S(1)}, u32[]{:S(2)}, u32[]{:S(2)}) %collective-permute-start.9) | collective-permute-done | bytes 147488 | tf_op jit(solution)/shard_map/ppermute | solution.py:83
  36.7 2.3 %shard_map.117 = (f32[1,256,512]{2,1,0:T(8,128)S(1)}, f32[1,256,512]{2,1,0:T(8,128)S(1)}, f32[1,12,40,512]{3,2,1,0:T(8,128)S(1)}) custom-call(s32[8]{0:T(128)S(1)} %concatenate.3.layout.refs_0_, bf16[1,1,8,32,1536]{4,3,2,1,0:T(8,128)(2,1)S(1)} %copy-done, bf16[144,512]{1,0:T(8,128)(2,1)S(1)} %collective-permute-done.7.refs_2_, ...), custom_call_target="tpu_custom_call" | custom-call | bytes 11070000 | tf_op jit(solution)/shard_map/pallas_call | solution.py:564
  39.0 2.5 %shard_map.118 = (bf16[80,512]{1,0:T(8,128)(2,1)S(1)}, f32[1,256,512]{2,1,0:T(8,128)S(1)}, f32[1,32,512]{2,1,0:T(8,128)S(1)}) custom-call(s32[8]{0:T(128)S(1)} %concatenate.3.layout.refs_0_, bf16[80,512]{1,0:T(8,128)(2,1)S(1)} %get-tuple-element.45.refs_1_, bf16[80,512]{1,0:T(8,128)(2,1)S(1)} %collective-permute-done.4.refs_2_, ...), custom_call_target="tpu_custom_call" | custom-call | bytes 11070000 | tf_op jit(solution)/shard_map/pallas_call | solution.py:564
  41.5 1.9 %collective-permute-start.12 = (bf16[80,512]{1,0:T(8,128)(2,1)S(1)}, bf16[80,512]{1,0:T(8,128)(2,1)S(1)}, u32[]{:S(2)}, u32[]{:S(2)}) collective-permute-start(bf16[80,512]{1,0:T(8,128)(2,1)S(1)} %get-tuple-element.52.refs_7_.refs_1_), channel_id=1, source_target_pairs={{0,24},{8,16},{16,8},{24,0},{1,25},{9,17},{17,9},{25,1},{2,26},{10... | collective-permute-start | bytes 245768 | tf_op jit(solution)/shard_map/ppermute | solution.py:95
  43.5 2.5 %collective-permute-start.10 = (bf16[80,512]{1,0:T(8,128)(2,1)S(1)}, bf16[80,512]{1,0:T(8,128)(2,1)S(1)}, u32[]{:S(2)}, u32[]{:S(2)}) collective-permute-start(bf16[80,512]{1,0:T(8,128)(2,1)S(1)} %get-tuple-element.52.refs_7_.refs_1_), channel_id=1, source_target_pairs={{0,8},{8,0},{16,24},{24,16},{1,9},{9,1},{17,25},{25,17},{2,10},{10... | collective-permute-start | bytes 245768 | tf_op jit(solution)/shard_map/ppermute | solution.py:95
  46.0 2.1 %shard_map.120 = (f32[4,8,512]{2,1,0:T(8,128)S(1)}, f32[4,8,512]{2,1,0:T(8,128)S(1)}) custom-call(s32[8]{0:T(128)S(1)} %concatenate.3.layout.refs_0_, f32[1,12,40,512]{3,2,1,0:T(8,128)S(1)} %get-tuple-element.57.refs_1_, f32[1,256,512]{2,1,0:T(8,128)S(1)} %get-tuple-element.55.refs_2_.refs_8_.refs_1_, f32[1,32,512]{2,1,0:T(8,128)S(1)} %get-tuple-element.58.refs_3_), custom_call_target="tpu_custom_call" | custom-call | bytes 7380000 | tf_op jit(solution)/shard_map/pallas_call | solution.py:564
  48.0 1.8 %shard_map.119 = (f32[1,256,512]{2,1,0:T(8,128)S(1)}, bf16[80,512]{1,0:T(8,128)(2,1)S(1)}) custom-call(s32[8]{0:T(128)S(1)} %concatenate.3.layout.refs_0_, bf16[144,512]{1,0:T(8,128)(2,1)S(1)} %get-tuple-element.48.refs_1_, bf16[144,512]{1,0:T(8,128)(2,1)S(1)} %collective-permute-done.7.refs_2_, bf16[144,512]{1,0:T(8,128)(2,1)S(1)} %collective-permute-done.8.refs_0_.refs_3_, ...), custom_call_target="tpu_custom_call" | custom-call | bytes 9225000 | tf_op jit(solution)/shard_map/pallas_call | solution.py:564
  49.8 2.3 %shard_map.121 = (f32[2,256,512]{2,1,0:T(8,128)S(1)}, f32[2,32,512]{2,1,0:T(8,128)S(1)}, bf16[272,512]{1,0:T(8,128)(2,1)S(1)}, bf16[272,512]{1,0:T(8,128)(2,1)S(1)}) custom-call(s32[8]{0:T(128)S(1)} %concatenate.3.layout.refs_0_, bf16[80,512]{1,0:T(8,128)(2,1)S(1)} %get-tuple-element.52.refs_7_.refs_1_, bf16[80,512]{1,0:T(8,128)(2,1)S(1)} %collective-permute-done.10.refs_2_, ...), custom_call_target="tpu_custom_call" | custom-call | bytes 11070000 | tf_op jit(solution)/shard_map/pallas_call | solution.py:564
  53.3 1.3 %collective-permute-start.13 = (bf16[272,512]{1,0:T(8,128)(2,1)S(1)}, bf16[272,512]{1,0:T(8,128)(2,1)S(1)}, u32[]{:S(2)}, u32[]{:S(2)}) collective-permute-start(bf16[272,512]{1,0:T(8,128)(2,1)S(1)} %get-tuple-element.61.refs_1_), channel_id=1, source_target_pairs={{0,8},{8,0},{16,24},{24,16},{1,9},{9,1},{17,25},{25,17},{2,10},{10... | collective-permute-start | bytes 835592 | tf_op jit(solution)/shard_map/ppermute | solution.py:81
  54.6 3.6 %shard_map.122 = (f32[4,8,1024]{2,1,0:T(8,128)S(1)}, f32[4,8,1024]{2,1,0:T(8,128)S(1)}) custom-call(s32[8]{0:T(128)S(1)} %concatenate.3.layout.refs_0_, f32[2,12,40,512]{3,2,1,0:T(8,128)S(1)} %get-tuple-element.64.refs_1_, f32[2,256,512]{2,1,0:T(8,128)S(1)} %get-tuple-element.60.refs_2_.refs_1_, f32[2,32,512]{2,1,0:T(8,128)S(1)} %get-tuple-element.65.refs_3_), custom_call_target="tpu_custom_call" | custom-call | bytes 14760000 | tf_op jit(solution)/shard_map/pallas_call | solution.py:564
  60.3 2.4 %collective-permute-done.14.refs_0_.refs_3_ = bf16[272,512]{1,0:T(8,128)(2,1)S(1)} collective-permute-done((bf16[272,512]{1,0:T(8,128)(2,1)S(1)}, bf16[272,512]{1,0:T(8,128)(2,1)S(1)}, u32[]{:S(2)}, u32[]{:S(2)}) %collective-permute-start.14) | collective-permute-done | bytes 278560 | tf_op jit(solution)/shard_map/ppermute | solution.py:81
  63.0 1.5 %collective-permute-start.18 = (f32[8,1536]{1,0:T(8,128)S(1)}, f32[8,1536]{1,0:T(8,128)S(1)}, u32[]{:S(2)}, u32[]{:S(2)}) collective-permute-start(f32[8,1536]{1,0:T(8,128)S(1)} %get-tuple-element.70), channel_id=1, source_target_pairs={{0,2},{1,3},{2,0},{3,1},{4,6},{5,7},{6,4},{7,5},{8,10},{9,11},{10,... | collective-permute-start | bytes 147464 | tf_op jit(solution)/shard_map/ppermute | solution.py:697
  64.5 1.6 %collective-permute-start.19 = (f32[8,1536]{1,0:T(8,128)S(1)}, f32[8,1536]{1,0:T(8,128)S(1)}, u32[]{:S(2)}, u32[]{:S(2)}) collective-permute-start(f32[8,1536]{1,0:T(8,128)S(1)} %get-tuple-element.71), channel_id=1, source_target_pairs={{0,4},{1,5},{2,6},{3,7},{4,0},{5,1},{6,2},{7,3},{8,12},{9,13},{10,... | collective-permute-start | bytes 147464 | tf_op jit(solution)/shard_map/ppermute | solution.py:697
  67.2 1.4 %collective-permute-done.19.refs_2_ = f32[8,1536]{1,0:T(8,128)S(1)} collective-permute-done((f32[8,1536]{1,0:T(8,128)S(1)}, f32[8,1536]{1,0:T(8,128)S(1)}, u32[]{:S(2)}, u32[]{:S(2)}) %collective-permute-start.19) | collective-permute-done | bytes 49184 | tf_op jit(solution)/shard_map/ppermute | solution.py:697
  68.6 2.5 %collective-permute-done.20.refs_3_ = f32[8,1536]{1,0:T(8,128)S(1)} collective-permute-done((f32[8,1536]{1,0:T(8,128)S(1)}, f32[8,1536]{1,0:T(8,128)S(1)}, u32[]{:S(2)}, u32[]{:S(2)}) %collective-permute-start.20) | collective-permute-done | bytes 49184 | tf_op jit(solution)/shard_map/ppermute | solution.py:697
  71.0 2.0 %collective-permute-start.23 = (f32[8,1536]{1,0:T(8,128)S(1)}, f32[8,1536]{1,0:T(8,128)S(1)}, u32[]{:S(2)}, u32[]{:S(2)}) collective-permute-start(f32[8,1536]{1,0:T(8,128)S(1)} %shard_map.128.refs_0_), channel_id=1, source_target_pairs={{0,24},{8,16},{16,8},{24,0},{1,25},{9,17},{17,9},{25,1},{2,26},{10... | collective-permute-start | bytes 147464 | tf_op jit(solution)/shard_map/ppermute | solution.py:95
  73.0 1.3 %collective-permute-start.22 = (f32[8,1536]{1,0:T(8,128)S(1)}, f32[8,1536]{1,0:T(8,128)S(1)}, u32[]{:S(2)}, u32[]{:S(2)}) collective-permute-start(f32[8,1536]{1,0:T(8,128)S(1)} %shard_map.128.refs_0_), channel_id=1, source_target_pairs={{0,16},{8,24},{16,0},{24,8},{1,17},{9,25},{17,1},{25,9},{2,18},{10... | collective-permute-start | bytes 147464 | tf_op jit(solution)/shard_map/ppermute | solution.py:95
  76.5 2.6 %shard_map.126.refs_7_.refs_4_ = bf16[1,1,8,32,1536]{4,3,2,1,0:T(8,128)(2,1)} custom-call(s32[8]{0:T(128)S(1)} %concatenate.3.layout.refs_0_, f32[1,256,512]{2,1,0:T(8,128)S(1)} %get-tuple-element.55.refs_2_.refs_8_.refs_1_, bf16[272,512]{1,0:T(8,128)(2,1)S(1)} %collective-permute-done.13.refs_1_.refs_2_, ...), custom_call_target="tpu_custom_call" | custom-call | bytes 7380000 | tf_op jit(solution)/shard_map/pallas_call | solution.py:564
  79.7 1.5 %collective-permute-start.25 = (f32[8,1536]{1,0:T(8,128)S(1)}, f32[8,1536]{1,0:T(8,128)S(1)}, u32[]{:S(2)}, u32[]{:S(2)}) collective-permute-start(f32[8,1536]{1,0:T(8,128)S(1)} %shard_map.129.refs_1_), channel_id=1, source_target_pairs={{0,4},{1,5},{2,6},{3,7},{4,0},{5,1},{6,2},{7,3},{8,12},{9,13},{10,... | collective-permute-start | bytes 147464 | tf_op jit(solution)/shard_map/ppermute | solution.py:95
  81.2 1.5 %collective-permute-start.24 = (f32[8,1536]{1,0:T(8,128)S(1)}, f32[8,1536]{1,0:T(8,128)S(1)}, u32[]{:S(2)}, u32[]{:S(2)}) collective-permute-start(f32[8,1536]{1,0:T(8,128)S(1)} %shard_map.129.refs_1_), channel_id=1, source_target_pairs={{0,2},{1,3},{2,0},{3,1},{4,6},{5,7},{6,4},{7,5},{8,10},{9,11},{10,... | collective-permute-start | bytes 147464 | tf_op jit(solution)/shard_map/ppermute | solution.py:95
  82.8 4.1 %shard_map.127.refs_5_ = bf16[1,1,8,32,1536]{4,3,2,1,0:T(8,128)(2,1)} custom-call(s32[8]{0:T(128)S(1)} %concatenate.3.layout.refs_0_, f32[2,256,512]{2,1,0:T(8,128)S(1)} %get-tuple-element.60.refs_2_.refs_1_, bf16[272,512]{1,0:T(8,128)(2,1)S(1)} %collective-permute-done.13.refs_1_.refs_2_, ...), custom_call_target="tpu_custom_call", output_to_operand_aliasing={{}: (7, {})} | custom-call | bytes 14760000 | tf_op jit(solution)/shard_map/pallas_call | solution.py:564
  87.5 1.4 %collective-permute-done.27.refs_2_ = f32[4,8,1536]{2,1,0:T(8,128)S(1)} collective-permute-done((f32[4,8,1536]{2,1,0:T(8,128)S(1)}, f32[4,8,1536]{2,1,0:T(8,128)S(1)}, u32[]{:S(2)}, u32[]{:S(2)}) %collective-permute-start.27) | collective-permute-done | bytes 196640 | tf_op jit(solution)/shard_map/ppermute | solution.py:95
  89.0 1.3 %shard_map.131 = (f32[25,1536]{1,0:T(8,128)}, f32[32,1536]{1,0:T(8,128)}) custom-call(s32[8]{0:T(128)S(1)} %concatenate.3.layout.refs_0_, f32[4,8,1536]{2,1,0:T(8,128)S(1)} %shard_map.130.refs_1_, f32[4,8,1536]{2,1,0:T(8,128)S(1)} %collective-permute-done.27.refs_2_), custom_call_target="tpu_custom_call" | custom-call | bytes 2952000 | tf_op jit(solution)/shard_map/pallas_call | solution.py:564
  (49 shorter events, 13.5 us)
Async XLA Ops:
  0.6 12.2 %copy-start = (bf16[1,1,8,32,1536]{4,3,2,1,0:T(8,128)(2,1)S(1)}, bf16[1,1,8,32,1536]{4,3,2,1,0:T(8,128)(2,1)}, u32[]{:S(2)}) copy-start(bf16[1,1,8,32,1536]{4,3,2,1,0:T(8,128)(2,1)} %refs_5_.3) | copy-start | bytes 2359300
  4.6 14.1 %collective-permute-start = (bf16[2,64,512]{2,1,0:T(8,128)(2,1)S(1)}, bf16[2,64,512]{2,1,0:T(8,128)(2,1)S(1)}, u32[]{:S(2)}, u32[]{:S(2)}) collective-permute-start(bf16[2,64,512]{2,1,0:T(8,128)(2,1)S(1)} %get-tuple-element.39), channel_id=1, source_target_pairs={{0,8},{8,0},{16,24},{24,16},{1,9},{9,1},{17,25},{25,17},{2,10},{10... | collective-permute-start | bytes 393224 | tf_op jit(solution)/shard_map/ppermute | solution.py:89
  7.7 11.0 %collective-permute-start.1 = (bf16[2,64,512]{2,1,0:T(8,128)(2,1)S(1)}, bf16[2,64,512]{2,1,0:T(8,128)(2,1)S(1)}, u32[]{:S(2)}, u32[]{:S(2)}) collective-permute-start(bf16[2,64,512]{2,1,0:T(8,128)(2,1)S(1)} %get-tuple-element.40), channel_id=1, source_target_pairs={{0,16},{8,24},{16,0},{24,8},{1,17},{9,25},{17,1},{25,9},{2,18},{10... | collective-permute-start | bytes 393224 | tf_op jit(solution)/shard_map/ppermute | solution.py:89
  10.2 8.4 %collective-permute-start.2 = (bf16[2,64,512]{2,1,0:T(8,128)(2,1)S(1)}, bf16[2,64,512]{2,1,0:T(8,128)(2,1)S(1)}, u32[]{:S(2)}, u32[]{:S(2)}) collective-permute-start(bf16[2,64,512]{2,1,0:T(8,128)(2,1)S(1)} %get-tuple-element.41), channel_id=1, source_target_pairs={{0,0},{8,16},{16,8},{24,24},{1,1},{9,17},{17,9},{25,25},{2,2},{10,... | collective-permute-start | bytes 393224 | tf_op jit(solution)/shard_map/ppermute | solution.py:89
  10.9 7.7 %collective-permute-start.3 = (bf16[2,16,512]{2,1,0:T(8,128)(2,1)S(1)}, bf16[2,16,512]{2,1,0:T(8,128)(2,1)S(1)}, u32[]{:S(2)}, u32[]{:S(2)}) collective-permute-start(bf16[2,16,512]{2,1,0:T(8,128)(2,1)S(1)} %get-tuple-element.42), channel_id=1, source_target_pairs={{0,24},{8,8},{16,16},{24,0},{1,25},{9,9},{17,17},{25,1},{2,26},{10... | collective-permute-start | bytes 98312 | tf_op jit(solution)/shard_map/ppermute | solution.py:89
  18.7 20.3 %copy-start.1 = (bf16[1,1,8,32,1024]{4,3,2,1,0:T(8,128)(2,1)S(1)}, bf16[1,1,8,32,1024]{4,3,2,1,0:T(8,128)(2,1)}, u32[]{:S(2)}) copy-start(bf16[1,1,8,32,1024]{4,3,2,1,0:T(8,128)(2,1)} %refs_6_.1) | copy-start | bytes 1572868
  18.7 9.3 %collective-permute-start.8 = (bf16[144,512]{1,0:T(8,128)(2,1)S(1)}, bf16[144,512]{1,0:T(8,128)(2,1)S(1)}, u32[]{:S(2)}, u32[]{:S(2)}) collective-permute-start(bf16[144,512]{1,0:T(8,128)(2,1)S(1)} %get-tuple-element.49), channel_id=1, source_target_pairs={{0,16},{8,24},{16,0},{24,8},{1,17},{9,25},{17,1},{25,9},{2,18},{10... | collective-permute-start | bytes 442376 | tf_op jit(solution)/shard_map/ppermute | solution.py:81
  21.6 11.2 %collective-permute-start.7 = (bf16[144,512]{1,0:T(8,128)(2,1)S(1)}, bf16[144,512]{1,0:T(8,128)(2,1)S(1)}, u32[]{:S(2)}, u32[]{:S(2)}) collective-permute-start(bf16[144,512]{1,0:T(8,128)(2,1)S(1)} %get-tuple-element.48.refs_1_), channel_id=1, source_target_pairs={{0,8},{8,0},{16,24},{24,16},{1,9},{9,1},{17,25},{25,17},{2,10},{10... | collective-permute-start | bytes 442376 | tf_op jit(solution)/shard_map/ppermute | solution.py:81
  28.0 8.7 %collective-permute-start.9 = (bf16[144,512]{1,0:T(8,128)(2,1)S(1)}, bf16[144,512]{1,0:T(8,128)(2,1)S(1)}, u32[]{:S(2)}, u32[]{:S(2)}) collective-permute-start(bf16[144,512]{1,0:T(8,128)(2,1)S(1)} %shard_map.116), channel_id=1, source_target_pairs={{0,8},{8,0},{16,24},{24,16},{1,9},{9,1},{17,25},{25,17},{2,10},{10... | collective-permute-start | bytes 442376 | tf_op jit(solution)/shard_map/ppermute | solution.py:83
  28.3 10.6 %collective-permute-start.6 = (bf16[80,512]{1,0:T(8,128)(2,1)S(1)}, bf16[80,512]{1,0:T(8,128)(2,1)S(1)}, u32[]{:S(2)}, u32[]{:S(2)}) collective-permute-start(bf16[80,512]{1,0:T(8,128)(2,1)S(1)} %get-tuple-element.45.refs_1_), channel_id=1, source_target_pairs={{0,24},{8,16},{16,8},{24,0},{1,25},{9,17},{17,9},{25,1},{2,26},{10... | collective-permute-start | bytes 245768 | tf_op jit(solution)/shard_map/ppermute | solution.py:95
  30.4 8.6 %collective-permute-start.5 = (bf16[80,512]{1,0:T(8,128)(2,1)S(1)}, bf16[80,512]{1,0:T(8,128)(2,1)S(1)}, u32[]{:S(2)}, u32[]{:S(2)}) collective-permute-start(bf16[80,512]{1,0:T(8,128)(2,1)S(1)} %get-tuple-element.45.refs_1_), channel_id=1, source_target_pairs={{0,16},{8,24},{16,0},{24,8},{1,17},{9,25},{17,1},{25,9},{2,18},{10... | collective-permute-start | bytes 245768 | tf_op jit(solution)/shard_map/ppermute | solution.py:95
  31.5 7.4 %collective-permute-start.4 = (bf16[80,512]{1,0:T(8,128)(2,1)S(1)}, bf16[80,512]{1,0:T(8,128)(2,1)S(1)}, u32[]{:S(2)}, u32[]{:S(2)}) collective-permute-start(bf16[80,512]{1,0:T(8,128)(2,1)S(1)} %get-tuple-element.45.refs_1_), channel_id=1, source_target_pairs={{0,8},{8,0},{16,24},{24,16},{1,9},{9,1},{17,25},{25,17},{2,10},{10... | collective-permute-start | bytes 245768 | tf_op jit(solution)/shard_map/ppermute | solution.py:95
  41.5 8.3 %collective-permute-start.12 = (bf16[80,512]{1,0:T(8,128)(2,1)S(1)}, bf16[80,512]{1,0:T(8,128)(2,1)S(1)}, u32[]{:S(2)}, u32[]{:S(2)}) collective-permute-start(bf16[80,512]{1,0:T(8,128)(2,1)S(1)} %get-tuple-element.52.refs_7_.refs_1_), channel_id=1, source_target_pairs={{0,24},{8,16},{16,8},{24,0},{1,25},{9,17},{17,9},{25,1},{2,26},{10... | collective-permute-start | bytes 245768 | tf_op jit(solution)/shard_map/ppermute | solution.py:95
  43.4 6.4 %collective-permute-start.11 = (bf16[80,512]{1,0:T(8,128)(2,1)S(1)}, bf16[80,512]{1,0:T(8,128)(2,1)S(1)}, u32[]{:S(2)}, u32[]{:S(2)}) collective-permute-start(bf16[80,512]{1,0:T(8,128)(2,1)S(1)} %get-tuple-element.52.refs_7_.refs_1_), channel_id=1, source_target_pairs={{0,16},{8,24},{16,0},{24,8},{1,17},{9,25},{17,1},{25,9},{2,18},{10... | collective-permute-start | bytes 245768 | tf_op jit(solution)/shard_map/ppermute | solution.py:95
  43.5 6.4 %collective-permute-start.10 = (bf16[80,512]{1,0:T(8,128)(2,1)S(1)}, bf16[80,512]{1,0:T(8,128)(2,1)S(1)}, u32[]{:S(2)}, u32[]{:S(2)}) collective-permute-start(bf16[80,512]{1,0:T(8,128)(2,1)S(1)} %get-tuple-element.52.refs_7_.refs_1_), channel_id=1, source_target_pairs={{0,8},{8,0},{16,24},{24,16},{1,9},{9,1},{17,25},{25,17},{2,10},{10... | collective-permute-start | bytes 245768 | tf_op jit(solution)/shard_map/ppermute | solution.py:95
  52.1 10.5 %collective-permute-start.14 = (bf16[272,512]{1,0:T(8,128)(2,1)S(1)}, bf16[272,512]{1,0:T(8,128)(2,1)S(1)}, u32[]{:S(2)}, u32[]{:S(2)}) collective-permute-start(bf16[272,512]{1,0:T(8,128)(2,1)S(1)} %get-tuple-element.62), channel_id=1, source_target_pairs={{0,16},{8,24},{16,0},{24,8},{1,17},{9,25},{17,1},{25,9},{2,18},{10... | collective-permute-start | bytes 835592 | tf_op jit(solution)/shard_map/ppermute | solution.py:81
  53.3 9.3 %collective-permute-start.13 = (bf16[272,512]{1,0:T(8,128)(2,1)S(1)}, bf16[272,512]{1,0:T(8,128)(2,1)S(1)}, u32[]{:S(2)}, u32[]{:S(2)}) collective-permute-start(bf16[272,512]{1,0:T(8,128)(2,1)S(1)} %get-tuple-element.61.refs_1_), channel_id=1, source_target_pairs={{0,8},{8,0},{16,24},{24,16},{1,9},{9,1},{17,25},{25,17},{2,10},{10... | collective-permute-start | bytes 835592 | tf_op jit(solution)/shard_map/ppermute | solution.py:81
  58.2 1.5 %collective-permute-start.16 = (f32[4,8,1024]{2,1,0:T(8,128)S(1)}, f32[4,8,1024]{2,1,0:T(8,128)S(1)}, u32[]{:S(2)}, u32[]{:S(2)}) collective-permute-start(f32[4,8,1024]{2,1,0:T(8,128)S(1)} %get-tuple-element.67), channel_id=1, source_target_pairs={{0,1},{1,0},{2,3},{3,2},{4,5},{5,4},{6,7},{7,6},{8,9},{9,8},{10,11... | collective-permute-start | bytes 393224 | tf_op jit(solution)/shard_map/ppermute | solution.py:95
  58.3 1.4 %collective-permute-start.15 = (f32[4,8,512]{2,1,0:T(8,128)S(1)}, f32[4,8,512]{2,1,0:T(8,128)S(1)}, u32[]{:S(2)}, u32[]{:S(2)}) collective-permute-start(f32[4,8,512]{2,1,0:T(8,128)S(1)} %get-tuple-element.59.refs_10_), channel_id=1, source_target_pairs={{0,1},{1,0},{2,3},{3,2},{4,5},{5,4},{6,7},{7,6},{8,9},{9,8},{10,11... | collective-permute-start | bytes 196616 | tf_op jit(solution)/shard_map/ppermute | solution.py:95
  62.7 12.8 %collective-permute-start.17 = (bf16[272,512]{1,0:T(8,128)(2,1)S(1)}, bf16[272,512]{1,0:T(8,128)(2,1)S(1)}, u32[]{:S(2)}, u32[]{:S(2)}) collective-permute-start(bf16[272,512]{1,0:T(8,128)(2,1)S(1)} %shard_map.124), channel_id=1, source_target_pairs={{0,8},{8,0},{16,24},{24,16},{1,9},{9,1},{17,25},{25,17},{2,10},{10... | collective-permute-start | bytes 835592 | tf_op jit(solution)/shard_map/ppermute | solution.py:83
  63.0 4.2 %collective-permute-start.18 = (f32[8,1536]{1,0:T(8,128)S(1)}, f32[8,1536]{1,0:T(8,128)S(1)}, u32[]{:S(2)}, u32[]{:S(2)}) collective-permute-start(f32[8,1536]{1,0:T(8,128)S(1)} %get-tuple-element.70), channel_id=1, source_target_pairs={{0,2},{1,3},{2,0},{3,1},{4,6},{5,7},{6,4},{7,5},{8,10},{9,11},{10,... | collective-permute-start | bytes 147464 | tf_op jit(solution)/shard_map/ppermute | solution.py:697
  64.5 4.1 %collective-permute-start.19 = (f32[8,1536]{1,0:T(8,128)S(1)}, f32[8,1536]{1,0:T(8,128)S(1)}, u32[]{:S(2)}, u32[]{:S(2)}) collective-permute-start(f32[8,1536]{1,0:T(8,128)S(1)} %get-tuple-element.71), channel_id=1, source_target_pairs={{0,4},{1,5},{2,6},{3,7},{4,0},{5,1},{6,2},{7,3},{8,12},{9,13},{10,... | collective-permute-start | bytes 147464 | tf_op jit(solution)/shard_map/ppermute | solution.py:697
  66.0 5.0 %collective-permute-start.20 = (f32[8,1536]{1,0:T(8,128)S(1)}, f32[8,1536]{1,0:T(8,128)S(1)}, u32[]{:S(2)}, u32[]{:S(2)}) collective-permute-start(f32[8,1536]{1,0:T(8,128)S(1)} %get-tuple-element.72), channel_id=1, source_target_pairs={{0,6},{1,7},{2,4},{3,5},{4,2},{5,3},{6,0},{7,1},{8,14},{9,15},{10,... | collective-permute-start | bytes 147464 | tf_op jit(solution)/shard_map/ppermute | solution.py:697
  71.0 8.1 %collective-permute-start.23 = (f32[8,1536]{1,0:T(8,128)S(1)}, f32[8,1536]{1,0:T(8,128)S(1)}, u32[]{:S(2)}, u32[]{:S(2)}) collective-permute-start(f32[8,1536]{1,0:T(8,128)S(1)} %shard_map.128.refs_0_), channel_id=1, source_target_pairs={{0,24},{8,16},{16,8},{24,0},{1,25},{9,17},{17,9},{25,1},{2,26},{10... | collective-permute-start | bytes 147464 | tf_op jit(solution)/shard_map/ppermute | solution.py:95
  73.0 6.1 %collective-permute-start.22 = (f32[8,1536]{1,0:T(8,128)S(1)}, f32[8,1536]{1,0:T(8,128)S(1)}, u32[]{:S(2)}, u32[]{:S(2)}) collective-permute-start(f32[8,1536]{1,0:T(8,128)S(1)} %shard_map.128.refs_0_), channel_id=1, source_target_pairs={{0,16},{8,24},{16,0},{24,8},{1,17},{9,25},{17,1},{25,9},{2,18},{10... | collective-permute-start | bytes 147464 | tf_op jit(solution)/shard_map/ppermute | solution.py:95
  74.3 4.9 %collective-permute-start.21 = (f32[8,1536]{1,0:T(8,128)S(1)}, f32[8,1536]{1,0:T(8,128)S(1)}, u32[]{:S(2)}, u32[]{:S(2)}) collective-permute-start(f32[8,1536]{1,0:T(8,128)S(1)} %shard_map.128.refs_0_), channel_id=1, source_target_pairs={{0,8},{8,0},{16,24},{24,16},{1,9},{9,1},{17,25},{25,17},{2,10},{10... | collective-permute-start | bytes 147464 | tf_op jit(solution)/shard_map/ppermute | solution.py:95
  79.2 7.6 %collective-permute-start.26 = (f32[8,1536]{1,0:T(8,128)S(1)}, f32[8,1536]{1,0:T(8,128)S(1)}, u32[]{:S(2)}, u32[]{:S(2)}) collective-permute-start(f32[8,1536]{1,0:T(8,128)S(1)} %shard_map.129.refs_1_), channel_id=1, source_target_pairs={{0,6},{1,7},{2,4},{3,5},{4,2},{5,3},{6,0},{7,1},{8,14},{9,15},{10,... | collective-permute-start | bytes 147464 | tf_op jit(solution)/shard_map/ppermute | solution.py:95
  79.7 7.1 %collective-permute-start.25 = (f32[8,1536]{1,0:T(8,128)S(1)}, f32[8,1536]{1,0:T(8,128)S(1)}, u32[]{:S(2)}, u32[]{:S(2)}) collective-permute-start(f32[8,1536]{1,0:T(8,128)S(1)} %shard_map.129.refs_1_), channel_id=1, source_target_pairs={{0,4},{1,5},{2,6},{3,7},{4,0},{5,1},{6,2},{7,3},{8,12},{9,13},{10,... | collective-permute-start | bytes 147464 | tf_op jit(solution)/shard_map/ppermute | solution.py:95
  81.2 5.6 %collective-permute-start.24 = (f32[8,1536]{1,0:T(8,128)S(1)}, f32[8,1536]{1,0:T(8,128)S(1)}, u32[]{:S(2)}, u32[]{:S(2)}) collective-permute-start(f32[8,1536]{1,0:T(8,128)S(1)} %shard_map.129.refs_1_), channel_id=1, source_target_pairs={{0,2},{1,3},{2,0},{3,1},{4,6},{5,7},{6,4},{7,5},{8,10},{9,11},{10,... | collective-permute-start | bytes 147464 | tf_op jit(solution)/shard_map/ppermute | solution.py:95
  87.5 1.5 %collective-permute-start.27 = (f32[4,8,1536]{2,1,0:T(8,128)S(1)}, f32[4,8,1536]{2,1,0:T(8,128)S(1)}, u32[]{:S(2)}, u32[]{:S(2)}) collective-permute-start(f32[4,8,1536]{2,1,0:T(8,128)S(1)} %shard_map.130.refs_1_), channel_id=1, source_target_pairs={{0,1},{1,0},{2,3},{3,2},{4,5},{5,4},{6,7},{7,6},{8,9},{9,8},{10,11... | collective-permute-start | bytes 589832 | tf_op jit(solution)/shard_map/ppermute | solution.py:95

commit v6 on v5

--- a/solution.py
+++ b/solution.py
@@ -158,7 +158,8 @@
 
 def pack_state(state, total):
     rows = jnp.concatenate([state, total, jnp.zeros((7, state.shape[1]), F32)], axis=0)
-    return jnp.concatenate(split(rows), axis=0)
+    high = rows.astype(BF16).astype(F32)
+    return jnp.concatenate([high, rows - high], axis=0).astype(BF16)
 
 
 def unpack_state(ref, offset):
@@ -454,7 +455,7 @@
             return tuple(new)
 
         zero = jnp.zeros((8, sub), F32)
-        totals = lax.fori_loop(0, tall, one_row, (zero,) * (taps * taps), unroll=2)
+        totals = lax.fori_loop(0, tall, one_row, (zero,) * (taps * taps), unroll=4)
         for tap in range(taps * taps):
             sum_ref[tap : tap + 1] = jnp.sum(totals[tap], axis=0, keepdims=True)
         sum_ref[taps * taps : start] = jnp.zeros((start - taps * taps, sub), F32)
@@ -543,7 +544,7 @@
         target = out_ref.at[0, 0, :, :, lanes_at(first * per + block)]
         return pltpu.make_async_copy(done_ref.at[block], target, sems.at[block])
 
-    lax.fori_loop(0, count * per, one_block, 0)
+    lax.fori_loop(0, count * per, one_block, 0, unroll=2)
     for block in range(count * per):
         write(block).wait()
 

time: 90.5 us -> 90.5 us (level)
  no operation moved by 1% of the time
where the time goes in v6:
time: 90.5 us; the launch traced here: 90.3 us
  starting transfers between devices  35.4 us (39%)
  Pallas kernels  32 us (35%)
  waiting for transfers between devices  19.1 us (21%)
  between operations  2.95 us (3%)
    pallas_call x19, Pallas kernels, call(): pl.pallas_call(body, in_specs=[pl.BlockSpec(memory_space=space) for space...  30.8 us
    ppermute x15, starting transfers between devices, exchange(): lax.ppermute(value, axis, [(s, s ^ m) for s in range(count)])  17.5 us
    ppermute x4, starting transfers between devices, move_direct(): lax.ppermute(part, 'tile', list(enumerate(to)))  8.26 us
    ppermute x4, starting transfers between devices, move(): lax.ppermute(part, 'tile', [(s, s ^ m) for s in range(count)])  5.4 us
    ppermute x3, waiting for transfers between devices, local(): lax.ppermute(share, 'img', [(s, s ^ 2 * m) for s in range(groups)])  4.53 us
    ppermute x4, waiting for transfers between devices, move_direct(): lax.ppermute(part, 'tile', list(enumerate(to)))  4.17 us
    ppermute x4, waiting for transfers between devices, move(): lax.ppermute(part, 'tile', [(s, s ^ m) for s in range(count)])  4.07 us
    ppermute x2, waiting for transfers between devices, move(): lax.ppermute(hand_on(near, far), 'tile', [(s, s ^ 1) for s in range(count)])  3.95 us
  transfers between devices with their start and end apart: 28, of which 9 were waited for; matrix products, arithmetic and copies ran while one was open for 0% of the time, Pallas kernels for 27%

profile of v6, /device:TPU:0, one launch (start us, length us, event | category | flops | bytes accessed | tf_op | source)
XLA Modules:
  0.0 90.3 jit_solution(1713537049696383403)
XLA Ops:
  4.6 3.1 %collective-permute-start = (bf16[2,64,512]{2,1,0:T(8,128)(2,1)S(1)}, bf16[2,64,512]{2,1,0:T(8,128)(2,1)S(1)}, u32[]{:S(2)}, u32[]{:S(2)}) collective-permute-start(bf16[2,64,512]{2,1,0:T(8,128)(2,1)S(1)} %get-tuple-element.39), channel_id=1, source_target_pairs={{0,8},{8,0},{16,24},{24,16},{1,9},{9,1},{17,25},{25,17},{2,10},{10... | collective-permute-start | bytes 393224 | tf_op jit(solution)/shard_map/ppermute | solution.py:89
  7.7 2.6 %collective-permute-start.1 = (bf16[2,64,512]{2,1,0:T(8,128)(2,1)S(1)}, bf16[2,64,512]{2,1,0:T(8,128)(2,1)S(1)}, u32[]{:S(2)}, u32[]{:S(2)}) collective-permute-start(bf16[2,64,512]{2,1,0:T(8,128)(2,1)S(1)} %get-tuple-element.40), channel_id=1, source_target_pairs={{0,16},{8,24},{16,0},{24,8},{1,17},{9,25},{17,1},{25,9},{2,18},{10... | collective-permute-start | bytes 393224 | tf_op jit(solution)/shard_map/ppermute | solution.py:89
  10.9 1.9 %collective-permute-start.3 = (bf16[2,16,512]{2,1,0:T(8,128)(2,1)S(1)}, bf16[2,16,512]{2,1,0:T(8,128)(2,1)S(1)}, u32[]{:S(2)}, u32[]{:S(2)}) collective-permute-start(bf16[2,16,512]{2,1,0:T(8,128)(2,1)S(1)} %get-tuple-element.42), channel_id=1, source_target_pairs={{0,24},{8,8},{16,16},{24,0},{1,25},{9,9},{17,17},{25,1},{2,26},{10... | collective-permute-start | bytes 98312 | tf_op jit(solution)/shard_map/ppermute | solution.py:89
  12.9 1.6 %shard_map.113 = (bf16[144,512]{1,0:T(8,128)(2,1)S(1)}, bf16[144,512]{1,0:T(8,128)(2,1)S(1)}, f32[25,1536]{1,0:T(8,128)S(1)}, f32[32,1536]{1,0:T(8,128)S(1)}) custom-call(s32[8]{0:T(128)S(1)} %concatenate.3.layout.refs_0_, bf16[1,1,8,32,1536]{4,3,2,1,0:T(8,128)(2,1)S(1)} %copy-done, f32[25,1536]{1,0:T(8,128)} %refs_2_.1, f32[32,1536]{1,0:T(8,128)} %refs_3_.1), custom_call_target="tpu_custom_call" | custom-call | bytes 3690000 | tf_op jit(solution)/shard_map/pallas_call | solution.py:565
  14.5 4.2 %collective-permute-done.3.refs_5_ = bf16[2,16,512]{2,1,0:T(8,128)(2,1)S(1)} collective-permute-done((bf16[2,16,512]{2,1,0:T(8,128)(2,1)S(1)}, bf16[2,16,512]{2,1,0:T(8,128)(2,1)S(1)}, u32[]{:S(2)}, u32[]{:S(2)}) %collective-permute-start.3) | collective-permute-done | bytes 32800 | tf_op jit(solution)/shard_map/ppermute | solution.py:89
  18.7 2.9 %collective-permute-start.8 = (bf16[144,512]{1,0:T(8,128)(2,1)S(1)}, bf16[144,512]{1,0:T(8,128)(2,1)S(1)}, u32[]{:S(2)}, u32[]{:S(2)}) collective-permute-start(bf16[144,512]{1,0:T(8,128)(2,1)S(1)} %get-tuple-element.49), channel_id=1, source_target_pairs={{0,16},{8,24},{16,0},{24,8},{1,17},{9,25},{17,1},{25,9},{2,18},{10... | collective-permute-start | bytes 442376 | tf_op jit(solution)/shard_map/ppermute | solution.py:81
  21.6 4.7 %shard_map.114 = (f32[2,256,512]{2,1,0:T(8,128)S(1)}, f32[2,256,512]{2,1,0:T(8,128)S(1)}, f32[2,12,40,512]{3,2,1,0:T(8,128)S(1)}, bf16[80,512]{1,0:T(8,128)(2,1)S(1)}) custom-call(s32[8]{0:T(128)S(1)} %concatenate.3.layout.refs_0_, bf16[1,1,8,32,1536]{4,3,2,1,0:T(8,128)(2,1)S(1)} %copy-done, bf16[2,64,512]{2,1,0:T(8,128)(2,1)S(1)} %collective-permute-done.refs_2_, ...), custom_call_target="tpu_custom_call" | custom-call | bytes 22140000 | tf_op jit(solution)/shard_map/pallas_call | solution.py:565
  26.2 1.7 %collective-permute-done.8.refs_0_.refs_3_ = bf16[144,512]{1,0:T(8,128)(2,1)S(1)} collective-permute-done((bf16[144,512]{1,0:T(8,128)(2,1)S(1)}, bf16[144,512]{1,0:T(8,128)(2,1)S(1)}, u32[]{:S(2)}, u32[]{:S(2)}) %collective-permute-start.8) | collective-permute-done | bytes 147488 | tf_op jit(solution)/shard_map/ppermute | solution.py:81
  28.4 2.0 %collective-permute-start.6 = (bf16[80,512]{1,0:T(8,128)(2,1)S(1)}, bf16[80,512]{1,0:T(8,128)(2,1)S(1)}, u32[]{:S(2)}, u32[]{:S(2)}) collective-permute-start(bf16[80,512]{1,0:T(8,128)(2,1)S(1)} %get-tuple-element.45.refs_1_), channel_id=1, source_target_pairs={{0,24},{8,16},{16,8},{24,0},{1,25},{9,17},{17,9},{25,1},{2,26},{10... | collective-permute-start | bytes 245768 | tf_op jit(solution)/shard_map/ppermute | solution.py:95
  32.7 4.0 %collective-permute-done.9.refs_4_ = bf16[144,512]{1,0:T(8,128)(2,1)S(1)} collective-permute-done((bf16[144,512]{1,0:T(8,128)(2,1)S(1)}, bf16[144,512]{1,0:T(8,128)(2,1)S(1)}, u32[]{:S(2)}, u32[]{:S(2)}) %collective-permute-start.9) | collective-permute-done | bytes 147488 | tf_op jit(solution)/shard_map/ppermute | solution.py:83
  36.7 2.3 %shard_map.117 = (f32[1,256,512]{2,1,0:T(8,128)S(1)}, f32[1,256,512]{2,1,0:T(8,128)S(1)}, f32[1,12,40,512]{3,2,1,0:T(8,128)S(1)}) custom-call(s32[8]{0:T(128)S(1)} %concatenate.3.layout.refs_0_, bf16[1,1,8,32,1536]{4,3,2,1,0:T(8,128)(2,1)S(1)} %copy-done, bf16[144,512]{1,0:T(8,128)(2,1)S(1)} %collective-permute-done.7.refs_2_, ...), custom_call_target="tpu_custom_call" | custom-call | bytes 11070000 | tf_op jit(solution)/shard_map/pallas_call | solution.py:565
  39.0 2.5 %shard_map.118 = (bf16[80,512]{1,0:T(8,128)(2,1)S(1)}, f32[1,256,512]{2,1,0:T(8,128)S(1)}, f32[1,32,512]{2,1,0:T(8,128)S(1)}) custom-call(s32[8]{0:T(128)S(1)} %concatenate.3.layout.refs_0_, bf16[80,512]{1,0:T(8,128)(2,1)S(1)} %get-tuple-element.45.refs_1_, bf16[80,512]{1,0:T(8,128)(2,1)S(1)} %collective-permute-done.4.refs_2_, ...), custom_call_target="tpu_custom_call" | custom-call | bytes 11070000 | tf_op jit(solution)/shard_map/pallas_call | solution.py:565
  41.5 2.0 %collective-permute-start.12 = (bf16[80,512]{1,0:T(8,128)(2,1)S(1)}, bf16[80,512]{1,0:T(8,128)(2,1)S(1)}, u32[]{:S(2)}, u32[]{:S(2)}) collective-permute-start(bf16[80,512]{1,0:T(8,128)(2,1)S(1)} %get-tuple-element.52.refs_7_.refs_1_), channel_id=1, source_target_pairs={{0,24},{8,16},{16,8},{24,0},{1,25},{9,17},{17,9},{25,1},{2,26},{10... | collective-permute-start | bytes 245768 | tf_op jit(solution)/shard_map/ppermute | solution.py:95
  43.5 2.5 %collective-permute-start.10 = (bf16[80,512]{1,0:T(8,128)(2,1)S(1)}, bf16[80,512]{1,0:T(8,128)(2,1)S(1)}, u32[]{:S(2)}, u32[]{:S(2)}) collective-permute-start(bf16[80,512]{1,0:T(8,128)(2,1)S(1)} %get-tuple-element.52.refs_7_.refs_1_), channel_id=1, source_target_pairs={{0,8},{8,0},{16,24},{24,16},{1,9},{9,1},{17,25},{25,17},{2,10},{10... | collective-permute-start | bytes 245768 | tf_op jit(solution)/shard_map/ppermute | solution.py:95
  46.0 2.0 %shard_map.120 = (f32[4,8,512]{2,1,0:T(8,128)S(1)}, f32[4,8,512]{2,1,0:T(8,128)S(1)}) custom-call(s32[8]{0:T(128)S(1)} %concatenate.3.layout.refs_0_, f32[1,12,40,512]{3,2,1,0:T(8,128)S(1)} %get-tuple-element.57.refs_1_, f32[1,256,512]{2,1,0:T(8,128)S(1)} %get-tuple-element.55.refs_2_.refs_8_.refs_1_, f32[1,32,512]{2,1,0:T(8,128)S(1)} %get-tuple-element.58.refs_3_), custom_call_target="tpu_custom_call" | custom-call | bytes 7380000 | tf_op jit(solution)/shard_map/pallas_call | solution.py:565
  47.9 1.8 %shard_map.119 = (f32[1,256,512]{2,1,0:T(8,128)S(1)}, bf16[80,512]{1,0:T(8,128)(2,1)S(1)}) custom-call(s32[8]{0:T(128)S(1)} %concatenate.3.layout.refs_0_, bf16[144,512]{1,0:T(8,128)(2,1)S(1)} %get-tuple-element.48.refs_1_, bf16[144,512]{1,0:T(8,128)(2,1)S(1)} %collective-permute-done.7.refs_2_, bf16[144,512]{1,0:T(8,128)(2,1)S(1)} %collective-permute-done.8.refs_0_.refs_3_, ...), custom_call_target="tpu_custom_call" | custom-call | bytes 9225000 | tf_op jit(solution)/shard_map/pallas_call | solution.py:565
  49.8 2.3 %shard_map.121 = (f32[2,256,512]{2,1,0:T(8,128)S(1)}, f32[2,32,512]{2,1,0:T(8,128)S(1)}, bf16[272,512]{1,0:T(8,128)(2,1)S(1)}, bf16[272,512]{1,0:T(8,128)(2,1)S(1)}) custom-call(s32[8]{0:T(128)S(1)} %concatenate.3.layout.refs_0_, bf16[80,512]{1,0:T(8,128)(2,1)S(1)} %get-tuple-element.52.refs_7_.refs_1_, bf16[80,512]{1,0:T(8,128)(2,1)S(1)} %collective-permute-done.10.refs_2_, ...), custom_call_target="tpu_custom_call" | custom-call | bytes 11070000 | tf_op jit(solution)/shard_map/pallas_call | solution.py:565
  52.1 1.3 %collective-permute-start.14 = (bf16[272,512]{1,0:T(8,128)(2,1)S(1)}, bf16[272,512]{1,0:T(8,128)(2,1)S(1)}, u32[]{:S(2)}, u32[]{:S(2)}) collective-permute-start(bf16[272,512]{1,0:T(8,128)(2,1)S(1)} %get-tuple-element.62), channel_id=1, source_target_pairs={{0,16},{8,24},{16,0},{24,8},{1,17},{9,25},{17,1},{25,9},{2,18},{10... | collective-permute-start | bytes 835592 | tf_op jit(solution)/shard_map/ppermute | solution.py:81
  54.6 3.6 %shard_map.122 = (f32[4,8,1024]{2,1,0:T(8,128)S(1)}, f32[4,8,1024]{2,1,0:T(8,128)S(1)}) custom-call(s32[8]{0:T(128)S(1)} %concatenate.3.layout.refs_0_, f32[2,12,40,512]{3,2,1,0:T(8,128)S(1)} %get-tuple-element.64.refs_1_, f32[2,256,512]{2,1,0:T(8,128)S(1)} %get-tuple-element.60.refs_2_.refs_1_, f32[2,32,512]{2,1,0:T(8,128)S(1)} %get-tuple-element.65.refs_3_), custom_call_target="tpu_custom_call" | custom-call | bytes 14760000 | tf_op jit(solution)/shard_map/pallas_call | solution.py:565
  60.2 2.3 %collective-permute-done.14.refs_0_.refs_3_ = bf16[272,512]{1,0:T(8,128)(2,1)S(1)} collective-permute-done((bf16[272,512]{1,0:T(8,128)(2,1)S(1)}, bf16[272,512]{1,0:T(8,128)(2,1)S(1)}, u32[]{:S(2)}, u32[]{:S(2)}) %collective-permute-start.14) | collective-permute-done | bytes 278560 | tf_op jit(solution)/shard_map/ppermute | solution.py:81
  63.1 1.5 %collective-permute-start.18 = (f32[8,1536]{1,0:T(8,128)S(1)}, f32[8,1536]{1,0:T(8,128)S(1)}, u32[]{:S(2)}, u32[]{:S(2)}) collective-permute-start(f32[8,1536]{1,0:T(8,128)S(1)} %get-tuple-element.70), channel_id=1, source_target_pairs={{0,2},{1,3},{2,0},{3,1},{4,6},{5,7},{6,4},{7,5},{8,10},{9,11},{10,... | collective-permute-start | bytes 147464 | tf_op jit(solution)/shard_map/ppermute | solution.py:698
  64.6 1.5 %collective-permute-start.19 = (f32[8,1536]{1,0:T(8,128)S(1)}, f32[8,1536]{1,0:T(8,128)S(1)}, u32[]{:S(2)}, u32[]{:S(2)}) collective-permute-start(f32[8,1536]{1,0:T(8,128)S(1)} %get-tuple-element.71), channel_id=1, source_target_pairs={{0,4},{1,5},{2,6},{3,7},{4,0},{5,1},{6,2},{7,3},{8,12},{9,13},{10,... | collective-permute-start | bytes 147464 | tf_op jit(solution)/shard_map/ppermute | solution.py:698
  67.3 1.4 %collective-permute-done.19.refs_2_ = f32[8,1536]{1,0:T(8,128)S(1)} collective-permute-done((f32[8,1536]{1,0:T(8,128)S(1)}, f32[8,1536]{1,0:T(8,128)S(1)}, u32[]{:S(2)}, u32[]{:S(2)}) %collective-permute-start.19) | collective-permute-done | bytes 49184 | tf_op jit(solution)/shard_map/ppermute | solution.py:698
  68.7 2.4 %collective-permute-done.20.refs_3_ = f32[8,1536]{1,0:T(8,128)S(1)} collective-permute-done((f32[8,1536]{1,0:T(8,128)S(1)}, f32[8,1536]{1,0:T(8,128)S(1)}, u32[]{:S(2)}, u32[]{:S(2)}) %collective-permute-start.20) | collective-permute-done | bytes 49184 | tf_op jit(solution)/shard_map/ppermute | solution.py:698
  71.1 2.0 %collective-permute-start.23 = (f32[8,1536]{1,0:T(8,128)S(1)}, f32[8,1536]{1,0:T(8,128)S(1)}, u32[]{:S(2)}, u32[]{:S(2)}) collective-permute-start(f32[8,1536]{1,0:T(8,128)S(1)} %shard_map.128.refs_0_), channel_id=1, source_target_pairs={{0,24},{8,16},{16,8},{24,0},{1,25},{9,17},{17,9},{25,1},{2,26},{10... | collective-permute-start | bytes 147464 | tf_op jit(solution)/shard_map/ppermute | solution.py:95
  74.2 1.3 %collective-permute-start.21 = (f32[8,1536]{1,0:T(8,128)S(1)}, f32[8,1536]{1,0:T(8,128)S(1)}, u32[]{:S(2)}, u32[]{:S(2)}) collective-permute-start(f32[8,1536]{1,0:T(8,128)S(1)} %shard_map.128.refs_0_), channel_id=1, source_target_pairs={{0,8},{8,0},{16,24},{24,16},{1,9},{9,1},{17,25},{25,17},{2,10},{10... | collective-permute-start | bytes 147464 | tf_op jit(solution)/shard_map/ppermute | solution.py:95
  76.6 2.6 %shard_map.126.refs_7_.refs_4_ = bf16[1,1,8,32,1536]{4,3,2,1,0:T(8,128)(2,1)} custom-call(s32[8]{0:T(128)S(1)} %concatenate.3.layout.refs_0_, f32[1,256,512]{2,1,0:T(8,128)S(1)} %get-tuple-element.55.refs_2_.refs_8_.refs_1_, bf16[272,512]{1,0:T(8,128)(2,1)S(1)} %collective-permute-done.13.refs_1_.refs_2_, ...), custom_call_target="tpu_custom_call" | custom-call | bytes 7380000 | tf_op jit(solution)/shard_map/pallas_call | solution.py:565
  79.8 1.5 %collective-permute-start.25 = (f32[8,1536]{1,0:T(8,128)S(1)}, f32[8,1536]{1,0:T(8,128)S(1)}, u32[]{:S(2)}, u32[]{:S(2)}) collective-permute-start(f32[8,1536]{1,0:T(8,128)S(1)} %shard_map.129.refs_1_), channel_id=1, source_target_pairs={{0,4},{1,5},{2,6},{3,7},{4,0},{5,1},{6,2},{7,3},{8,12},{9,13},{10,... | collective-permute-start | bytes 147464 | tf_op jit(solution)/shard_map/ppermute | solution.py:95
  81.3 1.5 %collective-permute-start.24 = (f32[8,1536]{1,0:T(8,128)S(1)}, f32[8,1536]{1,0:T(8,128)S(1)}, u32[]{:S(2)}, u32[]{:S(2)}) collective-permute-start(f32[8,1536]{1,0:T(8,128)S(1)} %shard_map.129.refs_1_), channel_id=1, source_target_pairs={{0,2},{1,3},{2,0},{3,1},{4,6},{5,7},{6,4},{7,5},{8,10},{9,11},{10,... | collective-permute-start | bytes 147464 | tf_op jit(solution)/shard_map/ppermute | solution.py:95
  82.8 4.0 %shard_map.127.refs_5_ = bf16[1,1,8,32,1536]{4,3,2,1,0:T(8,128)(2,1)} custom-call(s32[8]{0:T(128)S(1)} %concatenate.3.layout.refs_0_, f32[2,256,512]{2,1,0:T(8,128)S(1)} %get-tuple-element.60.refs_2_.refs_1_, bf16[272,512]{1,0:T(8,128)(2,1)S(1)} %collective-permute-done.13.refs_1_.refs_2_, ...), custom_call_target="tpu_custom_call", output_to_operand_aliasing={{}: (7, {})} | custom-call | bytes 14760000 | tf_op jit(solution)/shard_map/pallas_call | solution.py:565
  87.5 1.4 %collective-permute-done.27.refs_2_ = f32[4,8,1536]{2,1,0:T(8,128)S(1)} collective-permute-done((f32[4,8,1536]{2,1,0:T(8,128)S(1)}, f32[4,8,1536]{2,1,0:T(8,128)S(1)}, u32[]{:S(2)}, u32[]{:S(2)}) %collective-permute-start.27) | collective-permute-done | bytes 196640 | tf_op jit(solution)/shard_map/ppermute | solution.py:95
  88.9 1.3 %shard_map.131 = (f32[25,1536]{1,0:T(8,128)}, f32[32,1536]{1,0:T(8,128)}) custom-call(s32[8]{0:T(128)S(1)} %concatenate.3.layout.refs_0_, f32[4,8,1536]{2,1,0:T(8,128)S(1)} %shard_map.130.refs_1_, f32[4,8,1536]{2,1,0:T(8,128)S(1)} %collective-permute-done.27.refs_2_), custom_call_target="tpu_custom_call" | custom-call | bytes 2952000 | tf_op jit(solution)/shard_map/pallas_call | solution.py:565
  (49 shorter events, 13.7 us)
Async XLA Ops:
  0.6 12.2 %copy-start = (bf16[1,1,8,32,1536]{4,3,2,1,0:T(8,128)(2,1)S(1)}, bf16[1,1,8,32,1536]{4,3,2,1,0:T(8,128)(2,1)}, u32[]{:S(2)}) copy-start(bf16[1,1,8,32,1536]{4,3,2,1,0:T(8,128)(2,1)} %refs_5_.3) | copy-start | bytes 2359300
  4.6 14.1 %collective-permute-start = (bf16[2,64,512]{2,1,0:T(8,128)(2,1)S(1)}, bf16[2,64,512]{2,1,0:T(8,128)(2,1)S(1)}, u32[]{:S(2)}, u32[]{:S(2)}) collective-permute-start(bf16[2,64,512]{2,1,0:T(8,128)(2,1)S(1)} %get-tuple-element.39), channel_id=1, source_target_pairs={{0,8},{8,0},{16,24},{24,16},{1,9},{9,1},{17,25},{25,17},{2,10},{10... | collective-permute-start | bytes 393224 | tf_op jit(solution)/shard_map/ppermute | solution.py:89
  7.7 11.0 %collective-permute-start.1 = (bf16[2,64,512]{2,1,0:T(8,128)(2,1)S(1)}, bf16[2,64,512]{2,1,0:T(8,128)(2,1)S(1)}, u32[]{:S(2)}, u32[]{:S(2)}) collective-permute-start(bf16[2,64,512]{2,1,0:T(8,128)(2,1)S(1)} %get-tuple-element.40), channel_id=1, source_target_pairs={{0,16},{8,24},{16,0},{24,8},{1,17},{9,25},{17,1},{25,9},{2,18},{10... | collective-permute-start | bytes 393224 | tf_op jit(solution)/shard_map/ppermute | solution.py:89
  10.2 8.4 %collective-permute-start.2 = (bf16[2,64,512]{2,1,0:T(8,128)(2,1)S(1)}, bf16[2,64,512]{2,1,0:T(8,128)(2,1)S(1)}, u32[]{:S(2)}, u32[]{:S(2)}) collective-permute-start(bf16[2,64,512]{2,1,0:T(8,128)(2,1)S(1)} %get-tuple-element.41), channel_id=1, source_target_pairs={{0,0},{8,16},{16,8},{24,24},{1,1},{9,17},{17,9},{25,25},{2,2},{10,... | collective-permute-start | bytes 393224 | tf_op jit(solution)/shard_map/ppermute | solution.py:89
  10.9 7.7 %collective-permute-start.3 = (bf16[2,16,512]{2,1,0:T(8,128)(2,1)S(1)}, bf16[2,16,512]{2,1,0:T(8,128)(2,1)S(1)}, u32[]{:S(2)}, u32[]{:S(2)}) collective-permute-start(bf16[2,16,512]{2,1,0:T(8,128)(2,1)S(1)} %get-tuple-element.42), channel_id=1, source_target_pairs={{0,24},{8,8},{16,16},{24,0},{1,25},{9,9},{17,17},{25,1},{2,26},{10... | collective-permute-start | bytes 98312 | tf_op jit(solution)/shard_map/ppermute | solution.py:89
  18.7 20.3 %copy-start.1 = (bf16[1,1,8,32,1024]{4,3,2,1,0:T(8,128)(2,1)S(1)}, bf16[1,1,8,32,1024]{4,3,2,1,0:T(8,128)(2,1)}, u32[]{:S(2)}) copy-start(bf16[1,1,8,32,1024]{4,3,2,1,0:T(8,128)(2,1)} %refs_6_.1) | copy-start | bytes 1572868
  18.7 9.3 %collective-permute-start.8 = (bf16[144,512]{1,0:T(8,128)(2,1)S(1)}, bf16[144,512]{1,0:T(8,128)(2,1)S(1)}, u32[]{:S(2)}, u32[]{:S(2)}) collective-permute-start(bf16[144,512]{1,0:T(8,128)(2,1)S(1)} %get-tuple-element.49), channel_id=1, source_target_pairs={{0,16},{8,24},{16,0},{24,8},{1,17},{9,25},{17,1},{25,9},{2,18},{10... | collective-permute-start | bytes 442376 | tf_op jit(solution)/shard_map/ppermute | solution.py:81
  21.6 11.2 %collective-permute-start.7 = (bf16[144,512]{1,0:T(8,128)(2,1)S(1)}, bf16[144,512]{1,0:T(8,128)(2,1)S(1)}, u32[]{:S(2)}, u32[]{:S(2)}) collective-permute-start(bf16[144,512]{1,0:T(8,128)(2,1)S(1)} %get-tuple-element.48.refs_1_), channel_id=1, source_target_pairs={{0,8},{8,0},{16,24},{24,16},{1,9},{9,1},{17,25},{25,17},{2,10},{10... | collective-permute-start | bytes 442376 | tf_op jit(solution)/shard_map/ppermute | solution.py:81
  28.0 8.7 %collective-permute-start.9 = (bf16[144,512]{1,0:T(8,128)(2,1)S(1)}, bf16[144,512]{1,0:T(8,128)(2,1)S(1)}, u32[]{:S(2)}, u32[]{:S(2)}) collective-permute-start(bf16[144,512]{1,0:T(8,128)(2,1)S(1)} %shard_map.116), channel_id=1, source_target_pairs={{0,8},{8,0},{16,24},{24,16},{1,9},{9,1},{17,25},{25,17},{2,10},{10... | collective-permute-start | bytes 442376 | tf_op jit(solution)/shard_map/ppermute | solution.py:83
  28.4 10.6 %collective-permute-start.6 = (bf16[80,512]{1,0:T(8,128)(2,1)S(1)}, bf16[80,512]{1,0:T(8,128)(2,1)S(1)}, u32[]{:S(2)}, u32[]{:S(2)}) collective-permute-start(bf16[80,512]{1,0:T(8,128)(2,1)S(1)} %get-tuple-element.45.refs_1_), channel_id=1, source_target_pairs={{0,24},{8,16},{16,8},{24,0},{1,25},{9,17},{17,9},{25,1},{2,26},{10... | collective-permute-start | bytes 245768 | tf_op jit(solution)/shard_map/ppermute | solution.py:95
  30.4 8.6 %collective-permute-start.5 = (bf16[80,512]{1,0:T(8,128)(2,1)S(1)}, bf16[80,512]{1,0:T(8,128)(2,1)S(1)}, u32[]{:S(2)}, u32[]{:S(2)}) collective-permute-start(bf16[80,512]{1,0:T(8,128)(2,1)S(1)} %get-tuple-element.45.refs_1_), channel_id=1, source_target_pairs={{0,16},{8,24},{16,0},{24,8},{1,17},{9,25},{17,1},{25,9},{2,18},{10... | collective-permute-start | bytes 245768 | tf_op jit(solution)/shard_map/ppermute | solution.py:95
  31.5 7.4 %collective-permute-start.4 = (bf16[80,512]{1,0:T(8,128)(2,1)S(1)}, bf16[80,512]{1,0:T(8,128)(2,1)S(1)}, u32[]{:S(2)}, u32[]{:S(2)}) collective-permute-start(bf16[80,512]{1,0:T(8,128)(2,1)S(1)} %get-tuple-element.45.refs_1_), channel_id=1, source_target_pairs={{0,8},{8,0},{16,24},{24,16},{1,9},{9,1},{17,25},{25,17},{2,10},{10... | collective-permute-start | bytes 245768 | tf_op jit(solution)/shard_map/ppermute | solution.py:95
  41.5 8.2 %collective-permute-start.12 = (bf16[80,512]{1,0:T(8,128)(2,1)S(1)}, bf16[80,512]{1,0:T(8,128)(2,1)S(1)}, u32[]{:S(2)}, u32[]{:S(2)}) collective-permute-start(bf16[80,512]{1,0:T(8,128)(2,1)S(1)} %get-tuple-element.52.refs_7_.refs_1_), channel_id=1, source_target_pairs={{0,24},{8,16},{16,8},{24,0},{1,25},{9,17},{17,9},{25,1},{2,26},{10... | collective-permute-start | bytes 245768 | tf_op jit(solution)/shard_map/ppermute | solution.py:95
  43.5 6.3 %collective-permute-start.11 = (bf16[80,512]{1,0:T(8,128)(2,1)S(1)}, bf16[80,512]{1,0:T(8,128)(2,1)S(1)}, u32[]{:S(2)}, u32[]{:S(2)}) collective-permute-start(bf16[80,512]{1,0:T(8,128)(2,1)S(1)} %get-tuple-element.52.refs_7_.refs_1_), channel_id=1, source_target_pairs={{0,16},{8,24},{16,0},{24,8},{1,17},{9,25},{17,1},{25,9},{2,18},{10... | collective-permute-start | bytes 245768 | tf_op jit(solution)/shard_map/ppermute | solution.py:95
  43.5 6.3 %collective-permute-start.10 = (bf16[80,512]{1,0:T(8,128)(2,1)S(1)}, bf16[80,512]{1,0:T(8,128)(2,1)S(1)}, u32[]{:S(2)}, u32[]{:S(2)}) collective-permute-start(bf16[80,512]{1,0:T(8,128)(2,1)S(1)} %get-tuple-element.52.refs_7_.refs_1_), channel_id=1, source_target_pairs={{0,8},{8,0},{16,24},{24,16},{1,9},{9,1},{17,25},{25,17},{2,10},{10... | collective-permute-start | bytes 245768 | tf_op jit(solution)/shard_map/ppermute | solution.py:95
  52.1 10.5 %collective-permute-start.14 = (bf16[272,512]{1,0:T(8,128)(2,1)S(1)}, bf16[272,512]{1,0:T(8,128)(2,1)S(1)}, u32[]{:S(2)}, u32[]{:S(2)}) collective-permute-start(bf16[272,512]{1,0:T(8,128)(2,1)S(1)} %get-tuple-element.62), channel_id=1, source_target_pairs={{0,16},{8,24},{16,0},{24,8},{1,17},{9,25},{17,1},{25,9},{2,18},{10... | collective-permute-start | bytes 835592 | tf_op jit(solution)/shard_map/ppermute | solution.py:81
  53.4 9.2 %collective-permute-start.13 = (bf16[272,512]{1,0:T(8,128)(2,1)S(1)}, bf16[272,512]{1,0:T(8,128)(2,1)S(1)}, u32[]{:S(2)}, u32[]{:S(2)}) collective-permute-start(bf16[272,512]{1,0:T(8,128)(2,1)S(1)} %get-tuple-element.61.refs_1_), channel_id=1, source_target_pairs={{0,8},{8,0},{16,24},{24,16},{1,9},{9,1},{17,25},{25,17},{2,10},{10... | collective-permute-start | bytes 835592 | tf_op jit(solution)/shard_map/ppermute | solution.py:81
  58.2 1.5 %collective-permute-start.16 = (f32[4,8,1024]{2,1,0:T(8,128)S(1)}, f32[4,8,1024]{2,1,0:T(8,128)S(1)}, u32[]{:S(2)}, u32[]{:S(2)}) collective-permute-start(f32[4,8,1024]{2,1,0:T(8,128)S(1)} %get-tuple-element.67), channel_id=1, source_target_pairs={{0,1},{1,0},{2,3},{3,2},{4,5},{5,4},{6,7},{7,6},{8,9},{9,8},{10,11... | collective-permute-start | bytes 393224 | tf_op jit(solution)/shard_map/ppermute | solution.py:95
  58.2 1.4 %collective-permute-start.15 = (f32[4,8,512]{2,1,0:T(8,128)S(1)}, f32[4,8,512]{2,1,0:T(8,128)S(1)}, u32[]{:S(2)}, u32[]{:S(2)}) collective-permute-start(f32[4,8,512]{2,1,0:T(8,128)S(1)} %get-tuple-element.59.refs_10_), channel_id=1, source_target_pairs={{0,1},{1,0},{2,3},{3,2},{4,5},{5,4},{6,7},{7,6},{8,9},{9,8},{10,11... | collective-permute-start | bytes 196616 | tf_op jit(solution)/shard_map/ppermute | solution.py:95
  62.6 12.9 %collective-permute-start.17 = (bf16[272,512]{1,0:T(8,128)(2,1)S(1)}, bf16[272,512]{1,0:T(8,128)(2,1)S(1)}, u32[]{:S(2)}, u32[]{:S(2)}) collective-permute-start(bf16[272,512]{1,0:T(8,128)(2,1)S(1)} %shard_map.124), channel_id=1, source_target_pairs={{0,8},{8,0},{16,24},{24,16},{1,9},{9,1},{17,25},{25,17},{2,10},{10... | collective-permute-start | bytes 835592 | tf_op jit(solution)/shard_map/ppermute | solution.py:83
  63.1 4.2 %collective-permute-start.18 = (f32[8,1536]{1,0:T(8,128)S(1)}, f32[8,1536]{1,0:T(8,128)S(1)}, u32[]{:S(2)}, u32[]{:S(2)}) collective-permute-start(f32[8,1536]{1,0:T(8,128)S(1)} %get-tuple-element.70), channel_id=1, source_target_pairs={{0,2},{1,3},{2,0},{3,1},{4,6},{5,7},{6,4},{7,5},{8,10},{9,11},{10,... | collective-permute-start | bytes 147464 | tf_op jit(solution)/shard_map/ppermute | solution.py:698
  64.6 4.1 %collective-permute-start.19 = (f32[8,1536]{1,0:T(8,128)S(1)}, f32[8,1536]{1,0:T(8,128)S(1)}, u32[]{:S(2)}, u32[]{:S(2)}) collective-permute-start(f32[8,1536]{1,0:T(8,128)S(1)} %get-tuple-element.71), channel_id=1, source_target_pairs={{0,4},{1,5},{2,6},{3,7},{4,0},{5,1},{6,2},{7,3},{8,12},{9,13},{10,... | collective-permute-start | bytes 147464 | tf_op jit(solution)/shard_map/ppermute | solution.py:698
  66.1 5.0 %collective-permute-start.20 = (f32[8,1536]{1,0:T(8,128)S(1)}, f32[8,1536]{1,0:T(8,128)S(1)}, u32[]{:S(2)}, u32[]{:S(2)}) collective-permute-start(f32[8,1536]{1,0:T(8,128)S(1)} %get-tuple-element.72), channel_id=1, source_target_pairs={{0,6},{1,7},{2,4},{3,5},{4,2},{5,3},{6,0},{7,1},{8,14},{9,15},{10,... | collective-permute-start | bytes 147464 | tf_op jit(solution)/shard_map/ppermute | solution.py:698
  71.1 8.1 %collective-permute-start.23 = (f32[8,1536]{1,0:T(8,128)S(1)}, f32[8,1536]{1,0:T(8,128)S(1)}, u32[]{:S(2)}, u32[]{:S(2)}) collective-permute-start(f32[8,1536]{1,0:T(8,128)S(1)} %shard_map.128.refs_0_), channel_id=1, source_target_pairs={{0,24},{8,16},{16,8},{24,0},{1,25},{9,17},{17,9},{25,1},{2,26},{10... | collective-permute-start | bytes 147464 | tf_op jit(solution)/shard_map/ppermute | solution.py:95
  73.1 6.1 %collective-permute-start.22 = (f32[8,1536]{1,0:T(8,128)S(1)}, f32[8,1536]{1,0:T(8,128)S(1)}, u32[]{:S(2)}, u32[]{:S(2)}) collective-permute-start(f32[8,1536]{1,0:T(8,128)S(1)} %shard_map.128.refs_0_), channel_id=1, source_target_pairs={{0,16},{8,24},{16,0},{24,8},{1,17},{9,25},{17,1},{25,9},{2,18},{10... | collective-permute-start | bytes 147464 | tf_op jit(solution)/shard_map/ppermute | solution.py:95
  74.2 5.0 %collective-permute-start.21 = (f32[8,1536]{1,0:T(8,128)S(1)}, f32[8,1536]{1,0:T(8,128)S(1)}, u32[]{:S(2)}, u32[]{:S(2)}) collective-permute-start(f32[8,1536]{1,0:T(8,128)S(1)} %shard_map.128.refs_0_), channel_id=1, source_target_pairs={{0,8},{8,0},{16,24},{24,16},{1,9},{9,1},{17,25},{25,17},{2,10},{10... | collective-permute-start | bytes 147464 | tf_op jit(solution)/shard_map/ppermute | solution.py:95
  79.2 7.6 %collective-permute-start.26 = (f32[8,1536]{1,0:T(8,128)S(1)}, f32[8,1536]{1,0:T(8,128)S(1)}, u32[]{:S(2)}, u32[]{:S(2)}) collective-permute-start(f32[8,1536]{1,0:T(8,128)S(1)} %shard_map.129.refs_1_), channel_id=1, source_target_pairs={{0,6},{1,7},{2,4},{3,5},{4,2},{5,3},{6,0},{7,1},{8,14},{9,15},{10,... | collective-permute-start | bytes 147464 | tf_op jit(solution)/shard_map/ppermute | solution.py:95
  79.8 7.1 %collective-permute-start.25 = (f32[8,1536]{1,0:T(8,128)S(1)}, f32[8,1536]{1,0:T(8,128)S(1)}, u32[]{:S(2)}, u32[]{:S(2)}) collective-permute-start(f32[8,1536]{1,0:T(8,128)S(1)} %shard_map.129.refs_1_), channel_id=1, source_target_pairs={{0,4},{1,5},{2,6},{3,7},{4,0},{5,1},{6,2},{7,3},{8,12},{9,13},{10,... | collective-permute-start | bytes 147464 | tf_op jit(solution)/shard_map/ppermute | solution.py:95
  81.3 5.6 %collective-permute-start.24 = (f32[8,1536]{1,0:T(8,128)S(1)}, f32[8,1536]{1,0:T(8,128)S(1)}, u32[]{:S(2)}, u32[]{:S(2)}) collective-permute-start(f32[8,1536]{1,0:T(8,128)S(1)} %shard_map.129.refs_1_), channel_id=1, source_target_pairs={{0,2},{1,3},{2,0},{3,1},{4,6},{5,7},{6,4},{7,5},{8,10},{9,11},{10,... | collective-permute-start | bytes 147464 | tf_op jit(solution)/shard_map/ppermute | solution.py:95
  87.4 1.5 %collective-permute-start.27 = (f32[4,8,1536]{2,1,0:T(8,128)S(1)}, f32[4,8,1536]{2,1,0:T(8,128)S(1)}, u32[]{:S(2)}, u32[]{:S(2)}) collective-permute-start(f32[4,8,1536]{2,1,0:T(8,128)S(1)} %shard_map.130.refs_1_), channel_id=1, source_target_pairs={{0,1},{1,0},{2,3},{3,2},{4,5},{5,4},{6,7},{7,6},{8,9},{9,8},{10,11... | collective-permute-start | bytes 589832 | tf_op jit(solution)/shard_map/ppermute | solution.py:95

commit v7 on v6

--- a/solution.py
+++ b/solution.py
@@ -487,7 +487,11 @@
     parts, out_ref = [ref[...] for ref in refs[:-1]], refs[-1]
     while len(parts) > 1:
         parts = [parts[i] + parts[i + 1] for i in range(0, len(parts), 2)]
-    out_ref[...] = parts[0] * norm
+    total = parts[0] * norm
+    if out_ref.shape != total.shape:
+        half = total.shape[1] // 2
+        total = jnp.concatenate([total[:, :half], total[:, half:]], axis=0)
+    out_ref[...] = total.astype(out_ref.dtype)
 
 
 def collect_kernel(layout, *refs):
@@ -499,9 +503,14 @@
 
 def finish_kernel(taps, layout, own_ref, come_ref, dw_ref, pw_ref, whole_ref):
     odd = Place(layout).group % 2 == 1
-    quarters, rows = own_ref.shape[:2]
+    quarters, rows = own_ref.shape[0], own_ref.shape[1] // 2
+
+    def unfold(value):
+        value = value.astype(F32)
+        return jnp.concatenate([value[:rows], value[rows:]], axis=1)
+
     for part in range(quarters):
-        own, come = own_ref[part], come_ref[part]
+        own, come = unfold(own_ref[part]), unfold(come_ref[part])
         whole_ref[2 * part * rows : (2 * part + 1) * rows] = jnp.where(odd, come, own)
         whole_ref[(2 * part + 1) * rows : (2 * part + 2) * rows] = jnp.where(odd, own, come)
     dw_ref[...] = whole_ref[:taps]
@@ -730,12 +739,12 @@
     if halves:
         total = call(0.3, part(sum_kernel, 1.0), share_shape, [shares[0]] + moved)
         total = call(
-            0.3, part(sum_kernel, norm), share_shape, [total] + exchange(total, "tile"), after=(grad_query, grad0_kv)
+            0.3, part(sum_kernel, norm), narrow(2 * eighth, channels // 2), [total] + exchange(total, "tile"), after=(grad_query, grad0_kv)
         )
         quarters = call(
             0.5,
             collect_kernel,
-            wide(4, eighth, channels),
+            narrow(4, 2 * eighth, channels // 2),
             (layout, total, *exchange(total, "img", (2, 4, 6))),
             after=(in_hbm(grad_source),),
         )

time: 90.5 us -> 90.4 us (level)
  no operation moved by 1% of the time
where the time goes in v7:
time: 90.4 us; the launch traced here: 90.1 us
  starting transfers between devices  35.4 us (39%)
  Pallas kernels  32 us (35%)
  waiting for transfers between devices  19 us (21%)
  between operations  2.95 us (3%)
    pallas_call x19, Pallas kernels, call(): pl.pallas_call(body, in_specs=[pl.BlockSpec(memory_space=space) for space...  30.8 us
    ppermute x15, starting transfers between devices, exchange(): lax.ppermute(value, axis, [(s, s ^ m) for s in range(count)])  17.5 us
    ppermute x4, starting transfers between devices, move_direct(): lax.ppermute(part, 'tile', list(enumerate(to)))  8.26 us
    ppermute x4, starting transfers between devices, move(): lax.ppermute(part, 'tile', [(s, s ^ m) for s in range(count)])  5.4 us
    ppermute x3, waiting for transfers between devices, local(): lax.ppermute(share, 'img', [(s, s ^ 2 * m) for s in range(groups)])  4.53 us
    ppermute x4, waiting for transfers between devices, move_direct(): lax.ppermute(part, 'tile', list(enumerate(to)))  4.17 us
    ppermute x4, waiting for transfers between devices, move(): lax.ppermute(part, 'tile', [(s, s ^ m) for s in range(count)])  4.07 us
    ppermute x2, waiting for transfers between devices, move(): lax.ppermute(hand_on(near, far), 'tile', [(s, s ^ 1) for s in range(count)])  3.95 us
  transfers between devices with their start and end apart: 28, of which 9 were waited for; matrix products, arithmetic and copies ran while one was open for 0% of the time, Pallas kernels for 27%

profile of v7, /device:TPU:0, one launch (start us, length us, event | category | flops | bytes accessed | tf_op | source)
XLA Modules:
  0.0 90.1 jit_solution(7173568211570263724)
XLA Ops:
  4.6 3.1 %collective-permute-start = (bf16[2,64,512]{2,1,0:T(8,128)(2,1)S(1)}, bf16[2,64,512]{2,1,0:T(8,128)(2,1)S(1)}, u32[]{:S(2)}, u32[]{:S(2)}) collective-permute-start(bf16[2,64,512]{2,1,0:T(8,128)(2,1)S(1)} %get-tuple-element.39), channel_id=1, source_target_pairs={{0,8},{8,0},{16,24},{24,16},{1,9},{9,1},{17,25},{25,17},{2,10},{10... | collective-permute-start | bytes 393224 | tf_op jit(solution)/shard_map/ppermute | solution.py:89
  7.7 2.6 %collective-permute-start.1 = (bf16[2,64,512]{2,1,0:T(8,128)(2,1)S(1)}, bf16[2,64,512]{2,1,0:T(8,128)(2,1)S(1)}, u32[]{:S(2)}, u32[]{:S(2)}) collective-permute-start(bf16[2,64,512]{2,1,0:T(8,128)(2,1)S(1)} %get-tuple-element.40), channel_id=1, source_target_pairs={{0,16},{8,24},{16,0},{24,8},{1,17},{9,25},{17,1},{25,9},{2,18},{10... | collective-permute-start | bytes 393224 | tf_op jit(solution)/shard_map/ppermute | solution.py:89
  10.9 1.9 %collective-permute-start.3 = (bf16[2,16,512]{2,1,0:T(8,128)(2,1)S(1)}, bf16[2,16,512]{2,1,0:T(8,128)(2,1)S(1)}, u32[]{:S(2)}, u32[]{:S(2)}) collective-permute-start(bf16[2,16,512]{2,1,0:T(8,128)(2,1)S(1)} %get-tuple-element.42), channel_id=1, source_target_pairs={{0,24},{8,8},{16,16},{24,0},{1,25},{9,9},{17,17},{25,1},{2,26},{10... | collective-permute-start | bytes 98312 | tf_op jit(solution)/shard_map/ppermute | solution.py:89
  12.9 1.6 %shard_map.113 = (bf16[144,512]{1,0:T(8,128)(2,1)S(1)}, bf16[144,512]{1,0:T(8,128)(2,1)S(1)}, f32[25,1536]{1,0:T(8,128)S(1)}, f32[32,1536]{1,0:T(8,128)S(1)}) custom-call(s32[8]{0:T(128)S(1)} %concatenate.3.layout.refs_0_, bf16[1,1,8,32,1536]{4,3,2,1,0:T(8,128)(2,1)S(1)} %copy-done, f32[25,1536]{1,0:T(8,128)} %refs_2_.1, f32[32,1536]{1,0:T(8,128)} %refs_3_.1), custom_call_target="tpu_custom_call" | custom-call | bytes 3690000 | tf_op jit(solution)/shard_map/pallas_call | solution.py:574
  14.5 4.2 %collective-permute-done.3.refs_5_ = bf16[2,16,512]{2,1,0:T(8,128)(2,1)S(1)} collective-permute-done((bf16[2,16,512]{2,1,0:T(8,128)(2,1)S(1)}, bf16[2,16,512]{2,1,0:T(8,128)(2,1)S(1)}, u32[]{:S(2)}, u32[]{:S(2)}) %collective-permute-start.3) | collective-permute-done | bytes 32800 | tf_op jit(solution)/shard_map/ppermute | solution.py:89
  18.7 2.9 %collective-permute-start.8 = (bf16[144,512]{1,0:T(8,128)(2,1)S(1)}, bf16[144,512]{1,0:T(8,128)(2,1)S(1)}, u32[]{:S(2)}, u32[]{:S(2)}) collective-permute-start(bf16[144,512]{1,0:T(8,128)(2,1)S(1)} %get-tuple-element.49), channel_id=1, source_target_pairs={{0,16},{8,24},{16,0},{24,8},{1,17},{9,25},{17,1},{25,9},{2,18},{10... | collective-permute-start | bytes 442376 | tf_op jit(solution)/shard_map/ppermute | solution.py:81
  21.6 4.7 %shard_map.114 = (f32[2,256,512]{2,1,0:T(8,128)S(1)}, f32[2,256,512]{2,1,0:T(8,128)S(1)}, f32[2,12,40,512]{3,2,1,0:T(8,128)S(1)}, bf16[80,512]{1,0:T(8,128)(2,1)S(1)}) custom-call(s32[8]{0:T(128)S(1)} %concatenate.3.layout.refs_0_, bf16[1,1,8,32,1536]{4,3,2,1,0:T(8,128)(2,1)S(1)} %copy-done, bf16[2,64,512]{2,1,0:T(8,128)(2,1)S(1)} %collective-permute-done.refs_2_, ...), custom_call_target="tpu_custom_call" | custom-call | bytes 22140000 | tf_op jit(solution)/shard_map/pallas_call | solution.py:574
  26.2 1.7 %collective-permute-done.8.refs_0_.refs_3_ = bf16[144,512]{1,0:T(8,128)(2,1)S(1)} collective-permute-done((bf16[144,512]{1,0:T(8,128)(2,1)S(1)}, bf16[144,512]{1,0:T(8,128)(2,1)S(1)}, u32[]{:S(2)}, u32[]{:S(2)}) %collective-permute-start.8) | collective-permute-done | bytes 147488 | tf_op jit(solution)/shard_map/ppermute | solution.py:81
  28.4 2.0 %collective-permute-start.6 = (bf16[80,512]{1,0:T(8,128)(2,1)S(1)}, bf16[80,512]{1,0:T(8,128)(2,1)S(1)}, u32[]{:S(2)}, u32[]{:S(2)}) collective-permute-start(bf16[80,512]{1,0:T(8,128)(2,1)S(1)} %get-tuple-element.45.refs_1_), channel_id=1, source_target_pairs={{0,24},{8,16},{16,8},{24,0},{1,25},{9,17},{17,9},{25,1},{2,26},{10... | collective-permute-start | bytes 245768 | tf_op jit(solution)/shard_map/ppermute | solution.py:95
  32.7 4.0 %collective-permute-done.9.refs_4_ = bf16[144,512]{1,0:T(8,128)(2,1)S(1)} collective-permute-done((bf16[144,512]{1,0:T(8,128)(2,1)S(1)}, bf16[144,512]{1,0:T(8,128)(2,1)S(1)}, u32[]{:S(2)}, u32[]{:S(2)}) %collective-permute-start.9) | collective-permute-done | bytes 147488 | tf_op jit(solution)/shard_map/ppermute | solution.py:83
  36.7 2.3 %shard_map.117 = (f32[1,256,512]{2,1,0:T(8,128)S(1)}, f32[1,256,512]{2,1,0:T(8,128)S(1)}, f32[1,12,40,512]{3,2,1,0:T(8,128)S(1)}) custom-call(s32[8]{0:T(128)S(1)} %concatenate.3.layout.refs_0_, bf16[1,1,8,32,1536]{4,3,2,1,0:T(8,128)(2,1)S(1)} %copy-done, bf16[144,512]{1,0:T(8,128)(2,1)S(1)} %collective-permute-done.7.refs_2_, ...), custom_call_target="tpu_custom_call" | custom-call | bytes 11070000 | tf_op jit(solution)/shard_map/pallas_call | solution.py:574
  39.0 2.5 %shard_map.118 = (bf16[80,512]{1,0:T(8,128)(2,1)S(1)}, f32[1,256,512]{2,1,0:T(8,128)S(1)}, f32[1,32,512]{2,1,0:T(8,128)S(1)}) custom-call(s32[8]{0:T(128)S(1)} %concatenate.3.layout.refs_0_, bf16[80,512]{1,0:T(8,128)(2,1)S(1)} %get-tuple-element.45.refs_1_, bf16[80,512]{1,0:T(8,128)(2,1)S(1)} %collective-permute-done.4.refs_2_, ...), custom_call_target="tpu_custom_call" | custom-call | bytes 11070000 | tf_op jit(solution)/shard_map/pallas_call | solution.py:574
  41.5 2.0 %collective-permute-start.12 = (bf16[80,512]{1,0:T(8,128)(2,1)S(1)}, bf16[80,512]{1,0:T(8,128)(2,1)S(1)}, u32[]{:S(2)}, u32[]{:S(2)}) collective-permute-start(bf16[80,512]{1,0:T(8,128)(2,1)S(1)} %get-tuple-element.52.refs_7_.refs_1_), channel_id=1, source_target_pairs={{0,24},{8,16},{16,8},{24,0},{1,25},{9,17},{17,9},{25,1},{2,26},{10... | collective-permute-start | bytes 245768 | tf_op jit(solution)/shard_map/ppermute | solution.py:95
  43.5 2.5 %collective-permute-start.10 = (bf16[80,512]{1,0:T(8,128)(2,1)S(1)}, bf16[80,512]{1,0:T(8,128)(2,1)S(1)}, u32[]{:S(2)}, u32[]{:S(2)}) collective-permute-start(bf16[80,512]{1,0:T(8,128)(2,1)S(1)} %get-tuple-element.52.refs_7_.refs_1_), channel_id=1, source_target_pairs={{0,8},{8,0},{16,24},{24,16},{1,9},{9,1},{17,25},{25,17},{2,10},{10... | collective-permute-start | bytes 245768 | tf_op jit(solution)/shard_map/ppermute | solution.py:95
  46.0 2.0 %shard_map.120 = (f32[4,8,512]{2,1,0:T(8,128)S(1)}, f32[4,8,512]{2,1,0:T(8,128)S(1)}) custom-call(s32[8]{0:T(128)S(1)} %concatenate.3.layout.refs_0_, f32[1,12,40,512]{3,2,1,0:T(8,128)S(1)} %get-tuple-element.57.refs_1_, f32[1,256,512]{2,1,0:T(8,128)S(1)} %get-tuple-element.55.refs_2_.refs_8_.refs_1_, f32[1,32,512]{2,1,0:T(8,128)S(1)} %get-tuple-element.58.refs_3_), custom_call_target="tpu_custom_call" | custom-call | bytes 7380000 | tf_op jit(solution)/shard_map/pallas_call | solution.py:574
  47.9 1.8 %shard_map.119 = (f32[1,256,512]{2,1,0:T(8,128)S(1)}, bf16[80,512]{1,0:T(8,128)(2,1)S(1)}) custom-call(s32[8]{0:T(128)S(1)} %concatenate.3.layout.refs_0_, bf16[144,512]{1,0:T(8,128)(2,1)S(1)} %get-tuple-element.48.refs_1_, bf16[144,512]{1,0:T(8,128)(2,1)S(1)} %collective-permute-done.7.refs_2_, bf16[144,512]{1,0:T(8,128)(2,1)S(1)} %collective-permute-done.8.refs_0_.refs_3_, ...), custom_call_target="tpu_custom_call" | custom-call | bytes 9225000 | tf_op jit(solution)/shard_map/pallas_call | solution.py:574
  49.8 2.3 %shard_map.121 = (f32[2,256,512]{2,1,0:T(8,128)S(1)}, f32[2,32,512]{2,1,0:T(8,128)S(1)}, bf16[272,512]{1,0:T(8,128)(2,1)S(1)}, bf16[272,512]{1,0:T(8,128)(2,1)S(1)}) custom-call(s32[8]{0:T(128)S(1)} %concatenate.3.layout.refs_0_, bf16[80,512]{1,0:T(8,128)(2,1)S(1)} %get-tuple-element.52.refs_7_.refs_1_, bf16[80,512]{1,0:T(8,128)(2,1)S(1)} %collective-permute-done.10.refs_2_, ...), custom_call_target="tpu_custom_call" | custom-call | bytes 11070000 | tf_op jit(solution)/shard_map/pallas_call | solution.py:574
  52.1 1.3 %collective-permute-start.14 = (bf16[272,512]{1,0:T(8,128)(2,1)S(1)}, bf16[272,512]{1,0:T(8,128)(2,1)S(1)}, u32[]{:S(2)}, u32[]{:S(2)}) collective-permute-start(bf16[272,512]{1,0:T(8,128)(2,1)S(1)} %get-tuple-element.62), channel_id=1, source_target_pairs={{0,16},{8,24},{16,0},{24,8},{1,17},{9,25},{17,1},{25,9},{2,18},{10... | collective-permute-start | bytes 835592 | tf_op jit(solution)/shard_map/ppermute | solution.py:81
  54.6 3.6 %shard_map.122 = (f32[4,8,1024]{2,1,0:T(8,128)S(1)}, f32[4,8,1024]{2,1,0:T(8,128)S(1)}) custom-call(s32[8]{0:T(128)S(1)} %concatenate.3.layout.refs_0_, f32[2,12,40,512]{3,2,1,0:T(8,128)S(1)} %get-tuple-element.64.refs_1_, f32[2,256,512]{2,1,0:T(8,128)S(1)} %get-tuple-element.60.refs_2_.refs_1_, f32[2,32,512]{2,1,0:T(8,128)S(1)} %get-tuple-element.65.refs_3_), custom_call_target="tpu_custom_call" | custom-call | bytes 14760000 | tf_op jit(solution)/shard_map/pallas_call | solution.py:574
  60.2 2.3 %collective-permute-done.14.refs_0_.refs_3_ = bf16[272,512]{1,0:T(8,128)(2,1)S(1)} collective-permute-done((bf16[272,512]{1,0:T(8,128)(2,1)S(1)}, bf16[272,512]{1,0:T(8,128)(2,1)S(1)}, u32[]{:S(2)}, u32[]{:S(2)}) %collective-permute-start.14) | collective-permute-done | bytes 278560 | tf_op jit(solution)/shard_map/ppermute | solution.py:81
  63.1 1.5 %collective-permute-start.18 = (f32[8,1536]{1,0:T(8,128)S(1)}, f32[8,1536]{1,0:T(8,128)S(1)}, u32[]{:S(2)}, u32[]{:S(2)}) collective-permute-start(f32[8,1536]{1,0:T(8,128)S(1)} %get-tuple-element.70), channel_id=1, source_target_pairs={{0,2},{1,3},{2,0},{3,1},{4,6},{5,7},{6,4},{7,5},{8,10},{9,11},{10,... | collective-permute-start | bytes 147464 | tf_op jit(solution)/shard_map/ppermute | solution.py:707
  64.6 1.5 %collective-permute-start.19 = (f32[8,1536]{1,0:T(8,128)S(1)}, f32[8,1536]{1,0:T(8,128)S(1)}, u32[]{:S(2)}, u32[]{:S(2)}) collective-permute-start(f32[8,1536]{1,0:T(8,128)S(1)} %get-tuple-element.71), channel_id=1, source_target_pairs={{0,4},{1,5},{2,6},{3,7},{4,0},{5,1},{6,2},{7,3},{8,12},{9,13},{10,... | collective-permute-start | bytes 147464 | tf_op jit(solution)/shard_map/ppermute | solution.py:707
  67.3 1.4 %collective-permute-done.19.refs_2_ = f32[8,1536]{1,0:T(8,128)S(1)} collective-permute-done((f32[8,1536]{1,0:T(8,128)S(1)}, f32[8,1536]{1,0:T(8,128)S(1)}, u32[]{:S(2)}, u32[]{:S(2)}) %collective-permute-start.19) | collective-permute-done | bytes 49184 | tf_op jit(solution)/shard_map/ppermute | solution.py:707
  68.7 2.4 %collective-permute-done.20.refs_3_ = f32[8,1536]{1,0:T(8,128)S(1)} collective-permute-done((f32[8,1536]{1,0:T(8,128)S(1)}, f32[8,1536]{1,0:T(8,128)S(1)}, u32[]{:S(2)}, u32[]{:S(2)}) %collective-permute-start.20) | collective-permute-done | bytes 49184 | tf_op jit(solution)/shard_map/ppermute | solution.py:707
  71.1 2.0 %collective-permute-start.23 = (f32[8,1536]{1,0:T(8,128)S(1)}, f32[8,1536]{1,0:T(8,128)S(1)}, u32[]{:S(2)}, u32[]{:S(2)}) collective-permute-start(f32[8,1536]{1,0:T(8,128)S(1)} %shard_map.128.refs_0_), channel_id=1, source_target_pairs={{0,24},{8,16},{16,8},{24,0},{1,25},{9,17},{17,9},{25,1},{2,26},{10... | collective-permute-start | bytes 147464 | tf_op jit(solution)/shard_map/ppermute | solution.py:95
  74.2 1.3 %collective-permute-start.21 = (f32[8,1536]{1,0:T(8,128)S(1)}, f32[8,1536]{1,0:T(8,128)S(1)}, u32[]{:S(2)}, u32[]{:S(2)}) collective-permute-start(f32[8,1536]{1,0:T(8,128)S(1)} %shard_map.128.refs_0_), channel_id=1, source_target_pairs={{0,8},{8,0},{16,24},{24,16},{1,9},{9,1},{17,25},{25,17},{2,10},{10... | collective-permute-start | bytes 147464 | tf_op jit(solution)/shard_map/ppermute | solution.py:95
  76.6 2.6 %shard_map.126.refs_7_.refs_4_ = bf16[1,1,8,32,1536]{4,3,2,1,0:T(8,128)(2,1)} custom-call(s32[8]{0:T(128)S(1)} %concatenate.3.layout.refs_0_, f32[1,256,512]{2,1,0:T(8,128)S(1)} %get-tuple-element.55.refs_2_.refs_8_.refs_1_, bf16[272,512]{1,0:T(8,128)(2,1)S(1)} %collective-permute-done.13.refs_1_.refs_2_, ...), custom_call_target="tpu_custom_call" | custom-call | bytes 7380000 | tf_op jit(solution)/shard_map/pallas_call | solution.py:574
  79.8 1.5 %collective-permute-start.25 = (bf16[16,768]{1,0:T(8,128)(2,1)S(1)}, bf16[16,768]{1,0:T(8,128)(2,1)S(1)}, u32[]{:S(2)}, u32[]{:S(2)}) collective-permute-start(bf16[16,768]{1,0:T(8,128)(2,1)S(1)} %shard_map.129.refs_1_), channel_id=1, source_target_pairs={{0,4},{1,5},{2,6},{3,7},{4,0},{5,1},{6,2},{7,3},{8,12},{9,13},{10,... | collective-permute-start | bytes 73736 | tf_op jit(solution)/shard_map/ppermute | solution.py:95
  81.3 1.5 %collective-permute-start.24 = (bf16[16,768]{1,0:T(8,128)(2,1)S(1)}, bf16[16,768]{1,0:T(8,128)(2,1)S(1)}, u32[]{:S(2)}, u32[]{:S(2)}) collective-permute-start(bf16[16,768]{1,0:T(8,128)(2,1)S(1)} %shard_map.129.refs_1_), channel_id=1, source_target_pairs={{0,2},{1,3},{2,0},{3,1},{4,6},{5,7},{6,4},{7,5},{8,10},{9,11},{10,... | collective-permute-start | bytes 73736 | tf_op jit(solution)/shard_map/ppermute | solution.py:95
  82.8 4.0 %shard_map.127.refs_5_ = bf16[1,1,8,32,1536]{4,3,2,1,0:T(8,128)(2,1)} custom-call(s32[8]{0:T(128)S(1)} %concatenate.3.layout.refs_0_, f32[2,256,512]{2,1,0:T(8,128)S(1)} %get-tuple-element.60.refs_2_.refs_1_, bf16[272,512]{1,0:T(8,128)(2,1)S(1)} %collective-permute-done.13.refs_1_.refs_2_, ...), custom_call_target="tpu_custom_call", output_to_operand_aliasing={{}: (7, {})} | custom-call | bytes 14760000 | tf_op jit(solution)/shard_map/pallas_call | solution.py:574
  87.5 1.3 %collective-permute-done.27.refs_2_ = bf16[4,16,768]{2,1,0:T(8,128)(2,1)S(1)} collective-permute-done((bf16[4,16,768]{2,1,0:T(8,128)(2,1)S(1)}, bf16[4,16,768]{2,1,0:T(8,128)(2,1)S(1)}, u32[]{:S(2)}, u32[]{:S(2)}) %collective-permute-start.27) | collective-permute-done | bytes 98336 | tf_op jit(solution)/shard_map/ppermute | solution.py:95
  88.8 1.3 %shard_map.131 = (f32[25,1536]{1,0:T(8,128)}, f32[32,1536]{1,0:T(8,128)}) custom-call(s32[8]{0:T(128)S(1)} %concatenate.3.layout.refs_0_, bf16[4,16,768]{2,1,0:T(8,128)(2,1)S(1)} %shard_map.130.refs_1_, bf16[4,16,768]{2,1,0:T(8,128)(2,1)S(1)} %collective-permute-done.27.refs_2_), custom_call_target="tpu_custom_call" | custom-call | bytes 2952000 | tf_op jit(solution)/shard_map/pallas_call | solution.py:574
  (49 shorter events, 13.7 us)
Async XLA Ops:
  0.6 12.2 %copy-start = (bf16[1,1,8,32,1536]{4,3,2,1,0:T(8,128)(2,1)S(1)}, bf16[1,1,8,32,1536]{4,3,2,1,0:T(8,128)(2,1)}, u32[]{:S(2)}) copy-start(bf16[1,1,8,32,1536]{4,3,2,1,0:T(8,128)(2,1)} %refs_5_.3) | copy-start | bytes 2359300
  4.6 14.1 %collective-permute-start = (bf16[2,64,512]{2,1,0:T(8,128)(2,1)S(1)}, bf16[2,64,512]{2,1,0:T(8,128)(2,1)S(1)}, u32[]{:S(2)}, u32[]{:S(2)}) collective-permute-start(bf16[2,64,512]{2,1,0:T(8,128)(2,1)S(1)} %get-tuple-element.39), channel_id=1, source_target_pairs={{0,8},{8,0},{16,24},{24,16},{1,9},{9,1},{17,25},{25,17},{2,10},{10... | collective-permute-start | bytes 393224 | tf_op jit(solution)/shard_map/ppermute | solution.py:89
  7.7 11.0 %collective-permute-start.1 = (bf16[2,64,512]{2,1,0:T(8,128)(2,1)S(1)}, bf16[2,64,512]{2,1,0:T(8,128)(2,1)S(1)}, u32[]{:S(2)}, u32[]{:S(2)}) collective-permute-start(bf16[2,64,512]{2,1,0:T(8,128)(2,1)S(1)} %get-tuple-element.40), channel_id=1, source_target_pairs={{0,16},{8,24},{16,0},{24,8},{1,17},{9,25},{17,1},{25,9},{2,18},{10... | collective-permute-start | bytes 393224 | tf_op jit(solution)/shard_map/ppermute | solution.py:89
  10.2 8.4 %collective-permute-start.2 = (bf16[2,64,512]{2,1,0:T(8,128)(2,1)S(1)}, bf16[2,64,512]{2,1,0:T(8,128)(2,1)S(1)}, u32[]{:S(2)}, u32[]{:S(2)}) collective-permute-start(bf16[2,64,512]{2,1,0:T(8,128)(2,1)S(1)} %get-tuple-element.41), channel_id=1, source_target_pairs={{0,0},{8,16},{16,8},{24,24},{1,1},{9,17},{17,9},{25,25},{2,2},{10,... | collective-permute-start | bytes 393224 | tf_op jit(solution)/shard_map/ppermute | solution.py:89
  10.9 7.7 %collective-permute-start.3 = (bf16[2,16,512]{2,1,0:T(8,128)(2,1)S(1)}, bf16[2,16,512]{2,1,0:T(8,128)(2,1)S(1)}, u32[]{:S(2)}, u32[]{:S(2)}) collective-permute-start(bf16[2,16,512]{2,1,0:T(8,128)(2,1)S(1)} %get-tuple-element.42), channel_id=1, source_target_pairs={{0,24},{8,8},{16,16},{24,0},{1,25},{9,9},{17,17},{25,1},{2,26},{10... | collective-permute-start | bytes 98312 | tf_op jit(solution)/shard_map/ppermute | solution.py:89
  18.7 20.3 %copy-start.1 = (bf16[1,1,8,32,1024]{4,3,2,1,0:T(8,128)(2,1)S(1)}, bf16[1,1,8,32,1024]{4,3,2,1,0:T(8,128)(2,1)}, u32[]{:S(2)}) copy-start(bf16[1,1,8,32,1024]{4,3,2,1,0:T(8,128)(2,1)} %refs_6_.1) | copy-start | bytes 1572868
  18.7 9.3 %collective-permute-start.8 = (bf16[144,512]{1,0:T(8,128)(2,1)S(1)}, bf16[144,512]{1,0:T(8,128)(2,1)S(1)}, u32[]{:S(2)}, u32[]{:S(2)}) collective-permute-start(bf16[144,512]{1,0:T(8,128)(2,1)S(1)} %get-tuple-element.49), channel_id=1, source_target_pairs={{0,16},{8,24},{16,0},{24,8},{1,17},{9,25},{17,1},{25,9},{2,18},{10... | collective-permute-start | bytes 442376 | tf_op jit(solution)/shard_map/ppermute | solution.py:81
  21.6 11.2 %collective-permute-start.7 = (bf16[144,512]{1,0:T(8,128)(2,1)S(1)}, bf16[144,512]{1,0:T(8,128)(2,1)S(1)}, u32[]{:S(2)}, u32[]{:S(2)}) collective-permute-start(bf16[144,512]{1,0:T(8,128)(2,1)S(1)} %get-tuple-element.48.refs_1_), channel_id=1, source_target_pairs={{0,8},{8,0},{16,24},{24,16},{1,9},{9,1},{17,25},{25,17},{2,10},{10... | collective-permute-start | bytes 442376 | tf_op jit(solution)/shard_map/ppermute | solution.py:81
  28.0 8.7 %collective-permute-start.9 = (bf16[144,512]{1,0:T(8,128)(2,1)S(1)}, bf16[144,512]{1,0:T(8,128)(2,1)S(1)}, u32[]{:S(2)}, u32[]{:S(2)}) collective-permute-start(bf16[144,512]{1,0:T(8,128)(2,1)S(1)} %shard_map.116), channel_id=1, source_target_pairs={{0,8},{8,0},{16,24},{24,16},{1,9},{9,1},{17,25},{25,17},{2,10},{10... | collective-permute-start | bytes 442376 | tf_op jit(solution)/shard_map/ppermute | solution.py:83
  28.4 10.6 %collective-permute-start.6 = (bf16[80,512]{1,0:T(8,128)(2,1)S(1)}, bf16[80,512]{1,0:T(8,128)(2,1)S(1)}, u32[]{:S(2)}, u32[]{:S(2)}) collective-permute-start(bf16[80,512]{1,0:T(8,128)(2,1)S(1)} %get-tuple-element.45.refs_1_), channel_id=1, source_target_pairs={{0,24},{8,16},{16,8},{24,0},{1,25},{9,17},{17,9},{25,1},{2,26},{10... | collective-permute-start | bytes 245768 | tf_op jit(solution)/shard_map/ppermute | solution.py:95
  30.4 8.6 %collective-permute-start.5 = (bf16[80,512]{1,0:T(8,128)(2,1)S(1)}, bf16[80,512]{1,0:T(8,128)(2,1)S(1)}, u32[]{:S(2)}, u32[]{:S(2)}) collective-permute-start(bf16[80,512]{1,0:T(8,128)(2,1)S(1)} %get-tuple-element.45.refs_1_), channel_id=1, source_target_pairs={{0,16},{8,24},{16,0},{24,8},{1,17},{9,25},{17,1},{25,9},{2,18},{10... | collective-permute-start | bytes 245768 | tf_op jit(solution)/shard_map/ppermute | solution.py:95
  31.5 7.4 %collective-permute-start.4 = (bf16[80,512]{1,0:T(8,128)(2,1)S(1)}, bf16[80,512]{1,0:T(8,128)(2,1)S(1)}, u32[]{:S(2)}, u32[]{:S(2)}) collective-permute-start(bf16[80,512]{1,0:T(8,128)(2,1)S(1)} %get-tuple-element.45.refs_1_), channel_id=1, source_target_pairs={{0,8},{8,0},{16,24},{24,16},{1,9},{9,1},{17,25},{25,17},{2,10},{10... | collective-permute-start | bytes 245768 | tf_op jit(solution)/shard_map/ppermute | solution.py:95
  41.5 8.2 %collective-permute-start.12 = (bf16[80,512]{1,0:T(8,128)(2,1)S(1)}, bf16[80,512]{1,0:T(8,128)(2,1)S(1)}, u32[]{:S(2)}, u32[]{:S(2)}) collective-permute-start(bf16[80,512]{1,0:T(8,128)(2,1)S(1)} %get-tuple-element.52.refs_7_.refs_1_), channel_id=1, source_target_pairs={{0,24},{8,16},{16,8},{24,0},{1,25},{9,17},{17,9},{25,1},{2,26},{10... | collective-permute-start | bytes 245768 | tf_op jit(solution)/shard_map/ppermute | solution.py:95
  43.5 6.3 %collective-permute-start.11 = (bf16[80,512]{1,0:T(8,128)(2,1)S(1)}, bf16[80,512]{1,0:T(8,128)(2,1)S(1)}, u32[]{:S(2)}, u32[]{:S(2)}) collective-permute-start(bf16[80,512]{1,0:T(8,128)(2,1)S(1)} %get-tuple-element.52.refs_7_.refs_1_), channel_id=1, source_target_pairs={{0,16},{8,24},{16,0},{24,8},{1,17},{9,25},{17,1},{25,9},{2,18},{10... | collective-permute-start | bytes 245768 | tf_op jit(solution)/shard_map/ppermute | solution.py:95
  43.5 6.3 %collective-permute-start.10 = (bf16[80,512]{1,0:T(8,128)(2,1)S(1)}, bf16[80,512]{1,0:T(8,128)(2,1)S(1)}, u32[]{:S(2)}, u32[]{:S(2)}) collective-permute-start(bf16[80,512]{1,0:T(8,128)(2,1)S(1)} %get-tuple-element.52.refs_7_.refs_1_), channel_id=1, source_target_pairs={{0,8},{8,0},{16,24},{24,16},{1,9},{9,1},{17,25},{25,17},{2,10},{10... | collective-permute-start | bytes 245768 | tf_op jit(solution)/shard_map/ppermute | solution.py:95
  52.1 10.5 %collective-permute-start.14 = (bf16[272,512]{1,0:T(8,128)(2,1)S(1)}, bf16[272,512]{1,0:T(8,128)(2,1)S(1)}, u32[]{:S(2)}, u32[]{:S(2)}) collective-permute-start(bf16[272,512]{1,0:T(8,128)(2,1)S(1)} %get-tuple-element.62), channel_id=1, source_target_pairs={{0,16},{8,24},{16,0},{24,8},{1,17},{9,25},{17,1},{25,9},{2,18},{10... | collective-permute-start | bytes 835592 | tf_op jit(solution)/shard_map/ppermute | solution.py:81
  53.4 9.2 %collective-permute-start.13 = (bf16[272,512]{1,0:T(8,128)(2,1)S(1)}, bf16[272,512]{1,0:T(8,128)(2,1)S(1)}, u32[]{:S(2)}, u32[]{:S(2)}) collective-permute-start(bf16[272,512]{1,0:T(8,128)(2,1)S(1)} %get-tuple-element.61.refs_1_), channel_id=1, source_target_pairs={{0,8},{8,0},{16,24},{24,16},{1,9},{9,1},{17,25},{25,17},{2,10},{10... | collective-permute-start | bytes 835592 | tf_op jit(solution)/shard_map/ppermute | solution.py:81
  58.2 1.5 %collective-permute-start.16 = (f32[4,8,1024]{2,1,0:T(8,128)S(1)}, f32[4,8,1024]{2,1,0:T(8,128)S(1)}, u32[]{:S(2)}, u32[]{:S(2)}) collective-permute-start(f32[4,8,1024]{2,1,0:T(8,128)S(1)} %get-tuple-element.67), channel_id=1, source_target_pairs={{0,1},{1,0},{2,3},{3,2},{4,5},{5,4},{6,7},{7,6},{8,9},{9,8},{10,11... | collective-permute-start | bytes 393224 | tf_op jit(solution)/shard_map/ppermute | solution.py:95
  58.2 1.4 %collective-permute-start.15 = (f32[4,8,512]{2,1,0:T(8,128)S(1)}, f32[4,8,512]{2,1,0:T(8,128)S(1)}, u32[]{:S(2)}, u32[]{:S(2)}) collective-permute-start(f32[4,8,512]{2,1,0:T(8,128)S(1)} %get-tuple-element.59.refs_10_), channel_id=1, source_target_pairs={{0,1},{1,0},{2,3},{3,2},{4,5},{5,4},{6,7},{7,6},{8,9},{9,8},{10,11... | collective-permute-start | bytes 196616 | tf_op jit(solution)/shard_map/ppermute | solution.py:95
  62.6 12.9 %collective-permute-start.17 = (bf16[272,512]{1,0:T(8,128)(2,1)S(1)}, bf16[272,512]{1,0:T(8,128)(2,1)S(1)}, u32[]{:S(2)}, u32[]{:S(2)}) collective-permute-start(bf16[272,512]{1,0:T(8,128)(2,1)S(1)} %shard_map.124), channel_id=1, source_target_pairs={{0,8},{8,0},{16,24},{24,16},{1,9},{9,1},{17,25},{25,17},{2,10},{10... | collective-permute-start | bytes 835592 | tf_op jit(solution)/shard_map/ppermute | solution.py:83
  63.1 4.2 %collective-permute-start.18 = (f32[8,1536]{1,0:T(8,128)S(1)}, f32[8,1536]{1,0:T(8,128)S(1)}, u32[]{:S(2)}, u32[]{:S(2)}) collective-permute-start(f32[8,1536]{1,0:T(8,128)S(1)} %get-tuple-element.70), channel_id=1, source_target_pairs={{0,2},{1,3},{2,0},{3,1},{4,6},{5,7},{6,4},{7,5},{8,10},{9,11},{10,... | collective-permute-start | bytes 147464 | tf_op jit(solution)/shard_map/ppermute | solution.py:707
  64.6 4.1 %collective-permute-start.19 = (f32[8,1536]{1,0:T(8,128)S(1)}, f32[8,1536]{1,0:T(8,128)S(1)}, u32[]{:S(2)}, u32[]{:S(2)}) collective-permute-start(f32[8,1536]{1,0:T(8,128)S(1)} %get-tuple-element.71), channel_id=1, source_target_pairs={{0,4},{1,5},{2,6},{3,7},{4,0},{5,1},{6,2},{7,3},{8,12},{9,13},{10,... | collective-permute-start | bytes 147464 | tf_op jit(solution)/shard_map/ppermute | solution.py:707
  66.1 5.0 %collective-permute-start.20 = (f32[8,1536]{1,0:T(8,128)S(1)}, f32[8,1536]{1,0:T(8,128)S(1)}, u32[]{:S(2)}, u32[]{:S(2)}) collective-permute-start(f32[8,1536]{1,0:T(8,128)S(1)} %get-tuple-element.72), channel_id=1, source_target_pairs={{0,6},{1,7},{2,4},{3,5},{4,2},{5,3},{6,0},{7,1},{8,14},{9,15},{10,... | collective-permute-start | bytes 147464 | tf_op jit(solution)/shard_map/ppermute | solution.py:707
  71.1 8.1 %collective-permute-start.23 = (f32[8,1536]{1,0:T(8,128)S(1)}, f32[8,1536]{1,0:T(8,128)S(1)}, u32[]{:S(2)}, u32[]{:S(2)}) collective-permute-start(f32[8,1536]{1,0:T(8,128)S(1)} %shard_map.128.refs_0_), channel_id=1, source_target_pairs={{0,24},{8,16},{16,8},{24,0},{1,25},{9,17},{17,9},{25,1},{2,26},{10... | collective-permute-start | bytes 147464 | tf_op jit(solution)/shard_map/ppermute | solution.py:95
  73.1 6.1 %collective-permute-start.22 = (f32[8,1536]{1,0:T(8,128)S(1)}, f32[8,1536]{1,0:T(8,128)S(1)}, u32[]{:S(2)}, u32[]{:S(2)}) collective-permute-start(f32[8,1536]{1,0:T(8,128)S(1)} %shard_map.128.refs_0_), channel_id=1, source_target_pairs={{0,16},{8,24},{16,0},{24,8},{1,17},{9,25},{17,1},{25,9},{2,18},{10... | collective-permute-start | bytes 147464 | tf_op jit(solution)/shard_map/ppermute | solution.py:95
  74.2 5.0 %collective-permute-start.21 = (f32[8,1536]{1,0:T(8,128)S(1)}, f32[8,1536]{1,0:T(8,128)S(1)}, u32[]{:S(2)}, u32[]{:S(2)}) collective-permute-start(f32[8,1536]{1,0:T(8,128)S(1)} %shard_map.128.refs_0_), channel_id=1, source_target_pairs={{0,8},{8,0},{16,24},{24,16},{1,9},{9,1},{17,25},{25,17},{2,10},{10... | collective-permute-start | bytes 147464 | tf_op jit(solution)/shard_map/ppermute | solution.py:95
  79.2 7.6 %collective-permute-start.26 = (bf16[16,768]{1,0:T(8,128)(2,1)S(1)}, bf16[16,768]{1,0:T(8,128)(2,1)S(1)}, u32[]{:S(2)}, u32[]{:S(2)}) collective-permute-start(bf16[16,768]{1,0:T(8,128)(2,1)S(1)} %shard_map.129.refs_1_), channel_id=1, source_target_pairs={{0,6},{1,7},{2,4},{3,5},{4,2},{5,3},{6,0},{7,1},{8,14},{9,15},{10,... | collective-permute-start | bytes 73736 | tf_op jit(solution)/shard_map/ppermute | solution.py:95
  79.8 7.1 %collective-permute-start.25 = (bf16[16,768]{1,0:T(8,128)(2,1)S(1)}, bf16[16,768]{1,0:T(8,128)(2,1)S(1)}, u32[]{:S(2)}, u32[]{:S(2)}) collective-permute-start(bf16[16,768]{1,0:T(8,128)(2,1)S(1)} %shard_map.129.refs_1_), channel_id=1, source_target_pairs={{0,4},{1,5},{2,6},{3,7},{4,0},{5,1},{6,2},{7,3},{8,12},{9,13},{10,... | collective-permute-start | bytes 73736 | tf_op jit(solution)/shard_map/ppermute | solution.py:95
  81.3 5.6 %collective-permute-start.24 = (bf16[16,768]{1,0:T(8,128)(2,1)S(1)}, bf16[16,768]{1,0:T(8,128)(2,1)S(1)}, u32[]{:S(2)}, u32[]{:S(2)}) collective-permute-start(bf16[16,768]{1,0:T(8,128)(2,1)S(1)} %shard_map.129.refs_1_), channel_id=1, source_target_pairs={{0,2},{1,3},{2,0},{3,1},{4,6},{5,7},{6,4},{7,5},{8,10},{9,11},{10,... | collective-permute-start | bytes 73736 | tf_op jit(solution)/shard_map/ppermute | solution.py:95
  87.4 1.4 %collective-permute-start.27 = (bf16[4,16,768]{2,1,0:T(8,128)(2,1)S(1)}, bf16[4,16,768]{2,1,0:T(8,128)(2,1)S(1)}, u32[]{:S(2)}, u32[]{:S(2)}) collective-permute-start(bf16[4,16,768]{2,1,0:T(8,128)(2,1)S(1)} %shard_map.130.refs_1_), channel_id=1, source_target_pairs={{0,1},{1,0},{2,3},{3,2},{4,5},{5,4},{6,7},{7,6},{8,9},{9,8},{10,11... | collective-permute-start | bytes 294920 | tf_op jit(solution)/shard_map/ppermute | solution.py:95
